TPU v7x, 512 devices: a whole 4x4x16 slice. The times are simulated.
512 devices in a mesh: rows: 32 (over z_lo, y, core), gz: 16 (over z_hi, x).
Axes of the slice: x: 4, y: 4, z: 16 (z_hi: 4, z_lo: 4; z = z_hi * 4 + z_lo), core: 2. Of those that a mesh axis runs over, the one named last changes fastest.
Arguments:
- plane_colour_samples: int32 [32, 3, 1024, 2048], P('gz', None, 'rows'), may hold values from 0 to 255
- clarity_gain: float32 [32], P('gz'), may hold values from 0.01 to 4
Outputs:
- joined: float32 [3, 1024, 2048], P(None, 'rows')
All inputs are finite; a program needn't handle non-finite values.
Results may differ from a plain program's by a relative error of at most 0.000067.
Values sent between devices are 32-bit elements; how exact they have to be, the bound alone decides.
No kernel may reach another device: no remote copies, remote signals or barrier semaphores. Data moves between devices by JAX's collectives and lax.ppermute only.
A program may use at most 64 MiB of HBM per device.

v0:
```python
import jax
import jax.numpy as jnp
from jax import lax
from jax.sharding import PartitionSpec as P


def extended(block, sides, width):
    for axis, dim in sides:
        count = lax.axis_size(axis)
        forward = [(i, i + 1) for i in range(count - 1)]
        backward = [(target, source) for source, target in forward]
        low = lax.ppermute(
            lax.slice_in_dim(block, block.shape[dim] - width, None, axis=dim), axis, forward
        )
        high = lax.ppermute(lax.slice_in_dim(block, 0, width, axis=dim), axis, backward)
        block = jnp.concatenate([low, block, high], axis=dim)
    return block


def blur_rows(padded_image, count):
    return (
        padded_image[..., 0:count, :]
        + 4.0 * padded_image[..., 1 : count + 1, :]
        + 6.0 * padded_image[..., 2 : count + 2, :]
        + 4.0 * padded_image[..., 3 : count + 3, :]
        + padded_image[..., 4 : count + 4, :]
    ) / 16.0


def blur_cols(field):
    count = field.shape[-1]
    padded_image = jnp.pad(field, [(0, 0)] * (field.ndim - 1) + [(2, 2)])
    return (
        padded_image[..., 0:count]
        + 4.0 * padded_image[..., 1 : count + 1]
        + 6.0 * padded_image[..., 2 : count + 2]
        + 4.0 * padded_image[..., 3 : count + 3]
        + padded_image[..., 4 : count + 4]
    ) / 16.0


def upsampled_rows(padded_image, count):
    even = (
        padded_image[..., 0:count, :]
        + 6.0 * padded_image[..., 1 : count + 1, :]
        + padded_image[..., 2 : count + 2, :]
    ) / 8.0
    odd = (padded_image[..., 1 : count + 1, :] + padded_image[..., 2 : count + 2, :]) / 2.0
    shape = even.shape[:-2] + (2 * count, even.shape[-1])
    return jnp.stack([even, odd], axis=-2).reshape(shape)


def up_cols(field):
    count = field.shape[-1]
    padded_image = jnp.pad(field, [(0, 0)] * (field.ndim - 1) + [(1, 1)])
    even = (
        padded_image[..., 0:count]
        + 6.0 * padded_image[..., 1 : count + 1]
        + padded_image[..., 2 : count + 2]
    ) / 8.0
    odd = (padded_image[..., 1 : count + 1] + padded_image[..., 2 : count + 2]) / 2.0
    shape = field.shape[:-1] + (2 * count,)
    return jnp.stack([even, odd], axis=-1).reshape(shape)


def reduce_level(padded_image, count):
    return blur_cols(blur_rows(padded_image, count))[..., ::2, ::2]


def expand_level(padded_image, count):
    return up_cols(upsampled_rows(padded_image, count))


def octave_border(field):
    return extended(field, (("rows", 2),), 2)


def collapse(mixed_finest_band, mixed_coarse_band, blend2, strip):
    central_rows = mixed_coarse_band + expand_level(octave_border(blend2)[..., 1:-1, :], strip // 4)
    return mixed_finest_band + expand_level(octave_border(central_rows)[..., 1:-1, :], strip // 2)


def on_device(plane_colour_samples, clarity_gain):
    strip = plane_colour_samples.shape[2]
    image = plane_colour_samples.astype(jnp.float32) / 255.0
    padded_image = extended(image, (("rows", 2),), 5)
    grey = 0.299 * padded_image[:, 0] + 0.587 * padded_image[:, 1] + 0.114 * padded_image[:, 2]
    side = jnp.pad(grey, ((0, 0), (0, 0), (1, 1)))
    lap = (
        4.0 * grey[:, 1:-1, :]
        - grey[:, :-2, :]
        - grey[:, 2:, :]
        - side[:, 1:-1, :-2]
        - side[:, 1:-1, 2:]
    )
    height = strip * lax.axis_size("rows")
    first_row = lax.axis_index("rows") * strip - 4
    line_slice_from = first_row + jnp.arange(strip + 8, dtype=jnp.int32)
    inside = ((line_slice_from >= 0) & (line_slice_from < height)).astype(jnp.float32)
    squared = lap * lap * inside[None, :, None]
    summed = squared[:, 0:strip]
    for shift in range(1, 9):
        summed = summed + squared[:, shift : shift + strip]
    width = summed.shape[2]
    cols_pad = jnp.pad(summed, ((0, 0), (0, 0), (4, 4)))
    sharpness_measure_field = cols_pad[:, :, 0:width]
    for shift in range(1, 9):
        sharpness_measure_field = sharpness_measure_field + cols_pad[:, :, shift : shift + width]
    clarity_ratings = clarity_gain[:, None, None] * sharpness_measure_field
    top = lax.pmax(jnp.max(clarity_ratings, axis=0), "gz")
    expo = jnp.exp(clarity_ratings - top[None])
    total = lax.psum(jnp.sum(expo, axis=0), "gz")
    weight0 = (expo / total[None])[:, None]
    level1 = reduce_level(padded_image[..., 3:-3, :], strip)
    level1_pad = octave_border(level1)
    level2 = reduce_level(level1_pad, strip // 2)
    padded_level_second = octave_border(level2)
    detail0 = image - expand_level(level1_pad[..., 1:-1, :], strip // 2)
    detail1 = level1 - expand_level(padded_level_second[..., 1:-1, :], strip // 4)
    weight1 = reduce_level(octave_border(weight0), strip)
    weight_level2 = reduce_level(octave_border(weight1), strip // 2)
    mixed_finest_band = jnp.sum(weight0 * detail0, axis=0, keepdims=True)
    mixed_coarse_band = jnp.sum(weight1 * detail1, axis=0, keepdims=True)
    blend2 = jnp.sum(weight_level2 * level2, axis=0, keepdims=True)
    mixed_finest_band, mixed_coarse_band, blend2 = lax.psum(
        (mixed_finest_band, mixed_coarse_band, blend2), "gz"
    )
    joined = collapse(mixed_finest_band, mixed_coarse_band, blend2, strip)
    return joined[0]


def solution(mesh):
    placed = (P("gz", None, "rows", None), P("gz"))
    return jax.shard_map(
        on_device, mesh=mesh, in_specs=placed, out_specs=P(None, "rows", None), check_vma=False
    )
```

profile of v0, /device:TPU:24, one launch (start us, length us, event | category | flops | bytes accessed | tf_op | source)
XLA Modules:
  0.0 861.8 jit_solution(9867116555211420040)
XLA Ops:
  14.3 3.9 collective-permute-done
  24.3 17.7 %slice.380 = f32[2,3,16,1024]{3,2,1,0:T(8,128)S(1)} slice(f32[2,3,32,2048]{3,2,1,0:T(8,128)S(1)} %add_multiply_fusion), slice={[0:2:1], [0:3:1], [0:32:2], [0:2048:2]} | slice | bytes 786432 | tf_op jit(solution)/shard_map/slice | solution.py:67
  42.1 2.9 collective-permute-start.2
  45.0 2.6 collective-permute-start.3
  47.6 4.9 fusion.74
  54.4 4.3 slice.404
  59.4 6.2 collective-permute-start.6
  69.1 193.3 %all-reduce.15.cloned.1.call-done = f32[32,2048]{1,0:T(8,128)} async-done(((f32[32,2048]{1,0:T(8,128)}), f32[32,2048]{1,0:T(8,128)}) %all-reduce.15.cloned.1.call-update) | async-done | bytes 262160 | tf_op jit(solution)/shard_map/pmax | solution.py:110
  264.3 2.5 multiply_bitcast_fusion.2
  268.7 9.2 %copy.387 = f32[2,3,32,1024,2]{2,4,3,1,0:T(2,128)} copy(f32[2,3,32,1024,2]{3,0,2,1,4:T(2,128)} %pad_maximum_fusion.3) | data formatting | bytes 3145728 | tf_op jit(solution)/shard_map/stack | solution.py:63
  277.9 5.6 copy.388
  283.5 183.3 %all-reduce.17.cloned.1.call-done = f32[32,2048]{1,0:T(8,128)} async-done(((f32[32,2048]{1,0:T(8,128)}), f32[32,2048]{1,0:T(8,128)}) %all-reduce.17.cloned.1.call-update) | async-done | bytes 262160 | tf_op jit(solution)/shard_map/psum | solution.py:112
  469.9 3.9 collective-permute-start.5
  477.0 6.0 slice.397
  483.9 4.7 collective-permute-start.8
  490.7 2.4 multiply_reduce_fusion
  496.9 115.2 %psum.31 = f32[1,3,8,512]{2,3,1,0:T(8,128)} all-reduce(f32[1,3,8,512]{2,3,1,0:T(8,128)S(1)} %bitcast.84), channel_id=1, replica_groups=mesh['rows'=32,'gz'=16] {'gz'}, use_global_device_ids=true, to_apply=%region_9.10 | all-reduce | flops 12288 | bytes 98304 | tf_op jit(solution)/shard_map/psum | solution.py:125
  613.0 3.5 copy.396
  623.0 4.3 collective-permute-start.11
  633.4 201.2 %all-reduce.19.cloned.1.call-done = (f32[1,3,32,2048]{3,2,1,0:T(8,128)}, f32[1,3,16,1024]{3,2,1,0:T(8,128)}) async-done(((f32[1,3,32,2048]{3,2,1,0:T(8,128)}, f32[1,3,16,1024]{3,2,1,0:T(8,128)}), (f32[1,3,32,2048]{3,2,1,0:T(8,128)}, f32[1,3,16,1024]{3,2,1,0:T(8,128)})) %all-reduce.19.cloned.1.call-update) | async-done | bytes 983056 | tf_op jit(solution)/shard_map/psum | solution.py:125
  837.5 3.6 collective-permute-start.13
  843.2 2.5 multiply_bitcast_fusion.4
  847.3 3.7 copy.417
  852.9 2.3 add_bitcast_fusion
  (101 shorter events, 58.2 us)
Async XLA Ops:
  6.5 255.9 %all-reduce.15.cloned.1.call-start = ((), (), s32[]{:S(2)}) async-start(), calls=%async_computation | async-start | bytes 524288 | tf_op jit(solution)/shard_map/pmax | solution.py:110
  8.4 5.8 collective-permute-start.1
  10.7 7.5 collective-permute-start
  22.6 25.0 %copy-start.8 = (f32[2]{0:T(128)S(1)}, f32[2]{0:T(128)}, u32[]{:S(2)}) copy-start(f32[2]{0:T(128)} %param.3) | copy-start | bytes 28
  42.1 10.7 %collective-permute-start.2 = (f32[2,3,2,1024]{3,2,1,0:T(2,128)S(1)}, f32[2,3,2,1024]{3,2,1,0:T(2,128)S(1)}, u32[]{:S(2)}, u32[]{:S(2)}) collective-permute-start(f32[2,3,2,1024]{3,2,1,0:T(2,128)S(1)} %get-tuple-element.31), channel_id=1, source_target_pairs={{0,16},{16,32},{32,48},{48,64},{64,80},{80,96},{96,112},{112,128},... | collective-permute-start | bytes 147464 | tf_op jit(solution)/shard_map/ppermute | solution.py:12
  45.0 7.8 collective-permute-start.3
  52.6 414.2 %all-reduce.17.cloned.1.call-start = ((), (), s32[]{:S(2)}) async-start(), calls=%async_computation.1 | async-start | bytes 524288 | tf_op jit(solution)/shard_map/psum | solution.py:112
  58.7 10.4 %copy-start.7 = (f32[2,3,8,512]{3,2,1,0:T(8,128)}, f32[2,3,8,512]{3,2,1,0:T(8,128)S(1)}, u32[]{:S(2)}) copy-start(f32[2,3,8,512]{3,2,1,0:T(8,128)S(1)} %slice.404) | copy-start | bytes 294916
  59.4 435.2 %collective-permute-start.6 = (f32[2,3,2,512]{3,2,1,0:T(2,128)}, f32[2,3,2,512]{3,2,1,0:T(2,128)}, u32[]{:S(2)}, u32[]{:S(2)}) collective-permute-start(f32[2,3,2,512]{3,2,1,0:T(2,128)} %get-tuple-element.46), channel_id=1, source_target_pairs={{0,16},{16,32},{32,48},{48,64},{64,80},{80,96},{96,112},{112,128},... | collective-permute-start | bytes 73736 | tf_op jit(solution)/shard_map/ppermute | solution.py:12
  65.6 429.0 %collective-permute-start.7 = (f32[2,3,2,512]{3,2,1,0:T(2,128)}, f32[2,3,2,512]{3,2,1,0:T(2,128)}, u32[]{:S(2)}, u32[]{:S(2)}) collective-permute-start(f32[2,3,2,512]{3,2,1,0:T(2,128)} %get-tuple-element.47), channel_id=1, source_target_pairs={{16,0},{32,16},{48,32},{64,48},{80,64},{96,80},{112,96},{128,112},... | collective-permute-start | bytes 73736 | tf_op jit(solution)/shard_map/ppermute | solution.py:15
  69.1 195.2 %copy-start.4 = (f32[2,3,16,2,1024]{4,0,3,2,1:T(2,128)S(1)}, f32[2,3,16,2,1024]{4,0,3,2,1:T(2,128)}, u32[]{:S(2)}) copy-start(f32[2,3,16,2,1024]{4,0,3,2,1:T(2,128)} %copy.384) | copy-start | bytes 2359300
  264.2 570.4 %all-reduce.19.cloned.1.call-start = ((), (), s32[]{:S(2)}) async-start(), calls=%async_computation.2 | async-start | bytes 1966080 | tf_op jit(solution)/shard_map/psum | solution.py:125
  277.9 188.9 %copy-start.3 = (f32[32,2048]{1,0:T(8,128)S(1)}, f32[32,2048]{1,0:T(8,128)}, u32[]{:S(2)}) copy-start(f32[32,2048]{1,0:T(8,128)} %all-reduce.15.cloned.1.call-done) | copy-start | bytes 786436
  466.8 7.0 copy-start.5
  468.0 6.7 collective-permute-start.4
  469.9 5.2 collective-permute-start.5
  475.5 15.1 %copy-start.2 = (f32[2,3,32,2048]{3,2,1,0:T(8,128)S(1)}, f32[2,3,32,2048]{3,2,1,0:T(8,128)}, u32[]{:S(2)}) copy-start(f32[2,3,32,2048]{3,2,1,0:T(8,128)} %copy.388) | copy-start | bytes 4718596
  483.9 9.2 %collective-permute-start.8 = (f32[2,1,2,1024]{3,2,1,0:T(2,128)S(1)}, f32[2,1,2,1024]{3,2,1,0:T(2,128)S(1)}, u32[]{:S(2)}, u32[]{:S(2)}) collective-permute-start(f32[2,1,2,1024]{3,2,1,0:T(2,128)S(1)} %get-tuple-element.39), channel_id=1, source_target_pairs={{0,16},{16,32},{32,48},{48,64},{64,80},{80,96},{96,112},{112,128},... | collective-permute-start | bytes 49160 | tf_op jit(solution)/shard_map/ppermute | solution.py:12
  488.6 4.5 copy-start.6
  488.6 4.5 collective-permute-start.9
  620.8 6.5 collective-permute-start.10
  623.0 6.6 collective-permute-start.11
  835.6 5.6 collective-permute-start.12
  837.5 5.1 collective-permute-start.13
  (2 other events, 3.3 us)
Sparse Core Ops, SparseCore 0:
  52.7 209.7 all-reduce.14
  265.6 201.1 all-reduce.16
  620.4 214.1 all-reduce.18
where the time goes:
time: 867 us; the launch traced here: 862 us
  waiting for transfers between devices  587 us (68%)
  blocking collectives  115 us (13%)
  local copies, waits for them, and re-layouts  63.7 us (7%)
  starting transfers between devices  42.6 us (5%)
  other arithmetic  39.8 us (5%)
  between operations  13.6 us (2%)
    psum x1, waiting for transfers between devices, on_device(): lax.psum((mixed_finest_band, mixed_coarse_band, blend2), 'gz')  201 us
    pmax x1, waiting for transfers between devices, on_device(): top = lax.pmax(jnp.max(clarity_ratings, axis=0), 'gz')  193 us
    psum x1, waiting for transfers between devices, on_device(): total = lax.psum(jnp.sum(expo, axis=0), 'gz')  183 us
    psum x1, blocking collectives, on_device(): lax.psum((mixed_finest_band, mixed_coarse_band, blend2), 'gz')  115 us
    slice x4, local copies, waits for them, and re-layouts, reduce_level(): return blur_cols(blur_rows(padded_image, count))[..., ::2, ::2]  29.2 us
    ppermute x7, starting transfers between devices, extended(): lax.ppermute(lax.slice_in_dim(block, block.shape[dim] - width, None, axis...  21.8 us
    ppermute x7, starting transfers between devices, extended(): lax.ppermute(lax.slice_in_dim(block, 0, width, axis=dim), axis, backward)  20.5 us
  transfers between devices with their start and end apart: 17, of which 8 were waited for; matrix products, arithmetic and copies ran while one was open for 6% of the time, Pallas kernels for 0%

commit v1 on v0

v1 whole, which is shorter than its diff:
```python
import jax
import jax.numpy as jnp
import numpy as np
from jax import lax
from jax.experimental import pallas as pl
from jax.experimental.pallas import tpu as pltpu
from jax.sharding import Mesh
from jax.sharding import PartitionSpec as P

ROWS = ("zl", "y", "c")
GZ = ("zh", "x")
BF = jnp.bfloat16
F32 = jnp.float32
HALO = 16
VMEM_BYTES = 56 * 1024 * 1024


def down_taps():
    taps = np.zeros((768, 256), np.float32)
    for n in range(256):
        for k, tap in enumerate((1, 4, 6, 4, 1)):
            taps[2 * n + 126 + k, n] = tap / 16.0
    return taps


def up_taps():
    taps = np.zeros((384, 256), np.float32)
    for n in range(256):
        half = n // 2
        if n % 2 == 0:
            taps[half + 127, n] = 0.125
            taps[half + 128, n] = 0.75
            taps[half + 129, n] = 0.125
        else:
            taps[half + 128, n] = 0.5
            taps[half + 129, n] = 0.5
    return taps


def energy_kernel(strip_ref, main_ref, top_ref, bot_ref, gain_ref, logit_ref, lse_ref, grey_ref):
    rows, wide = grey_ref.shape
    width = main_ref.shape[3]
    first = strip_ref[0] * 32 - HALO
    row = lax.broadcasted_iota(jnp.int32, (rows, wide), 0) + first
    col = lax.broadcasted_iota(jnp.int32, (rows, wide), 1)
    keep = (row >= 0) & (row < 1024) & (col < width)
    grey_ref[:, width:] = jnp.zeros((rows, wide - width), F32)

    def grey_of(ref, p):
        return (
            ref[p, 0].astype(F32) * (0.299 / 255.0)
            + ref[p, 1].astype(F32) * (0.587 / 255.0)
            + ref[p, 2].astype(F32) * (0.114 / 255.0)
        )

    for p in range(2):
        grey_ref[0:16, 0:width] = grey_of(top_ref, p)
        grey_ref[16:48, 0:width] = grey_of(main_ref, p)
        grey_ref[48:64, 0:width] = grey_of(bot_ref, p)
        grey = grey_ref[...]
        lap = (
            4.0 * grey
            - pltpu.roll(grey, 1, 0)
            - pltpu.roll(grey, rows - 1, 0)
            - pltpu.roll(grey, 1, 1)
            - pltpu.roll(grey, wide - 1, 1)
        )
        field = jnp.where(keep, lap * lap, 0.0)
        for axis, size in ((0, rows), (1, wide)):
            two = field + pltpu.roll(field, size - 1, axis)
            four = two + pltpu.roll(two, size - 2, axis)
            eight = four + pltpu.roll(four, size - 4, axis)
            field = pltpu.roll(eight, 4, axis) + pltpu.roll(field, size - 4, axis)
        logit_ref[p] = gain_ref[p] * field[:, 0:width]
    a = logit_ref[0, 16:48]
    b = logit_ref[1, 16:48]
    lse_ref[...] = jnp.maximum(a, b) + jnp.log(1.0 + jnp.exp(-jnp.abs(a - b)))


def split2(value):
    high = value.astype(BF)
    low = (value - high.astype(F32)).astype(BF)
    return high, low


def stacked(value):
    return jnp.concatenate(split2(value), axis=0)


def dot(a, b):
    return jnp.dot(a, b, preferred_element_type=F32)


def iota2(shape):
    return lax.broadcasted_iota(jnp.int32, shape, 0), lax.broadcasted_iota(jnp.int32, shape, 1)


def down_rows(count, inputs, copies, first, limit):
    q, e = iota2((count, inputs * copies))
    for c in range(1, copies):
        e = jnp.where(e >= inputs, e - inputs, e)
    gap = jnp.abs(e - 2 * q)
    taps = jnp.where(gap == 0, 0.375, jnp.where(gap == 1, 0.25, jnp.where(gap == 2, 0.0625, 0.0)))
    inside = (q + first >= 0) & (q + first < limit)
    return jnp.where(inside, taps, 0.0).astype(BF)


def up_rows(count, inputs, offset, first, limit):
    r, q = iota2((count, 2 * inputs))
    q = jnp.where(q >= inputs, q - inputs, q)
    gap = jnp.abs(2 * q - (r + offset))
    even = (r & 1) == 0
    taps = jnp.where(
        even,
        jnp.where(gap == 0, 0.75, jnp.where(gap == 2, 0.125, 0.0)),
        jnp.where(gap == 1, 0.5, 0.0),
    )
    inside = (r + first >= 0) & (r + first < limit)
    return jnp.where(inside, taps, 0.0).astype(BF)


def blend_kernel(
    strip_ref, main_ref, top_ref, bot_ref, logit_ref, lse_ref, lse_top_ref, lse_bot_ref, down_ref, up_ref,
    out_ref, w0_ref, x_ref, s1_ref, l1_ref, s2_ref, l2_ref, s3_ref, c1_ref, s4_ref,
):
    strip = strip_ref[0]
    for ref in (s1_ref, s2_ref, s3_ref, s4_ref):
        edge = jnp.zeros((ref.shape[0], 128), BF)
        ref[:, 0:128] = edge
        ref[:, ref.shape[1] - 128 :] = edge
    v1 = down_rows(32, 64, 1, strip * 16 - 8, 512)
    v1w = down_rows(32, 64, 2, strip * 16 - 8, 512)
    v2 = down_rows(16, 32, 2, strip * 8 - 4, 256)
    p2 = up_rows(32, 16, 0, strip * 16 - 8, 512)
    p1 = up_rows(32, 32, 16, 0, 32)

    def put(ref, n, a, count, value):
        high, low = split2(value)
        width = value.shape[1]
        ref[a * count : (a + 1) * count, 128 : 128 + width] = high
        ref[(n + a) * count : (n + a + 1) * count, 128 : 128 + width] = low

    def row_mask(rows, offset):
        r = lax.broadcasted_iota(jnp.int32, (rows, 2048), 0) + offset
        g = r + strip * 32
        return (r >= -10) & (r <= 42) & (g >= 0) & (g < 1024)

    for p in range(2):
        for lo, count, ref in ((0, 16, lse_top_ref), (16, 32, lse_ref), (48, 16, lse_bot_ref)):
            w0_ref[lo : lo + count] = jnp.where(
                row_mask(count, lo - 16), jnp.exp(logit_ref[p, lo : lo + count] - ref[...]), 0.0
            )
        put(s1_ref, 8, 6 + p, 32, dot(v1w, stacked(w0_ref[...])))
        for c in range(3):
            a = p * 3 + c
            x_ref[0:16] = top_ref[p, c].astype(F32).astype(BF)
            x_ref[16:48] = main_ref[p, c].astype(F32).astype(BF)
            x_ref[48:64] = bot_ref[p, c].astype(F32).astype(BF)
            put(s1_ref, 8, a, 32, dot(v1, x_ref[...]))
    for t in range(4):
        both = dot(s1_ref[:, 512 * t : 512 * t + 768], down_ref[...])
        l1_ref[:, 256 * t : 256 * t + 256] = both[0:256] + both[256:512]
    for a in range(8):
        put(s2_ref, 8, a, 16, dot(v2, stacked(l1_ref[a * 32 : a * 32 + 32])))
    for t in range(2):
        both = dot(s2_ref[:, 512 * t : 512 * t + 768], down_ref[...])
        l2_ref[:, 256 * t : 256 * t + 256] = both[0:128] + both[128:256]
    for a in range(6):
        put(s3_ref, 9, a, 32, dot(p2, stacked(l2_ref[a * 16 : a * 16 + 16])))
    for c in range(3):
        blend2 = l2_ref[96:112] * l2_ref[c * 16 : c * 16 + 16] + l2_ref[112:128] * l2_ref[(3 + c) * 16 : (4 + c) * 16]
        put(s3_ref, 9, 6 + c, 32, dot(p2, stacked(blend2)))
    for t in range(4):
        both = dot(s3_ref[:, 128 * t : 128 * t + 384], up_ref[...])
        part = both[0:288] + both[288:576]
        cols = slice(256 * t, 256 * t + 256)
        for c in range(3):
            total = part[(6 + c) * 32 : (7 + c) * 32]
            for p in range(2):
                a = p * 3 + c
                total = total + l1_ref[(6 + p) * 32 : (7 + p) * 32, cols] * (
                    l1_ref[a * 32 : a * 32 + 32, cols] - part[a * 32 : a * 32 + 32]
                )
            c1_ref[c * 32 : c * 32 + 32, cols] = total
    for a in range(9):
        source = l1_ref[a * 32 : a * 32 + 32] if a < 6 else c1_ref[(a - 6) * 32 : (a - 5) * 32]
        put(s4_ref, 9, a, 32, dot(p1, stacked(source)))
    for t in range(8):
        both = dot(s4_ref[:, 128 * t : 128 * t + 384], up_ref[...])
        part = both[0:288] + both[288:576]
        cols = slice(256 * t, 256 * t + 256)
        weight = [jnp.exp(logit_ref[p, 16:48, cols] - lse_ref[:, cols]) for p in range(2)]
        for c in range(3):
            total = part[(6 + c) * 32 : (7 + c) * 32]
            for p in range(2):
                a = p * 3 + c
                total = total + weight[p] * (main_ref[p, c, :, cols].astype(F32) - part[a * 32 : a * 32 + 32])
            total = total * (1.0 / 255.0)
            for k in range(4):
                out_ref[k, c, :, cols] = total[8 * k : 8 * k + 8]


def vmem(count):
    return [pl.BlockSpec(memory_space=pltpu.VMEM)] * count


def smem():
    return pl.BlockSpec(memory_space=pltpu.SMEM)


def neighbours(low_part, high_part):
    count = lax.axis_size(ROWS)
    forward = [(i, i + 1) for i in range(count - 1)]
    backward = [(i + 1, i) for i in range(count - 1)]
    return lax.ppermute(high_part, ROWS, forward), lax.ppermute(low_part, ROWS, backward)


def pairwise(value, combine):
    half = value.shape[-1] // 2
    left, right = value[..., :half], value[..., half:]
    one = [(i, i ^ 1) for i in range(4)]
    three = [(i, i ^ 3) for i in range(4)]
    for a, b in ((one, three), (three, one)):
        left_in = lax.ppermute(left, "zh", a)
        right_in = lax.ppermute(right, "zh", b)
        left, right = combine(left, left_in), combine(right, right_in)
    return jnp.concatenate([left, right], axis=-1)


def on_device(samples, gain):
    strip = lax.axis_index(ROWS).astype(jnp.int32).reshape(1)
    top, bot = neighbours(samples[:, :, :HALO], samples[:, :, 32 - HALO :])
    logits, lse = pl.pallas_call(
        energy_kernel,
        out_shape=(jax.ShapeDtypeStruct((2, 64, 2048), F32), jax.ShapeDtypeStruct((32, 2048), F32)),
        in_specs=[smem()] + vmem(3) + [smem()],
        out_specs=tuple(vmem(2)),
        scratch_shapes=[pltpu.VMEM((64, 2176), F32)],
        compiler_params=pltpu.CompilerParams(vmem_limit_bytes=VMEM_BYTES),
        name="energy",
    )(strip, samples, top, bot, gain)

    parts = lax.all_to_all(lse.reshape(4, 8, 2048), "x", 0, 0)
    peak = jnp.max(parts, axis=0)
    part = peak + jnp.log(jnp.sum(jnp.exp(parts - peak), axis=0))
    whole = pairwise(part, jnp.logaddexp)
    lse = lax.all_to_all(jnp.broadcast_to(whole, (4, 8, 2048)), "x", 0, 0).reshape(32, 2048)
    lse_top, lse_bot = neighbours(lse[:HALO], lse[32 - HALO :])

    mine = pl.pallas_call(
        blend_kernel,
        out_shape=jax.ShapeDtypeStruct((4, 3, 8, 2048), F32),
        in_specs=[smem()] + vmem(9),
        out_specs=vmem(1)[0],
        scratch_shapes=[
            pltpu.VMEM((64, 2048), F32),
            pltpu.VMEM((64, 2048), BF),
            pltpu.VMEM((512, 2304), BF),
            pltpu.VMEM((256, 1024), F32),
            pltpu.VMEM((256, 1280), BF),
            pltpu.VMEM((128, 512), F32),
            pltpu.VMEM((576, 768), BF),
            pltpu.VMEM((96, 1024), F32),
            pltpu.VMEM((576, 1280), BF),
        ],
        compiler_params=pltpu.CompilerParams(vmem_limit_bytes=VMEM_BYTES),
        name="blend",
    )(strip, samples, top, bot, logits, lse, lse_top, lse_bot, jnp.asarray(down_taps(), BF), jnp.asarray(up_taps(), BF))

    part = jnp.sum(lax.all_to_all(mine, "x", 0, 0), axis=0)
    whole = pairwise(part, jnp.add)
    joined = lax.all_to_all(jnp.broadcast_to(whole, (4, 3, 8, 2048)), "x", 0, 0)
    return joined.transpose(1, 0, 2, 3).reshape(3, 32, 2048)


def solution(mesh):
    fine = Mesh(mesh.devices.reshape(4, 4, 2, 4, 4), ROWS + GZ)
    return jax.shard_map(
        on_device,
        mesh=fine,
        in_specs=(P(GZ, None, ROWS, None), P(GZ)),
        out_specs=P(None, ROWS, None),
        check_vma=False,
    )
```

time: 867 us -> 169 us (0.19)
  waiting for transfers between devices: 587 us -> 37.3 us
  blocking collectives: 115 us -> 53.5 us
  local copies, waits for them, and re-layouts: 63.7 us -> 4.06 us
  other arithmetic: 39.8 us -> 0.3 us
  starting transfers between devices: 42.6 us -> 58 us
  Pallas kernels: 0 us -> 13.6 us
  between operations: 13.6 us -> 0.24 us
    psum x2 -> x0, waiting for transfers between devices: 385 us -> none  [the longest x1 201 us: on_device(): lax.psum((mixed_finest_band, mixed_coarse_band, blend2), 'gz')]
    pmax x1 -> x0, waiting for transfers between devices: 193 us -> none  [on_device(): top = lax.pmax(jnp.max(clarity_ratings, axis=0), 'gz')]
    psum x1 -> x0, blocking collectives: 115 us -> none  [on_device(): lax.psum((mixed_finest_band, mixed_coarse_band, blend2), 'gz')]
    all_to_all x0 -> x4, blocking collectives: none -> 53.5 us  [the longest x1 17.1 us: on_device(): part = jnp.sum(lax.all_to_all(mine, 'x', 0, 0), axis=0)]
    slice x15 -> x4, local copies, waits for them, and re-layouts: 32.1 us -> 1.51 us  [the longest x1 1.47 us: on_device(): top, bot = neighbours(samples[:, :, :HALO], samples[:, :, 32 - HALO:])]
    ppermute x14 -> x12, waiting for transfers between devices: 8.99 us -> 37.3 us  [the longest x4 14.8 us: pairwise(): right_in = lax.ppermute(right, 'zh', b)]
    another operation x8 -> x0, local copies, waits for them, and re-layouts: 19.7 us -> none  [the longest x4 17.2 us: up_cols(): return jnp.stack([even, odd], axis=-1).reshape(shape)]
    ppermute x14 -> x12, starting transfers between devices: 42.3 us -> 58 us  [the longest x4 25.3 us: pairwise(): left_in = lax.ppermute(left, 'zh', a)]
  transfers between devices with their start and end apart: 17 -> 12, of which waited for: 8 -> 9; matrix products, arithmetic and copies ran while one was open for 6% -> 0% of each run, Pallas kernels for 0% -> 0%
where the time goes in v1:
time: 169 us; the launch traced here: 167 us
  starting transfers between devices  58 us (34%)
  blocking collectives  53.5 us (32%)
  waiting for transfers between devices  37.3 us (22%)
  Pallas kernels  13.6 us (8%)
  local copies, waits for them, and re-layouts  4.06 us (2%)
    ppermute x4, starting transfers between devices, pairwise(): left_in = lax.ppermute(left, 'zh', a)  25.3 us
    ppermute x4, starting transfers between devices, pairwise(): right_in = lax.ppermute(right, 'zh', b)  24 us
    all_to_all x1, blocking collectives, on_device(): part = jnp.sum(lax.all_to_all(mine, 'x', 0, 0), axis=0)  17.1 us
    all_to_all x1, blocking collectives, on_device(): joined = lax.all_to_all(jnp.broadcast_to(whole, (4, 3, 8, 2048)), 'x', 0, 0)  15.2 us
    ppermute x4, waiting for transfers between devices, pairwise(): right_in = lax.ppermute(right, 'zh', b)  14.8 us
    all_to_all x1, blocking collectives, on_device(): parts = lax.all_to_all(lse.reshape(4, 8, 2048), 'x', 0, 0)  12.2 us
    all_to_all x1, blocking collectives, on_device(): lax.all_to_all(jnp.broadcast_to(whole, (4, 8, 2048)), 'x', 0, 0)  9.07 us
    pallas_call x1, Pallas kernels, on_device(): pl.pallas_call(blend_kernel, out_shape=jax.ShapeDtypeStruct((4, 3, 8, 204...  8.11 us
  transfers between devices with their start and end apart: 12, of which 9 were waited for; matrix products, arithmetic and copies ran while one was open for 0% of the time, Pallas kernels for 0%

profile of v1, /device:TPU:24, one launch (start us, length us, event | category | flops | bytes accessed | tf_op | source)
XLA Modules:
  0.0 167.0 jit_solution(17764391629664826671)
XLA Ops:
  1.5 2.1 %collective-permute-start.1 = (s32[2,3,16,2048]{3,2,1,0:T(8,128)S(1)}, s32[2,3,16,2048]{3,2,1,0:T(8,128)S(1)}, u32[]{:S(2)}, u32[]{:S(2)}) collective-permute-start(s32[2,3,16,2048]{3,2,1,0:T(8,128)S(1)} %get-tuple-element.9), channel_id=1, source_target_pairs={{16,0},{32,16},{48,32},{64,48},{80,64},{96,80},{112,96},{128,112},... | collective-permute-start | bytes 2359304 | tf_op jit(solution)/shard_map/ppermute | solution.py:215
  3.6 2.2 %collective-permute-start = (s32[2,3,16,2048]{3,2,1,0:T(8,128)S(1)}, s32[2,3,16,2048]{3,2,1,0:T(8,128)S(1)}, u32[]{:S(2)}, u32[]{:S(2)}) collective-permute-start(s32[2,3,16,2048]{3,2,1,0:T(8,128)S(1)} %get-tuple-element.10), channel_id=1, source_target_pairs={{0,16},{16,32},{32,48},{48,64},{64,80},{80,96},{96,112},{112,128},... | collective-permute-start | bytes 2359304 | tf_op jit(solution)/shard_map/ppermute | solution.py:215
  5.8 7.2 %collective-permute-done.1.bot_ref = s32[2,3,16,2048]{3,2,1,0:T(8,128)S(1)} collective-permute-done((s32[2,3,16,2048]{3,2,1,0:T(8,128)S(1)}, s32[2,3,16,2048]{3,2,1,0:T(8,128)S(1)}, u32[]{:S(2)}, u32[]{:S(2)}) %collective-permute-start.1) | collective-permute-done | bytes 786464 | tf_op jit(solution)/shard_map/ppermute | solution.py:215
  13.1 3.8 %collective-permute-done.top_ref = s32[2,3,16,2048]{3,2,1,0:T(8,128)S(1)} collective-permute-done((s32[2,3,16,2048]{3,2,1,0:T(8,128)S(1)}, s32[2,3,16,2048]{3,2,1,0:T(8,128)S(1)}, u32[]{:S(2)}, u32[]{:S(2)}) %collective-permute-start) | collective-permute-done | bytes 786464 | tf_op jit(solution)/shard_map/ppermute | solution.py:215
  17.8 5.5 %energy.1 = (f32[2,64,2048]{2,1,0:T(8,128)}, f32[32,2048]{1,0:T(8,128)}) custom-call(s32[1]{0:T(128)} %bitcast.strip_ref, s32[2,3,32,2048]{3,2,1,0:T(8,128)} %main_ref.3, s32[2,3,16,2048]{3,2,1,0:T(8,128)} %copy-done.1, s32[2,3,16,2048]{3,2,1,0:T(8,128)} %copy-done, f32[2]{0:T(128)} %gain_ref.1), custom_call_target="tpu_custom_call" | custom-call | tf_op jit(solution)/shard_map/energy/pallas_call | solution.py:233
  23.3 12.2 %all_to_all.20 = f32[4,8,2048]{2,1,0:T(8,128)S(1)} all-to-all(f32[4,8,2048]{2,1,0:T(8,128)} %bitcast.13), channel_id=1, replica_groups=mesh['zl'=4,'y'=4,'c'=2,'zh'=4,'x'=4] {'x'}, dimensions={0} | all-to-all | bytes 524288 | tf_op jit(solution)/shard_map/all_to_all | solution.py:243
  35.5 9.1 %collective-permute-start.2 = (f32[8,1024]{1,0:T(8,128)S(1)}, f32[8,1024]{1,0:T(8,128)S(1)}, u32[]{:S(2)}, u32[]{:S(2)}) collective-permute-start(f32[8,1024]{1,0:T(8,128)S(1)} %get-tuple-element.19), channel_id=1, source_target_pairs={{0,4},{4,0},{8,12},{12,8},{1,5},{5,1},{9,13},{13,9},{2,6},{6,2},{1... | collective-permute-start | bytes 98312 | tf_op jit(solution)/shard_map/ppermute | solution.py:224
  44.6 9.1 %collective-permute-start.4 = (f32[8,1024]{1,0:T(8,128)S(1)}, f32[8,1024]{1,0:T(8,128)S(1)}, u32[]{:S(2)}, u32[]{:S(2)}) collective-permute-start(f32[8,1024]{1,0:T(8,128)S(1)} %get-tuple-element.20), channel_id=1, source_target_pairs={{0,12},{4,8},{8,4},{12,0},{1,13},{5,9},{9,5},{13,1},{2,14},{6,10},... | collective-permute-start | bytes 98312 | tf_op jit(solution)/shard_map/ppermute | solution.py:225
  55.7 8.9 %collective-permute-start.3 = (f32[8,1024]{1,0:T(8,128)S(1)}, f32[8,1024]{1,0:T(8,128)S(1)}, u32[]{:S(2)}, u32[]{:S(2)}) collective-permute-start(f32[8,1024]{1,0:T(8,128)S(1)} %get-tuple-element.17), channel_id=1, source_target_pairs={{0,12},{4,8},{8,4},{12,0},{1,13},{5,9},{9,5},{13,1},{2,14},{6,10},... | collective-permute-start | bytes 98312 | tf_op jit(solution)/shard_map/ppermute | solution.py:224
  64.5 3.2 %collective-permute-start.5 = (f32[8,1024]{1,0:T(8,128)S(1)}, f32[8,1024]{1,0:T(8,128)S(1)}, u32[]{:S(2)}, u32[]{:S(2)}) collective-permute-start(f32[8,1024]{1,0:T(8,128)S(1)} %get-tuple-element.18), channel_id=1, source_target_pairs={{0,4},{4,0},{8,12},{12,8},{1,5},{5,1},{9,13},{13,9},{2,6},{6,2},{1... | collective-permute-start | bytes 98312 | tf_op jit(solution)/shard_map/ppermute | solution.py:225
  67.8 6.7 %collective-permute-done.5 = f32[8,1024]{1,0:T(8,128)S(1)} collective-permute-done((f32[8,1024]{1,0:T(8,128)S(1)}, f32[8,1024]{1,0:T(8,128)S(1)}, u32[]{:S(2)}, u32[]{:S(2)}) %collective-permute-start.5) | collective-permute-done | bytes 32800 | tf_op jit(solution)/shard_map/ppermute | solution.py:225
  74.6 9.1 %all_to_all.21 = f32[4,8,2048]{2,1,0:T(8,128)S(1)} all-to-all(f32[4,8,2048]{2,1,0:T(8,128)S(1)} %broadcast_in_dim.7), channel_id=1, replica_groups=mesh['zl'=4,'y'=4,'c'=2,'zh'=4,'x'=4] {'x'}, dimensions={0} | all-to-all | bytes 524288 | tf_op jit(solution)/shard_map/all_to_all | solution.py:247
  83.7 1.9 %collective-permute-start.7 = (f32[16,2048]{1,0:T(8,128)S(1)}, f32[16,2048]{1,0:T(8,128)S(1)}, u32[]{:S(2)}, u32[]{:S(2)}) collective-permute-start(f32[16,2048]{1,0:T(8,128)S(1)} %get-tuple-element.11), channel_id=1, source_target_pairs={{16,0},{32,16},{48,32},{64,48},{80,64},{96,80},{112,96},{128,112},... | collective-permute-start | bytes 393224 | tf_op jit(solution)/shard_map/ppermute | solution.py:215
  85.6 2.4 %collective-permute-start.6 = (f32[16,2048]{1,0:T(8,128)S(1)}, f32[16,2048]{1,0:T(8,128)S(1)}, u32[]{:S(2)}, u32[]{:S(2)}) collective-permute-start(f32[16,2048]{1,0:T(8,128)S(1)} %get-tuple-element.12), channel_id=1, source_target_pairs={{0,16},{16,32},{32,48},{48,64},{64,80},{80,96},{96,112},{112,128},... | collective-permute-start | bytes 393224 | tf_op jit(solution)/shard_map/ppermute | solution.py:215
  88.1 3.8 %collective-permute-done.6.lse_top_ref = f32[16,2048]{1,0:T(8,128)S(1)} collective-permute-done((f32[16,2048]{1,0:T(8,128)S(1)}, f32[16,2048]{1,0:T(8,128)S(1)}, u32[]{:S(2)}, u32[]{:S(2)}) %collective-permute-start.6) | collective-permute-done | bytes 131104 | tf_op jit(solution)/shard_map/ppermute | solution.py:215
  92.6 8.1 %blend.1 = f32[4,3,8,2048]{3,2,1,0:T(8,128)} custom-call(s32[1]{0:T(128)} %bitcast.strip_ref, s32[2,3,32,2048]{3,2,1,0:T(8,128)} %main_ref.3, s32[2,3,16,2048]{3,2,1,0:T(8,128)} %copy-done.1, s32[2,3,16,2048]{3,2,1,0:T(8,128)} %copy-done, f32[2,64,2048]{2,1,0:T(8,128)} %get-tuple-element.7.logit_ref, f32[32,2048]{1,0:T(8,128)} %bitcast.12, ...), custom_call_target="tpu_custom_call" | custom-call | tf_op jit(solution)/shard_map/blend/pallas_call | solution.py:250
  100.7 17.1 %all_to_all.22 = f32[4,3,8,2048]{3,2,1,0:T(8,128)S(1)} all-to-all(f32[4,3,8,2048]{3,2,1,0:T(8,128)} %blend.1), channel_id=1, replica_groups=mesh['zl'=4,'y'=4,'c'=2,'zh'=4,'x'=4] {'x'}, dimensions={0} | all-to-all | bytes 1572864 | tf_op jit(solution)/shard_map/all_to_all | solution.py:270
  117.9 1.9 %collective-permute-start.8 = (f32[3,8,1024]{2,1,0:T(8,128)S(1)}, f32[3,8,1024]{2,1,0:T(8,128)S(1)}, u32[]{:S(2)}, u32[]{:S(2)}) collective-permute-start(f32[3,8,1024]{2,1,0:T(8,128)S(1)} %get-tuple-element.15), channel_id=1, source_target_pairs={{0,4},{4,0},{8,12},{12,8},{1,5},{5,1},{9,13},{13,9},{2,6},{6,2},{1... | collective-permute-start | bytes 294920 | tf_op jit(solution)/shard_map/ppermute | solution.py:224
  119.8 4.4 %collective-permute-start.10 = (f32[3,8,1024]{2,1,0:T(8,128)S(1)}, f32[3,8,1024]{2,1,0:T(8,128)S(1)}, u32[]{:S(2)}, u32[]{:S(2)}) collective-permute-start(f32[3,8,1024]{2,1,0:T(8,128)S(1)} %get-tuple-element.16), channel_id=1, source_target_pairs={{0,12},{4,8},{8,4},{12,0},{1,13},{5,9},{9,5},{13,1},{2,14},{6,10},... | collective-permute-start | bytes 294920 | tf_op jit(solution)/shard_map/ppermute | solution.py:225
  124.2 7.6 %collective-permute-done.8 = f32[3,8,1024]{2,1,0:T(8,128)S(1)} collective-permute-done((f32[3,8,1024]{2,1,0:T(8,128)S(1)}, f32[3,8,1024]{2,1,0:T(8,128)S(1)}, u32[]{:S(2)}, u32[]{:S(2)}) %collective-permute-start.8) | collective-permute-done | bytes 98336 | tf_op jit(solution)/shard_map/ppermute | solution.py:224
  133.3 5.4 %collective-permute-start.9 = (f32[3,8,1024]{2,1,0:T(8,128)S(1)}, f32[3,8,1024]{2,1,0:T(8,128)S(1)}, u32[]{:S(2)}, u32[]{:S(2)}) collective-permute-start(f32[3,8,1024]{2,1,0:T(8,128)S(1)} %get-tuple-element.13), channel_id=1, source_target_pairs={{0,12},{4,8},{8,4},{12,0},{1,13},{5,9},{9,5},{13,1},{2,14},{6,10},... | collective-permute-start | bytes 294920 | tf_op jit(solution)/shard_map/ppermute | solution.py:224
  138.7 7.3 %collective-permute-start.11 = (f32[3,8,1024]{2,1,0:T(8,128)S(1)}, f32[3,8,1024]{2,1,0:T(8,128)S(1)}, u32[]{:S(2)}, u32[]{:S(2)}) collective-permute-start(f32[3,8,1024]{2,1,0:T(8,128)S(1)} %get-tuple-element.14), channel_id=1, source_target_pairs={{0,4},{4,0},{8,12},{12,8},{1,5},{5,1},{9,13},{13,9},{2,6},{6,2},{1... | collective-permute-start | bytes 294920 | tf_op jit(solution)/shard_map/ppermute | solution.py:225
  146.0 4.8 %collective-permute-done.11 = f32[3,8,1024]{2,1,0:T(8,128)S(1)} collective-permute-done((f32[3,8,1024]{2,1,0:T(8,128)S(1)}, f32[3,8,1024]{2,1,0:T(8,128)S(1)}, u32[]{:S(2)}, u32[]{:S(2)}) %collective-permute-start.11) | collective-permute-done | bytes 98336 | tf_op jit(solution)/shard_map/ppermute | solution.py:225
  150.9 15.2 %all_to_all.23 = f32[4,3,8,2048]{3,2,1,0:T(8,128)S(1)} all-to-all(f32[4,3,8,2048]{3,2,1,0:T(8,128)S(1)} %broadcast_in_dim.8), channel_id=1, replica_groups=mesh['zl'=4,'y'=4,'c'=2,'zh'=4,'x'=4] {'x'}, dimensions={0} | all-to-all | bytes 1572864 | tf_op jit(solution)/shard_map/all_to_all | solution.py:272
  (35 shorter events, 7.8 us)
Async XLA Ops:
  1.5 11.6 %collective-permute-start.1 = (s32[2,3,16,2048]{3,2,1,0:T(8,128)S(1)}, s32[2,3,16,2048]{3,2,1,0:T(8,128)S(1)}, u32[]{:S(2)}, u32[]{:S(2)}) collective-permute-start(s32[2,3,16,2048]{3,2,1,0:T(8,128)S(1)} %get-tuple-element.9), channel_id=1, source_target_pairs={{16,0},{32,16},{48,32},{64,48},{80,64},{96,80},{112,96},{128,112},... | collective-permute-start | bytes 2359304 | tf_op jit(solution)/shard_map/ppermute | solution.py:215
  3.6 13.3 %collective-permute-start = (s32[2,3,16,2048]{3,2,1,0:T(8,128)S(1)}, s32[2,3,16,2048]{3,2,1,0:T(8,128)S(1)}, u32[]{:S(2)}, u32[]{:S(2)}) collective-permute-start(s32[2,3,16,2048]{3,2,1,0:T(8,128)S(1)} %get-tuple-element.10), channel_id=1, source_target_pairs={{0,16},{16,32},{32,48},{48,64},{64,80},{80,96},{96,112},{112,128},... | collective-permute-start | bytes 2359304 | tf_op jit(solution)/shard_map/ppermute | solution.py:215
  13.1 3.8 %copy-start = (s32[2,3,16,2048]{3,2,1,0:T(8,128)}, s32[2,3,16,2048]{3,2,1,0:T(8,128)S(1)}, u32[]{:S(2)}) copy-start(s32[2,3,16,2048]{3,2,1,0:T(8,128)S(1)} %collective-permute-done.1.bot_ref) | copy-start | bytes 2359300
  16.9 0.9 copy-start.1
  35.5 18.2 %collective-permute-start.2 = (f32[8,1024]{1,0:T(8,128)S(1)}, f32[8,1024]{1,0:T(8,128)S(1)}, u32[]{:S(2)}, u32[]{:S(2)}) collective-permute-start(f32[8,1024]{1,0:T(8,128)S(1)} %get-tuple-element.19), channel_id=1, source_target_pairs={{0,4},{4,0},{8,12},{12,8},{1,5},{5,1},{9,13},{13,9},{2,6},{6,2},{1... | collective-permute-start | bytes 98312 | tf_op jit(solution)/shard_map/ppermute | solution.py:224
  44.6 11.0 %collective-permute-start.4 = (f32[8,1024]{1,0:T(8,128)S(1)}, f32[8,1024]{1,0:T(8,128)S(1)}, u32[]{:S(2)}, u32[]{:S(2)}) collective-permute-start(f32[8,1024]{1,0:T(8,128)S(1)} %get-tuple-element.20), channel_id=1, source_target_pairs={{0,12},{4,8},{8,4},{12,0},{1,13},{5,9},{9,5},{13,1},{2,14},{6,10},... | collective-permute-start | bytes 98312 | tf_op jit(solution)/shard_map/ppermute | solution.py:225
  55.7 12.1 %collective-permute-start.3 = (f32[8,1024]{1,0:T(8,128)S(1)}, f32[8,1024]{1,0:T(8,128)S(1)}, u32[]{:S(2)}, u32[]{:S(2)}) collective-permute-start(f32[8,1024]{1,0:T(8,128)S(1)} %get-tuple-element.17), channel_id=1, source_target_pairs={{0,12},{4,8},{8,4},{12,0},{1,13},{5,9},{9,5},{13,1},{2,14},{6,10},... | collective-permute-start | bytes 98312 | tf_op jit(solution)/shard_map/ppermute | solution.py:224
  64.5 10.0 %collective-permute-start.5 = (f32[8,1024]{1,0:T(8,128)S(1)}, f32[8,1024]{1,0:T(8,128)S(1)}, u32[]{:S(2)}, u32[]{:S(2)}) collective-permute-start(f32[8,1024]{1,0:T(8,128)S(1)} %get-tuple-element.18), channel_id=1, source_target_pairs={{0,4},{4,0},{8,12},{12,8},{1,5},{5,1},{9,13},{13,9},{2,6},{6,2},{1... | collective-permute-start | bytes 98312 | tf_op jit(solution)/shard_map/ppermute | solution.py:225
  83.7 8.2 %copy-start.2 = (f32[4,8,2048]{2,1,0:T(8,128)}, f32[4,8,2048]{2,1,0:T(8,128)S(1)}, u32[]{:S(2)}) copy-start(f32[4,8,2048]{2,1,0:T(8,128)S(1)} %all_to_all.21) | copy-start | bytes 786436
  83.7 4.4 %collective-permute-start.7 = (f32[16,2048]{1,0:T(8,128)S(1)}, f32[16,2048]{1,0:T(8,128)S(1)}, u32[]{:S(2)}, u32[]{:S(2)}) collective-permute-start(f32[16,2048]{1,0:T(8,128)S(1)} %get-tuple-element.11), channel_id=1, source_target_pairs={{16,0},{32,16},{48,32},{64,48},{80,64},{96,80},{112,96},{128,112},... | collective-permute-start | bytes 393224 | tf_op jit(solution)/shard_map/ppermute | solution.py:215
  85.6 6.3 %collective-permute-start.6 = (f32[16,2048]{1,0:T(8,128)S(1)}, f32[16,2048]{1,0:T(8,128)S(1)}, u32[]{:S(2)}, u32[]{:S(2)}) collective-permute-start(f32[16,2048]{1,0:T(8,128)S(1)} %get-tuple-element.12), channel_id=1, source_target_pairs={{0,16},{16,32},{32,48},{48,64},{64,80},{80,96},{96,112},{112,128},... | collective-permute-start | bytes 393224 | tf_op jit(solution)/shard_map/ppermute | solution.py:215
  88.1 3.8 %copy-start.3 = (f32[16,2048]{1,0:T(8,128)}, f32[16,2048]{1,0:T(8,128)S(1)}, u32[]{:S(2)}) copy-start(f32[16,2048]{1,0:T(8,128)S(1)} %collective-permute-done.7.lse_bot_ref) | copy-start | bytes 393220
  91.9 0.6 copy-start.4
  117.9 13.9 %collective-permute-start.8 = (f32[3,8,1024]{2,1,0:T(8,128)S(1)}, f32[3,8,1024]{2,1,0:T(8,128)S(1)}, u32[]{:S(2)}, u32[]{:S(2)}) collective-permute-start(f32[3,8,1024]{2,1,0:T(8,128)S(1)} %get-tuple-element.15), channel_id=1, source_target_pairs={{0,4},{4,0},{8,12},{12,8},{1,5},{5,1},{9,13},{13,9},{2,6},{6,2},{1... | collective-permute-start | bytes 294920 | tf_op jit(solution)/shard_map/ppermute | solution.py:224
  119.8 13.5 %collective-permute-start.10 = (f32[3,8,1024]{2,1,0:T(8,128)S(1)}, f32[3,8,1024]{2,1,0:T(8,128)S(1)}, u32[]{:S(2)}, u32[]{:S(2)}) collective-permute-start(f32[3,8,1024]{2,1,0:T(8,128)S(1)} %get-tuple-element.16), channel_id=1, source_target_pairs={{0,12},{4,8},{8,4},{12,0},{1,13},{5,9},{9,5},{13,1},{2,14},{6,10},... | collective-permute-start | bytes 294920 | tf_op jit(solution)/shard_map/ppermute | solution.py:225
  133.3 12.7 %collective-permute-start.9 = (f32[3,8,1024]{2,1,0:T(8,128)S(1)}, f32[3,8,1024]{2,1,0:T(8,128)S(1)}, u32[]{:S(2)}, u32[]{:S(2)}) collective-permute-start(f32[3,8,1024]{2,1,0:T(8,128)S(1)} %get-tuple-element.13), channel_id=1, source_target_pairs={{0,12},{4,8},{8,4},{12,0},{1,13},{5,9},{9,5},{13,1},{2,14},{6,10},... | collective-permute-start | bytes 294920 | tf_op jit(solution)/shard_map/ppermute | solution.py:224
  138.7 12.1 %collective-permute-start.11 = (f32[3,8,1024]{2,1,0:T(8,128)S(1)}, f32[3,8,1024]{2,1,0:T(8,128)S(1)}, u32[]{:S(2)}, u32[]{:S(2)}) collective-permute-start(f32[3,8,1024]{2,1,0:T(8,128)S(1)} %get-tuple-element.14), channel_id=1, source_target_pairs={{0,4},{4,0},{8,12},{12,8},{1,5},{5,1},{9,13},{13,9},{2,6},{6,2},{1... | collective-permute-start | bytes 294920 | tf_op jit(solution)/shard_map/ppermute | solution.py:225

commit v2 on v0

v2 whole, which is shorter than its diff:
```python
import functools

import jax
import jax.numpy as jnp
import numpy as np
from jax import lax
from jax.experimental import pallas as pl
from jax.experimental.pallas import tpu as pltpu
from jax.sharding import Mesh
from jax.sharding import PartitionSpec as P

ROWS = ("zl", "y", "c")
GZ = ("zh", "x")
BF = jnp.bfloat16
F32 = jnp.float32
GREY = (0.299 / 255.0, 0.587 / 255.0, 0.114 / 255.0)
W0, W1, W2 = 640, 384, 256
M0, M1, M2 = 512, 256, 128
PARAMS = pltpu.CompilerParams(vmem_limit_bytes=56 * 1024 * 1024)


def lane_of(col, main, wide):
    if 0 <= col < main + 64:
        return col
    if -64 <= col < 0:
        return wide + col
    return None


def column_taps(kind, main_in, wide_in, main_out, wide_out):
    taps = np.zeros((wide_in, wide_out), np.float32)
    for lane in range(wide_out):
        col = lane if lane < main_out + 64 else lane - wide_out
        if kind == "down":
            picks = [(2 * col + d, t / 16.0) for d, t in zip(range(-2, 3), (1, 4, 6, 4, 1))]
        elif col % 2 == 0:
            picks = [(col // 2 - 1, 0.125), (col // 2, 0.75), (col // 2 + 1, 0.125)]
        else:
            picks = [(col // 2, 0.5), (col // 2 + 1, 0.5)]
        for source, tap in picks:
            at = lane_of(source, main_in, wide_in)
            if at is not None:
                taps[at, lane] += tap
    return taps


def pack_kernel(samples_ref, gain_ref, out_ref):
    lane = lax.broadcasted_iota(jnp.int32, (16, 128), 1)
    for j in range(4):
        for h in range(2):
            rows = slice(16 * h, 16 * h + 16)
            tiles = [
                jnp.zeros((16, 128), F32),
                jnp.where(lane < 64, 0.0, jnp.where(lane < 96, gain_ref[0], gain_ref[1])),
            ]
            for a in range(6):
                p, c = divmod(a, 3)
                out_ref[j, h, 16 * a : 16 * a + 16, :] = samples_ref[p, c, rows, 512 * j : 512 * j + 512].astype(F32)
                at, t = 32 * (a % 4), a // 4
                if j > 0:
                    piece = samples_ref[p, c, rows, 512 * j - 128 : 512 * j].astype(F32)
                    piece = pltpu.roll(piece, (at - 112) % 128, 1)
                    tiles[t] = jnp.where((lane >= at) & (lane < at + 16), piece, tiles[t])
                if j < 3:
                    piece = samples_ref[p, c, rows, 512 * j + 512 : 512 * j + 640].astype(F32)
                    piece = pltpu.roll(piece, (at + 16) % 128, 1)
                    tiles[t] = jnp.where((lane >= at + 16) & (lane < at + 32), piece, tiles[t])
            out_ref[j, h, 96:104, 0:128] = tiles[0][0:8]
            out_ref[j, h, 96:104, 128:256] = tiles[1][0:8]
            out_ref[j, h, 96:104, 256:384] = tiles[0][8:16]
            out_ref[j, h, 96:104, 384:512] = tiles[1][8:16]


def blocks_of(main_ref, top_ref, bot_ref, s):
    return (top_ref.at[s], main_ref.at[s, 0], main_ref.at[s, 1], bot_ref.at[s])


def halo_tile(block, a):
    base, at = 128 * (a // 4), 32 * (a % 4)
    tile = jnp.concatenate([block[96:104, base : base + 128], block[96:104, 256 + base : 384 + base]], axis=0)
    lane = lax.broadcasted_iota(jnp.int32, (16, 128), 1)
    return jnp.where((lane < 16) | (lane >= 112), pltpu.roll(tile, (112 - at) % 128, 1), 0.0)


def column_of(shape, main, wide):
    lane = lax.broadcasted_iota(jnp.int32, shape, len(shape) - 1)
    return jnp.where(lane < main + 64, lane, lane - wide)


def energy_kernel(place_ref, main_ref, top_ref, bot_ref, logit_ref, lse_ref, grey_ref):
    row = lax.broadcasted_iota(jnp.int32, (64, W0), 0) + (place_ref[0] * 32 - 16)
    col = column_of((64, W0), M0, W0) + place_ref[1] * M0
    keep = (row >= 0) & (row < 1024) & (col >= 0) & (col < 2048)

    @pl.loop(0, 4)
    def _(s):
        for p in range(2):
            for b, block in enumerate(blocks_of(main_ref, top_ref, bot_ref, s)):
                main = 0.0
                tile = 0.0
                for c in range(3):
                    a = 3 * p + c
                    main = main + block[16 * a : 16 * a + 16, :] * GREY[c]
                    tile = tile + halo_tile(block, a) * GREY[c]
                grey_ref[16 * b : 16 * b + 16, 0:M0] = main
                grey_ref[16 * b : 16 * b + 16, M0:W0] = tile
            grey = grey_ref[...]
            lap = (
                4.0 * grey
                - pltpu.roll(grey, 1, 0)
                - pltpu.roll(grey, 63, 0)
                - pltpu.roll(grey, 1, 1)
                - pltpu.roll(grey, W0 - 1, 1)
            )
            field = jnp.where(keep, lap * lap, 0.0)
            for axis, size in ((0, 64), (1, W0)):
                two = field + pltpu.roll(field, size - 1, axis)
                four = two + pltpu.roll(two, size - 2, axis)
                eight = four + pltpu.roll(four, size - 4, axis)
                field = pltpu.roll(eight, 4, axis) + pltpu.roll(field, size - 4, axis)
            gain = main_ref[s, 0, 96:97, 192 + 32 * p : 193 + 32 * p]
            logit_ref[2 * s + p] = gain * field

    peak = logit_ref[0, 16:48]
    for i in range(1, 8):
        peak = jnp.maximum(peak, logit_ref[i, 16:48])
    total = 0.0
    for i in range(8):
        total = total + jnp.exp(logit_ref[i, 16:48] - peak)
    lse_ref[...] = peak + jnp.log(total)


def split2(value):
    high = value.astype(BF)
    low = (value - high.astype(F32)).astype(BF)
    return high, low


def stacked(value):
    return jnp.concatenate(split2(value), axis=0)


def dot(a, b):
    return jnp.dot(a, b, preferred_element_type=F32)


def iota2(shape):
    return lax.broadcasted_iota(jnp.int32, shape, 0), lax.broadcasted_iota(jnp.int32, shape, 1)


def down_rows(count, inputs, copies, first, limit):
    q, e = iota2((count, inputs * copies))
    if copies == 2:
        e = jnp.where(e >= inputs, e - inputs, e)
    gap = jnp.abs(e - 2 * q)
    taps = jnp.where(gap == 0, 0.375, jnp.where(gap == 1, 0.25, jnp.where(gap == 2, 0.0625, 0.0)))
    inside = (q + first >= 0) & (q + first < limit)
    return jnp.where(inside, taps, 0.0).astype(BF)


def up_rows(count, inputs, offset, first, limit):
    r, q = iota2((count, 2 * inputs))
    q = jnp.where(q >= inputs, q - inputs, q)
    gap = jnp.abs(2 * q - (r + offset))
    even = (r & 1) == 0
    taps = jnp.where(
        even,
        jnp.where(gap == 0, 0.75, jnp.where(gap == 2, 0.125, 0.0)),
        jnp.where(gap == 1, 0.5, 0.0),
    )
    inside = (r + first >= 0) & (r + first < limit)
    return jnp.where(inside, taps, 0.0).astype(BF)


def row_matrices(strip):
    v2 = down_rows(16, 32, 2, strip * 8 - 4, 256)
    p2 = up_rows(32, 16, 0, strip * 16 - 8, 512)
    p1 = up_rows(32, 32, 16, 0, 32)
    return v2, p2, p1


def level_masks(rows1, rows2, k):
    col1 = column_of((rows1, W1), M1, W1) + k * M1
    col2 = column_of((rows2, W2), M2, W2) + k * M2
    return (col1 >= 0) & (col1 < 1024), (col2 >= 0) & (col2 < 512)


def put(ref, n, a, count, value):
    high, low = split2(value)
    ref[a * count : (a + 1) * count] = high
    ref[(n + a) * count : (n + a + 1) * count] = low


def resampled(source_ref, taps_ref):
    both = dot(source_ref[...], taps_ref[...])
    half = both.shape[0] // 2
    return both[:half] + both[half:]


def pyramid_kernel(
    sources, place_ref, main_ref, top_ref, bot_ref, d1_ref, d2_ref, u2_ref, u1_ref,
    detail0_ref, detail1_ref, l2_ref, x_ref, s1_ref, l1_ref, s2_ref, s3_ref, s4_ref,
):
    strip = place_ref[0]
    v1 = down_rows(32, 64, 1, strip * 16 - 8, 512)
    v2, p2, p1 = row_matrices(strip)
    inside1, inside2 = level_masks(192, 96, place_ref[1])
    for i, s in enumerate(sources):
        blocks = blocks_of(main_ref, top_ref, bot_ref, s)
        for a in range(6):
            for b, block in enumerate(blocks):
                x_ref[16 * b : 16 * b + 16, 0:M0] = block[16 * a : 16 * a + 16, :].astype(BF)
                x_ref[16 * b : 16 * b + 16, M0:W0] = halo_tile(block, a).astype(BF)
            put(s1_ref, 6, a, 32, dot(v1, x_ref[...]))
        l1_ref[...] = jnp.where(inside1, resampled(s1_ref, d1_ref), 0.0)
        for a in range(6):
            both = stacked(l1_ref[a * 32 : a * 32 + 32])
            put(s2_ref, 6, a, 16, dot(v2, both))
            put(s4_ref, 6, a, 32, dot(p1, both))
        l2 = jnp.where(inside2, resampled(s2_ref, d2_ref), 0.0)
        l2_ref[i * 96 : i * 96 + 96] = l2
        for a in range(6):
            put(s3_ref, 6, a, 32, dot(p2, stacked(l2[a * 16 : a * 16 + 16])))
        detail1_ref[i * 192 : i * 192 + 192] = l1_ref[...] - resampled(s3_ref, u2_ref)
        part = resampled(s4_ref, u1_ref)
        for a in range(6):
            for h in range(2):
                at = a * 32 + 16 * h
                detail0_ref[i * 192 + at : i * 192 + at + 16] = (
                    main_ref[s, h, 16 * a : 16 * a + 16, :] - part[at : at + 16]
                )


def mix_kernel(
    place_ref, logit_ref, lse_ref, lse_top_ref, lse_bot_ref,
    fine_a_ref, mid_a_ref, low_a_ref, fine_b_ref, mid_b_ref, low_b_ref,
    d1_ref, d2_ref, u2_ref, u1_ref,
    left_ref, right_ref, w0_ref, s1_ref, w1_ref, s2_ref, s3_ref, s4_ref,
):
    strip, k = place_ref[0], place_ref[1]
    v1 = down_rows(32, 64, 2, strip * 16 - 8, 512)
    v2, p2, p1 = row_matrices(strip)
    col = column_of((16, W0), M0, W0)
    inside_col = (col >= -10) & (col <= 522) & (col + k * M0 >= 0) & (col + k * M0 < 2048)
    row = lax.broadcasted_iota(jnp.int32, (16, W0), 0)
    lses = (lse_top_ref[...], lse_ref[0:16], lse_ref[16:32], lse_bot_ref[...])
    keeps = []
    for b in range(4):
        r = row + (16 * b - 16)
        g = r + strip * 32
        keeps.append(inside_col & (r >= -10) & (r <= 42) & (g >= 0) & (g < 1024))
    for i in range(8):
        for b in range(4):
            rows = slice(16 * b, 16 * b + 16)
            w0_ref[i, rows] = jnp.where(keeps[b], jnp.exp(logit_ref[i, rows] - lses[b]), 0.0)
        put(s1_ref, 8, i, 32, dot(v1, stacked(w0_ref[i])))
    inside1, inside2 = level_masks(32, 16, k)
    w1_ref[...] = resampled(s1_ref, d1_ref)
    for i in range(8):
        w1 = jnp.where(inside1, w1_ref[i * 32 : i * 32 + 32], 0.0)
        w1_ref[i * 32 : i * 32 + 32] = w1
        put(s2_ref, 8, i, 16, dot(v2, stacked(w1)))
    w2 = resampled(s2_ref, d2_ref)

    def piece(pair, i, c, rows):
        ref = pair[i // 4]
        at = ((i % 4) * 3 + c) * rows
        return ref[at : at + rows]

    for c in range(3):
        blend2 = 0.0
        for i in range(8):
            blend2 = blend2 + w2[i * 16 : i * 16 + 16] * piece((low_a_ref, low_b_ref), i, c, 16)
        put(s3_ref, 3, c, 32, dot(p2, stacked(blend2)))
    rise = resampled(s3_ref, u2_ref)
    for c in range(3):
        total = jnp.where(inside1, rise[c * 32 : c * 32 + 32], 0.0)
        for i in range(8):
            total = total + w1_ref[i * 32 : i * 32 + 32] * piece((mid_a_ref, mid_b_ref), i, c, 32)
        put(s4_ref, 3, c, 32, dot(p1, stacked(total)))
    rise = resampled(s4_ref, u1_ref)
    for c in range(3):
        total = rise[c * 32 : c * 32 + 32]
        for i in range(8):
            total = total + w0_ref[i, 16:48, 0:M0] * piece((fine_a_ref, fine_b_ref), i, c, 32)
        total = total * (1.0 / 255.0)
        left_ref[c] = total[:, :256]
        right_ref[c] = total[:, 256:]


def vmem(count):
    return [pl.BlockSpec(memory_space=pltpu.VMEM)] * count


def smem():
    return [pl.BlockSpec(memory_space=pltpu.SMEM)]


def neighbours(low_part, high_part):
    count = lax.axis_size(ROWS)
    forward = [(i, i + 1) for i in range(count - 1)]
    backward = [(i + 1, i) for i in range(count - 1)]
    return lax.ppermute(high_part, ROWS, forward), lax.ppermute(low_part, ROWS, backward)


def partner(value, flip):
    return lax.ppermute(value, "zh", [(i, i ^ flip) for i in range(4)])


def join_lse(a, b):
    return jnp.maximum(a, b) + jnp.log(1.0 + jnp.exp(-jnp.abs(a - b)))


def on_device(samples, gain):
    place = jnp.stack([lax.axis_index(ROWS), lax.axis_index("x")]).astype(jnp.int32)
    packed = pl.pallas_call(
        pack_kernel,
        out_shape=jax.ShapeDtypeStruct((4, 2, 104, 512), F32),
        in_specs=vmem(1) + smem(),
        out_specs=vmem(1)[0],
        compiler_params=PARAMS,
        name="pack",
    )(samples, gain)
    main = lax.all_to_all(packed, "x", 0, 0)
    top, bot = neighbours(main[:, 0], main[:, 1])
    logits, lse = pl.pallas_call(
        energy_kernel,
        out_shape=(jax.ShapeDtypeStruct((8, 64, W0), F32), jax.ShapeDtypeStruct((32, W0), F32)),
        in_specs=smem() + vmem(3),
        out_specs=tuple(vmem(2)),
        scratch_shapes=[pltpu.VMEM((64, W0), F32)],
        compiler_params=PARAMS,
        name="energy",
    )(place, main, top, bot)

    taps = [
        jnp.asarray(t, BF)
        for t in (
            column_taps("down", M0, W0, M1, W1),
            column_taps("down", M1, W1, M2, W2),
            column_taps("up", M2, W2, M1, W1),
            column_taps("up", M1, W1, M0, W0)[:, :M0],
        )
    ]
    details = []
    for step, flip in enumerate((1, 3)):
        other = partner(lse, flip)
        detail = pl.pallas_call(
            functools.partial(pyramid_kernel, (2 * step, 2 * step + 1)),
            out_shape=(
                jax.ShapeDtypeStruct((384, M0), F32),
                jax.ShapeDtypeStruct((384, W1), F32),
                jax.ShapeDtypeStruct((192, W2), F32),
            ),
            in_specs=smem() + vmem(7),
            out_specs=tuple(vmem(3)),
            scratch_shapes=[
                pltpu.VMEM((64, W0), BF),
                pltpu.VMEM((384, W0), BF),
                pltpu.VMEM((192, W1), F32),
                pltpu.VMEM((192, W1), BF),
                pltpu.VMEM((384, W2), BF),
                pltpu.VMEM((384, W1), BF),
            ],
            compiler_params=PARAMS,
            cost_estimate=pl.CostEstimate(flops=2_000_000_000, bytes_accessed=6_000_000, transcendentals=0),
            name="pyramid",
        )(place, main, top, bot, *taps)
        other, *detail = lax.optimization_barrier((other, *detail))
        details += detail
        lse = join_lse(lse, other)
    lse_top, lse_bot = neighbours(lse[:16], lse[16:])

    left, right = pl.pallas_call(
        mix_kernel,
        out_shape=(jax.ShapeDtypeStruct((3, 32, 256), F32),) * 2,
        in_specs=smem() + vmem(14),
        out_specs=tuple(vmem(2)),
        scratch_shapes=[
            pltpu.VMEM((8, 64, W0), F32),
            pltpu.VMEM((512, W0), BF),
            pltpu.VMEM((256, W1), F32),
            pltpu.VMEM((256, W1), BF),
            pltpu.VMEM((192, W2), BF),
            pltpu.VMEM((192, W1), BF),
        ],
        compiler_params=PARAMS,
        name="mix",
    )(place, logits, lse, lse_top, lse_bot, *details, *taps)

    for a, b in ((1, 3), (3, 1)):
        left_in, right_in = partner(left, a), partner(right, b)
        left, right = left + left_in, right + right_in
    whole = jnp.concatenate([left, right], axis=-1)
    joined = lax.all_to_all(jnp.broadcast_to(whole, (4, 3, 32, 512)), "x", 0, 0)
    return joined.transpose(1, 2, 0, 3).reshape(3, 32, 2048)


def solution(mesh):
    fine = Mesh(mesh.devices.reshape(4, 4, 2, 4, 4), ROWS + GZ)
    return jax.shard_map(
        on_device,
        mesh=fine,
        in_specs=(P(GZ, None, ROWS, None), P(GZ)),
        out_specs=P(None, ROWS, None),
        check_vma=False,
    )
```

time: 867 us -> 152 us (0.18)
  the two profiles are of different devices: /device:TPU:24 before, /device:TPU:88 now
where the time goes in v2:
time: 152 us
  starting transfers between devices  47.5 us (31%)
  blocking collectives  41.7 us (27%)
  Pallas kernels  28.5 us (19%)
  waiting for transfers between devices  27.7 us (18%)
  local copies, waits for them, and re-layouts  3.81 us (3%)
  other arithmetic  2.58 us (2%)
    ppermute x6, starting transfers between devices, partner(): return lax.ppermute(value, 'zh', [(i, i ^ flip) for i in range(4)])  38.8 us
    all_to_all x1, blocking collectives, on_device(): main = lax.all_to_all(packed, 'x', 0, 0)  26.4 us
    all_to_all x1, blocking collectives, on_device(): joined = lax.all_to_all(jnp.broadcast_to(whole, (4, 3, 32, 512)), 'x', 0, 0)  15.3 us
    ppermute x6, waiting for transfers between devices, partner(): return lax.ppermute(value, 'zh', [(i, i ^ flip) for i in range(4)])  13.8 us
    pallas_call x2, Pallas kernels, on_device(): pl.pallas_call(functools.partial(pyramid_kernel, (2 * step, 2 * step + 1)...  12.4 us
    pallas_call x1, Pallas kernels, on_device(): pl.pallas_call(energy_kernel, out_shape=(jax.ShapeDtypeStruct((8, 64, W0)...  7.68 us
    ppermute x2, waiting for transfers between devices, neighbours(): lax.ppermute(low_part, ROWS, backward)  7.13 us
    ppermute x2, waiting for transfers between devices, neighbours(): lax.ppermute(high_part, ROWS, forward)  6.71 us
  transfers between devices with their start and end apart: 10, of which 5 were waited for; matrix products, arithmetic and copies ran while one was open for 2% of the time, Pallas kernels for 8%

profile of v2, /device:TPU:88, one launch (start us, length us, event | category | flops | bytes accessed | tf_op | source)
XLA Modules:
  0.0 151.9 jit_solution(14950874787901573981)
XLA Ops:
  0.0 2.9 %pack.1 = f32[4,2,104,512]{3,2,1,0:T(8,128)} custom-call(s32[2,3,32,2048]{3,2,1,0:T(8,128)} %samples_ref.1, f32[2]{0:T(128)} %gain_ref.1), custom_call_target="tpu_custom_call" | custom-call | tf_op jit(solution)/shard_map/pack/pallas_call | solution.py:316
  2.9 26.4 %all_to_all.10.main_ref = f32[4,2,104,512]{3,2,1,0:T(8,128)S(1)} all-to-all(f32[4,2,104,512]{3,2,1,0:T(8,128)} %pack.1), channel_id=1, replica_groups=mesh['zl'=4,'y'=4,'c'=2,'zh'=4,'x'=4] {'x'}, dimensions={0} | all-to-all | bytes 3407872 | tf_op jit(solution)/shard_map/all_to_all | solution.py:324
  29.5 1.1 copy-done
  30.6 1.9 %collective-permute-start.1 = (f32[4,104,512]{2,1,0:T(8,128)S(1)}, f32[4,104,512]{2,1,0:T(8,128)S(1)}, u32[]{:S(2)}, u32[]{:S(2)}) collective-permute-start(f32[4,104,512]{2,1,0:T(8,128)S(1)} %get-tuple-element.41), channel_id=1, source_target_pairs={{16,0},{32,16},{48,32},{64,48},{80,64},{96,80},{112,96},{128,112},... | collective-permute-start | bytes 2555912 | tf_op jit(solution)/shard_map/ppermute | solution.py:303
  32.5 2.4 %collective-permute-start = (f32[4,104,512]{2,1,0:T(8,128)S(1)}, f32[4,104,512]{2,1,0:T(8,128)S(1)}, u32[]{:S(2)}, u32[]{:S(2)}) collective-permute-start(f32[4,104,512]{2,1,0:T(8,128)S(1)} %get-tuple-element.42), channel_id=1, source_target_pairs={{0,16},{16,32},{32,48},{48,64},{64,80},{80,96},{96,112},{112,128},... | collective-permute-start | bytes 2555912 | tf_op jit(solution)/shard_map/ppermute | solution.py:303
  35.5 7.1 %collective-permute-done.1.bot_ref = f32[4,104,512]{2,1,0:T(8,128)S(1)} collective-permute-done((f32[4,104,512]{2,1,0:T(8,128)S(1)}, f32[4,104,512]{2,1,0:T(8,128)S(1)}, u32[]{:S(2)}, u32[]{:S(2)}) %collective-permute-start.1) | collective-permute-done | bytes 852000 | tf_op jit(solution)/shard_map/ppermute | solution.py:303
  42.7 3.8 %collective-permute-done.top_ref = f32[4,104,512]{2,1,0:T(8,128)S(1)} collective-permute-done((f32[4,104,512]{2,1,0:T(8,128)S(1)}, f32[4,104,512]{2,1,0:T(8,128)S(1)}, u32[]{:S(2)}, u32[]{:S(2)}) %collective-permute-start) | collective-permute-done | bytes 852000 | tf_op jit(solution)/shard_map/ppermute | solution.py:303
  47.4 7.7 %energy.1 = (f32[8,64,640]{2,1,0:T(8,128)}, f32[32,640]{1,0:T(8,128)}) custom-call(s32[2]{0:T(128)} %pad_add_fusion.place_ref, f32[4,2,104,512]{3,2,1,0:T(8,128)} %copy-done, f32[4,104,512]{2,1,0:T(8,128)} %copy-done.2, f32[4,104,512]{2,1,0:T(8,128)} %copy-done.1), custom_call_target="tpu_custom_call" | custom-call | tf_op jit(solution)/shard_map/energy/pallas_call | solution.py:326
  55.1 9.2 %collective-permute-start.2 = (f32[32,640]{1,0:T(8,128)}, f32[32,640]{1,0:T(8,128)S(1)}, u32[]{:S(2)}, u32[]{:S(2)}) collective-permute-start(f32[32,640]{1,0:T(8,128)} %get-tuple-element.24), channel_id=1, source_target_pairs={{0,4},{4,0},{8,12},{12,8},{1,5},{5,1},{9,13},{13,9},{2,6},{6,2},{1... | collective-permute-start | bytes 245768 | tf_op jit(solution)/shard_map/ppermute | solution.py:307
  64.3 6.2 %pyramid.2 = (f32[384,512]{1,0:T(8,128)}, f32[384,384]{1,0:T(8,128)}, f32[192,256]{1,0:T(8,128)}) custom-call(s32[2]{0:T(128)} %pad_add_fusion.place_ref, f32[4,2,104,512]{3,2,1,0:T(8,128)} %copy-done, f32[4,104,512]{2,1,0:T(8,128)} %copy-done.2, f32[4,104,512]{2,1,0:T(8,128)} %copy-done.1, bf16[640,384]{1,0:T(8,128)(2,1)} %constant.32.clone.d1_ref, ...), custom_call_target="tpu_custom_call" | custom-call | flops 2000000000 | bytes 6000000 | tf_op jit(solution)/shard_map/pyramid/pallas_call | solution.py:348
  70.6 10.4 %collective-permute-start.3 = (f32[32,640]{1,0:T(8,128)S(1)}, f32[32,640]{1,0:T(8,128)S(1)}, u32[]{:S(2)}, u32[]{:S(2)}) collective-permute-start(f32[32,640]{1,0:T(8,128)S(1)} %log_add_fusion.1), channel_id=1, source_target_pairs={{0,12},{4,8},{8,4},{12,0},{1,13},{5,9},{9,5},{13,1},{2,14},{6,10},... | collective-permute-start | bytes 245768 | tf_op jit(solution)/shard_map/ppermute | solution.py:307
  81.0 6.2 %pyramid.3 = (f32[384,512]{1,0:T(8,128)}, f32[384,384]{1,0:T(8,128)}, f32[192,256]{1,0:T(8,128)}) custom-call(s32[2]{0:T(128)} %pad_add_fusion.place_ref, f32[4,2,104,512]{3,2,1,0:T(8,128)} %copy-done, f32[4,104,512]{2,1,0:T(8,128)} %copy-done.2, f32[4,104,512]{2,1,0:T(8,128)} %copy-done.1, bf16[640,384]{1,0:T(8,128)(2,1)} %constant.32.clone.d1_ref, ...), custom_call_target="tpu_custom_call" | custom-call | flops 2000000000 | bytes 6000000 | tf_op jit(solution)/shard_map/pyramid/pallas_call | solution.py:348
  87.3 1.9 %collective-permute-start.5 = (f32[16,640]{1,0:T(8,128)S(1)}, f32[16,640]{1,0:T(8,128)S(1)}, u32[]{:S(2)}, u32[]{:S(2)}) collective-permute-start(f32[16,640]{1,0:T(8,128)S(1)} %get-tuple-element.43), channel_id=1, source_target_pairs={{16,0},{32,16},{48,32},{64,48},{80,64},{96,80},{112,96},{128,112},... | collective-permute-start | bytes 122888 | tf_op jit(solution)/shard_map/ppermute | solution.py:303
  89.2 2.4 %collective-permute-start.4 = (f32[16,640]{1,0:T(8,128)S(1)}, f32[16,640]{1,0:T(8,128)S(1)}, u32[]{:S(2)}, u32[]{:S(2)}) collective-permute-start(f32[16,640]{1,0:T(8,128)S(1)} %get-tuple-element.44), channel_id=1, source_target_pairs={{0,16},{16,32},{32,48},{48,64},{64,80},{80,96},{96,112},{112,128},... | collective-permute-start | bytes 122888 | tf_op jit(solution)/shard_map/ppermute | solution.py:303
  91.6 2.9 %collective-permute-done.4.lse_top_ref = f32[16,640]{1,0:T(8,128)S(1)} collective-permute-done((f32[16,640]{1,0:T(8,128)S(1)}, f32[16,640]{1,0:T(8,128)S(1)}, u32[]{:S(2)}, u32[]{:S(2)}) %collective-permute-start.4) | collective-permute-done | bytes 40992 | tf_op jit(solution)/shard_map/ppermute | solution.py:303
  95.1 5.5 %mix.1 = (f32[3,32,256]{2,1,0:T(8,128)}, f32[3,32,256]{2,1,0:T(8,128)}) custom-call(s32[2]{0:T(128)} %pad_add_fusion.place_ref, f32[8,64,640]{2,1,0:T(8,128)} %get-tuple-element.23.logit_ref, f32[32,640]{1,0:T(8,128)} %copy-done.3, f32[16,640]{1,0:T(8,128)} %copy-done.6, f32[16,640]{1,0:T(8,128)} %copy-done.5, f32[384,512]{1,0:T(8,128)} %get-tuple-element.33.fine_a_ref, ...), custom_call_target="tpu_custom_call" | custom-call | tf_op jit(solution)/shard_map/mix/pallas_call | solution.py:374
  100.7 2.1 %collective-permute-start.6 = (f32[3,32,256]{2,1,0:T(8,128)}, f32[3,32,256]{2,1,0:T(8,128)S(1)}, u32[]{:S(2)}, u32[]{:S(2)}) collective-permute-start(f32[3,32,256]{2,1,0:T(8,128)} %get-tuple-element.39), channel_id=1, source_target_pairs={{0,4},{4,0},{8,12},{12,8},{1,5},{5,1},{9,13},{13,9},{2,6},{6,2},{1... | collective-permute-start | bytes 294920 | tf_op jit(solution)/shard_map/ppermute | solution.py:307
  102.8 4.9 %collective-permute-start.8 = (f32[3,32,256]{2,1,0:T(8,128)}, f32[3,32,256]{2,1,0:T(8,128)S(1)}, u32[]{:S(2)}, u32[]{:S(2)}) collective-permute-start(f32[3,32,256]{2,1,0:T(8,128)} %get-tuple-element.40), channel_id=1, source_target_pairs={{0,12},{4,8},{8,4},{12,0},{1,13},{5,9},{9,5},{13,1},{2,14},{6,10},... | collective-permute-start | bytes 294920 | tf_op jit(solution)/shard_map/ppermute | solution.py:307
  107.7 5.6 %collective-permute-done.6 = f32[3,32,256]{2,1,0:T(8,128)S(1)} collective-permute-done((f32[3,32,256]{2,1,0:T(8,128)}, f32[3,32,256]{2,1,0:T(8,128)S(1)}, u32[]{:S(2)}, u32[]{:S(2)}) %collective-permute-start.6) | collective-permute-done | bytes 98336 | tf_op jit(solution)/shard_map/ppermute | solution.py:307
  114.2 7.9 %collective-permute-start.7 = (f32[3,32,256]{2,1,0:T(8,128)S(1)}, f32[3,32,256]{2,1,0:T(8,128)S(1)}, u32[]{:S(2)}, u32[]{:S(2)}) collective-permute-start(f32[3,32,256]{2,1,0:T(8,128)S(1)} %add.36), channel_id=1, source_target_pairs={{0,12},{4,8},{8,4},{12,0},{1,13},{5,9},{9,5},{13,1},{2,14},{6,10},... | collective-permute-start | bytes 294920 | tf_op jit(solution)/shard_map/ppermute | solution.py:307
  122.9 4.3 %collective-permute-start.9 = (f32[3,32,256]{2,1,0:T(8,128)S(1)}, f32[3,32,256]{2,1,0:T(8,128)S(1)}, u32[]{:S(2)}, u32[]{:S(2)}) collective-permute-start(f32[3,32,256]{2,1,0:T(8,128)S(1)} %add.38), channel_id=1, source_target_pairs={{0,4},{4,0},{8,12},{12,8},{1,5},{5,1},{9,13},{13,9},{2,6},{6,2},{1... | collective-permute-start | bytes 294920 | tf_op jit(solution)/shard_map/ppermute | solution.py:307
  127.3 8.3 %collective-permute-done.9 = f32[3,32,256]{2,1,0:T(8,128)S(1)} collective-permute-done((f32[3,32,256]{2,1,0:T(8,128)S(1)}, f32[3,32,256]{2,1,0:T(8,128)S(1)}, u32[]{:S(2)}, u32[]{:S(2)}) %collective-permute-start.9) | collective-permute-done | bytes 98336 | tf_op jit(solution)/shard_map/ppermute | solution.py:307
  135.7 15.3 %all_to_all.11 = f32[4,3,32,512]{3,2,1,0:T(8,128)S(1)} all-to-all(f32[4,3,32,512]{3,2,1,0:T(8,128)S(1)} %broadcast_in_dim.3), channel_id=1, replica_groups=mesh['zl'=4,'y'=4,'c'=2,'zh'=4,'x'=4] {'x'}, dimensions={0} | all-to-all | bytes 1572864 | tf_op jit(solution)/shard_map/all_to_all | solution.py:395
  151.0 0.9 copy.18
  (29 shorter events, 4.4 us)
Async XLA Ops:
  29.3 1.2 copy-start
  30.6 12.1 %collective-permute-start.1 = (f32[4,104,512]{2,1,0:T(8,128)S(1)}, f32[4,104,512]{2,1,0:T(8,128)S(1)}, u32[]{:S(2)}, u32[]{:S(2)}) collective-permute-start(f32[4,104,512]{2,1,0:T(8,128)S(1)} %get-tuple-element.41), channel_id=1, source_target_pairs={{16,0},{32,16},{48,32},{64,48},{80,64},{96,80},{112,96},{128,112},... | collective-permute-start | bytes 2555912 | tf_op jit(solution)/shard_map/ppermute | solution.py:303
  32.5 14.0 %collective-permute-start = (f32[4,104,512]{2,1,0:T(8,128)S(1)}, f32[4,104,512]{2,1,0:T(8,128)S(1)}, u32[]{:S(2)}, u32[]{:S(2)}) collective-permute-start(f32[4,104,512]{2,1,0:T(8,128)S(1)} %get-tuple-element.42), channel_id=1, source_target_pairs={{0,16},{16,32},{32,48},{48,64},{64,80},{80,96},{96,112},{112,128},... | collective-permute-start | bytes 2555912 | tf_op jit(solution)/shard_map/ppermute | solution.py:303
  42.7 3.8 %copy-start.1 = (f32[4,104,512]{2,1,0:T(8,128)}, f32[4,104,512]{2,1,0:T(8,128)S(1)}, u32[]{:S(2)}) copy-start(f32[4,104,512]{2,1,0:T(8,128)S(1)} %collective-permute-done.1.bot_ref) | copy-start | bytes 2555908
  46.5 0.9 copy-start.2
  55.1 15.4 %copy-start.4 = (f32[32,640]{1,0:T(8,128)S(1)}, f32[32,640]{1,0:T(8,128)}, u32[]{:S(2)}) copy-start(f32[32,640]{1,0:T(8,128)} %get-tuple-element.24) | copy-start | bytes 245764
  55.1 15.4 %collective-permute-start.2 = (f32[32,640]{1,0:T(8,128)}, f32[32,640]{1,0:T(8,128)S(1)}, u32[]{:S(2)}, u32[]{:S(2)}) collective-permute-start(f32[32,640]{1,0:T(8,128)} %get-tuple-element.24), channel_id=1, source_target_pairs={{0,4},{4,0},{8,12},{12,8},{1,5},{5,1},{9,13},{13,9},{2,6},{6,2},{1... | collective-permute-start | bytes 245768 | tf_op jit(solution)/shard_map/ppermute | solution.py:307
  70.6 16.6 %collective-permute-start.3 = (f32[32,640]{1,0:T(8,128)S(1)}, f32[32,640]{1,0:T(8,128)S(1)}, u32[]{:S(2)}, u32[]{:S(2)}) collective-permute-start(f32[32,640]{1,0:T(8,128)S(1)} %log_add_fusion.1), channel_id=1, source_target_pairs={{0,12},{4,8},{8,4},{12,0},{1,13},{5,9},{9,5},{13,1},{2,14},{6,10},... | collective-permute-start | bytes 245768 | tf_op jit(solution)/shard_map/ppermute | solution.py:307
  87.2 7.3 %copy-start.3 = (f32[32,640]{1,0:T(8,128)}, f32[32,640]{1,0:T(8,128)S(1)}, u32[]{:S(2)}) copy-start(f32[32,640]{1,0:T(8,128)S(1)} %log_add_fusion.lse_ref) | copy-start | bytes 245764
  87.3 4.3 %collective-permute-start.5 = (f32[16,640]{1,0:T(8,128)S(1)}, f32[16,640]{1,0:T(8,128)S(1)}, u32[]{:S(2)}, u32[]{:S(2)}) collective-permute-start(f32[16,640]{1,0:T(8,128)S(1)} %get-tuple-element.43), channel_id=1, source_target_pairs={{16,0},{32,16},{48,32},{64,48},{80,64},{96,80},{112,96},{128,112},... | collective-permute-start | bytes 122888 | tf_op jit(solution)/shard_map/ppermute | solution.py:303
  89.2 5.3 %collective-permute-start.4 = (f32[16,640]{1,0:T(8,128)S(1)}, f32[16,640]{1,0:T(8,128)S(1)}, u32[]{:S(2)}, u32[]{:S(2)}) collective-permute-start(f32[16,640]{1,0:T(8,128)S(1)} %get-tuple-element.44), channel_id=1, source_target_pairs={{0,16},{16,32},{32,48},{48,64},{64,80},{80,96},{96,112},{112,128},... | collective-permute-start | bytes 122888 | tf_op jit(solution)/shard_map/ppermute | solution.py:303
  91.6 2.9 %copy-start.5 = (f32[16,640]{1,0:T(8,128)}, f32[16,640]{1,0:T(8,128)S(1)}, u32[]{:S(2)}) copy-start(f32[16,640]{1,0:T(8,128)S(1)} %collective-permute-done.5.lse_bot_ref) | copy-start | bytes 122884
  94.5 0.6 copy-start.6
  100.7 12.6 %collective-permute-start.6 = (f32[3,32,256]{2,1,0:T(8,128)}, f32[3,32,256]{2,1,0:T(8,128)S(1)}, u32[]{:S(2)}, u32[]{:S(2)}) collective-permute-start(f32[3,32,256]{2,1,0:T(8,128)} %get-tuple-element.39), channel_id=1, source_target_pairs={{0,4},{4,0},{8,12},{12,8},{1,5},{5,1},{9,13},{13,9},{2,6},{6,2},{1... | collective-permute-start | bytes 294920 | tf_op jit(solution)/shard_map/ppermute | solution.py:307
  102.8 19.3 %collective-permute-start.8 = (f32[3,32,256]{2,1,0:T(8,128)}, f32[3,32,256]{2,1,0:T(8,128)S(1)}, u32[]{:S(2)}, u32[]{:S(2)}) collective-permute-start(f32[3,32,256]{2,1,0:T(8,128)} %get-tuple-element.40), channel_id=1, source_target_pairs={{0,12},{4,8},{8,4},{12,0},{1,13},{5,9},{9,5},{13,1},{2,14},{6,10},... | collective-permute-start | bytes 294920 | tf_op jit(solution)/shard_map/ppermute | solution.py:307
  114.2 13.1 %collective-permute-start.7 = (f32[3,32,256]{2,1,0:T(8,128)S(1)}, f32[3,32,256]{2,1,0:T(8,128)S(1)}, u32[]{:S(2)}, u32[]{:S(2)}) collective-permute-start(f32[3,32,256]{2,1,0:T(8,128)S(1)} %add.36), channel_id=1, source_target_pairs={{0,12},{4,8},{8,4},{12,0},{1,13},{5,9},{9,5},{13,1},{2,14},{6,10},... | collective-permute-start | bytes 294920 | tf_op jit(solution)/shard_map/ppermute | solution.py:307
  122.9 12.6 %collective-permute-start.9 = (f32[3,32,256]{2,1,0:T(8,128)S(1)}, f32[3,32,256]{2,1,0:T(8,128)S(1)}, u32[]{:S(2)}, u32[]{:S(2)}) collective-permute-start(f32[3,32,256]{2,1,0:T(8,128)S(1)} %add.38), channel_id=1, source_target_pairs={{0,4},{4,0},{8,12},{12,8},{1,5},{5,1},{9,13},{13,9},{2,6},{6,2},{1... | collective-permute-start | bytes 294920 | tf_op jit(solution)/shard_map/ppermute | solution.py:307

commit v3 on v2

--- a/solution.py
+++ b/solution.py
@@ -16,7 +16,7 @@
 GREY = (0.299 / 255.0, 0.587 / 255.0, 0.114 / 255.0)
 W0, W1, W2 = 640, 384, 256
 M0, M1, M2 = 512, 256, 128
-PARAMS = pltpu.CompilerParams(vmem_limit_bytes=56 * 1024 * 1024)
+PARAMS = pltpu.CompilerParams(vmem_limit_bytes=20 * 1024 * 1024)
 
 
 def lane_of(col, main, wide):
@@ -342,9 +342,9 @@
             column_taps("up", M1, W1, M0, W0)[:, :M0],
         )
     ]
+    parts = lax.all_to_all(jnp.broadcast_to(lse, (4, 32, W0)), "zh", 0, 0)
     details = []
     for step, flip in enumerate((1, 3)):
-        other = partner(lse, flip)
         detail = pl.pallas_call(
             functools.partial(pyramid_kernel, (2 * step, 2 * step + 1)),
             out_shape=(
@@ -366,9 +366,10 @@
             cost_estimate=pl.CostEstimate(flops=2_000_000_000, bytes_accessed=6_000_000, transcendentals=0),
             name="pyramid",
         )(place, main, top, bot, *taps)
-        other, *detail = lax.optimization_barrier((other, *detail))
         details += detail
-        lse = join_lse(lse, other)
+    parts, *details = lax.optimization_barrier((parts, *details))
+    peak = jnp.max(parts, axis=0)
+    lse = peak + jnp.log(jnp.sum(jnp.exp(parts - peak), axis=0))
     lse_top, lse_bot = neighbours(lse[:16], lse[16:])
 
     left, right = pl.pallas_call(

time: 152 us -> 168 us (1.11)
  the two profiles are of different devices: /device:TPU:88 before, /device:TPU:40 now
where the time goes in v3:
time: 168 us; the launch traced here: 167 us
  waiting for transfers between devices  42.4 us (25%)
  blocking collectives  41.4 us (25%)
  starting transfers between devices  37.7 us (22%)
  local copies, waits for them, and re-layouts  27.3 us (16%)
  Pallas kernels  15.9 us (9%)
  other arithmetic  2.2 us (1%)
    all_to_all x1, blocking collectives, on_device(): main = lax.all_to_all(packed, 'x', 0, 0)  26.2 us
    ppermute x4, waiting for transfers between devices, partner(): return lax.ppermute(value, 'zh', [(i, i ^ flip) for i in range(4)])  24.7 us
    unnamed x54, local copies, waits for them, and re-layouts  24.1 us
    all_to_all x1, blocking collectives, on_device(): joined = lax.all_to_all(jnp.broadcast_to(whole, (4, 3, 32, 512)), 'x', 0, 0)  15.2 us
    all_to_all x1, starting transfers between devices, on_device(): parts = lax.all_to_all(jnp.broadcast_to(lse, (4, 32, W0)), 'zh', 0, 0)  14.2 us
    ppermute x4, starting transfers between devices, partner(): return lax.ppermute(value, 'zh', [(i, i ^ flip) for i in range(4)])  12.4 us
    ppermute x2, waiting for transfers between devices, neighbours(): lax.ppermute(high_part, ROWS, forward)  8.56 us
    pallas_call x2, Pallas kernels, on_device(): pl.pallas_call(functools.partial(pyramid_kernel, (2 * step, 2 * step + 1)...  7.03 us
  transfers between devices with their start and end apart: 9, of which 8 were waited for; matrix products, arithmetic and copies ran while one was open for 0% of the time, Pallas kernels for 4%

profile of v3, /device:TPU:40, one launch (start us, length us, event | category | flops | bytes accessed | tf_op | source)
XLA Modules:
  0.0 167.1 jit_solution(14476844951531891204)
XLA Ops:
  0.0 1.4 copy-done
  2.9 26.2 %all_to_all.15.main_ref = f32[4,2,104,512]{3,2,1,0:T(8,128)S(1)} all-to-all(f32[4,2,104,512]{3,2,1,0:T(8,128)S(1)} %pack.1), channel_id=1, replica_groups=mesh['zl'=4,'y'=4,'c'=2,'zh'=4,'x'=4] {'x'}, dimensions={0} | all-to-all | bytes 3407872 | tf_op jit(solution)/shard_map/all_to_all | solution.py:324
  29.1 1.4 slice_bitcast_fusion
  30.4 1.9 %collective-permute-start = (f32[4,104,512]{2,1,0:T(8,128)}, f32[4,104,512]{2,1,0:T(8,128)S(1)}, u32[]{:S(2)}, u32[]{:S(2)}) collective-permute-start(f32[4,104,512]{2,1,0:T(8,128)} %get-tuple-element.40), channel_id=1, source_target_pairs={{0,16},{16,32},{32,48},{48,64},{64,80},{80,96},{96,112},{112,128},... | collective-permute-start | bytes 2555912 | tf_op jit(solution)/shard_map/ppermute | solution.py:303
  32.4 3.6 %collective-permute-start.1 = (f32[4,104,512]{2,1,0:T(8,128)}, f32[4,104,512]{2,1,0:T(8,128)S(1)}, u32[]{:S(2)}, u32[]{:S(2)}) collective-permute-start(f32[4,104,512]{2,1,0:T(8,128)} %get-tuple-element.39), channel_id=1, source_target_pairs={{16,0},{32,16},{48,32},{64,48},{80,64},{96,80},{112,96},{128,112},... | collective-permute-start | bytes 2555912 | tf_op jit(solution)/shard_map/ppermute | solution.py:303
  36.1 8.6 %collective-permute-done.top_ref = f32[4,104,512]{2,1,0:T(8,128)S(1)} collective-permute-done((f32[4,104,512]{2,1,0:T(8,128)}, f32[4,104,512]{2,1,0:T(8,128)S(1)}, u32[]{:S(2)}, u32[]{:S(2)}) %collective-permute-start) | collective-permute-done | bytes 852000 | tf_op jit(solution)/shard_map/ppermute | solution.py:303
  49.7 5.3 %energy.1 = (f32[8,64,640]{2,1,0:T(8,128)S(1)}, f32[32,640]{1,0:T(8,128)S(1)}) custom-call(s32[2]{0:T(128)S(1)} %pad_add_fusion.place_ref, f32[4,2,104,512]{3,2,1,0:T(8,128)S(1)} %all_to_all.15.main_ref, f32[4,104,512]{2,1,0:T(8,128)S(1)} %copy-done.2, f32[4,104,512]{2,1,0:T(8,128)S(1)} %copy-done.5), custom_call_target="tpu_custom_call" | custom-call | tf_op jit(solution)/shard_map/energy/pallas_call | solution.py:326
  55.8 14.2 %all-to-all-start.1 = ((f32[4,32,640]{2,1,0:T(8,128)}), f32[4,32,640]{2,1,0:T(8,128)}, u32[]{:S(2)}, u32[]{:S(2)}) async-start(f32[4,32,640]{2,1,0:T(8,128)} %broadcast_in_dim.7), calls=%async_computation.1 | async-start | bytes 655360 | tf_op jit(solution)/shard_map/all_to_all | solution.py:345
  70.0 1.2 copy-done.3
  75.2 3.5 %pyramid.3 = (f32[384,512]{1,0:T(8,128)S(1)}, f32[384,384]{1,0:T(8,128)S(1)}, f32[192,256]{1,0:T(8,128)S(1)}) custom-call(s32[2]{0:T(128)S(1)} %pad_add_fusion.place_ref, f32[4,2,104,512]{3,2,1,0:T(8,128)S(1)} %all_to_all.15.main_ref, f32[4,104,512]{2,1,0:T(8,128)S(1)} %copy-done.3, f32[4,104,512]{2,1,0:T(8,128)S(1)} %copy-done.6, ...), custom_call_target="tpu_custom_call" | custom-call | flops 2000000000 | bytes 6000000 | tf_op jit(solution)/shard_map/pyramid/pallas_call | solution.py:348
  81.1 3.5 %pyramid.2 = (f32[384,512]{1,0:T(8,128)S(1)}, f32[384,384]{1,0:T(8,128)S(1)}, f32[192,256]{1,0:T(8,128)S(1)}) custom-call(s32[2]{0:T(128)S(1)} %pad_add_fusion.place_ref, f32[4,2,104,512]{3,2,1,0:T(8,128)S(1)} %all_to_all.15.main_ref, f32[4,104,512]{2,1,0:T(8,128)S(1)} %copy-done.3, f32[4,104,512]{2,1,0:T(8,128)S(1)} %copy-done.6, ...), custom_call_target="tpu_custom_call" | custom-call | flops 2000000000 | bytes 6000000 | tf_op jit(solution)/shard_map/pyramid/pallas_call | solution.py:348
  87.0 6.6 %all-to-all-done.1 = f32[4,32,640]{2,1,0:T(8,128)} async-done(((f32[4,32,640]{2,1,0:T(8,128)}), f32[4,32,640]{2,1,0:T(8,128)}, u32[]{:S(2)}, u32[]{:S(2)}) %all-to-all-start.1) | async-done | bytes 327712 | tf_op jit(solution)/shard_map/all_to_all | solution.py:345
  95.7 2.8 %collective-permute-start.2 = (f32[16,640]{1,0:T(8,128)S(1)}, f32[16,640]{1,0:T(8,128)S(1)}, u32[]{:S(2)}, u32[]{:S(2)}) collective-permute-start(f32[16,640]{1,0:T(8,128)S(1)} %get-tuple-element.42), channel_id=1, source_target_pairs={{0,16},{16,32},{32,48},{48,64},{64,80},{80,96},{96,112},{112,128},... | collective-permute-start | bytes 122888 | tf_op jit(solution)/shard_map/ppermute | solution.py:303
  98.5 2.7 %collective-permute-start.3 = (f32[16,640]{1,0:T(8,128)S(1)}, f32[16,640]{1,0:T(8,128)S(1)}, u32[]{:S(2)}, u32[]{:S(2)}) collective-permute-start(f32[16,640]{1,0:T(8,128)S(1)} %get-tuple-element.41), channel_id=1, source_target_pairs={{16,0},{32,16},{48,32},{64,48},{80,64},{96,80},{112,96},{128,112},... | collective-permute-start | bytes 122888 | tf_op jit(solution)/shard_map/ppermute | solution.py:303
  101.3 1.6 collective-permute-done.3.lse_bot_ref
  110.9 2.7 %mix.1 = (f32[3,32,256]{2,1,0:T(8,128)S(1)}, f32[3,32,256]{2,1,0:T(8,128)S(1)}) custom-call(s32[2]{0:T(128)S(1)} %pad_add_fusion.place_ref, f32[8,64,640]{2,1,0:T(8,128)S(1)} %get-tuple-element.22.logit_ref, f32[32,640]{1,0:T(8,128)S(1)} %log_add_fusion.lse_ref, f32[16,640]{1,0:T(8,128)S(1)} %collective-permute-done.2.lse_top_ref, ...), custom_call_target="tpu_custom_call" | custom-call | tf_op jit(solution)/shard_map/mix/pallas_call | solution.py:375
  113.6 4.6 %collective-permute-start.4 = (f32[3,32,256]{2,1,0:T(8,128)S(1)}, f32[3,32,256]{2,1,0:T(8,128)S(1)}, u32[]{:S(2)}, u32[]{:S(2)}) collective-permute-start(f32[3,32,256]{2,1,0:T(8,128)S(1)} %get-tuple-element.37), channel_id=1, source_target_pairs={{0,4},{4,0},{8,12},{12,8},{1,5},{5,1},{9,13},{13,9},{2,6},{6,2},{1... | collective-permute-start | bytes 294920 | tf_op jit(solution)/shard_map/ppermute | solution.py:307
  118.2 4.0 %collective-permute-start.6 = (f32[3,32,256]{2,1,0:T(8,128)S(1)}, f32[3,32,256]{2,1,0:T(8,128)S(1)}, u32[]{:S(2)}, u32[]{:S(2)}) collective-permute-start(f32[3,32,256]{2,1,0:T(8,128)S(1)} %get-tuple-element.38), channel_id=1, source_target_pairs={{0,12},{4,8},{8,4},{12,0},{1,13},{5,9},{9,5},{13,1},{2,14},{6,10},... | collective-permute-start | bytes 294920 | tf_op jit(solution)/shard_map/ppermute | solution.py:307
  122.2 6.4 %collective-permute-done.4 = f32[3,32,256]{2,1,0:T(8,128)S(1)} collective-permute-done((f32[3,32,256]{2,1,0:T(8,128)S(1)}, f32[3,32,256]{2,1,0:T(8,128)S(1)}, u32[]{:S(2)}, u32[]{:S(2)}) %collective-permute-start.4) | collective-permute-done | bytes 98336 | tf_op jit(solution)/shard_map/ppermute | solution.py:307
  128.6 1.9 %collective-permute-start.5 = (f32[3,32,256]{2,1,0:T(8,128)S(1)}, f32[3,32,256]{2,1,0:T(8,128)S(1)}, u32[]{:S(2)}, u32[]{:S(2)}) collective-permute-start(f32[3,32,256]{2,1,0:T(8,128)S(1)} %add.24), channel_id=1, source_target_pairs={{0,12},{4,8},{8,4},{12,0},{1,13},{5,9},{9,5},{13,1},{2,14},{6,10},... | collective-permute-start | bytes 294920 | tf_op jit(solution)/shard_map/ppermute | solution.py:307
  130.5 6.6 %collective-permute-done.6 = f32[3,32,256]{2,1,0:T(8,128)S(1)} collective-permute-done((f32[3,32,256]{2,1,0:T(8,128)S(1)}, f32[3,32,256]{2,1,0:T(8,128)S(1)}, u32[]{:S(2)}, u32[]{:S(2)}) %collective-permute-start.6) | collective-permute-done | bytes 98336 | tf_op jit(solution)/shard_map/ppermute | solution.py:307
  137.2 1.9 %collective-permute-start.7 = (f32[3,32,256]{2,1,0:T(8,128)S(1)}, f32[3,32,256]{2,1,0:T(8,128)S(1)}, u32[]{:S(2)}, u32[]{:S(2)}) collective-permute-start(f32[3,32,256]{2,1,0:T(8,128)S(1)} %add.26), channel_id=1, source_target_pairs={{0,4},{4,0},{8,12},{12,8},{1,5},{5,1},{9,13},{13,9},{2,6},{6,2},{1... | collective-permute-start | bytes 294920 | tf_op jit(solution)/shard_map/ppermute | solution.py:307
  139.7 11.1 %collective-permute-done.7 = f32[3,32,256]{2,1,0:T(8,128)S(1)} collective-permute-done((f32[3,32,256]{2,1,0:T(8,128)S(1)}, f32[3,32,256]{2,1,0:T(8,128)S(1)}, u32[]{:S(2)}, u32[]{:S(2)}) %collective-permute-start.7) | collective-permute-done | bytes 98336 | tf_op jit(solution)/shard_map/ppermute | solution.py:307
  150.9 15.2 %all_to_all.16 = f32[4,3,32,512]{3,2,1,0:T(8,128)S(1)} all-to-all(f32[4,3,32,512]{3,2,1,0:T(8,128)S(1)} %broadcast_in_dim.8), channel_id=1, replica_groups=mesh['zl'=4,'y'=4,'c'=2,'zh'=4,'x'=4] {'x'}, dimensions={0} | all-to-all | bytes 1572864 | tf_op jit(solution)/shard_map/all_to_all | solution.py:396
  (69 shorter events, 27.8 us)
Async XLA Ops:
  0.0 1.4 copy-start
  30.4 14.2 %collective-permute-start = (f32[4,104,512]{2,1,0:T(8,128)}, f32[4,104,512]{2,1,0:T(8,128)S(1)}, u32[]{:S(2)}, u32[]{:S(2)}) collective-permute-start(f32[4,104,512]{2,1,0:T(8,128)} %get-tuple-element.40), channel_id=1, source_target_pairs={{0,16},{16,32},{32,48},{48,64},{64,80},{80,96},{96,112},{112,128},... | collective-permute-start | bytes 2555912 | tf_op jit(solution)/shard_map/ppermute | solution.py:303
  32.4 14.2 %collective-permute-start.1 = (f32[4,104,512]{2,1,0:T(8,128)}, f32[4,104,512]{2,1,0:T(8,128)S(1)}, u32[]{:S(2)}, u32[]{:S(2)}) collective-permute-start(f32[4,104,512]{2,1,0:T(8,128)} %get-tuple-element.39), channel_id=1, source_target_pairs={{16,0},{32,16},{48,32},{64,48},{80,64},{96,80},{112,96},{128,112},... | collective-permute-start | bytes 2555912 | tf_op jit(solution)/shard_map/ppermute | solution.py:303
  47.4 1.2 copy-start.2
  48.6 1.2 copy-start.5
  49.7 20.3 %copy-start.15 = (bf16[640,384]{1,0:T(8,128)(2,1)S(1)}, bf16[640,384]{1,0:T(8,128)(2,1)}, u32[]{:S(2)}) copy-start(bf16[640,384]{1,0:T(8,128)(2,1)} %constant.34.clone.d1_ref) | copy-start | bytes 1474564
  55.8 37.8 %all-to-all-start.1 = ((f32[4,32,640]{2,1,0:T(8,128)}), f32[4,32,640]{2,1,0:T(8,128)}, u32[]{:S(2)}, u32[]{:S(2)}) async-start(f32[4,32,640]{2,1,0:T(8,128)} %broadcast_in_dim.7), calls=%async_computation.1 | async-start | bytes 655360 | tf_op jit(solution)/shard_map/all_to_all | solution.py:345
  70.0 1.2 copy-start.3
  71.2 1.2 copy-start.6
  72.3 1.0 copy-start.16
  73.3 0.9 copy-start.18
  74.3 0.9 copy-start.20
  87.0 15.9 %copy-start.8 = (f32[384,512]{1,0:T(8,128)S(1)}, f32[384,512]{1,0:T(8,128)}, u32[]{:S(2)}) copy-start(f32[384,512]{1,0:T(8,128)} %copy-done.7) | copy-start | bytes 2359300
  95.7 5.6 %collective-permute-start.2 = (f32[16,640]{1,0:T(8,128)S(1)}, f32[16,640]{1,0:T(8,128)S(1)}, u32[]{:S(2)}, u32[]{:S(2)}) collective-permute-start(f32[16,640]{1,0:T(8,128)S(1)} %get-tuple-element.42), channel_id=1, source_target_pairs={{0,16},{16,32},{32,48},{48,64},{64,80},{80,96},{96,112},{112,128},... | collective-permute-start | bytes 122888 | tf_op jit(solution)/shard_map/ppermute | solution.py:303
  98.5 4.4 %collective-permute-start.3 = (f32[16,640]{1,0:T(8,128)S(1)}, f32[16,640]{1,0:T(8,128)S(1)}, u32[]{:S(2)}, u32[]{:S(2)}) collective-permute-start(f32[16,640]{1,0:T(8,128)S(1)} %get-tuple-element.41), channel_id=1, source_target_pairs={{16,0},{32,16},{48,32},{64,48},{80,64},{96,80},{112,96},{128,112},... | collective-permute-start | bytes 122888 | tf_op jit(solution)/shard_map/ppermute | solution.py:303
  102.9 1.1 copy-start.10
  104.1 1.1 copy-start.12
  105.1 1.1 copy-start.14
  106.2 1.0 copy-start.17
  107.2 0.9 copy-start.19
  113.6 15.0 %collective-permute-start.4 = (f32[3,32,256]{2,1,0:T(8,128)S(1)}, f32[3,32,256]{2,1,0:T(8,128)S(1)}, u32[]{:S(2)}, u32[]{:S(2)}) collective-permute-start(f32[3,32,256]{2,1,0:T(8,128)S(1)} %get-tuple-element.37), channel_id=1, source_target_pairs={{0,4},{4,0},{8,12},{12,8},{1,5},{5,1},{9,13},{13,9},{2,6},{6,2},{1... | collective-permute-start | bytes 294920 | tf_op jit(solution)/shard_map/ppermute | solution.py:307
  118.2 18.9 %collective-permute-start.6 = (f32[3,32,256]{2,1,0:T(8,128)S(1)}, f32[3,32,256]{2,1,0:T(8,128)S(1)}, u32[]{:S(2)}, u32[]{:S(2)}) collective-permute-start(f32[3,32,256]{2,1,0:T(8,128)S(1)} %get-tuple-element.38), channel_id=1, source_target_pairs={{0,12},{4,8},{8,4},{12,0},{1,13},{5,9},{9,5},{13,1},{2,14},{6,10},... | collective-permute-start | bytes 294920 | tf_op jit(solution)/shard_map/ppermute | solution.py:307
  128.6 11.1 %collective-permute-start.5 = (f32[3,32,256]{2,1,0:T(8,128)S(1)}, f32[3,32,256]{2,1,0:T(8,128)S(1)}, u32[]{:S(2)}, u32[]{:S(2)}) collective-permute-start(f32[3,32,256]{2,1,0:T(8,128)S(1)} %add.24), channel_id=1, source_target_pairs={{0,12},{4,8},{8,4},{12,0},{1,13},{5,9},{9,5},{13,1},{2,14},{6,10},... | collective-permute-start | bytes 294920 | tf_op jit(solution)/shard_map/ppermute | solution.py:307
  137.2 13.6 %collective-permute-start.7 = (f32[3,32,256]{2,1,0:T(8,128)S(1)}, f32[3,32,256]{2,1,0:T(8,128)S(1)}, u32[]{:S(2)}, u32[]{:S(2)}) collective-permute-start(f32[3,32,256]{2,1,0:T(8,128)S(1)} %add.26), channel_id=1, source_target_pairs={{0,4},{4,0},{8,12},{12,8},{1,5},{5,1},{9,13},{13,9},{2,6},{6,2},{1... | collective-permute-start | bytes 294920 | tf_op jit(solution)/shard_map/ppermute | solution.py:307
  (12 other events, 10.0 us)

commit v4 on v2

--- a/solution.py
+++ b/solution.py
@@ -16,7 +16,7 @@
 GREY = (0.299 / 255.0, 0.587 / 255.0, 0.114 / 255.0)
 W0, W1, W2 = 640, 384, 256
 M0, M1, M2 = 512, 256, 128
-PARAMS = pltpu.CompilerParams(vmem_limit_bytes=56 * 1024 * 1024)
+PARAMS = pltpu.CompilerParams(vmem_limit_bytes=20 * 1024 * 1024)
 
 
 def lane_of(col, main, wide):

time: 152 us -> 145 us (0.954)
  Pallas kernels: 28.5 us -> 15.9 us
  starting transfers between devices: 47.5 us -> 54.8 us
  other arithmetic: 2.58 us -> 0.22 us
    ppermute x6, starting transfers between devices: 38.8 us -> 46.2 us  [partner(): return lax.ppermute(value, 'zh', [(i, i ^ flip) for i in range(4)])]
    pallas_call x2, Pallas kernels: 12.4 us -> 7.04 us  [on_device(): pl.pallas_call(functools.partial(pyramid_kernel, (2 * step, 2 * step + 1)...]
    pallas_call x1, Pallas kernels: 5.52 us -> 2.79 us  [on_device(): pl.pallas_call(mix_kernel, out_shape=(jax.ShapeDtypeStruct((3, 32, 256),...]
    pallas_call x1, Pallas kernels: 7.68 us -> 5.33 us  [on_device(): pl.pallas_call(energy_kernel, out_shape=(jax.ShapeDtypeStruct((8, 64, W0)...]
    pallas_call x1, Pallas kernels: 2.9 us -> 0.78 us  [on_device(): pl.pallas_call(pack_kernel, out_shape=jax.ShapeDtypeStruct((4, 2, 104, 51...]
    add x4, other arithmetic: 1.85 us -> 0.06 us  [on_device(): left, right = (left + left_in, right + right_in)]
  transfers between devices with their start and end apart: 10 -> 10, of which waited for: 5 -> 8; matrix products, arithmetic and copies ran while one was open for 2% -> 0% of each run, Pallas kernels for 8% -> 5%
where the time goes in v4:
time: 145 us; the launch traced here: 144 us
  starting transfers between devices  54.8 us (38%)
  blocking collectives  41.4 us (29%)
  waiting for transfers between devices  27.3 us (19%)
  Pallas kernels  15.9 us (11%)
  local copies, waits for them, and re-layouts  4.52 us (3%)
    ppermute x6, starting transfers between devices, partner(): return lax.ppermute(value, 'zh', [(i, i ^ flip) for i in range(4)])  46.2 us
    all_to_all x1, blocking collectives, on_device(): main = lax.all_to_all(packed, 'x', 0, 0)  26.2 us
    all_to_all x1, blocking collectives, on_device(): joined = lax.all_to_all(jnp.broadcast_to(whole, (4, 3, 32, 512)), 'x', 0, 0)  15.2 us
    ppermute x6, waiting for transfers between devices, partner(): return lax.ppermute(value, 'zh', [(i, i ^ flip) for i in range(4)])  12.7 us
    ppermute x2, waiting for transfers between devices, neighbours(): lax.ppermute(low_part, ROWS, backward)  8 us
    pallas_call x2, Pallas kernels, on_device(): pl.pallas_call(functools.partial(pyramid_kernel, (2 * step, 2 * step + 1)...  7.04 us
    ppermute x2, waiting for transfers between devices, neighbours(): lax.ppermute(high_part, ROWS, forward)  6.61 us
    pallas_call x1, Pallas kernels, on_device(): pl.pallas_call(energy_kernel, out_shape=(jax.ShapeDtypeStruct((8, 64, W0)...  5.33 us
  transfers between devices with their start and end apart: 10, of which 8 were waited for; matrix products, arithmetic and copies ran while one was open for 0% of the time, Pallas kernels for 5%

profile of v4, /device:TPU:88, one launch (start us, length us, event | category | flops | bytes accessed | tf_op | source)
XLA Modules:
  0.0 144.3 jit_solution(11226039636601556408)
XLA Ops:
  0.0 1.4 copy-done
  2.9 26.2 %all_to_all.10.main_ref = f32[4,2,104,512]{3,2,1,0:T(8,128)S(1)} all-to-all(f32[4,2,104,512]{3,2,1,0:T(8,128)S(1)} %pack.1), channel_id=1, replica_groups=mesh['zl'=4,'y'=4,'c'=2,'zh'=4,'x'=4] {'x'}, dimensions={0} | all-to-all | bytes 3407872 | tf_op jit(solution)/shard_map/all_to_all | solution.py:324
  29.1 1.4 slice_bitcast_fusion
  30.5 1.9 %collective-permute-start.1 = (f32[4,104,512]{2,1,0:T(8,128)}, f32[4,104,512]{2,1,0:T(8,128)S(1)}, u32[]{:S(2)}, u32[]{:S(2)}) collective-permute-start(f32[4,104,512]{2,1,0:T(8,128)} %get-tuple-element.41), channel_id=1, source_target_pairs={{16,0},{32,16},{48,32},{64,48},{80,64},{96,80},{112,96},{128,112},... | collective-permute-start | bytes 2555912 | tf_op jit(solution)/shard_map/ppermute | solution.py:303
  32.4 2.4 %collective-permute-start = (f32[4,104,512]{2,1,0:T(8,128)}, f32[4,104,512]{2,1,0:T(8,128)S(1)}, u32[]{:S(2)}, u32[]{:S(2)}) collective-permute-start(f32[4,104,512]{2,1,0:T(8,128)} %get-tuple-element.42), channel_id=1, source_target_pairs={{0,16},{16,32},{32,48},{48,64},{64,80},{80,96},{96,112},{112,128},... | collective-permute-start | bytes 2555912 | tf_op jit(solution)/shard_map/ppermute | solution.py:303
  34.9 8.0 %collective-permute-done.1.bot_ref = f32[4,104,512]{2,1,0:T(8,128)S(1)} collective-permute-done((f32[4,104,512]{2,1,0:T(8,128)}, f32[4,104,512]{2,1,0:T(8,128)S(1)}, u32[]{:S(2)}, u32[]{:S(2)}) %collective-permute-start.1) | collective-permute-done | bytes 852000 | tf_op jit(solution)/shard_map/ppermute | solution.py:303
  42.9 3.7 %collective-permute-done.top_ref = f32[4,104,512]{2,1,0:T(8,128)S(1)} collective-permute-done((f32[4,104,512]{2,1,0:T(8,128)}, f32[4,104,512]{2,1,0:T(8,128)S(1)}, u32[]{:S(2)}, u32[]{:S(2)}) %collective-permute-start) | collective-permute-done | bytes 852000 | tf_op jit(solution)/shard_map/ppermute | solution.py:303
  46.6 5.3 %energy.1 = (f32[8,64,640]{2,1,0:T(8,128)S(1)}, f32[32,640]{1,0:T(8,128)S(1)}) custom-call(s32[2]{0:T(128)S(1)} %pad_add_fusion.place_ref, f32[4,2,104,512]{3,2,1,0:T(8,128)S(1)} %all_to_all.10.main_ref, f32[4,104,512]{2,1,0:T(8,128)S(1)} %collective-permute-done.top_ref, f32[4,104,512]{2,1,0:T(8,128)S(1)} %collective-permute-done.1.bot_ref), custom_call_target="tpu_custom_call" | custom-call | tf_op jit(solution)/shard_map/energy/pallas_call | solution.py:326
  51.9 9.1 %collective-permute-start.2 = (f32[32,640]{1,0:T(8,128)S(1)}, f32[32,640]{1,0:T(8,128)S(1)}, u32[]{:S(2)}, u32[]{:S(2)}) collective-permute-start(f32[32,640]{1,0:T(8,128)S(1)} %get-tuple-element.24), channel_id=1, source_target_pairs={{0,4},{4,0},{8,12},{12,8},{1,5},{5,1},{9,13},{13,9},{2,6},{6,2},{1... | collective-permute-start | bytes 245768 | tf_op jit(solution)/shard_map/ppermute | solution.py:307
  61.1 3.5 %pyramid.2 = (f32[384,512]{1,0:T(8,128)S(1)}, f32[384,384]{1,0:T(8,128)S(1)}, f32[192,256]{1,0:T(8,128)S(1)}) custom-call(s32[2]{0:T(128)S(1)} %pad_add_fusion.place_ref, f32[4,2,104,512]{3,2,1,0:T(8,128)S(1)} %all_to_all.10.main_ref, f32[4,104,512]{2,1,0:T(8,128)S(1)} %collective-permute-done.top_ref, f32[4,104,512]{2,1,0:T(8,128)S(1)} %collective-permute-done.1.bot_ref, ...), custom_call_target="tpu_custom_call" | custom-call | flops 2000000000 | bytes 6000000 | tf_op jit(solution)/shard_map/pyramid/pallas_call | solution.py:348
  64.6 1.9 %collective-permute-done.2 = f32[32,640]{1,0:T(8,128)S(1)} collective-permute-done((f32[32,640]{1,0:T(8,128)S(1)}, f32[32,640]{1,0:T(8,128)S(1)}, u32[]{:S(2)}, u32[]{:S(2)}) %collective-permute-start.2) | collective-permute-done | bytes 81952 | tf_op jit(solution)/shard_map/ppermute | solution.py:307
  66.5 11.1 %collective-permute-start.3 = (f32[32,640]{1,0:T(8,128)S(1)}, f32[32,640]{1,0:T(8,128)S(1)}, u32[]{:S(2)}, u32[]{:S(2)}) collective-permute-start(f32[32,640]{1,0:T(8,128)S(1)} %log_add_fusion.1), channel_id=1, source_target_pairs={{0,12},{4,8},{8,4},{12,0},{1,13},{5,9},{9,5},{13,1},{2,14},{6,10},... | collective-permute-start | bytes 245768 | tf_op jit(solution)/shard_map/ppermute | solution.py:307
  77.6 3.5 %pyramid.3 = (f32[384,512]{1,0:T(8,128)S(1)}, f32[384,384]{1,0:T(8,128)S(1)}, f32[192,256]{1,0:T(8,128)S(1)}) custom-call(s32[2]{0:T(128)S(1)} %pad_add_fusion.place_ref, f32[4,2,104,512]{3,2,1,0:T(8,128)S(1)} %all_to_all.10.main_ref, f32[4,104,512]{2,1,0:T(8,128)S(1)} %collective-permute-done.top_ref, f32[4,104,512]{2,1,0:T(8,128)S(1)} %collective-permute-done.1.bot_ref, ...), custom_call_target="tpu_custom_call" | custom-call | flops 2000000000 | bytes 6000000 | tf_op jit(solution)/shard_map/pyramid/pallas_call | solution.py:348
  81.3 1.9 %collective-permute-start.5 = (f32[16,640]{1,0:T(8,128)S(1)}, f32[16,640]{1,0:T(8,128)S(1)}, u32[]{:S(2)}, u32[]{:S(2)}) collective-permute-start(f32[16,640]{1,0:T(8,128)S(1)} %get-tuple-element.43), channel_id=1, source_target_pairs={{16,0},{32,16},{48,32},{64,48},{80,64},{96,80},{112,96},{128,112},... | collective-permute-start | bytes 122888 | tf_op jit(solution)/shard_map/ppermute | solution.py:303
  83.2 2.4 %collective-permute-start.4 = (f32[16,640]{1,0:T(8,128)S(1)}, f32[16,640]{1,0:T(8,128)S(1)}, u32[]{:S(2)}, u32[]{:S(2)}) collective-permute-start(f32[16,640]{1,0:T(8,128)S(1)} %get-tuple-element.44), channel_id=1, source_target_pairs={{0,16},{16,32},{32,48},{48,64},{64,80},{80,96},{96,112},{112,128},... | collective-permute-start | bytes 122888 | tf_op jit(solution)/shard_map/ppermute | solution.py:303
  85.7 2.9 %collective-permute-done.4.lse_top_ref = f32[16,640]{1,0:T(8,128)S(1)} collective-permute-done((f32[16,640]{1,0:T(8,128)S(1)}, f32[16,640]{1,0:T(8,128)S(1)}, u32[]{:S(2)}, u32[]{:S(2)}) %collective-permute-start.4) | collective-permute-done | bytes 40992 | tf_op jit(solution)/shard_map/ppermute | solution.py:303
  88.6 2.8 %mix.1 = (f32[3,32,256]{2,1,0:T(8,128)S(1)}, f32[3,32,256]{2,1,0:T(8,128)S(1)}) custom-call(s32[2]{0:T(128)S(1)} %pad_add_fusion.place_ref, f32[8,64,640]{2,1,0:T(8,128)S(1)} %get-tuple-element.23.logit_ref, f32[32,640]{1,0:T(8,128)S(1)} %log_add_fusion.lse_ref, f32[16,640]{1,0:T(8,128)S(1)} %collective-permute-done.4.lse_top_ref, ...), custom_call_target="tpu_custom_call" | custom-call | tf_op jit(solution)/shard_map/mix/pallas_call | solution.py:374
  91.4 4.3 %collective-permute-start.6 = (f32[3,32,256]{2,1,0:T(8,128)S(1)}, f32[3,32,256]{2,1,0:T(8,128)S(1)}, u32[]{:S(2)}, u32[]{:S(2)}) collective-permute-start(f32[3,32,256]{2,1,0:T(8,128)S(1)} %get-tuple-element.39), channel_id=1, source_target_pairs={{0,4},{4,0},{8,12},{12,8},{1,5},{5,1},{9,13},{13,9},{2,6},{6,2},{1... | collective-permute-start | bytes 294920 | tf_op jit(solution)/shard_map/ppermute | solution.py:307
  95.7 5.2 %collective-permute-start.8 = (f32[3,32,256]{2,1,0:T(8,128)S(1)}, f32[3,32,256]{2,1,0:T(8,128)S(1)}, u32[]{:S(2)}, u32[]{:S(2)}) collective-permute-start(f32[3,32,256]{2,1,0:T(8,128)S(1)} %get-tuple-element.40), channel_id=1, source_target_pairs={{0,12},{4,8},{8,4},{12,0},{1,13},{5,9},{9,5},{13,1},{2,14},{6,10},... | collective-permute-start | bytes 294920 | tf_op jit(solution)/shard_map/ppermute | solution.py:307
  100.9 3.0 %collective-permute-done.6 = f32[3,32,256]{2,1,0:T(8,128)S(1)} collective-permute-done((f32[3,32,256]{2,1,0:T(8,128)S(1)}, f32[3,32,256]{2,1,0:T(8,128)S(1)}, u32[]{:S(2)}, u32[]{:S(2)}) %collective-permute-start.6) | collective-permute-done | bytes 98336 | tf_op jit(solution)/shard_map/ppermute | solution.py:307
  104.0 9.7 %collective-permute-start.7 = (f32[3,32,256]{2,1,0:T(8,128)S(1)}, f32[3,32,256]{2,1,0:T(8,128)S(1)}, u32[]{:S(2)}, u32[]{:S(2)}) collective-permute-start(f32[3,32,256]{2,1,0:T(8,128)S(1)} %add.36), channel_id=1, source_target_pairs={{0,12},{4,8},{8,4},{12,0},{1,13},{5,9},{9,5},{13,1},{2,14},{6,10},... | collective-permute-start | bytes 294920 | tf_op jit(solution)/shard_map/ppermute | solution.py:307
  113.7 6.8 %collective-permute-start.9 = (f32[3,32,256]{2,1,0:T(8,128)S(1)}, f32[3,32,256]{2,1,0:T(8,128)S(1)}, u32[]{:S(2)}, u32[]{:S(2)}) collective-permute-start(f32[3,32,256]{2,1,0:T(8,128)S(1)} %add.38), channel_id=1, source_target_pairs={{0,4},{4,0},{8,12},{12,8},{1,5},{5,1},{9,13},{13,9},{2,6},{6,2},{1... | collective-permute-start | bytes 294920 | tf_op jit(solution)/shard_map/ppermute | solution.py:307
  120.8 7.3 %collective-permute-done.9 = f32[3,32,256]{2,1,0:T(8,128)S(1)} collective-permute-done((f32[3,32,256]{2,1,0:T(8,128)S(1)}, f32[3,32,256]{2,1,0:T(8,128)S(1)}, u32[]{:S(2)}, u32[]{:S(2)}) %collective-permute-start.9) | collective-permute-done | bytes 98336 | tf_op jit(solution)/shard_map/ppermute | solution.py:307
  128.2 15.2 %all_to_all.11 = f32[4,3,32,512]{3,2,1,0:T(8,128)S(1)} all-to-all(f32[4,3,32,512]{3,2,1,0:T(8,128)S(1)} %broadcast_in_dim.3), channel_id=1, replica_groups=mesh['zl'=4,'y'=4,'c'=2,'zh'=4,'x'=4] {'x'}, dimensions={0} | all-to-all | bytes 1572864 | tf_op jit(solution)/shard_map/all_to_all | solution.py:395
  (27 shorter events, 3.2 us)
Async XLA Ops:
  0.0 1.4 copy-start
  1.4 0.7 copy-start.5
  30.5 12.4 %collective-permute-start.1 = (f32[4,104,512]{2,1,0:T(8,128)}, f32[4,104,512]{2,1,0:T(8,128)S(1)}, u32[]{:S(2)}, u32[]{:S(2)}) collective-permute-start(f32[4,104,512]{2,1,0:T(8,128)} %get-tuple-element.41), channel_id=1, source_target_pairs={{16,0},{32,16},{48,32},{64,48},{80,64},{96,80},{112,96},{128,112},... | collective-permute-start | bytes 2555912 | tf_op jit(solution)/shard_map/ppermute | solution.py:303
  32.4 14.2 %collective-permute-start = (f32[4,104,512]{2,1,0:T(8,128)}, f32[4,104,512]{2,1,0:T(8,128)S(1)}, u32[]{:S(2)}, u32[]{:S(2)}) collective-permute-start(f32[4,104,512]{2,1,0:T(8,128)} %get-tuple-element.42), channel_id=1, source_target_pairs={{0,16},{16,32},{32,48},{48,64},{64,80},{80,96},{96,112},{112,128},... | collective-permute-start | bytes 2555912 | tf_op jit(solution)/shard_map/ppermute | solution.py:303
  34.9 26.2 %copy-start.1 = (bf16[640,384]{1,0:T(8,128)(2,1)S(1)}, bf16[640,384]{1,0:T(8,128)(2,1)}, u32[]{:S(2)}) copy-start(bf16[640,384]{1,0:T(8,128)(2,1)} %constant.32.clone.d1_ref) | copy-start | bytes 1474564
  34.9 26.2 %copy-start.2 = (bf16[384,512]{1,0:T(8,128)(2,1)S(1)}, bf16[384,512]{1,0:T(8,128)(2,1)}, u32[]{:S(2)}) copy-start(bf16[384,512]{1,0:T(8,128)(2,1)} %constant.35.clone.u1_ref) | copy-start | bytes 1179652
  34.9 26.2 %copy-start.3 = (bf16[256,384]{1,0:T(8,128)(2,1)S(1)}, bf16[256,384]{1,0:T(8,128)(2,1)}, u32[]{:S(2)}) copy-start(bf16[256,384]{1,0:T(8,128)(2,1)} %constant.34.clone.u2_ref) | copy-start | bytes 589828
  34.9 26.2 %copy-start.4 = (bf16[384,256]{1,0:T(8,128)(2,1)S(1)}, bf16[384,256]{1,0:T(8,128)(2,1)}, u32[]{:S(2)}) copy-start(bf16[384,256]{1,0:T(8,128)(2,1)} %constant.33.clone.d2_ref) | copy-start | bytes 589828
  51.9 14.5 %collective-permute-start.2 = (f32[32,640]{1,0:T(8,128)S(1)}, f32[32,640]{1,0:T(8,128)S(1)}, u32[]{:S(2)}, u32[]{:S(2)}) collective-permute-start(f32[32,640]{1,0:T(8,128)S(1)} %get-tuple-element.24), channel_id=1, source_target_pairs={{0,4},{4,0},{8,12},{12,8},{1,5},{5,1},{9,13},{13,9},{2,6},{6,2},{1... | collective-permute-start | bytes 245768 | tf_op jit(solution)/shard_map/ppermute | solution.py:307
  66.5 14.7 %collective-permute-start.3 = (f32[32,640]{1,0:T(8,128)S(1)}, f32[32,640]{1,0:T(8,128)S(1)}, u32[]{:S(2)}, u32[]{:S(2)}) collective-permute-start(f32[32,640]{1,0:T(8,128)S(1)} %log_add_fusion.1), channel_id=1, source_target_pairs={{0,12},{4,8},{8,4},{12,0},{1,13},{5,9},{9,5},{13,1},{2,14},{6,10},... | collective-permute-start | bytes 245768 | tf_op jit(solution)/shard_map/ppermute | solution.py:307
  81.3 4.3 %collective-permute-start.5 = (f32[16,640]{1,0:T(8,128)S(1)}, f32[16,640]{1,0:T(8,128)S(1)}, u32[]{:S(2)}, u32[]{:S(2)}) collective-permute-start(f32[16,640]{1,0:T(8,128)S(1)} %get-tuple-element.43), channel_id=1, source_target_pairs={{16,0},{32,16},{48,32},{64,48},{80,64},{96,80},{112,96},{128,112},... | collective-permute-start | bytes 122888 | tf_op jit(solution)/shard_map/ppermute | solution.py:303
  83.2 5.3 %collective-permute-start.4 = (f32[16,640]{1,0:T(8,128)S(1)}, f32[16,640]{1,0:T(8,128)S(1)}, u32[]{:S(2)}, u32[]{:S(2)}) collective-permute-start(f32[16,640]{1,0:T(8,128)S(1)} %get-tuple-element.44), channel_id=1, source_target_pairs={{0,16},{16,32},{32,48},{48,64},{64,80},{80,96},{96,112},{112,128},... | collective-permute-start | bytes 122888 | tf_op jit(solution)/shard_map/ppermute | solution.py:303
  91.4 12.6 %collective-permute-start.6 = (f32[3,32,256]{2,1,0:T(8,128)S(1)}, f32[3,32,256]{2,1,0:T(8,128)S(1)}, u32[]{:S(2)}, u32[]{:S(2)}) collective-permute-start(f32[3,32,256]{2,1,0:T(8,128)S(1)} %get-tuple-element.39), channel_id=1, source_target_pairs={{0,4},{4,0},{8,12},{12,8},{1,5},{5,1},{9,13},{13,9},{2,6},{6,2},{1... | collective-permute-start | bytes 294920 | tf_op jit(solution)/shard_map/ppermute | solution.py:307
  95.7 18.0 %collective-permute-start.8 = (f32[3,32,256]{2,1,0:T(8,128)S(1)}, f32[3,32,256]{2,1,0:T(8,128)S(1)}, u32[]{:S(2)}, u32[]{:S(2)}) collective-permute-start(f32[3,32,256]{2,1,0:T(8,128)S(1)} %get-tuple-element.40), channel_id=1, source_target_pairs={{0,12},{4,8},{8,4},{12,0},{1,13},{5,9},{9,5},{13,1},{2,14},{6,10},... | collective-permute-start | bytes 294920 | tf_op jit(solution)/shard_map/ppermute | solution.py:307
  104.0 16.8 %collective-permute-start.7 = (f32[3,32,256]{2,1,0:T(8,128)S(1)}, f32[3,32,256]{2,1,0:T(8,128)S(1)}, u32[]{:S(2)}, u32[]{:S(2)}) collective-permute-start(f32[3,32,256]{2,1,0:T(8,128)S(1)} %add.36), channel_id=1, source_target_pairs={{0,12},{4,8},{8,4},{12,0},{1,13},{5,9},{9,5},{13,1},{2,14},{6,10},... | collective-permute-start | bytes 294920 | tf_op jit(solution)/shard_map/ppermute | solution.py:307
  113.7 14.4 %collective-permute-start.9 = (f32[3,32,256]{2,1,0:T(8,128)S(1)}, f32[3,32,256]{2,1,0:T(8,128)S(1)}, u32[]{:S(2)}, u32[]{:S(2)}) collective-permute-start(f32[3,32,256]{2,1,0:T(8,128)S(1)} %add.38), channel_id=1, source_target_pairs={{0,4},{4,0},{8,12},{12,8},{1,5},{5,1},{9,13},{13,9},{2,6},{6,2},{1... | collective-permute-start | bytes 294920 | tf_op jit(solution)/shard_map/ppermute | solution.py:307

commit v5 on v4

--- a/solution.py
+++ b/solution.py
@@ -71,13 +71,27 @@
             out_ref[j, h, 96:104, 384:512] = tiles[1][8:16]
 
 
-def blocks_of(main_ref, top_ref, bot_ref, s):
-    return (top_ref.at[s], main_ref.at[s, 0], main_ref.at[s, 1], bot_ref.at[s])
-
-
-def halo_tile(block, a):
+class Strips:
+    def __init__(self, place_ref, main_ref, near_ref, far_ref):
+        self.even = place_ref[2] == 0
+        self.main, self.near, self.far = main_ref, near_ref, far_ref
+
+    def get(self, s, b, rows, cols):
+        if b in (1, 2):
+            return self.main[s, b - 1, rows, cols]
+        near, far = self.near[s, rows, cols], self.far[s, rows, cols]
+        return jnp.where(self.even, far, near) if b == 0 else jnp.where(self.even, near, far)
+
+    def samples(self, s, b, a):
+        return self.get(s, b, slice(16 * a, 16 * a + 16), slice(0, M0))
+
+    def halo(self, s, b, a):
+        return halo_tile(lambda cols: self.get(s, b, slice(96, 104), cols), a)
+
+
+def halo_tile(read, a):
     base, at = 128 * (a // 4), 32 * (a % 4)
-    tile = jnp.concatenate([block[96:104, base : base + 128], block[96:104, 256 + base : 384 + base]], axis=0)
+    tile = jnp.concatenate([read(slice(base, base + 128)), read(slice(256 + base, 384 + base))], axis=0)
     lane = lax.broadcasted_iota(jnp.int32, (16, 128), 1)
     return jnp.where((lane < 16) | (lane >= 112), pltpu.roll(tile, (112 - at) % 128, 1), 0.0)
 
@@ -87,21 +101,23 @@
     return jnp.where(lane < main + 64, lane, lane - wide)
 
 
-def energy_kernel(place_ref, main_ref, top_ref, bot_ref, logit_ref, lse_ref, grey_ref):
+def energy_kernel(place_ref, main_ref, near_ref, far_ref, logit_ref, lse_ref, grey_ref):
     row = lax.broadcasted_iota(jnp.int32, (64, W0), 0) + (place_ref[0] * 32 - 16)
     col = column_of((64, W0), M0, W0) + place_ref[1] * M0
     keep = (row >= 0) & (row < 1024) & (col >= 0) & (col < 2048)
 
+    strips = Strips(place_ref, main_ref, near_ref, far_ref)
+
     @pl.loop(0, 4)
     def _(s):
         for p in range(2):
-            for b, block in enumerate(blocks_of(main_ref, top_ref, bot_ref, s)):
+            for b in range(4):
                 main = 0.0
                 tile = 0.0
                 for c in range(3):
                     a = 3 * p + c
-                    main = main + block[16 * a : 16 * a + 16, :] * GREY[c]
-                    tile = tile + halo_tile(block, a) * GREY[c]
+                    main = main + strips.samples(s, b, a) * GREY[c]
+                    tile = tile + strips.halo(s, b, a) * GREY[c]
                 grey_ref[16 * b : 16 * b + 16, 0:M0] = main
                 grey_ref[16 * b : 16 * b + 16, M0:W0] = tile
             grey = grey_ref[...]
@@ -198,19 +214,19 @@
 
 
 def pyramid_kernel(
-    sources, place_ref, main_ref, top_ref, bot_ref, d1_ref, d2_ref, u2_ref, u1_ref,
+    sources, place_ref, main_ref, near_ref, far_ref, d1_ref, d2_ref, u2_ref, u1_ref,
     detail0_ref, detail1_ref, l2_ref, x_ref, s1_ref, l1_ref, s2_ref, s3_ref, s4_ref,
 ):
     strip = place_ref[0]
     v1 = down_rows(32, 64, 1, strip * 16 - 8, 512)
     v2, p2, p1 = row_matrices(strip)
     inside1, inside2 = level_masks(192, 96, place_ref[1])
+    strips = Strips(place_ref, main_ref, near_ref, far_ref)
     for i, s in enumerate(sources):
-        blocks = blocks_of(main_ref, top_ref, bot_ref, s)
         for a in range(6):
-            for b, block in enumerate(blocks):
-                x_ref[16 * b : 16 * b + 16, 0:M0] = block[16 * a : 16 * a + 16, :].astype(BF)
-                x_ref[16 * b : 16 * b + 16, M0:W0] = halo_tile(block, a).astype(BF)
+            for b in range(4):
+                x_ref[16 * b : 16 * b + 16, 0:M0] = strips.samples(s, b, a).astype(BF)
+                x_ref[16 * b : 16 * b + 16, M0:W0] = strips.halo(s, b, a).astype(BF)
             put(s1_ref, 6, a, 32, dot(v1, x_ref[...]))
         l1_ref[...] = jnp.where(inside1, resampled(s1_ref, d1_ref), 0.0)
         for a in range(6):
@@ -232,7 +248,7 @@
 
 
 def mix_kernel(
-    place_ref, logit_ref, lse_ref, lse_top_ref, lse_bot_ref,
+    place_ref, logit_ref, lse_ref, near_ref, far_ref,
     fine_a_ref, mid_a_ref, low_a_ref, fine_b_ref, mid_b_ref, low_b_ref,
     d1_ref, d2_ref, u2_ref, u1_ref,
     left_ref, right_ref, w0_ref, s1_ref, w1_ref, s2_ref, s3_ref, s4_ref,
@@ -243,7 +259,13 @@
     col = column_of((16, W0), M0, W0)
     inside_col = (col >= -10) & (col <= 522) & (col + k * M0 >= 0) & (col + k * M0 < 2048)
     row = lax.broadcasted_iota(jnp.int32, (16, W0), 0)
-    lses = (lse_top_ref[...], lse_ref[0:16], lse_ref[16:32], lse_bot_ref[...])
+    even = place_ref[2] == 0
+    lses = (
+        jnp.where(even, far_ref[...], near_ref[...]),
+        lse_ref[0:16],
+        lse_ref[16:32],
+        jnp.where(even, near_ref[...], far_ref[...]),
+    )
     keeps = []
     for b in range(4):
         r = row + (16 * b - 16)
@@ -296,23 +318,33 @@
     return [pl.BlockSpec(memory_space=pltpu.SMEM)]
 
 
-def neighbours(low_part, high_part):
+def neighbours(halves, core):
     count = lax.axis_size(ROWS)
-    forward = [(i, i + 1) for i in range(count - 1)]
-    backward = [(i + 1, i) for i in range(count - 1)]
-    return lax.ppermute(high_part, ROWS, forward), lax.ppermute(low_part, ROWS, backward)
+    swaps = [(i, i + 1) for i in range(1, count - 1, 2)]
+    swaps += [(b, a) for a, b in swaps]
+    pick = functools.partial(lax.dynamic_index_in_dim, halves, axis=-3, keepdims=False)
+    near = lax.ppermute(pick(1 - core), "c", [(0, 1), (1, 0)])
+    far = lax.ppermute(pick(core), ROWS, swaps)
+    return near, far
 
 
 def partner(value, flip):
     return lax.ppermute(value, "zh", [(i, i ^ flip) for i in range(4)])
 
 
+def crossed(value, flips):
+    pairs = [(4 * c + i, 4 * c + (i ^ flip)) for c, flip in enumerate(flips) for i in range(4)]
+    return lax.ppermute(value, ("c", "zh"), pairs)
+
+
 def join_lse(a, b):
     return jnp.maximum(a, b) + jnp.log(1.0 + jnp.exp(-jnp.abs(a - b)))
 
 
 def on_device(samples, gain):
-    place = jnp.stack([lax.axis_index(ROWS), lax.axis_index("x")]).astype(jnp.int32)
+    samples, strip, column, core = lax.optimization_barrier(
+        (samples, lax.axis_index(ROWS), lax.axis_index("x"), lax.axis_index("c"))
+    )
     packed = pl.pallas_call(
         pack_kernel,
         out_shape=jax.ShapeDtypeStruct((4, 2, 104, 512), F32),
@@ -322,7 +354,9 @@
         name="pack",
     )(samples, gain)
     main = lax.all_to_all(packed, "x", 0, 0)
-    top, bot = neighbours(main[:, 0], main[:, 1])
+    main, strip, column, core = lax.optimization_barrier((main, strip, column, core))
+    near, far = neighbours(main, core)
+    place = jnp.stack([strip, column, core]).astype(jnp.int32)
     logits, lse = pl.pallas_call(
         energy_kernel,
         out_shape=(jax.ShapeDtypeStruct((8, 64, W0), F32), jax.ShapeDtypeStruct((32, W0), F32)),
@@ -331,7 +365,7 @@
         scratch_shapes=[pltpu.VMEM((64, W0), F32)],
         compiler_params=PARAMS,
         name="energy",
-    )(place, main, top, bot)
+    )(place, main, near, far)
 
     taps = [
         jnp.asarray(t, BF)
@@ -343,8 +377,8 @@
         )
     ]
     details = []
-    for step, flip in enumerate((1, 3)):
-        other = partner(lse, flip)
+    for step, flips in enumerate(((1, 3), (3, 1))):
+        other = crossed(lse, flips)
         detail = pl.pallas_call(
             functools.partial(pyramid_kernel, (2 * step, 2 * step + 1)),
             out_shape=(
@@ -365,11 +399,11 @@
             compiler_params=PARAMS,
             cost_estimate=pl.CostEstimate(flops=2_000_000_000, bytes_accessed=6_000_000, transcendentals=0),
             name="pyramid",
-        )(place, main, top, bot, *taps)
+        )(place, main, near, far, *taps)
         other, *detail = lax.optimization_barrier((other, *detail))
         details += detail
         lse = join_lse(lse, other)
-    lse_top, lse_bot = neighbours(lse[:16], lse[16:])
+    lse_near, lse_far = neighbours(lse.reshape(2, 16, W0), core)
 
     left, right = pl.pallas_call(
         mix_kernel,
@@ -386,7 +420,7 @@
         ],
         compiler_params=PARAMS,
         name="mix",
-    )(place, logits, lse, lse_top, lse_bot, *details, *taps)
+    )(place, logits, lse, lse_near, lse_far, *details, *taps)
 
     for a, b in ((1, 3), (3, 1)):
         left_in, right_in = partner(left, a), partner(right, b)

time: 145 us -> 145 us (level)
  the two profiles are of different devices: /device:TPU:88 before, /device:TPU:24 now
where the time goes in v5:
time: 145 us
  starting transfers between devices  57.8 us (40%)
  blocking collectives  41.5 us (29%)
  waiting for transfers between devices  25.7 us (18%)
  Pallas kernels  16 us (11%)
  local copies, waits for them, and re-layouts  3.26 us (2%)
    ppermute x4, starting transfers between devices, partner(): return lax.ppermute(value, 'zh', [(i, i ^ flip) for i in range(4)])  27.2 us
    all_to_all x1, blocking collectives, on_device(): main = lax.all_to_all(packed, 'x', 0, 0)  26.2 us
    ppermute x2, starting transfers between devices, crossed(): return lax.ppermute(value, ('c', 'zh'), pairs)  19.7 us
    all_to_all x1, blocking collectives, on_device(): joined = lax.all_to_all(jnp.broadcast_to(whole, (4, 3, 32, 512)), 'x', 0, 0)  15.3 us
    ppermute x2, waiting for transfers between devices, neighbours(): far = lax.ppermute(pick(core), ROWS, swaps)  14 us
    ppermute x4, waiting for transfers between devices, partner(): return lax.ppermute(value, 'zh', [(i, i ^ flip) for i in range(4)])  11.7 us
    pallas_call x2, Pallas kernels, on_device(): pl.pallas_call(functools.partial(pyramid_kernel, (2 * step, 2 * step + 1)...  7.06 us
    ppermute x2, starting transfers between devices, neighbours(): near = lax.ppermute(pick(1 - core), 'c', [(0, 1), (1, 0)])  5.73 us
  transfers between devices with their start and end apart: 10, of which 6 were waited for; matrix products, arithmetic and copies ran while one was open for 0% of the time, Pallas kernels for 5%

profile of v5, /device:TPU:24, one launch (start us, length us, event | category | flops | bytes accessed | tf_op | source)
XLA Modules:
  0.0 144.7 jit_solution(294669061692720059)
XLA Ops:
  0.0 1.4 copy-done
  2.1 0.8 pack.1
  2.9 26.2 %all_to_all.10.main_ref = f32[4,2,104,512]{3,2,1,0:T(8,128)S(1)} all-to-all(f32[4,2,104,512]{3,2,1,0:T(8,128)S(1)} %pack.1), channel_id=1, replica_groups=mesh['zl'=4,'y'=4,'c'=2,'zh'=4,'x'=4] {'x'}, dimensions={0} | all-to-all | bytes 3407872 | tf_op jit(solution)/shard_map/all_to_all | solution.py:356
  29.2 1.9 %collective-permute-start = (f32[4,104,512]{2,1,0:T(8,128)S(1)}, f32[4,104,512]{2,1,0:T(8,128)S(1)}, u32[]{:S(2)}, u32[]{:S(2)}) collective-permute-start(f32[4,104,512]{2,1,0:T(8,128)S(1)} %get-tuple-element.58), channel_id=1, source_target_pairs={{0,16},{16,0},{1,17},{17,1},{2,18},{18,2},{3,19},{19,3},{4,20},{20... | collective-permute-start | bytes 2555912 | tf_op jit(solution)/shard_map/ppermute | solution.py:326
  31.1 2.8 %collective-permute-start.1 = (f32[4,104,512]{2,1,0:T(8,128)S(1)}, f32[4,104,512]{2,1,0:T(8,128)S(1)}, u32[]{:S(2)}, u32[]{:S(2)}) collective-permute-start(f32[4,104,512]{2,1,0:T(8,128)S(1)} %get-tuple-element.57), channel_id=1, source_target_pairs={{16,32},{48,64},{80,96},{112,128},{144,160},{176,192},{208,224},{2... | collective-permute-start | bytes 2555912 | tf_op jit(solution)/shard_map/ppermute | solution.py:327
  34.0 11.1 %collective-permute-done.1.far_ref = f32[4,104,512]{2,1,0:T(8,128)S(1)} collective-permute-done((f32[4,104,512]{2,1,0:T(8,128)S(1)}, f32[4,104,512]{2,1,0:T(8,128)S(1)}, u32[]{:S(2)}, u32[]{:S(2)}) %collective-permute-start.1) | collective-permute-done | bytes 852000 | tf_op jit(solution)/shard_map/ppermute | solution.py:327
  45.1 5.4 %energy.1 = (f32[8,64,640]{2,1,0:T(8,128)S(1)}, f32[32,640]{1,0:T(8,128)S(1)}) custom-call(s32[3]{0:T(128)S(1)} %pad_add_fusion.place_ref, f32[4,2,104,512]{3,2,1,0:T(8,128)S(1)} %all_to_all.10.main_ref, f32[4,104,512]{2,1,0:T(8,128)S(1)} %collective-permute-done.near_ref, f32[4,104,512]{2,1,0:T(8,128)S(1)} %collective-permute-done.1.far_ref), custom_call_target="tpu_custom_call" | custom-call | tf_op jit(solution)/shard_map/energy/pallas_call | solution.py:360
  50.5 9.1 %collective-permute-start.2 = (f32[32,640]{1,0:T(8,128)S(1)}, f32[32,640]{1,0:T(8,128)S(1)}, u32[]{:S(2)}, u32[]{:S(2)}) collective-permute-start(f32[32,640]{1,0:T(8,128)S(1)} %get-tuple-element.40), channel_id=1, source_target_pairs={{0,4},{4,0},{8,12},{12,8},{16,28},{20,24},{24,20},{28,16},{1,5},{5... | collective-permute-start | bytes 245768 | tf_op jit(solution)/shard_map/ppermute | solution.py:337
  59.6 3.5 %pyramid.2 = (f32[384,512]{1,0:T(8,128)S(1)}, f32[384,384]{1,0:T(8,128)S(1)}, f32[192,256]{1,0:T(8,128)S(1)}) custom-call(s32[3]{0:T(128)S(1)} %pad_add_fusion.place_ref, f32[4,2,104,512]{3,2,1,0:T(8,128)S(1)} %all_to_all.10.main_ref, f32[4,104,512]{2,1,0:T(8,128)S(1)} %collective-permute-done.near_ref, f32[4,104,512]{2,1,0:T(8,128)S(1)} %collective-permute-done.1.far_ref, ...), custom_call_target="tpu_custom_call" | custom-call | flops 2000000000 | bytes 6000000 | tf_op jit(solution)/shard_map/pyramid/pallas_call | solution.py:382
  63.2 10.6 %collective-permute-start.3 = (f32[32,640]{1,0:T(8,128)S(1)}, f32[32,640]{1,0:T(8,128)S(1)}, u32[]{:S(2)}, u32[]{:S(2)}) collective-permute-start(f32[32,640]{1,0:T(8,128)S(1)} %log_add_fusion.1), channel_id=1, source_target_pairs={{0,12},{4,8},{8,4},{12,0},{16,20},{20,16},{24,28},{28,24},{1,13},{... | collective-permute-start | bytes 245768 | tf_op jit(solution)/shard_map/ppermute | solution.py:337
  73.8 3.5 %pyramid.3 = (f32[384,512]{1,0:T(8,128)S(1)}, f32[384,384]{1,0:T(8,128)S(1)}, f32[192,256]{1,0:T(8,128)S(1)}) custom-call(s32[3]{0:T(128)S(1)} %pad_add_fusion.place_ref, f32[4,2,104,512]{3,2,1,0:T(8,128)S(1)} %all_to_all.10.main_ref, f32[4,104,512]{2,1,0:T(8,128)S(1)} %collective-permute-done.near_ref, f32[4,104,512]{2,1,0:T(8,128)S(1)} %collective-permute-done.1.far_ref, ...), custom_call_target="tpu_custom_call" | custom-call | flops 2000000000 | bytes 6000000 | tf_op jit(solution)/shard_map/pyramid/pallas_call | solution.py:382
  77.5 3.8 %collective-permute-start.4 = (f32[16,640]{1,0:T(8,128)S(1)}, f32[16,640]{1,0:T(8,128)S(1)}, u32[]{:S(2)}, u32[]{:S(2)}) collective-permute-start(f32[16,640]{1,0:T(8,128)S(1)} %get-tuple-element.60), channel_id=1, source_target_pairs={{0,16},{16,0},{1,17},{17,1},{2,18},{18,2},{3,19},{19,3},{4,20},{20... | collective-permute-start | bytes 122888 | tf_op jit(solution)/shard_map/ppermute | solution.py:326
  81.3 2.4 %collective-permute-start.5 = (f32[16,640]{1,0:T(8,128)S(1)}, f32[16,640]{1,0:T(8,128)S(1)}, u32[]{:S(2)}, u32[]{:S(2)}) collective-permute-start(f32[16,640]{1,0:T(8,128)S(1)} %get-tuple-element.59), channel_id=1, source_target_pairs={{16,32},{48,64},{80,96},{112,128},{144,160},{176,192},{208,224},{2... | collective-permute-start | bytes 122888 | tf_op jit(solution)/shard_map/ppermute | solution.py:327
  83.7 2.9 %collective-permute-done.5.far_ref = f32[16,640]{1,0:T(8,128)S(1)} collective-permute-done((f32[16,640]{1,0:T(8,128)S(1)}, f32[16,640]{1,0:T(8,128)S(1)}, u32[]{:S(2)}, u32[]{:S(2)}) %collective-permute-start.5) | collective-permute-done | bytes 40992 | tf_op jit(solution)/shard_map/ppermute | solution.py:327
  86.6 2.8 %mix.1 = (f32[3,32,256]{2,1,0:T(8,128)S(1)}, f32[3,32,256]{2,1,0:T(8,128)S(1)}) custom-call(s32[3]{0:T(128)S(1)} %pad_add_fusion.place_ref, f32[8,64,640]{2,1,0:T(8,128)S(1)} %get-tuple-element.39.logit_ref, f32[32,640]{1,0:T(8,128)S(1)} %log_add_fusion.lse_ref, f32[16,640]{1,0:T(8,128)S(1)} %collective-permute-done.4.near_ref, ...), custom_call_target="tpu_custom_call" | custom-call | tf_op jit(solution)/shard_map/mix/pallas_call | solution.py:408
  89.4 7.2 %collective-permute-start.6 = (f32[3,32,256]{2,1,0:T(8,128)S(1)}, f32[3,32,256]{2,1,0:T(8,128)S(1)}, u32[]{:S(2)}, u32[]{:S(2)}) collective-permute-start(f32[3,32,256]{2,1,0:T(8,128)S(1)} %get-tuple-element.55), channel_id=1, source_target_pairs={{0,4},{4,0},{8,12},{12,8},{1,5},{5,1},{9,13},{13,9},{2,6},{6,2},{1... | collective-permute-start | bytes 294920 | tf_op jit(solution)/shard_map/ppermute | solution.py:332
  96.6 6.9 %collective-permute-start.8 = (f32[3,32,256]{2,1,0:T(8,128)S(1)}, f32[3,32,256]{2,1,0:T(8,128)S(1)}, u32[]{:S(2)}, u32[]{:S(2)}) collective-permute-start(f32[3,32,256]{2,1,0:T(8,128)S(1)} %get-tuple-element.56), channel_id=1, source_target_pairs={{0,12},{4,8},{8,4},{12,0},{1,13},{5,9},{9,5},{13,1},{2,14},{6,10},... | collective-permute-start | bytes 294920 | tf_op jit(solution)/shard_map/ppermute | solution.py:332
  103.5 2.4 %collective-permute-done.6 = f32[3,32,256]{2,1,0:T(8,128)S(1)} collective-permute-done((f32[3,32,256]{2,1,0:T(8,128)S(1)}, f32[3,32,256]{2,1,0:T(8,128)S(1)}, u32[]{:S(2)}, u32[]{:S(2)}) %collective-permute-start.6) | collective-permute-done | bytes 98336 | tf_op jit(solution)/shard_map/ppermute | solution.py:332
  105.9 5.6 %collective-permute-start.7 = (f32[3,32,256]{2,1,0:T(8,128)S(1)}, f32[3,32,256]{2,1,0:T(8,128)S(1)}, u32[]{:S(2)}, u32[]{:S(2)}) collective-permute-start(f32[3,32,256]{2,1,0:T(8,128)S(1)} %add.49), channel_id=1, source_target_pairs={{0,12},{4,8},{8,4},{12,0},{1,13},{5,9},{9,5},{13,1},{2,14},{6,10},... | collective-permute-start | bytes 294920 | tf_op jit(solution)/shard_map/ppermute | solution.py:332
  111.7 7.5 %collective-permute-start.9 = (f32[3,32,256]{2,1,0:T(8,128)S(1)}, f32[3,32,256]{2,1,0:T(8,128)S(1)}, u32[]{:S(2)}, u32[]{:S(2)}) collective-permute-start(f32[3,32,256]{2,1,0:T(8,128)S(1)} %add.51), channel_id=1, source_target_pairs={{0,4},{4,0},{8,12},{12,8},{1,5},{5,1},{9,13},{13,9},{2,6},{6,2},{1... | collective-permute-start | bytes 294920 | tf_op jit(solution)/shard_map/ppermute | solution.py:332
  119.2 0.8 collective-permute-done.7
  120.0 8.3 %collective-permute-done.9 = f32[3,32,256]{2,1,0:T(8,128)S(1)} collective-permute-done((f32[3,32,256]{2,1,0:T(8,128)S(1)}, f32[3,32,256]{2,1,0:T(8,128)S(1)}, u32[]{:S(2)}, u32[]{:S(2)}) %collective-permute-start.9) | collective-permute-done | bytes 98336 | tf_op jit(solution)/shard_map/ppermute | solution.py:332
  128.5 15.3 %all_to_all.11 = f32[4,3,32,512]{3,2,1,0:T(8,128)S(1)} all-to-all(f32[4,3,32,512]{3,2,1,0:T(8,128)S(1)} %broadcast_in_dim.3), channel_id=1, replica_groups=mesh['zl'=4,'y'=4,'c'=2,'zh'=4,'x'=4] {'x'}, dimensions={0} | all-to-all | bytes 1572864 | tf_op jit(solution)/shard_map/all_to_all | solution.py:429
  143.7 0.9 copy.8
  (27 shorter events, 1.3 us)
Async XLA Ops:
  0.0 1.4 copy-start
  1.4 0.7 copy-start.5
  29.2 4.8 %collective-permute-start = (f32[4,104,512]{2,1,0:T(8,128)S(1)}, f32[4,104,512]{2,1,0:T(8,128)S(1)}, u32[]{:S(2)}, u32[]{:S(2)}) collective-permute-start(f32[4,104,512]{2,1,0:T(8,128)S(1)} %get-tuple-element.58), channel_id=1, source_target_pairs={{0,16},{16,0},{1,17},{17,1},{2,18},{18,2},{3,19},{19,3},{4,20},{20... | collective-permute-start | bytes 2555912 | tf_op jit(solution)/shard_map/ppermute | solution.py:326
  31.1 14.0 %collective-permute-start.1 = (f32[4,104,512]{2,1,0:T(8,128)S(1)}, f32[4,104,512]{2,1,0:T(8,128)S(1)}, u32[]{:S(2)}, u32[]{:S(2)}) collective-permute-start(f32[4,104,512]{2,1,0:T(8,128)S(1)} %get-tuple-element.57), channel_id=1, source_target_pairs={{16,32},{48,64},{80,96},{112,128},{144,160},{176,192},{208,224},{2... | collective-permute-start | bytes 2555912 | tf_op jit(solution)/shard_map/ppermute | solution.py:327
  34.0 25.6 %copy-start.1 = (bf16[640,384]{1,0:T(8,128)(2,1)S(1)}, bf16[640,384]{1,0:T(8,128)(2,1)}, u32[]{:S(2)}) copy-start(bf16[640,384]{1,0:T(8,128)(2,1)} %constant.49.clone.d1_ref) | copy-start | bytes 1474564
  34.0 25.6 %copy-start.2 = (bf16[384,512]{1,0:T(8,128)(2,1)S(1)}, bf16[384,512]{1,0:T(8,128)(2,1)}, u32[]{:S(2)}) copy-start(bf16[384,512]{1,0:T(8,128)(2,1)} %constant.52.clone.u1_ref) | copy-start | bytes 1179652
  34.0 25.7 %copy-start.3 = (bf16[384,256]{1,0:T(8,128)(2,1)S(1)}, bf16[384,256]{1,0:T(8,128)(2,1)}, u32[]{:S(2)}) copy-start(bf16[384,256]{1,0:T(8,128)(2,1)} %constant.50.clone.d2_ref) | copy-start | bytes 589828
  34.0 25.7 %copy-start.4 = (bf16[256,384]{1,0:T(8,128)(2,1)S(1)}, bf16[256,384]{1,0:T(8,128)(2,1)}, u32[]{:S(2)}) copy-start(bf16[256,384]{1,0:T(8,128)(2,1)} %constant.51.clone.u2_ref) | copy-start | bytes 589828
  50.5 12.7 %collective-permute-start.2 = (f32[32,640]{1,0:T(8,128)S(1)}, f32[32,640]{1,0:T(8,128)S(1)}, u32[]{:S(2)}, u32[]{:S(2)}) collective-permute-start(f32[32,640]{1,0:T(8,128)S(1)} %get-tuple-element.40), channel_id=1, source_target_pairs={{0,4},{4,0},{8,12},{12,8},{16,28},{20,24},{24,20},{28,16},{1,5},{5... | collective-permute-start | bytes 245768 | tf_op jit(solution)/shard_map/ppermute | solution.py:337
  63.2 14.1 %collective-permute-start.3 = (f32[32,640]{1,0:T(8,128)S(1)}, f32[32,640]{1,0:T(8,128)S(1)}, u32[]{:S(2)}, u32[]{:S(2)}) collective-permute-start(f32[32,640]{1,0:T(8,128)S(1)} %log_add_fusion.1), channel_id=1, source_target_pairs={{0,12},{4,8},{8,4},{12,0},{16,20},{20,16},{24,28},{28,24},{1,13},{... | collective-permute-start | bytes 245768 | tf_op jit(solution)/shard_map/ppermute | solution.py:337
  77.5 6.3 %collective-permute-start.4 = (f32[16,640]{1,0:T(8,128)S(1)}, f32[16,640]{1,0:T(8,128)S(1)}, u32[]{:S(2)}, u32[]{:S(2)}) collective-permute-start(f32[16,640]{1,0:T(8,128)S(1)} %get-tuple-element.60), channel_id=1, source_target_pairs={{0,16},{16,0},{1,17},{17,1},{2,18},{18,2},{3,19},{19,3},{4,20},{20... | collective-permute-start | bytes 122888 | tf_op jit(solution)/shard_map/ppermute | solution.py:326
  81.3 5.3 %collective-permute-start.5 = (f32[16,640]{1,0:T(8,128)S(1)}, f32[16,640]{1,0:T(8,128)S(1)}, u32[]{:S(2)}, u32[]{:S(2)}) collective-permute-start(f32[16,640]{1,0:T(8,128)S(1)} %get-tuple-element.59), channel_id=1, source_target_pairs={{16,32},{48,64},{80,96},{112,128},{144,160},{176,192},{208,224},{2... | collective-permute-start | bytes 122888 | tf_op jit(solution)/shard_map/ppermute | solution.py:327
  89.4 16.5 %collective-permute-start.6 = (f32[3,32,256]{2,1,0:T(8,128)S(1)}, f32[3,32,256]{2,1,0:T(8,128)S(1)}, u32[]{:S(2)}, u32[]{:S(2)}) collective-permute-start(f32[3,32,256]{2,1,0:T(8,128)S(1)} %get-tuple-element.55), channel_id=1, source_target_pairs={{0,4},{4,0},{8,12},{12,8},{1,5},{5,1},{9,13},{13,9},{2,6},{6,2},{1... | collective-permute-start | bytes 294920 | tf_op jit(solution)/shard_map/ppermute | solution.py:332
  96.6 15.1 %collective-permute-start.8 = (f32[3,32,256]{2,1,0:T(8,128)S(1)}, f32[3,32,256]{2,1,0:T(8,128)S(1)}, u32[]{:S(2)}, u32[]{:S(2)}) collective-permute-start(f32[3,32,256]{2,1,0:T(8,128)S(1)} %get-tuple-element.56), channel_id=1, source_target_pairs={{0,12},{4,8},{8,4},{12,0},{1,13},{5,9},{9,5},{13,1},{2,14},{6,10},... | collective-permute-start | bytes 294920 | tf_op jit(solution)/shard_map/ppermute | solution.py:332
  105.9 14.1 %collective-permute-start.7 = (f32[3,32,256]{2,1,0:T(8,128)S(1)}, f32[3,32,256]{2,1,0:T(8,128)S(1)}, u32[]{:S(2)}, u32[]{:S(2)}) collective-permute-start(f32[3,32,256]{2,1,0:T(8,128)S(1)} %add.49), channel_id=1, source_target_pairs={{0,12},{4,8},{8,4},{12,0},{1,13},{5,9},{9,5},{13,1},{2,14},{6,10},... | collective-permute-start | bytes 294920 | tf_op jit(solution)/shard_map/ppermute | solution.py:332
  111.7 16.6 %collective-permute-start.9 = (f32[3,32,256]{2,1,0:T(8,128)S(1)}, f32[3,32,256]{2,1,0:T(8,128)S(1)}, u32[]{:S(2)}, u32[]{:S(2)}) collective-permute-start(f32[3,32,256]{2,1,0:T(8,128)S(1)} %add.51), channel_id=1, source_target_pairs={{0,4},{4,0},{8,12},{12,8},{1,5},{5,1},{9,13},{13,9},{2,6},{6,2},{1... | collective-permute-start | bytes 294920 | tf_op jit(solution)/shard_map/ppermute | solution.py:332

commit v6 on v5

--- a/solution.py
+++ b/solution.py
@@ -137,13 +137,13 @@
             gain = main_ref[s, 0, 96:97, 192 + 32 * p : 193 + 32 * p]
             logit_ref[2 * s + p] = gain * field
 
-    peak = logit_ref[0, 16:48]
+    peak = logit_ref[0]
     for i in range(1, 8):
-        peak = jnp.maximum(peak, logit_ref[i, 16:48])
+        peak = jnp.maximum(peak, logit_ref[i])
     total = 0.0
     for i in range(8):
-        total = total + jnp.exp(logit_ref[i, 16:48] - peak)
-    lse_ref[...] = peak + jnp.log(total)
+        total = total + jnp.exp(logit_ref[i] - peak)
+    lse_ref[...] = pltpu.roll(peak + jnp.log(total), 58, 0)[0:56]
 
 
 def split2(value):
@@ -248,7 +248,7 @@
 
 
 def mix_kernel(
-    place_ref, logit_ref, lse_ref, near_ref, far_ref,
+    place_ref, logit_ref, lse_ref,
     fine_a_ref, mid_a_ref, low_a_ref, fine_b_ref, mid_b_ref, low_b_ref,
     d1_ref, d2_ref, u2_ref, u1_ref,
     left_ref, right_ref, w0_ref, s1_ref, w1_ref, s2_ref, s3_ref, s4_ref,
@@ -259,13 +259,7 @@
     col = column_of((16, W0), M0, W0)
     inside_col = (col >= -10) & (col <= 522) & (col + k * M0 >= 0) & (col + k * M0 < 2048)
     row = lax.broadcasted_iota(jnp.int32, (16, W0), 0)
-    even = place_ref[2] == 0
-    lses = (
-        jnp.where(even, far_ref[...], near_ref[...]),
-        lse_ref[0:16],
-        lse_ref[16:32],
-        jnp.where(even, near_ref[...], far_ref[...]),
-    )
+    lse = pltpu.roll(jnp.concatenate([lse_ref[...], jnp.zeros((8, W0), F32)], axis=0), 6, 0)
     keeps = []
     for b in range(4):
         r = row + (16 * b - 16)
@@ -274,7 +268,7 @@
     for i in range(8):
         for b in range(4):
             rows = slice(16 * b, 16 * b + 16)
-            w0_ref[i, rows] = jnp.where(keeps[b], jnp.exp(logit_ref[i, rows] - lses[b]), 0.0)
+            w0_ref[i, rows] = jnp.where(keeps[b], jnp.exp(logit_ref[i, rows] - lse[rows]), 0.0)
         put(s1_ref, 8, i, 32, dot(v1, stacked(w0_ref[i])))
     inside1, inside2 = level_masks(32, 16, k)
     w1_ref[...] = resampled(s1_ref, d1_ref)
@@ -310,6 +304,14 @@
         right_ref[c] = total[:, 256:]
 
 
+def gather_kernel(place_ref, *refs):
+    out_ref = refs[-1]
+    for half in range(2):
+        for n, flip in enumerate((0, 1, 3, 2)):
+            at = (place_ref[1] ^ flip) * 512 + half * 256
+            out_ref[:, :, pl.ds(pl.multiple_of(at, 256), 256)] = refs[4 * half + n][...]
+
+
 def vmem(count):
     return [pl.BlockSpec(memory_space=pltpu.VMEM)] * count
 
@@ -359,7 +361,7 @@
     place = jnp.stack([strip, column, core]).astype(jnp.int32)
     logits, lse = pl.pallas_call(
         energy_kernel,
-        out_shape=(jax.ShapeDtypeStruct((8, 64, W0), F32), jax.ShapeDtypeStruct((32, W0), F32)),
+        out_shape=(jax.ShapeDtypeStruct((8, 64, W0), F32), jax.ShapeDtypeStruct((56, W0), F32)),
         in_specs=smem() + vmem(3),
         out_specs=tuple(vmem(2)),
         scratch_shapes=[pltpu.VMEM((64, W0), F32)],
@@ -403,12 +405,11 @@
         other, *detail = lax.optimization_barrier((other, *detail))
         details += detail
         lse = join_lse(lse, other)
-    lse_near, lse_far = neighbours(lse.reshape(2, 16, W0), core)
 
     left, right = pl.pallas_call(
         mix_kernel,
         out_shape=(jax.ShapeDtypeStruct((3, 32, 256), F32),) * 2,
-        in_specs=smem() + vmem(14),
+        in_specs=smem() + vmem(12),
         out_specs=tuple(vmem(2)),
         scratch_shapes=[
             pltpu.VMEM((8, 64, W0), F32),
@@ -420,14 +421,24 @@
         ],
         compiler_params=PARAMS,
         name="mix",
-    )(place, logits, lse, lse_near, lse_far, *details, *taps)
+    )(place, logits, lse, *details, *taps)
 
     for a, b in ((1, 3), (3, 1)):
         left_in, right_in = partner(left, a), partner(right, b)
         left, right = left + left_in, right + right_in
-    whole = jnp.concatenate([left, right], axis=-1)
-    joined = lax.all_to_all(jnp.broadcast_to(whole, (4, 3, 32, 512)), "x", 0, 0)
-    return joined.transpose(1, 2, 0, 3).reshape(3, 32, 2048)
+    pieces = []
+    for half in (left, right):
+        pieces.append(half)
+        for flip in (1, 3, 2):
+            pieces.append(lax.ppermute(half, "x", [(i, i ^ flip) for i in range(4)]))
+    return pl.pallas_call(
+        gather_kernel,
+        out_shape=jax.ShapeDtypeStruct((3, 32, 2048), F32),
+        in_specs=smem() + vmem(8),
+        out_specs=vmem(1)[0],
+        compiler_params=PARAMS,
+        name="gather",
+    )(place, *pieces)
 
 
 def solution(mesh):

time: 145 us -> 142 us (0.979)
  blocking collectives: 41.5 us -> 26.2 us
  starting transfers between devices: 57.8 us -> 69.6 us
  Pallas kernels: 16 us -> 17.6 us
    ppermute x0 -> x6, starting transfers between devices: none -> 19.6 us  [on_device(): pieces.append(lax.ppermute(half, 'x', [(i, i ^ flip) for i in range(4)]))]
    all_to_all x1 -> x0, blocking collectives: 15.3 us -> none  [on_device(): joined = lax.all_to_all(jnp.broadcast_to(whole, (4, 3, 32, 512)), 'x', 0, 0)]
    ppermute x4, waiting for transfers between devices: 11.7 us -> 4.59 us  [partner(): return lax.ppermute(value, 'zh', [(i, i ^ flip) for i in range(4)])]
    ppermute x2, waiting for transfers between devices: 0.01 us -> 6.18 us  [crossed(): return lax.ppermute(value, ('c', 'zh'), pairs)]
    ppermute x2 -> x1, starting transfers between devices: 5.73 us -> 1.92 us  [neighbours(): near = lax.ppermute(pick(1 - core), 'c', [(0, 1), (1, 0)])]
    ppermute x0 -> x6, waiting for transfers between devices: none -> 3.42 us  [on_device(): pieces.append(lax.ppermute(half, 'x', [(i, i ^ flip) for i in range(4)]))]
    ppermute x2, starting transfers between devices: 19.7 us -> 16.3 us  [crossed(): return lax.ppermute(value, ('c', 'zh'), pairs)]
    ppermute x2 -> x1, waiting for transfers between devices: 14 us -> 11.1 us  [neighbours(): far = lax.ppermute(pick(core), ROWS, swaps)]
  transfers between devices with their start and end apart: 10 -> 14, of which waited for: 6 -> 7; matrix products, arithmetic and copies ran while one was open for 0% -> 0% of each run, Pallas kernels for 5% -> 5%
where the time goes in v6:
time: 142 us
  starting transfers between devices  69.6 us (49%)
  blocking collectives  26.2 us (18%)
  waiting for transfers between devices  25.3 us (18%)
  Pallas kernels  17.6 us (12%)
  local copies, waits for them, and re-layouts  2.23 us (2%)
    ppermute x4, starting transfers between devices, partner(): return lax.ppermute(value, 'zh', [(i, i ^ flip) for i in range(4)])  29 us
    all_to_all x1, blocking collectives, on_device(): main = lax.all_to_all(packed, 'x', 0, 0)  26.2 us
    ppermute x6, starting transfers between devices, on_device(): pieces.append(lax.ppermute(half, 'x', [(i, i ^ flip) for i in range(4)]))  19.6 us
    ppermute x2, starting transfers between devices, crossed(): return lax.ppermute(value, ('c', 'zh'), pairs)  16.3 us
    ppermute x1, waiting for transfers between devices, neighbours(): far = lax.ppermute(pick(core), ROWS, swaps)  11.1 us
    pallas_call x2, Pallas kernels, on_device(): pl.pallas_call(functools.partial(pyramid_kernel, (2 * step, 2 * step + 1)...  7.07 us
    ppermute x2, waiting for transfers between devices, crossed(): return lax.ppermute(value, ('c', 'zh'), pairs)  6.18 us
    pallas_call x1, Pallas kernels, on_device(): pl.pallas_call(energy_kernel, out_shape=(jax.ShapeDtypeStruct((8, 64, W0)...  5.48 us
  transfers between devices with their start and end apart: 14, of which 7 were waited for; matrix products, arithmetic and copies ran while one was open for 0% of the time, Pallas kernels for 5%

profile of v6, /device:TPU:24, one launch (start us, length us, event | category | flops | bytes accessed | tf_op | source)
XLA Modules:
  0.0 141.5 jit_solution(2958074948862682106)
XLA Ops:
  2.9 26.2 %all_to_all.5.main_ref = f32[4,2,104,512]{3,2,1,0:T(8,128)S(1)} all-to-all(f32[4,2,104,512]{3,2,1,0:T(8,128)S(1)} %pack.1), channel_id=1, replica_groups=mesh['zl'=4,'y'=4,'c'=2,'zh'=4,'x'=4] {'x'}, dimensions={0} | all-to-all | bytes 3407872 | tf_op jit(solution)/shard_map/all_to_all | solution.py:358
  29.2 1.9 %collective-permute-start = (f32[4,104,512]{2,1,0:T(8,128)S(1)}, f32[4,104,512]{2,1,0:T(8,128)S(1)}, u32[]{:S(2)}, u32[]{:S(2)}) collective-permute-start(f32[4,104,512]{2,1,0:T(8,128)S(1)} %get-tuple-element.58), channel_id=1, source_target_pairs={{0,16},{16,0},{1,17},{17,1},{2,18},{18,2},{3,19},{19,3},{4,20},{20... | collective-permute-start | bytes 2555912 | tf_op jit(solution)/shard_map/ppermute | solution.py:328
  31.2 2.8 %collective-permute-start.1 = (f32[4,104,512]{2,1,0:T(8,128)S(1)}, f32[4,104,512]{2,1,0:T(8,128)S(1)}, u32[]{:S(2)}, u32[]{:S(2)}) collective-permute-start(f32[4,104,512]{2,1,0:T(8,128)S(1)} %get-tuple-element.57), channel_id=1, source_target_pairs={{16,32},{48,64},{80,96},{112,128},{144,160},{176,192},{208,224},{2... | collective-permute-start | bytes 2555912 | tf_op jit(solution)/shard_map/ppermute | solution.py:329
  34.0 11.1 %collective-permute-done.1.far_ref = f32[4,104,512]{2,1,0:T(8,128)S(1)} collective-permute-done((f32[4,104,512]{2,1,0:T(8,128)S(1)}, f32[4,104,512]{2,1,0:T(8,128)S(1)}, u32[]{:S(2)}, u32[]{:S(2)}) %collective-permute-start.1) | collective-permute-done | bytes 852000 | tf_op jit(solution)/shard_map/ppermute | solution.py:329
  45.2 5.5 %energy.1 = (f32[8,64,640]{2,1,0:T(8,128)S(1)}, f32[56,640]{1,0:T(8,128)S(1)}) custom-call(s32[3]{0:T(128)S(1)} %pad_add_fusion.place_ref, f32[4,2,104,512]{3,2,1,0:T(8,128)S(1)} %all_to_all.5.main_ref, f32[4,104,512]{2,1,0:T(8,128)S(1)} %collective-permute-done.near_ref, f32[4,104,512]{2,1,0:T(8,128)S(1)} %collective-permute-done.1.far_ref), custom_call_target="tpu_custom_call" | custom-call | tf_op jit(solution)/shard_map/energy/pallas_call | solution.py:362
  50.7 9.1 %collective-permute-start.2 = (f32[56,640]{1,0:T(8,128)S(1)}, f32[56,640]{1,0:T(8,128)S(1)}, u32[]{:S(2)}, u32[]{:S(2)}) collective-permute-start(f32[56,640]{1,0:T(8,128)S(1)} %get-tuple-element.40), channel_id=1, source_target_pairs={{0,4},{4,0},{8,12},{12,8},{16,28},{20,24},{24,20},{28,16},{1,5},{5... | collective-permute-start | bytes 430088 | tf_op jit(solution)/shard_map/ppermute | solution.py:339
  59.8 3.5 %pyramid.2 = (f32[384,512]{1,0:T(8,128)S(1)}, f32[384,384]{1,0:T(8,128)S(1)}, f32[192,256]{1,0:T(8,128)S(1)}) custom-call(s32[3]{0:T(128)S(1)} %pad_add_fusion.place_ref, f32[4,2,104,512]{3,2,1,0:T(8,128)S(1)} %all_to_all.5.main_ref, f32[4,104,512]{2,1,0:T(8,128)S(1)} %collective-permute-done.near_ref, f32[4,104,512]{2,1,0:T(8,128)S(1)} %collective-permute-done.1.far_ref, ...), custom_call_target="tpu_custom_call" | custom-call | flops 2000000000 | bytes 6000000 | tf_op jit(solution)/shard_map/pyramid/pallas_call | solution.py:384
  63.3 5.7 %collective-permute-done.2 = f32[56,640]{1,0:T(8,128)S(1)} collective-permute-done((f32[56,640]{1,0:T(8,128)S(1)}, f32[56,640]{1,0:T(8,128)S(1)}, u32[]{:S(2)}, u32[]{:S(2)}) %collective-permute-start.2) | collective-permute-done | bytes 143392 | tf_op jit(solution)/shard_map/ppermute | solution.py:339
  69.1 7.2 %collective-permute-start.3 = (f32[56,640]{1,0:T(8,128)S(1)}, f32[56,640]{1,0:T(8,128)S(1)}, u32[]{:S(2)}, u32[]{:S(2)}) collective-permute-start(f32[56,640]{1,0:T(8,128)S(1)} %log_add_fusion.1), channel_id=1, source_target_pairs={{0,12},{4,8},{8,4},{12,0},{16,20},{20,16},{24,28},{28,24},{1,13},{... | collective-permute-start | bytes 430088 | tf_op jit(solution)/shard_map/ppermute | solution.py:339
  76.4 3.5 %pyramid.3 = (f32[384,512]{1,0:T(8,128)S(1)}, f32[384,384]{1,0:T(8,128)S(1)}, f32[192,256]{1,0:T(8,128)S(1)}) custom-call(s32[3]{0:T(128)S(1)} %pad_add_fusion.place_ref, f32[4,2,104,512]{3,2,1,0:T(8,128)S(1)} %all_to_all.5.main_ref, f32[4,104,512]{2,1,0:T(8,128)S(1)} %collective-permute-done.near_ref, f32[4,104,512]{2,1,0:T(8,128)S(1)} %collective-permute-done.1.far_ref, ...), custom_call_target="tpu_custom_call" | custom-call | flops 2000000000 | bytes 6000000 | tf_op jit(solution)/shard_map/pyramid/pallas_call | solution.py:384
  80.4 2.8 %mix.1 = (f32[3,32,256]{2,1,0:T(8,128)S(1)}, f32[3,32,256]{2,1,0:T(8,128)S(1)}) custom-call(s32[3]{0:T(128)S(1)} %pad_add_fusion.place_ref, f32[8,64,640]{2,1,0:T(8,128)S(1)} %get-tuple-element.39.logit_ref, f32[56,640]{1,0:T(8,128)S(1)} %log_add_fusion.lse_ref, f32[384,512]{1,0:T(8,128)S(1)} %get-tuple-element.49.fine_a_ref, ...), custom_call_target="tpu_custom_call" | custom-call | tf_op jit(solution)/shard_map/mix/pallas_call | solution.py:409
  83.2 8.0 %collective-permute-start.9 = (f32[3,32,256]{2,1,0:T(8,128)S(1)}, f32[3,32,256]{2,1,0:T(8,128)S(1)}, u32[]{:S(2)}, u32[]{:S(2)}) collective-permute-start(f32[3,32,256]{2,1,0:T(8,128)S(1)} %get-tuple-element.56), channel_id=1, source_target_pairs={{0,12},{4,8},{8,4},{12,0},{1,13},{5,9},{9,5},{13,1},{2,14},{6,10},... | collective-permute-start | bytes 294920 | tf_op jit(solution)/shard_map/ppermute | solution.py:334
  91.2 11.3 %collective-permute-start.4 = (f32[3,32,256]{2,1,0:T(8,128)S(1)}, f32[3,32,256]{2,1,0:T(8,128)S(1)}, u32[]{:S(2)}, u32[]{:S(2)}) collective-permute-start(f32[3,32,256]{2,1,0:T(8,128)S(1)} %get-tuple-element.55), channel_id=1, source_target_pairs={{0,4},{4,0},{8,12},{12,8},{1,5},{5,1},{9,13},{13,9},{2,6},{6,2},{1... | collective-permute-start | bytes 294920 | tf_op jit(solution)/shard_map/ppermute | solution.py:334
  102.5 4.9 %collective-permute-start.10 = (f32[3,32,256]{2,1,0:T(8,128)S(1)}, f32[3,32,256]{2,1,0:T(8,128)S(1)}, u32[]{:S(2)}, u32[]{:S(2)}) collective-permute-start(f32[3,32,256]{2,1,0:T(8,128)S(1)} %add.48), channel_id=1, source_target_pairs={{0,4},{4,0},{8,12},{12,8},{1,5},{5,1},{9,13},{13,9},{2,6},{6,2},{1... | collective-permute-start | bytes 294920 | tf_op jit(solution)/shard_map/ppermute | solution.py:334
  107.5 1.8 %collective-permute-done.4 = f32[3,32,256]{2,1,0:T(8,128)S(1)} collective-permute-done((f32[3,32,256]{2,1,0:T(8,128)S(1)}, f32[3,32,256]{2,1,0:T(8,128)S(1)}, u32[]{:S(2)}, u32[]{:S(2)}) %collective-permute-start.4) | collective-permute-done | bytes 98336 | tf_op jit(solution)/shard_map/ppermute | solution.py:334
  109.3 4.8 %collective-permute-start.5 = (f32[3,32,256]{2,1,0:T(8,128)S(1)}, f32[3,32,256]{2,1,0:T(8,128)S(1)}, u32[]{:S(2)}, u32[]{:S(2)}) collective-permute-start(f32[3,32,256]{2,1,0:T(8,128)S(1)} %add.46), channel_id=1, source_target_pairs={{0,12},{4,8},{8,4},{12,0},{1,13},{5,9},{9,5},{13,1},{2,14},{6,10},... | collective-permute-start | bytes 294920 | tf_op jit(solution)/shard_map/ppermute | solution.py:334
  114.0 2.8 %collective-permute-done.10 = f32[3,32,256]{2,1,0:T(8,128)S(1)} collective-permute-done((f32[3,32,256]{2,1,0:T(8,128)S(1)}, f32[3,32,256]{2,1,0:T(8,128)S(1)}, u32[]{:S(2)}, u32[]{:S(2)}) %collective-permute-start.10) | collective-permute-done | bytes 98336 | tf_op jit(solution)/shard_map/ppermute | solution.py:334
  116.9 2.5 %collective-permute-start.11 = (f32[3,32,256]{2,1,0:T(8,128)S(1)}, f32[3,32,256]{2,1,0:T(8,128)S(1)}, u32[]{:S(2)}, u32[]{:S(2)}) collective-permute-start(f32[3,32,256]{2,1,0:T(8,128)S(1)} %add.49.refs_4_), channel_id=1, source_target_pairs={{0,1},{1,0},{2,3},{3,2},{4,5},{5,4},{6,7},{7,6},{8,9},{9,8},{10,11... | collective-permute-start | bytes 294920 | tf_op jit(solution)/shard_map/ppermute | solution.py:433
  119.4 2.8 %collective-permute-start.12 = (f32[3,32,256]{2,1,0:T(8,128)S(1)}, f32[3,32,256]{2,1,0:T(8,128)S(1)}, u32[]{:S(2)}, u32[]{:S(2)}) collective-permute-start(f32[3,32,256]{2,1,0:T(8,128)S(1)} %add.49.refs_4_), channel_id=1, source_target_pairs={{0,3},{1,2},{2,1},{3,0},{4,7},{5,6},{6,5},{7,4},{8,11},{9,10},{10,... | collective-permute-start | bytes 294920 | tf_op jit(solution)/shard_map/ppermute | solution.py:433
  122.2 4.6 %collective-permute-start.13 = (f32[3,32,256]{2,1,0:T(8,128)S(1)}, f32[3,32,256]{2,1,0:T(8,128)S(1)}, u32[]{:S(2)}, u32[]{:S(2)}) collective-permute-start(f32[3,32,256]{2,1,0:T(8,128)S(1)} %add.49.refs_4_), channel_id=1, source_target_pairs={{0,2},{1,3},{2,0},{3,1},{4,6},{5,7},{6,4},{7,5},{8,10},{9,11},{10,... | collective-permute-start | bytes 294920 | tf_op jit(solution)/shard_map/ppermute | solution.py:433
  126.8 2.5 %collective-permute-start.6 = (f32[3,32,256]{2,1,0:T(8,128)S(1)}, f32[3,32,256]{2,1,0:T(8,128)S(1)}, u32[]{:S(2)}, u32[]{:S(2)}) collective-permute-start(f32[3,32,256]{2,1,0:T(8,128)S(1)} %add.47.refs_0_), channel_id=1, source_target_pairs={{0,1},{1,0},{2,3},{3,2},{4,5},{5,4},{6,7},{7,6},{8,9},{9,8},{10,11... | collective-permute-start | bytes 294920 | tf_op jit(solution)/shard_map/ppermute | solution.py:433
  129.2 2.8 %collective-permute-start.7 = (f32[3,32,256]{2,1,0:T(8,128)S(1)}, f32[3,32,256]{2,1,0:T(8,128)S(1)}, u32[]{:S(2)}, u32[]{:S(2)}) collective-permute-start(f32[3,32,256]{2,1,0:T(8,128)S(1)} %add.47.refs_0_), channel_id=1, source_target_pairs={{0,3},{1,2},{2,1},{3,0},{4,7},{5,6},{6,5},{7,4},{8,11},{9,10},{10,... | collective-permute-start | bytes 294920 | tf_op jit(solution)/shard_map/ppermute | solution.py:433
  132.0 4.6 %collective-permute-start.8 = (f32[3,32,256]{2,1,0:T(8,128)S(1)}, f32[3,32,256]{2,1,0:T(8,128)S(1)}, u32[]{:S(2)}, u32[]{:S(2)}) collective-permute-start(f32[3,32,256]{2,1,0:T(8,128)S(1)} %add.47.refs_0_), channel_id=1, source_target_pairs={{0,2},{1,3},{2,0},{3,1},{4,6},{5,7},{6,4},{7,5},{8,10},{9,11},{10,... | collective-permute-start | bytes 294920 | tf_op jit(solution)/shard_map/ppermute | solution.py:433
  138.0 2.0 %collective-permute-done.8.refs_3_ = f32[3,32,256]{2,1,0:T(8,128)S(1)} collective-permute-done((f32[3,32,256]{2,1,0:T(8,128)S(1)}, f32[3,32,256]{2,1,0:T(8,128)S(1)}, u32[]{:S(2)}, u32[]{:S(2)}) %collective-permute-start.8) | collective-permute-done | bytes 98336 | tf_op jit(solution)/shard_map/ppermute | solution.py:433
  (31 shorter events, 6.6 us)
Async XLA Ops:
  0.0 1.4 copy-start
  1.4 0.7 copy-start.5
  29.2 4.8 %collective-permute-start = (f32[4,104,512]{2,1,0:T(8,128)S(1)}, f32[4,104,512]{2,1,0:T(8,128)S(1)}, u32[]{:S(2)}, u32[]{:S(2)}) collective-permute-start(f32[4,104,512]{2,1,0:T(8,128)S(1)} %get-tuple-element.58), channel_id=1, source_target_pairs={{0,16},{16,0},{1,17},{17,1},{2,18},{18,2},{3,19},{19,3},{4,20},{20... | collective-permute-start | bytes 2555912 | tf_op jit(solution)/shard_map/ppermute | solution.py:328
  31.2 14.0 %collective-permute-start.1 = (f32[4,104,512]{2,1,0:T(8,128)S(1)}, f32[4,104,512]{2,1,0:T(8,128)S(1)}, u32[]{:S(2)}, u32[]{:S(2)}) collective-permute-start(f32[4,104,512]{2,1,0:T(8,128)S(1)} %get-tuple-element.57), channel_id=1, source_target_pairs={{16,32},{48,64},{80,96},{112,128},{144,160},{176,192},{208,224},{2... | collective-permute-start | bytes 2555912 | tf_op jit(solution)/shard_map/ppermute | solution.py:329
  34.0 25.8 %copy-start.1 = (bf16[640,384]{1,0:T(8,128)(2,1)S(1)}, bf16[640,384]{1,0:T(8,128)(2,1)}, u32[]{:S(2)}) copy-start(bf16[640,384]{1,0:T(8,128)(2,1)} %constant.43.clone.d1_ref) | copy-start | bytes 1474564
  34.0 25.8 %copy-start.2 = (bf16[384,512]{1,0:T(8,128)(2,1)S(1)}, bf16[384,512]{1,0:T(8,128)(2,1)}, u32[]{:S(2)}) copy-start(bf16[384,512]{1,0:T(8,128)(2,1)} %constant.46.clone.u1_ref) | copy-start | bytes 1179652
  34.0 25.8 %copy-start.3 = (bf16[384,256]{1,0:T(8,128)(2,1)S(1)}, bf16[384,256]{1,0:T(8,128)(2,1)}, u32[]{:S(2)}) copy-start(bf16[384,256]{1,0:T(8,128)(2,1)} %constant.44.clone.d2_ref) | copy-start | bytes 589828
  34.0 25.8 %copy-start.4 = (bf16[256,384]{1,0:T(8,128)(2,1)S(1)}, bf16[256,384]{1,0:T(8,128)(2,1)}, u32[]{:S(2)}) copy-start(bf16[256,384]{1,0:T(8,128)(2,1)} %constant.45.clone.u2_ref) | copy-start | bytes 589828
  50.7 18.4 %collective-permute-start.2 = (f32[56,640]{1,0:T(8,128)S(1)}, f32[56,640]{1,0:T(8,128)S(1)}, u32[]{:S(2)}, u32[]{:S(2)}) collective-permute-start(f32[56,640]{1,0:T(8,128)S(1)} %get-tuple-element.40), channel_id=1, source_target_pairs={{0,4},{4,0},{8,12},{12,8},{16,28},{20,24},{24,20},{28,16},{1,5},{5... | collective-permute-start | bytes 430088 | tf_op jit(solution)/shard_map/ppermute | solution.py:339
  69.1 11.2 %collective-permute-start.3 = (f32[56,640]{1,0:T(8,128)S(1)}, f32[56,640]{1,0:T(8,128)S(1)}, u32[]{:S(2)}, u32[]{:S(2)}) collective-permute-start(f32[56,640]{1,0:T(8,128)S(1)} %log_add_fusion.1), channel_id=1, source_target_pairs={{0,12},{4,8},{8,4},{12,0},{16,20},{20,16},{24,28},{28,24},{1,13},{... | collective-permute-start | bytes 430088 | tf_op jit(solution)/shard_map/ppermute | solution.py:339
  83.2 19.3 %collective-permute-start.9 = (f32[3,32,256]{2,1,0:T(8,128)S(1)}, f32[3,32,256]{2,1,0:T(8,128)S(1)}, u32[]{:S(2)}, u32[]{:S(2)}) collective-permute-start(f32[3,32,256]{2,1,0:T(8,128)S(1)} %get-tuple-element.56), channel_id=1, source_target_pairs={{0,12},{4,8},{8,4},{12,0},{1,13},{5,9},{9,5},{13,1},{2,14},{6,10},... | collective-permute-start | bytes 294920 | tf_op jit(solution)/shard_map/ppermute | solution.py:334
  91.2 18.0 %collective-permute-start.4 = (f32[3,32,256]{2,1,0:T(8,128)S(1)}, f32[3,32,256]{2,1,0:T(8,128)S(1)}, u32[]{:S(2)}, u32[]{:S(2)}) collective-permute-start(f32[3,32,256]{2,1,0:T(8,128)S(1)} %get-tuple-element.55), channel_id=1, source_target_pairs={{0,4},{4,0},{8,12},{12,8},{1,5},{5,1},{9,13},{13,9},{2,6},{6,2},{1... | collective-permute-start | bytes 294920 | tf_op jit(solution)/shard_map/ppermute | solution.py:334
  102.5 14.3 %collective-permute-start.10 = (f32[3,32,256]{2,1,0:T(8,128)S(1)}, f32[3,32,256]{2,1,0:T(8,128)S(1)}, u32[]{:S(2)}, u32[]{:S(2)}) collective-permute-start(f32[3,32,256]{2,1,0:T(8,128)S(1)} %add.48), channel_id=1, source_target_pairs={{0,4},{4,0},{8,12},{12,8},{1,5},{5,1},{9,13},{13,9},{2,6},{6,2},{1... | collective-permute-start | bytes 294920 | tf_op jit(solution)/shard_map/ppermute | solution.py:334
  109.3 17.5 %collective-permute-start.5 = (f32[3,32,256]{2,1,0:T(8,128)S(1)}, f32[3,32,256]{2,1,0:T(8,128)S(1)}, u32[]{:S(2)}, u32[]{:S(2)}) collective-permute-start(f32[3,32,256]{2,1,0:T(8,128)S(1)} %add.46), channel_id=1, source_target_pairs={{0,12},{4,8},{8,4},{12,0},{1,13},{5,9},{9,5},{13,1},{2,14},{6,10},... | collective-permute-start | bytes 294920 | tf_op jit(solution)/shard_map/ppermute | solution.py:334
  116.9 15.1 %collective-permute-start.11 = (f32[3,32,256]{2,1,0:T(8,128)S(1)}, f32[3,32,256]{2,1,0:T(8,128)S(1)}, u32[]{:S(2)}, u32[]{:S(2)}) collective-permute-start(f32[3,32,256]{2,1,0:T(8,128)S(1)} %add.49.refs_4_), channel_id=1, source_target_pairs={{0,1},{1,0},{2,3},{3,2},{4,5},{5,4},{6,7},{7,6},{8,9},{9,8},{10,11... | collective-permute-start | bytes 294920 | tf_op jit(solution)/shard_map/ppermute | solution.py:433
  119.4 17.2 %collective-permute-start.12 = (f32[3,32,256]{2,1,0:T(8,128)S(1)}, f32[3,32,256]{2,1,0:T(8,128)S(1)}, u32[]{:S(2)}, u32[]{:S(2)}) collective-permute-start(f32[3,32,256]{2,1,0:T(8,128)S(1)} %add.49.refs_4_), channel_id=1, source_target_pairs={{0,3},{1,2},{2,1},{3,0},{4,7},{5,6},{6,5},{7,4},{8,11},{9,10},{10,... | collective-permute-start | bytes 294920 | tf_op jit(solution)/shard_map/ppermute | solution.py:433
  122.2 14.5 %collective-permute-start.13 = (f32[3,32,256]{2,1,0:T(8,128)S(1)}, f32[3,32,256]{2,1,0:T(8,128)S(1)}, u32[]{:S(2)}, u32[]{:S(2)}) collective-permute-start(f32[3,32,256]{2,1,0:T(8,128)S(1)} %add.49.refs_4_), channel_id=1, source_target_pairs={{0,2},{1,3},{2,0},{3,1},{4,6},{5,7},{6,4},{7,5},{8,10},{9,11},{10,... | collective-permute-start | bytes 294920 | tf_op jit(solution)/shard_map/ppermute | solution.py:433
  126.8 9.9 %collective-permute-start.6 = (f32[3,32,256]{2,1,0:T(8,128)S(1)}, f32[3,32,256]{2,1,0:T(8,128)S(1)}, u32[]{:S(2)}, u32[]{:S(2)}) collective-permute-start(f32[3,32,256]{2,1,0:T(8,128)S(1)} %add.47.refs_0_), channel_id=1, source_target_pairs={{0,1},{1,0},{2,3},{3,2},{4,5},{5,4},{6,7},{7,6},{8,9},{9,8},{10,11... | collective-permute-start | bytes 294920 | tf_op jit(solution)/shard_map/ppermute | solution.py:433
  129.2 8.8 %collective-permute-start.7 = (f32[3,32,256]{2,1,0:T(8,128)S(1)}, f32[3,32,256]{2,1,0:T(8,128)S(1)}, u32[]{:S(2)}, u32[]{:S(2)}) collective-permute-start(f32[3,32,256]{2,1,0:T(8,128)S(1)} %add.47.refs_0_), channel_id=1, source_target_pairs={{0,3},{1,2},{2,1},{3,0},{4,7},{5,6},{6,5},{7,4},{8,11},{9,10},{10,... | collective-permute-start | bytes 294920 | tf_op jit(solution)/shard_map/ppermute | solution.py:433
  132.0 8.0 %collective-permute-start.8 = (f32[3,32,256]{2,1,0:T(8,128)S(1)}, f32[3,32,256]{2,1,0:T(8,128)S(1)}, u32[]{:S(2)}, u32[]{:S(2)}) collective-permute-start(f32[3,32,256]{2,1,0:T(8,128)S(1)} %add.47.refs_0_), channel_id=1, source_target_pairs={{0,2},{1,3},{2,0},{3,1},{4,6},{5,7},{6,4},{7,5},{8,10},{9,11},{10,... | collective-permute-start | bytes 294920 | tf_op jit(solution)/shard_map/ppermute | solution.py:433

commit v7 on v5

--- a/solution.py
+++ b/solution.py
@@ -44,7 +44,29 @@
     return taps
 
 
-def pack_kernel(samples_ref, gain_ref, out_ref):
+def pack_kernel(samples_ref, gain_hbm_ref, packed_ref, held_ref, gain_ref, out_ref, sems, gain_sem, out_sems):
+    copies = []
+    for a in range(6):
+        p, c = divmod(a, 3)
+        copies.append(pltpu.make_async_copy(samples_ref.at[p, c], held_ref.at[a], sems.at[a]))
+        copies[a].start()
+    gain_copy = pltpu.make_async_copy(gain_hbm_ref, gain_ref, gain_sem)
+    gain_copy.start()
+    written = []
+
+    def write(n, lo, hi):
+        written.append(pltpu.make_async_copy(out_ref.at[:, :, lo:hi], packed_ref.at[:, :, lo:hi], out_sems.at[n]))
+        written[n].start()
+
+    for a in range(6):
+        copies[a].wait()
+        for j in range(4):
+            for h in range(2):
+                out_ref[j, h, 16 * a : 16 * a + 16, :] = held_ref[
+                    a, 16 * h : 16 * h + 16, 512 * j : 512 * j + 512
+                ].astype(F32)
+        write(a, 16 * a, 16 * a + 16)
+    gain_copy.wait()
     lane = lax.broadcasted_iota(jnp.int32, (16, 128), 1)
     for j in range(4):
         for h in range(2):
@@ -54,32 +76,34 @@
                 jnp.where(lane < 64, 0.0, jnp.where(lane < 96, gain_ref[0], gain_ref[1])),
             ]
             for a in range(6):
-                p, c = divmod(a, 3)
-                out_ref[j, h, 16 * a : 16 * a + 16, :] = samples_ref[p, c, rows, 512 * j : 512 * j + 512].astype(F32)
                 at, t = 32 * (a % 4), a // 4
                 if j > 0:
-                    piece = samples_ref[p, c, rows, 512 * j - 128 : 512 * j].astype(F32)
+                    piece = held_ref[a, rows, 512 * j - 128 : 512 * j].astype(F32)
                     piece = pltpu.roll(piece, (at - 112) % 128, 1)
                     tiles[t] = jnp.where((lane >= at) & (lane < at + 16), piece, tiles[t])
                 if j < 3:
-                    piece = samples_ref[p, c, rows, 512 * j + 512 : 512 * j + 640].astype(F32)
+                    piece = held_ref[a, rows, 512 * j + 512 : 512 * j + 640].astype(F32)
                     piece = pltpu.roll(piece, (at + 16) % 128, 1)
                     tiles[t] = jnp.where((lane >= at + 16) & (lane < at + 32), piece, tiles[t])
             out_ref[j, h, 96:104, 0:128] = tiles[0][0:8]
             out_ref[j, h, 96:104, 128:256] = tiles[1][0:8]
             out_ref[j, h, 96:104, 256:384] = tiles[0][8:16]
             out_ref[j, h, 96:104, 384:512] = tiles[1][8:16]
+    write(6, 96, 104)
+    for copy in written:
+        copy.wait()
 
 
 class Strips:
-    def __init__(self, place_ref, main_ref, near_ref, far_ref):
+    def __init__(self, first, place_ref, main_ref, near_ref, far_ref):
+        self.first = first
         self.even = place_ref[2] == 0
         self.main, self.near, self.far = main_ref, near_ref, far_ref
 
     def get(self, s, b, rows, cols):
         if b in (1, 2):
             return self.main[s, b - 1, rows, cols]
-        near, far = self.near[s, rows, cols], self.far[s, rows, cols]
+        near, far = self.near[s, rows, cols], self.far[s - self.first, rows, cols]
         return jnp.where(self.even, far, near) if b == 0 else jnp.where(self.even, near, far)
 
     def samples(self, s, b, a):
@@ -101,15 +125,17 @@
     return jnp.where(lane < main + 64, lane, lane - wide)
 
 
-def energy_kernel(place_ref, main_ref, near_ref, far_ref, logit_ref, lse_ref, grey_ref):
+def energy_kernel(first, place_ref, main_ref, near_ref, far_ref, *refs):
+    earlier_ref, logit_ref, lse_ref, grey_ref = refs if first else (None, refs[0], None, refs[1])
     row = lax.broadcasted_iota(jnp.int32, (64, W0), 0) + (place_ref[0] * 32 - 16)
     col = column_of((64, W0), M0, W0) + place_ref[1] * M0
     keep = (row >= 0) & (row < 1024) & (col >= 0) & (col < 2048)
 
-    strips = Strips(place_ref, main_ref, near_ref, far_ref)
-
-    @pl.loop(0, 4)
-    def _(s):
+    strips = Strips(first, place_ref, main_ref, near_ref, far_ref)
+
+    @pl.loop(0, 2)
+    def _(t):
+        s = first + t
         for p in range(2):
             for b in range(4):
                 main = 0.0
@@ -135,15 +161,17 @@
                 eight = four + pltpu.roll(four, size - 4, axis)
                 field = pltpu.roll(eight, 4, axis) + pltpu.roll(field, size - 4, axis)
             gain = main_ref[s, 0, 96:97, 192 + 32 * p : 193 + 32 * p]
-            logit_ref[2 * s + p] = gain * field
-
-    peak = logit_ref[0, 16:48]
-    for i in range(1, 8):
-        peak = jnp.maximum(peak, logit_ref[i, 16:48])
-    total = 0.0
-    for i in range(8):
-        total = total + jnp.exp(logit_ref[i, 16:48] - peak)
-    lse_ref[...] = peak + jnp.log(total)
+            logit_ref[2 * t + p] = gain * field
+
+    if first:
+        logits = [ref.at[i] for ref in (earlier_ref, logit_ref) for i in range(4)]
+        peak = logits[0][...]
+        for ref in logits[1:]:
+            peak = jnp.maximum(peak, ref[...])
+        total = 0.0
+        for ref in logits:
+            total = total + jnp.exp(ref[...] - peak)
+        lse_ref[...] = pltpu.roll(peak + jnp.log(total), 58, 0)[0:56]
 
 
 def split2(value):
@@ -221,7 +249,7 @@
     v1 = down_rows(32, 64, 1, strip * 16 - 8, 512)
     v2, p2, p1 = row_matrices(strip)
     inside1, inside2 = level_masks(192, 96, place_ref[1])
-    strips = Strips(place_ref, main_ref, near_ref, far_ref)
+    strips = Strips(sources[0], place_ref, main_ref, near_ref, far_ref)
     for i, s in enumerate(sources):
         for a in range(6):
             for b in range(4):
@@ -248,7 +276,7 @@
 
 
 def mix_kernel(
-    place_ref, logit_ref, lse_ref, near_ref, far_ref,
+    place_ref, logit_a_ref, logit_b_ref, lse_ref,
     fine_a_ref, mid_a_ref, low_a_ref, fine_b_ref, mid_b_ref, low_b_ref,
     d1_ref, d2_ref, u2_ref, u1_ref,
     left_ref, right_ref, w0_ref, s1_ref, w1_ref, s2_ref, s3_ref, s4_ref,
@@ -259,22 +287,17 @@
     col = column_of((16, W0), M0, W0)
     inside_col = (col >= -10) & (col <= 522) & (col + k * M0 >= 0) & (col + k * M0 < 2048)
     row = lax.broadcasted_iota(jnp.int32, (16, W0), 0)
-    even = place_ref[2] == 0
-    lses = (
-        jnp.where(even, far_ref[...], near_ref[...]),
-        lse_ref[0:16],
-        lse_ref[16:32],
-        jnp.where(even, near_ref[...], far_ref[...]),
-    )
+    lse = pltpu.roll(jnp.concatenate([lse_ref[...], jnp.zeros((8, W0), F32)], axis=0), 6, 0)
     keeps = []
     for b in range(4):
         r = row + (16 * b - 16)
         g = r + strip * 32
         keeps.append(inside_col & (r >= -10) & (r <= 42) & (g >= 0) & (g < 1024))
     for i in range(8):
+        logit_ref = (logit_a_ref, logit_b_ref)[i // 4]
         for b in range(4):
             rows = slice(16 * b, 16 * b + 16)
-            w0_ref[i, rows] = jnp.where(keeps[b], jnp.exp(logit_ref[i, rows] - lses[b]), 0.0)
+            w0_ref[i, rows] = jnp.where(keeps[b], jnp.exp(logit_ref[i % 4, rows] - lse[rows]), 0.0)
         put(s1_ref, 8, i, 32, dot(v1, stacked(w0_ref[i])))
     inside1, inside2 = level_masks(32, 16, k)
     w1_ref[...] = resampled(s1_ref, d1_ref)
@@ -322,10 +345,10 @@
     count = lax.axis_size(ROWS)
     swaps = [(i, i + 1) for i in range(1, count - 1, 2)]
     swaps += [(b, a) for a, b in swaps]
-    pick = functools.partial(lax.dynamic_index_in_dim, halves, axis=-3, keepdims=False)
+    pick = functools.partial(lax.dynamic_index_in_dim, halves, axis=1, keepdims=False)
     near = lax.ppermute(pick(1 - core), "c", [(0, 1), (1, 0)])
-    far = lax.ppermute(pick(core), ROWS, swaps)
-    return near, far
+    far = pick(core)
+    return near, lax.ppermute(far[:2], ROWS, swaps), lax.ppermute(far[2:], ROWS, swaps)
 
 
 def partner(value, flip):
@@ -348,24 +371,40 @@
     packed = pl.pallas_call(
         pack_kernel,
         out_shape=jax.ShapeDtypeStruct((4, 2, 104, 512), F32),
-        in_specs=vmem(1) + smem(),
-        out_specs=vmem(1)[0],
-        compiler_params=PARAMS,
+        in_specs=[pl.BlockSpec(memory_space=pltpu.HBM)] * 2,
+        out_specs=pl.BlockSpec(memory_space=pltpu.HBM),
+        scratch_shapes=[
+            pltpu.VMEM((6, 32, 2048), jnp.int32),
+            pltpu.SMEM((2,), F32),
+            pltpu.VMEM((4, 2, 104, 512), F32),
+            pltpu.SemaphoreType.DMA((6,)),
+            pltpu.SemaphoreType.DMA,
+            pltpu.SemaphoreType.DMA((7,)),
+        ],
+        compiler_params=pltpu.CompilerParams(vmem_limit_bytes=60 * 1024 * 1024),
         name="pack",
     )(samples, gain)
     main = lax.all_to_all(packed, "x", 0, 0)
     main, strip, column, core = lax.optimization_barrier((main, strip, column, core))
-    near, far = neighbours(main, core)
+    near, *far = neighbours(main, core)
     place = jnp.stack([strip, column, core]).astype(jnp.int32)
-    logits, lse = pl.pallas_call(
-        energy_kernel,
-        out_shape=(jax.ShapeDtypeStruct((8, 64, W0), F32), jax.ShapeDtypeStruct((32, W0), F32)),
-        in_specs=smem() + vmem(3),
-        out_specs=tuple(vmem(2)),
-        scratch_shapes=[pltpu.VMEM((64, W0), F32)],
-        compiler_params=PARAMS,
-        name="energy",
-    )(place, main, near, far)
+    logit_shape = jax.ShapeDtypeStruct((4, 64, W0), F32)
+
+    def energy(first, *earlier):
+        return pl.pallas_call(
+            functools.partial(energy_kernel, first),
+            out_shape=(logit_shape,) + (jax.ShapeDtypeStruct((56, W0), F32),) * len(earlier),
+            in_specs=smem() + vmem(3 + len(earlier)),
+            out_specs=tuple(vmem(1 + len(earlier))),
+            scratch_shapes=[pltpu.VMEM((64, W0), F32)],
+            compiler_params=PARAMS,
+            cost_estimate=pl.CostEstimate(flops=2_000_000_000, bytes_accessed=6_000_000, transcendentals=0),
+            name="energy",
+        )(place, main, near, far[first // 2], *earlier)
+
+    logits = energy(0)
+    *more, lse = energy(2, *logits)
+    logits = [*logits, *more]
 
     taps = [
         jnp.asarray(t, BF)
@@ -399,16 +438,15 @@
             compiler_params=PARAMS,
             cost_estimate=pl.CostEstimate(flops=2_000_000_000, bytes_accessed=6_000_000, transcendentals=0),
             name="pyramid",
-        )(place, main, near, far, *taps)
+        )(place, main, near, far[step], *taps)
         other, *detail = lax.optimization_barrier((other, *detail))
         details += detail
         lse = join_lse(lse, other)
-    lse_near, lse_far = neighbours(lse.reshape(2, 16, W0), core)
 
     left, right = pl.pallas_call(
         mix_kernel,
         out_shape=(jax.ShapeDtypeStruct((3, 32, 256), F32),) * 2,
-        in_specs=smem() + vmem(14),
+        in_specs=smem() + vmem(13),
         out_specs=tuple(vmem(2)),
         scratch_shapes=[
             pltpu.VMEM((8, 64, W0), F32),
@@ -420,7 +458,7 @@
         ],
         compiler_params=PARAMS,
         name="mix",
-    )(place, logits, lse, lse_near, lse_far, *details, *taps)
+    )(place, *logits, lse, *details, *taps)
 
     for a, b in ((1, 3), (3, 1)):
         left_in, right_in = partner(left, a), partner(right, b)

time: 145 us -> 136 us (0.938)
  starting transfers between devices: 57.8 us -> 52.2 us
  blocking collectives: 41.5 us -> 38.3 us
  Pallas kernels: 16 us -> 18.3 us
  local copies, waits for them, and re-layouts: 3.26 us -> 1.2 us
  waiting for transfers between devices: 25.7 us -> 24 us
    ppermute x2, waiting for transfers between devices: 14 us -> 5.38 us  [the longest x1 3.79 us: neighbours(): lax.ppermute(far[:2], ROWS, swaps)]
    ppermute x2, waiting for transfers between devices: 0.01 us -> 4.1 us  [crossed(): return lax.ppermute(value, ('c', 'zh'), pairs)]
    ppermute x2 -> x1, starting transfers between devices: 5.73 us -> 1.92 us  [neighbours(): near = lax.ppermute(pick(1 - core), 'c', [(0, 1), (1, 0)])]
    all_to_all x1, blocking collectives: 15.3 us -> 11.9 us  [on_device(): joined = lax.all_to_all(jnp.broadcast_to(whole, (4, 3, 32, 512)), 'x', 0, 0)]
    ppermute x4, waiting for transfers between devices: 11.7 us -> 14.5 us  [partner(): return lax.ppermute(value, 'zh', [(i, i ^ flip) for i in range(4)])]
    unnamed x12 -> x8, local copies, waits for them, and re-layouts: 2.08 us -> 0.03 us
    pallas_call x1, Pallas kernels: 0.78 us -> 2.36 us  [on_device(): pl.pallas_call(pack_kernel, out_shape=jax.ShapeDtypeStruct((4, 2, 104, 51...]
    pallas_call x1 -> x2, Pallas kernels: 5.36 us -> 6.07 us  [energy(): pl.pallas_call(functools.partial(energy_kernel, first), out_shape=(logit_...]
  transfers between devices with their start and end apart: 10 -> 9, of which waited for: 6 -> 5; matrix products, arithmetic and copies ran while one was open for 0% -> 0% of each run, Pallas kernels for 5% -> 7%
where the time goes in v7:
time: 136 us; the launch traced here: 134 us
  starting transfers between devices  52.2 us (38%)
  blocking collectives  38.3 us (28%)
  waiting for transfers between devices  24 us (18%)
  Pallas kernels  18.3 us (13%)
    all_to_all x1, blocking collectives, on_device(): main = lax.all_to_all(packed, 'x', 0, 0)  26.4 us
    ppermute x4, starting transfers between devices, partner(): return lax.ppermute(value, 'zh', [(i, i ^ flip) for i in range(4)])  26.4 us
    ppermute x2, starting transfers between devices, crossed(): return lax.ppermute(value, ('c', 'zh'), pairs)  18.3 us
    ppermute x4, waiting for transfers between devices, partner(): return lax.ppermute(value, 'zh', [(i, i ^ flip) for i in range(4)])  14.5 us
    all_to_all x1, blocking collectives, on_device(): joined = lax.all_to_all(jnp.broadcast_to(whole, (4, 3, 32, 512)), 'x', 0, 0)  11.9 us
    pallas_call x2, Pallas kernels, on_device(): pl.pallas_call(functools.partial(pyramid_kernel, (2 * step, 2 * step + 1)...  7.05 us
    pallas_call x2, Pallas kernels, energy(): pl.pallas_call(functools.partial(energy_kernel, first), out_shape=(logit_...  6.07 us
    ppermute x2, waiting for transfers between devices, crossed(): return lax.ppermute(value, ('c', 'zh'), pairs)  4.1 us
  transfers between devices with their start and end apart: 9, of which 5 were waited for; matrix products, arithmetic and copies ran while one was open for 0% of the time, Pallas kernels for 7%

profile of v7, /device:TPU:24, one launch (start us, length us, event | category | flops | bytes accessed | tf_op | source)
XLA Modules:
  0.0 134.5 jit_solution(6133244206576701124)
XLA Ops:
  0.0 2.4 %pack.1 = f32[4,2,104,512]{3,2,1,0:T(8,128)} custom-call(s32[2,3,32,2048]{3,2,1,0:T(8,128)} %samples_ref, f32[2]{0:T(128)} %gain_hbm_ref.1), custom_call_target="tpu_custom_call" | custom-call | tf_op jit(solution)/shard_map/pack/pallas_call | solution.py:371
  2.4 26.4 %all_to_all.10.main_ref = f32[4,2,104,512]{3,2,1,0:T(8,128)S(1)} all-to-all(f32[4,2,104,512]{3,2,1,0:T(8,128)} %pack.1), channel_id=1, replica_groups=mesh['zl'=4,'y'=4,'c'=2,'zh'=4,'x'=4] {'x'}, dimensions={0} | all-to-all | bytes 3407872 | tf_op jit(solution)/shard_map/all_to_all | solution.py:387
  28.9 1.9 %collective-permute-start = (f32[4,104,512]{2,1,0:T(8,128)S(1)}, f32[4,104,512]{2,1,0:T(8,128)S(1)}, u32[]{:S(2)}, u32[]{:S(2)}) collective-permute-start(f32[4,104,512]{2,1,0:T(8,128)S(1)} %dynamic-slice_bitcast_fusion), channel_id=1, source_target_pairs={{0,16},{16,0},{1,17},{17,1},{2,18},{18,2},{3,19},{19,3},{4,20},{20... | collective-permute-start | bytes 2555912 | tf_op jit(solution)/shard_map/ppermute | solution.py:349
  30.9 2.8 %collective-permute-start.1 = (f32[2,104,512]{2,1,0:T(8,128)S(1)}, f32[2,104,512]{2,1,0:T(8,128)S(1)}, u32[]{:S(2)}, u32[]{:S(2)}) collective-permute-start(f32[2,104,512]{2,1,0:T(8,128)S(1)} %get-tuple-element.58), channel_id=1, source_target_pairs={{16,32},{48,64},{80,96},{112,128},{144,160},{176,192},{208,224},{2... | collective-permute-start | bytes 1277960 | tf_op jit(solution)/shard_map/ppermute | solution.py:351
  33.6 2.8 %collective-permute-start.2 = (f32[2,104,512]{2,1,0:T(8,128)S(1)}, f32[2,104,512]{2,1,0:T(8,128)S(1)}, u32[]{:S(2)}, u32[]{:S(2)}) collective-permute-start(f32[2,104,512]{2,1,0:T(8,128)S(1)} %get-tuple-element.57), channel_id=1, source_target_pairs={{16,32},{48,64},{80,96},{112,128},{144,160},{176,192},{208,224},{2... | collective-permute-start | bytes 1277960 | tf_op jit(solution)/shard_map/ppermute | solution.py:351
  36.5 3.8 %collective-permute-done.1.far_ref = f32[2,104,512]{2,1,0:T(8,128)S(1)} collective-permute-done((f32[2,104,512]{2,1,0:T(8,128)S(1)}, f32[2,104,512]{2,1,0:T(8,128)S(1)}, u32[]{:S(2)}, u32[]{:S(2)}) %collective-permute-start.1) | collective-permute-done | bytes 426016 | tf_op jit(solution)/shard_map/ppermute | solution.py:351
  40.3 2.9 %energy.2.refs_0_.logit_a_ref = f32[4,64,640]{2,1,0:T(8,128)S(1)} custom-call(s32[3]{0:T(128)S(1)} %pad_add_fusion.place_ref, f32[4,2,104,512]{3,2,1,0:T(8,128)S(1)} %all_to_all.10.main_ref, f32[4,104,512]{2,1,0:T(8,128)S(1)} %collective-permute-done.near_ref, f32[2,104,512]{2,1,0:T(8,128)S(1)} %collective-permute-done.1.far_ref), custom_call_target="tpu_custom_call" | custom-call | flops 2000000000 | bytes 6000000 | tf_op jit(solution)/shard_map/energy/pallas_call | solution.py:394
  43.3 1.6 %collective-permute-done.2.far_ref = f32[2,104,512]{2,1,0:T(8,128)S(1)} collective-permute-done((f32[2,104,512]{2,1,0:T(8,128)S(1)}, f32[2,104,512]{2,1,0:T(8,128)S(1)}, u32[]{:S(2)}, u32[]{:S(2)}) %collective-permute-start.2) | collective-permute-done | bytes 426016 | tf_op jit(solution)/shard_map/ppermute | solution.py:351
  44.9 3.2 %energy.3 = (f32[4,64,640]{2,1,0:T(8,128)S(1)}, f32[56,640]{1,0:T(8,128)S(1)}) custom-call(s32[3]{0:T(128)S(1)} %pad_add_fusion.place_ref, f32[4,2,104,512]{3,2,1,0:T(8,128)S(1)} %all_to_all.10.main_ref, f32[4,104,512]{2,1,0:T(8,128)S(1)} %collective-permute-done.near_ref, f32[2,104,512]{2,1,0:T(8,128)S(1)} %collective-permute-done.2.far_ref, ...), custom_call_target="tpu_custom_call" | custom-call | flops 2000000000 | bytes 6000000 | tf_op jit(solution)/shard_map/energy/pallas_call | solution.py:394
  48.0 9.1 %collective-permute-start.3 = (f32[56,640]{1,0:T(8,128)S(1)}, f32[56,640]{1,0:T(8,128)S(1)}, u32[]{:S(2)}, u32[]{:S(2)}) collective-permute-start(f32[56,640]{1,0:T(8,128)S(1)} %get-tuple-element.40), channel_id=1, source_target_pairs={{0,4},{4,0},{8,12},{12,8},{16,28},{20,24},{24,20},{28,16},{1,5},{5... | collective-permute-start | bytes 430088 | tf_op jit(solution)/shard_map/ppermute | solution.py:360
  57.2 3.5 %pyramid.2 = (f32[384,512]{1,0:T(8,128)S(1)}, f32[384,384]{1,0:T(8,128)S(1)}, f32[192,256]{1,0:T(8,128)S(1)}) custom-call(s32[3]{0:T(128)S(1)} %pad_add_fusion.place_ref, f32[4,2,104,512]{3,2,1,0:T(8,128)S(1)} %all_to_all.10.main_ref, f32[4,104,512]{2,1,0:T(8,128)S(1)} %collective-permute-done.near_ref, f32[2,104,512]{2,1,0:T(8,128)S(1)} %collective-permute-done.1.far_ref, ...), custom_call_target="tpu_custom_call" | custom-call | flops 2000000000 | bytes 6000000 | tf_op jit(solution)/shard_map/pyramid/pallas_call | solution.py:421
  60.7 4.1 %collective-permute-done.3 = f32[56,640]{1,0:T(8,128)S(1)} collective-permute-done((f32[56,640]{1,0:T(8,128)S(1)}, f32[56,640]{1,0:T(8,128)S(1)}, u32[]{:S(2)}, u32[]{:S(2)}) %collective-permute-start.3) | collective-permute-done | bytes 143392 | tf_op jit(solution)/shard_map/ppermute | solution.py:360
  64.9 9.2 %collective-permute-start.4 = (f32[56,640]{1,0:T(8,128)S(1)}, f32[56,640]{1,0:T(8,128)S(1)}, u32[]{:S(2)}, u32[]{:S(2)}) collective-permute-start(f32[56,640]{1,0:T(8,128)S(1)} %log_add_fusion.1), channel_id=1, source_target_pairs={{0,12},{4,8},{8,4},{12,0},{16,20},{20,16},{24,28},{28,24},{1,13},{... | collective-permute-start | bytes 430088 | tf_op jit(solution)/shard_map/ppermute | solution.py:360
  74.1 3.5 %pyramid.3 = (f32[384,512]{1,0:T(8,128)S(1)}, f32[384,384]{1,0:T(8,128)S(1)}, f32[192,256]{1,0:T(8,128)S(1)}) custom-call(s32[3]{0:T(128)S(1)} %pad_add_fusion.place_ref, f32[4,2,104,512]{3,2,1,0:T(8,128)S(1)} %all_to_all.10.main_ref, f32[4,104,512]{2,1,0:T(8,128)S(1)} %collective-permute-done.near_ref, f32[2,104,512]{2,1,0:T(8,128)S(1)} %collective-permute-done.2.far_ref, ...), custom_call_target="tpu_custom_call" | custom-call | flops 2000000000 | bytes 6000000 | tf_op jit(solution)/shard_map/pyramid/pallas_call | solution.py:421
  77.7 2.8 %mix.1 = (f32[3,32,256]{2,1,0:T(8,128)S(1)}, f32[3,32,256]{2,1,0:T(8,128)S(1)}) custom-call(s32[3]{0:T(128)S(1)} %pad_add_fusion.place_ref, f32[4,64,640]{2,1,0:T(8,128)S(1)} %energy.2.refs_0_.logit_a_ref, f32[4,64,640]{2,1,0:T(8,128)S(1)} %get-tuple-element.39.logit_b_ref, f32[56,640]{1,0:T(8,128)S(1)} %log_add_fusion.lse_ref, ...), custom_call_target="tpu_custom_call" | custom-call | tf_op jit(solution)/shard_map/mix/pallas_call | solution.py:446
  80.5 11.5 %collective-permute-start.5 = (f32[3,32,256]{2,1,0:T(8,128)S(1)}, f32[3,32,256]{2,1,0:T(8,128)S(1)}, u32[]{:S(2)}, u32[]{:S(2)}) collective-permute-start(f32[3,32,256]{2,1,0:T(8,128)S(1)} %get-tuple-element.55), channel_id=1, source_target_pairs={{0,4},{4,0},{8,12},{12,8},{1,5},{5,1},{9,13},{13,9},{2,6},{6,2},{1... | collective-permute-start | bytes 294920 | tf_op jit(solution)/shard_map/ppermute | solution.py:355
  92.0 8.3 %collective-permute-start.7 = (f32[3,32,256]{2,1,0:T(8,128)S(1)}, f32[3,32,256]{2,1,0:T(8,128)S(1)}, u32[]{:S(2)}, u32[]{:S(2)}) collective-permute-start(f32[3,32,256]{2,1,0:T(8,128)S(1)} %get-tuple-element.56), channel_id=1, source_target_pairs={{0,12},{4,8},{8,4},{12,0},{1,13},{5,9},{9,5},{13,1},{2,14},{6,10},... | collective-permute-start | bytes 294920 | tf_op jit(solution)/shard_map/ppermute | solution.py:355
  100.4 4.1 %collective-permute-start.6 = (f32[3,32,256]{2,1,0:T(8,128)S(1)}, f32[3,32,256]{2,1,0:T(8,128)S(1)}, u32[]{:S(2)}, u32[]{:S(2)}) collective-permute-start(f32[3,32,256]{2,1,0:T(8,128)S(1)} %add.46), channel_id=1, source_target_pairs={{0,12},{4,8},{8,4},{12,0},{1,13},{5,9},{9,5},{13,1},{2,14},{6,10},... | collective-permute-start | bytes 294920 | tf_op jit(solution)/shard_map/ppermute | solution.py:355
  104.5 6.0 %collective-permute-done.7 = f32[3,32,256]{2,1,0:T(8,128)S(1)} collective-permute-done((f32[3,32,256]{2,1,0:T(8,128)S(1)}, f32[3,32,256]{2,1,0:T(8,128)S(1)}, u32[]{:S(2)}, u32[]{:S(2)}) %collective-permute-start.7) | collective-permute-done | bytes 98336 | tf_op jit(solution)/shard_map/ppermute | solution.py:355
  110.5 2.4 %collective-permute-start.8 = (f32[3,32,256]{2,1,0:T(8,128)S(1)}, f32[3,32,256]{2,1,0:T(8,128)S(1)}, u32[]{:S(2)}, u32[]{:S(2)}) collective-permute-start(f32[3,32,256]{2,1,0:T(8,128)S(1)} %add.48), channel_id=1, source_target_pairs={{0,4},{4,0},{8,12},{12,8},{1,5},{5,1},{9,13},{13,9},{2,6},{6,2},{1... | collective-permute-start | bytes 294920 | tf_op jit(solution)/shard_map/ppermute | solution.py:355
  113.0 8.5 %collective-permute-done.8 = f32[3,32,256]{2,1,0:T(8,128)S(1)} collective-permute-done((f32[3,32,256]{2,1,0:T(8,128)S(1)}, f32[3,32,256]{2,1,0:T(8,128)S(1)}, u32[]{:S(2)}, u32[]{:S(2)}) %collective-permute-start.8) | collective-permute-done | bytes 98336 | tf_op jit(solution)/shard_map/ppermute | solution.py:355
  121.5 0.1 broadcast_in_dim.3
  121.6 11.9 %all_to_all.11 = f32[4,3,32,512]{3,2,1,0:T(8,128)S(1)} all-to-all(f32[4,3,32,512]{3,2,1,0:T(8,128)S(1)} %broadcast_in_dim.3), channel_id=1, replica_groups=mesh['zl'=4,'y'=4,'c'=2,'zh'=4,'x'=4] {'x'}, dimensions={0} | all-to-all | bytes 1572864 | tf_op jit(solution)/shard_map/all_to_all | solution.py:467
  133.5 0.9 copy.15
  (22 shorter events, 0.4 us)
Async XLA Ops:
  28.9 11.5 %collective-permute-start = (f32[4,104,512]{2,1,0:T(8,128)S(1)}, f32[4,104,512]{2,1,0:T(8,128)S(1)}, u32[]{:S(2)}, u32[]{:S(2)}) collective-permute-start(f32[4,104,512]{2,1,0:T(8,128)S(1)} %dynamic-slice_bitcast_fusion), channel_id=1, source_target_pairs={{0,16},{16,0},{1,17},{17,1},{2,18},{18,2},{3,19},{19,3},{4,20},{20... | collective-permute-start | bytes 2555912 | tf_op jit(solution)/shard_map/ppermute | solution.py:349
  30.9 9.4 %collective-permute-start.1 = (f32[2,104,512]{2,1,0:T(8,128)S(1)}, f32[2,104,512]{2,1,0:T(8,128)S(1)}, u32[]{:S(2)}, u32[]{:S(2)}) collective-permute-start(f32[2,104,512]{2,1,0:T(8,128)S(1)} %get-tuple-element.58), channel_id=1, source_target_pairs={{16,32},{48,64},{80,96},{112,128},{144,160},{176,192},{208,224},{2... | collective-permute-start | bytes 1277960 | tf_op jit(solution)/shard_map/ppermute | solution.py:351
  33.6 11.2 %collective-permute-start.2 = (f32[2,104,512]{2,1,0:T(8,128)S(1)}, f32[2,104,512]{2,1,0:T(8,128)S(1)}, u32[]{:S(2)}, u32[]{:S(2)}) collective-permute-start(f32[2,104,512]{2,1,0:T(8,128)S(1)} %get-tuple-element.57), channel_id=1, source_target_pairs={{16,32},{48,64},{80,96},{112,128},{144,160},{176,192},{208,224},{2... | collective-permute-start | bytes 1277960 | tf_op jit(solution)/shard_map/ppermute | solution.py:351
  43.2 13.9 %copy-start = (bf16[640,384]{1,0:T(8,128)(2,1)S(1)}, bf16[640,384]{1,0:T(8,128)(2,1)}, u32[]{:S(2)}) copy-start(bf16[640,384]{1,0:T(8,128)(2,1)} %constant.43.clone.d1_ref) | copy-start | bytes 1474564
  43.2 13.9 %copy-start.1 = (bf16[384,512]{1,0:T(8,128)(2,1)S(1)}, bf16[384,512]{1,0:T(8,128)(2,1)}, u32[]{:S(2)}) copy-start(bf16[384,512]{1,0:T(8,128)(2,1)} %constant.46.clone.u1_ref) | copy-start | bytes 1179652
  43.3 13.9 %copy-start.2 = (bf16[384,256]{1,0:T(8,128)(2,1)S(1)}, bf16[384,256]{1,0:T(8,128)(2,1)}, u32[]{:S(2)}) copy-start(bf16[384,256]{1,0:T(8,128)(2,1)} %constant.44.clone.d2_ref) | copy-start | bytes 589828
  43.3 13.9 %copy-start.3 = (bf16[256,384]{1,0:T(8,128)(2,1)S(1)}, bf16[256,384]{1,0:T(8,128)(2,1)}, u32[]{:S(2)}) copy-start(bf16[256,384]{1,0:T(8,128)(2,1)} %constant.45.clone.u2_ref) | copy-start | bytes 589828
  48.0 16.8 %collective-permute-start.3 = (f32[56,640]{1,0:T(8,128)S(1)}, f32[56,640]{1,0:T(8,128)S(1)}, u32[]{:S(2)}, u32[]{:S(2)}) collective-permute-start(f32[56,640]{1,0:T(8,128)S(1)} %get-tuple-element.40), channel_id=1, source_target_pairs={{0,4},{4,0},{8,12},{12,8},{16,28},{20,24},{24,20},{28,16},{1,5},{5... | collective-permute-start | bytes 430088 | tf_op jit(solution)/shard_map/ppermute | solution.py:360
  64.9 12.7 %collective-permute-start.4 = (f32[56,640]{1,0:T(8,128)S(1)}, f32[56,640]{1,0:T(8,128)S(1)}, u32[]{:S(2)}, u32[]{:S(2)}) collective-permute-start(f32[56,640]{1,0:T(8,128)S(1)} %log_add_fusion.1), channel_id=1, source_target_pairs={{0,12},{4,8},{8,4},{12,0},{16,20},{20,16},{24,28},{28,24},{1,13},{... | collective-permute-start | bytes 430088 | tf_op jit(solution)/shard_map/ppermute | solution.py:360
  80.5 19.9 %collective-permute-start.5 = (f32[3,32,256]{2,1,0:T(8,128)S(1)}, f32[3,32,256]{2,1,0:T(8,128)S(1)}, u32[]{:S(2)}, u32[]{:S(2)}) collective-permute-start(f32[3,32,256]{2,1,0:T(8,128)S(1)} %get-tuple-element.55), channel_id=1, source_target_pairs={{0,4},{4,0},{8,12},{12,8},{1,5},{5,1},{9,13},{13,9},{2,6},{6,2},{1... | collective-permute-start | bytes 294920 | tf_op jit(solution)/shard_map/ppermute | solution.py:355
  92.0 18.5 %collective-permute-start.7 = (f32[3,32,256]{2,1,0:T(8,128)S(1)}, f32[3,32,256]{2,1,0:T(8,128)S(1)}, u32[]{:S(2)}, u32[]{:S(2)}) collective-permute-start(f32[3,32,256]{2,1,0:T(8,128)S(1)} %get-tuple-element.56), channel_id=1, source_target_pairs={{0,12},{4,8},{8,4},{12,0},{1,13},{5,9},{9,5},{13,1},{2,14},{6,10},... | collective-permute-start | bytes 294920 | tf_op jit(solution)/shard_map/ppermute | solution.py:355
  100.4 12.5 %collective-permute-start.6 = (f32[3,32,256]{2,1,0:T(8,128)S(1)}, f32[3,32,256]{2,1,0:T(8,128)S(1)}, u32[]{:S(2)}, u32[]{:S(2)}) collective-permute-start(f32[3,32,256]{2,1,0:T(8,128)S(1)} %add.46), channel_id=1, source_target_pairs={{0,12},{4,8},{8,4},{12,0},{1,13},{5,9},{9,5},{13,1},{2,14},{6,10},... | collective-permute-start | bytes 294920 | tf_op jit(solution)/shard_map/ppermute | solution.py:355
  110.5 11.0 %collective-permute-start.8 = (f32[3,32,256]{2,1,0:T(8,128)S(1)}, f32[3,32,256]{2,1,0:T(8,128)S(1)}, u32[]{:S(2)}, u32[]{:S(2)}) collective-permute-start(f32[3,32,256]{2,1,0:T(8,128)S(1)} %add.48), channel_id=1, source_target_pairs={{0,4},{4,0},{8,12},{12,8},{1,5},{5,1},{9,13},{13,9},{2,6},{6,2},{1... | collective-permute-start | bytes 294920 | tf_op jit(solution)/shard_map/ppermute | solution.py:355

commit v8 on v7

--- a/solution.py
+++ b/solution.py
@@ -16,6 +16,7 @@
 GREY = (0.299 / 255.0, 0.587 / 255.0, 0.114 / 255.0)
 W0, W1, W2 = 640, 384, 256
 M0, M1, M2 = 512, 256, 128
+FLIPS = (0, 1, 3, 2)
 PARAMS = pltpu.CompilerParams(vmem_limit_bytes=20 * 1024 * 1024)
 
 
@@ -44,7 +45,8 @@
     return taps
 
 
-def pack_kernel(samples_ref, gain_hbm_ref, packed_ref, held_ref, gain_ref, out_ref, sems, gain_sem, out_sems):
+def pack_kernel(samples_ref, gain_hbm_ref, *refs):
+    packed_refs, (held_ref, gain_ref, out_ref, sems, gain_sem, out_sems) = refs[:4], refs[4:]
     copies = []
     for a in range(6):
         p, c = divmod(a, 3)
@@ -52,23 +54,22 @@
         copies[a].start()
     gain_copy = pltpu.make_async_copy(gain_hbm_ref, gain_ref, gain_sem)
     gain_copy.start()
+    mine = lax.axis_index("x")
+    lane = lax.broadcasted_iota(jnp.int32, (16, 128), 1)
     written = []
-
-    def write(n, lo, hi):
-        written.append(pltpu.make_async_copy(out_ref.at[:, :, lo:hi], packed_ref.at[:, :, lo:hi], out_sems.at[n]))
-        written[n].start()
-
-    for a in range(6):
-        copies[a].wait()
-        for j in range(4):
+    for m, flip in enumerate(FLIPS):
+        j = mine ^ flip
+        base = pl.multiple_of(512 * j, 512)
+        before = pl.multiple_of(jnp.maximum(base - 128, 0), 128)
+        after = pl.multiple_of(jnp.minimum(base + 512, 1920), 128)
+        has_before, has_after = j > 0, j < 3
+        for a in range(6):
+            if m == 0:
+                copies[a].wait()
             for h in range(2):
-                out_ref[j, h, 16 * a : 16 * a + 16, :] = held_ref[
-                    a, 16 * h : 16 * h + 16, 512 * j : 512 * j + 512
-                ].astype(F32)
-        write(a, 16 * a, 16 * a + 16)
-    gain_copy.wait()
-    lane = lax.broadcasted_iota(jnp.int32, (16, 128), 1)
-    for j in range(4):
+                out_ref[m, h, 16 * a : 16 * a + 16, :] = held_ref[a, 16 * h : 16 * h + 16, pl.ds(base, 512)].astype(F32)
+        if m == 0:
+            gain_copy.wait()
         for h in range(2):
             rows = slice(16 * h, 16 * h + 16)
             tiles = [
@@ -77,33 +78,31 @@
             ]
             for a in range(6):
                 at, t = 32 * (a % 4), a // 4
-                if j > 0:
-                    piece = held_ref[a, rows, 512 * j - 128 : 512 * j].astype(F32)
-                    piece = pltpu.roll(piece, (at - 112) % 128, 1)
-                    tiles[t] = jnp.where((lane >= at) & (lane < at + 16), piece, tiles[t])
-                if j < 3:
-                    piece = held_ref[a, rows, 512 * j + 512 : 512 * j + 640].astype(F32)
-                    piece = pltpu.roll(piece, (at + 16) % 128, 1)
-                    tiles[t] = jnp.where((lane >= at + 16) & (lane < at + 32), piece, tiles[t])
-            out_ref[j, h, 96:104, 0:128] = tiles[0][0:8]
-            out_ref[j, h, 96:104, 128:256] = tiles[1][0:8]
-            out_ref[j, h, 96:104, 256:384] = tiles[0][8:16]
-            out_ref[j, h, 96:104, 384:512] = tiles[1][8:16]
-    write(6, 96, 104)
+                piece = pltpu.roll(held_ref[a, rows, pl.ds(before, 128)].astype(F32), (at - 112) % 128, 1)
+                piece = jnp.where(has_before, piece, 0.0)
+                tiles[t] = jnp.where((lane >= at) & (lane < at + 16), piece, tiles[t])
+                piece = pltpu.roll(held_ref[a, rows, pl.ds(after, 128)].astype(F32), (at + 16) % 128, 1)
+                piece = jnp.where(has_after, piece, 0.0)
+                tiles[t] = jnp.where((lane >= at + 16) & (lane < at + 32), piece, tiles[t])
+            out_ref[m, h, 96:104, 0:128] = tiles[0][0:8]
+            out_ref[m, h, 96:104, 128:256] = tiles[1][0:8]
+            out_ref[m, h, 96:104, 256:384] = tiles[0][8:16]
+            out_ref[m, h, 96:104, 384:512] = tiles[1][8:16]
+        written.append(pltpu.make_async_copy(out_ref.at[m], packed_refs[m], out_sems.at[m]))
+        written[m].start()
     for copy in written:
         copy.wait()
 
 
 class Strips:
-    def __init__(self, first, place_ref, main_ref, near_ref, far_ref):
-        self.first = first
+    def __init__(self, place_ref, mains, near_ref, far_ref):
         self.even = place_ref[2] == 0
-        self.main, self.near, self.far = main_ref, near_ref, far_ref
+        self.mains, self.near, self.far = mains, near_ref, far_ref
 
     def get(self, s, b, rows, cols):
         if b in (1, 2):
-            return self.main[s, b - 1, rows, cols]
-        near, far = self.near[s, rows, cols], self.far[s - self.first, rows, cols]
+            return self.mains[s][b - 1, rows, cols]
+        near, far = self.near[s, rows, cols], self.far[s, rows, cols]
         return jnp.where(self.even, far, near) if b == 0 else jnp.where(self.even, near, far)
 
     def samples(self, s, b, a):
@@ -125,17 +124,15 @@
     return jnp.where(lane < main + 64, lane, lane - wide)
 
 
-def energy_kernel(first, place_ref, main_ref, near_ref, far_ref, *refs):
-    earlier_ref, logit_ref, lse_ref, grey_ref = refs if first else (None, refs[0], None, refs[1])
+def energy_kernel(second, place_ref, main_a_ref, main_b_ref, near_ref, far_ref, *refs):
+    earlier_ref, logit_ref, lse_ref, grey_ref = refs if second else (None, refs[0], None, refs[1])
     row = lax.broadcasted_iota(jnp.int32, (64, W0), 0) + (place_ref[0] * 32 - 16)
     col = column_of((64, W0), M0, W0) + place_ref[1] * M0
     keep = (row >= 0) & (row < 1024) & (col >= 0) & (col < 2048)
 
-    strips = Strips(first, place_ref, main_ref, near_ref, far_ref)
-
-    @pl.loop(0, 2)
-    def _(t):
-        s = first + t
+    mains = (main_a_ref, main_b_ref)
+    strips = Strips(place_ref, mains, near_ref, far_ref)
+    for s in range(2):
         for p in range(2):
             for b in range(4):
                 main = 0.0
@@ -160,10 +157,10 @@
                 four = two + pltpu.roll(two, size - 2, axis)
                 eight = four + pltpu.roll(four, size - 4, axis)
                 field = pltpu.roll(eight, 4, axis) + pltpu.roll(field, size - 4, axis)
-            gain = main_ref[s, 0, 96:97, 192 + 32 * p : 193 + 32 * p]
-            logit_ref[2 * t + p] = gain * field
-
-    if first:
+            gain = mains[s][0, 96:97, 192 + 32 * p : 193 + 32 * p]
+            logit_ref[2 * s + p] = gain * field
+
+    if second:
         logits = [ref.at[i] for ref in (earlier_ref, logit_ref) for i in range(4)]
         peak = logits[0][...]
         for ref in logits[1:]:
@@ -242,19 +239,20 @@
 
 
 def pyramid_kernel(
-    sources, place_ref, main_ref, near_ref, far_ref, d1_ref, d2_ref, u2_ref, u1_ref,
+    place_ref, main_a_ref, main_b_ref, near_ref, far_ref, d1_ref, d2_ref, u2_ref, u1_ref,
     detail0_ref, detail1_ref, l2_ref, x_ref, s1_ref, l1_ref, s2_ref, s3_ref, s4_ref,
 ):
     strip = place_ref[0]
     v1 = down_rows(32, 64, 1, strip * 16 - 8, 512)
     v2, p2, p1 = row_matrices(strip)
     inside1, inside2 = level_masks(192, 96, place_ref[1])
-    strips = Strips(sources[0], place_ref, main_ref, near_ref, far_ref)
-    for i, s in enumerate(sources):
+    mains = (main_a_ref, main_b_ref)
+    strips = Strips(place_ref, mains, near_ref, far_ref)
+    for i in range(2):
         for a in range(6):
             for b in range(4):
-                x_ref[16 * b : 16 * b + 16, 0:M0] = strips.samples(s, b, a).astype(BF)
-                x_ref[16 * b : 16 * b + 16, M0:W0] = strips.halo(s, b, a).astype(BF)
+                x_ref[16 * b : 16 * b + 16, 0:M0] = strips.samples(i, b, a).astype(BF)
+                x_ref[16 * b : 16 * b + 16, M0:W0] = strips.halo(i, b, a).astype(BF)
             put(s1_ref, 6, a, 32, dot(v1, x_ref[...]))
         l1_ref[...] = jnp.where(inside1, resampled(s1_ref, d1_ref), 0.0)
         for a in range(6):
@@ -271,7 +269,7 @@
             for h in range(2):
                 at = a * 32 + 16 * h
                 detail0_ref[i * 192 + at : i * 192 + at + 16] = (
-                    main_ref[s, h, 16 * a : 16 * a + 16, :] - part[at : at + 16]
+                    mains[i][h, 16 * a : 16 * a + 16, :] - part[at : at + 16]
                 )
 
 
@@ -341,14 +339,15 @@
     return [pl.BlockSpec(memory_space=pltpu.SMEM)]
 
 
-def neighbours(halves, core):
+def neighbours(group, core):
     count = lax.axis_size(ROWS)
     swaps = [(i, i + 1) for i in range(1, count - 1, 2)]
     swaps += [(b, a) for a, b in swaps]
-    pick = functools.partial(lax.dynamic_index_in_dim, halves, axis=1, keepdims=False)
-    near = lax.ppermute(pick(1 - core), "c", [(0, 1), (1, 0)])
-    far = pick(core)
-    return near, lax.ppermute(far[:2], ROWS, swaps), lax.ppermute(far[2:], ROWS, swaps)
+
+    def half(index):
+        return jnp.stack([lax.dynamic_index_in_dim(main, index, axis=0, keepdims=False) for main in group])
+
+    return lax.ppermute(half(1 - core), "c", [(0, 1), (1, 0)]), lax.ppermute(half(core), ROWS, swaps)
 
 
 def partner(value, flip):
@@ -370,40 +369,41 @@
     )
     packed = pl.pallas_call(
         pack_kernel,
-        out_shape=jax.ShapeDtypeStruct((4, 2, 104, 512), F32),
+        out_shape=(jax.ShapeDtypeStruct((2, 104, 512), F32),) * 4,
         in_specs=[pl.BlockSpec(memory_space=pltpu.HBM)] * 2,
-        out_specs=pl.BlockSpec(memory_space=pltpu.HBM),
+        out_specs=(pl.BlockSpec(memory_space=pltpu.HBM),) * 4,
         scratch_shapes=[
             pltpu.VMEM((6, 32, 2048), jnp.int32),
             pltpu.SMEM((2,), F32),
             pltpu.VMEM((4, 2, 104, 512), F32),
             pltpu.SemaphoreType.DMA((6,)),
             pltpu.SemaphoreType.DMA,
-            pltpu.SemaphoreType.DMA((7,)),
+            pltpu.SemaphoreType.DMA((4,)),
         ],
         compiler_params=pltpu.CompilerParams(vmem_limit_bytes=60 * 1024 * 1024),
         name="pack",
     )(samples, gain)
-    main = lax.all_to_all(packed, "x", 0, 0)
-    main, strip, column, core = lax.optimization_barrier((main, strip, column, core))
-    near, *far = neighbours(main, core)
+    mains = [packed[0]] + [
+        lax.ppermute(packed[m], "x", [(i, i ^ FLIPS[m]) for i in range(4)]) for m in (1, 2, 3)
+    ]
     place = jnp.stack([strip, column, core]).astype(jnp.int32)
+    groups = [(*pair, *neighbours(pair, core)) for pair in (mains[:2], mains[2:])]
     logit_shape = jax.ShapeDtypeStruct((4, 64, W0), F32)
 
-    def energy(first, *earlier):
+    def energy(step, *earlier):
         return pl.pallas_call(
-            functools.partial(energy_kernel, first),
-            out_shape=(logit_shape,) + (jax.ShapeDtypeStruct((56, W0), F32),) * len(earlier),
-            in_specs=smem() + vmem(3 + len(earlier)),
-            out_specs=tuple(vmem(1 + len(earlier))),
+            functools.partial(energy_kernel, step == 1),
+            out_shape=(logit_shape,) + (jax.ShapeDtypeStruct((56, W0), F32),) * step,
+            in_specs=smem() + vmem(4 + step),
+            out_specs=tuple(vmem(1 + step)),
             scratch_shapes=[pltpu.VMEM((64, W0), F32)],
             compiler_params=PARAMS,
             cost_estimate=pl.CostEstimate(flops=2_000_000_000, bytes_accessed=6_000_000, transcendentals=0),
             name="energy",
-        )(place, main, near, far[first // 2], *earlier)
+        )(place, *groups[step], *earlier)
 
     logits = energy(0)
-    *more, lse = energy(2, *logits)
+    *more, lse = energy(1, *logits)
     logits = [*logits, *more]
 
     taps = [
@@ -419,13 +419,13 @@
     for step, flips in enumerate(((1, 3), (3, 1))):
         other = crossed(lse, flips)
         detail = pl.pallas_call(
-            functools.partial(pyramid_kernel, (2 * step, 2 * step + 1)),
+            pyramid_kernel,
             out_shape=(
                 jax.ShapeDtypeStruct((384, M0), F32),
                 jax.ShapeDtypeStruct((384, W1), F32),
                 jax.ShapeDtypeStruct((192, W2), F32),
             ),
-            in_specs=smem() + vmem(7),
+            in_specs=smem() + vmem(8),
             out_specs=tuple(vmem(3)),
             scratch_shapes=[
                 pltpu.VMEM((64, W0), BF),
@@ -438,7 +438,7 @@
             compiler_params=PARAMS,
             cost_estimate=pl.CostEstimate(flops=2_000_000_000, bytes_accessed=6_000_000, transcendentals=0),
             name="pyramid",
-        )(place, main, near, far[step], *taps)
+        )(place, *groups[step], *taps)
         other, *detail = lax.optimization_barrier((other, *detail))
         details += detail
         lse = join_lse(lse, other)

time: 136 us -> 131 us (0.963)
  blocking collectives: 38.3 us -> 12.7 us
  starting transfers between devices: 52.2 us -> 63.2 us
  waiting for transfers between devices: 24 us -> 32.7 us
    all_to_all x1 -> x0, blocking collectives: 26.4 us -> none  [on_device(): main = lax.all_to_all(packed, 'x', 0, 0)]
    ppermute x3 -> x7, starting transfers between devices: 7.48 us -> 19.4 us  [the longest x3 9.96 us: on_device(): lax.ppermute(packed[m], 'x', [(i, i ^ FLIPS[m]) for i in range(4)])]
    ppermute x3 -> x7, waiting for transfers between devices: 5.38 us -> 14.7 us  [the longest x3 11.1 us: on_device(): lax.ppermute(packed[m], 'x', [(i, i ^ FLIPS[m]) for i in range(4)])]
  transfers between devices with their start and end apart: 9 -> 13, of which waited for: 5 -> 8; matrix products, arithmetic and copies ran while one was open for 0% -> 1% of each run, Pallas kernels for 7% -> 8%
where the time goes in v8:
time: 131 us; the launch traced here: 130 us
  starting transfers between devices  63.2 us (48%)
  waiting for transfers between devices  32.7 us (25%)
  Pallas kernels  18.7 us (14%)
  blocking collectives  12.7 us (10%)
  local copies, waits for them, and re-layouts  2.23 us (2%)
    ppermute x4, starting transfers between devices, partner(): return lax.ppermute(value, 'zh', [(i, i ^ flip) for i in range(4)])  26 us
    ppermute x2, starting transfers between devices, crossed(): return lax.ppermute(value, ('c', 'zh'), pairs)  17.7 us
    ppermute x4, waiting for transfers between devices, partner(): return lax.ppermute(value, 'zh', [(i, i ^ flip) for i in range(4)])  13.3 us
    all_to_all x1, blocking collectives, on_device(): joined = lax.all_to_all(jnp.broadcast_to(whole, (4, 3, 32, 512)), 'x', 0, 0)  12.7 us
    ppermute x3, waiting for transfers between devices, on_device(): lax.ppermute(packed[m], 'x', [(i, i ^ FLIPS[m]) for i in range(4)])  11.1 us
    ppermute x3, starting transfers between devices, on_device(): lax.ppermute(packed[m], 'x', [(i, i ^ FLIPS[m]) for i in range(4)])  9.96 us
    pallas_call x2, Pallas kernels, on_device(): pl.pallas_call(pyramid_kernel, out_shape=(jax.ShapeDtypeStruct((384, M0),...  7.05 us
    pallas_call x2, Pallas kernels, energy(): pl.pallas_call(functools.partial(energy_kernel, step == 1), out_shape=(lo...  6.14 us
  transfers between devices with their start and end apart: 13, of which 8 were waited for; matrix products, arithmetic and copies ran while one was open for 1% of the time, Pallas kernels for 8%

profile of v8, /device:TPU:24, one launch (start us, length us, event | category | flops | bytes accessed | tf_op | source)
XLA Modules:
  0.0 130.2 jit_solution(3357970004689254259)
XLA Ops:
  0.0 2.8 %pack.1 = (f32[2,104,512]{2,1,0:T(8,128)}, f32[2,104,512]{2,1,0:T(8,128)}, f32[2,104,512]{2,1,0:T(8,128)}, f32[2,104,512]{2,1,0:T(8,128)}) custom-call(s32[2,3,32,2048]{3,2,1,0:T(8,128)} %samples_ref, f32[2]{0:T(128)} %gain_hbm_ref.1), custom_call_target="tpu_custom_call" | custom-call | tf_op jit(solution)/shard_map/pack/pallas_call | solution.py:370
  2.8 3.4 %collective-permute-start = (f32[2,104,512]{2,1,0:T(8,128)}, f32[2,104,512]{2,1,0:T(8,128)S(1)}, u32[]{:S(2)}, u32[]{:S(2)}) collective-permute-start(f32[2,104,512]{2,1,0:T(8,128)} %get-tuple-element.36), channel_id=1, source_target_pairs={{0,1},{1,0},{2,3},{3,2},{4,5},{5,4},{6,7},{7,6},{8,9},{9,8},{10,11... | collective-permute-start | bytes 1277960 | tf_op jit(solution)/shard_map/ppermute | solution.py:387
  6.2 4.0 %collective-permute-start.3 = (f32[2,104,512]{2,1,0:T(8,128)}, f32[2,104,512]{2,1,0:T(8,128)S(1)}, u32[]{:S(2)}, u32[]{:S(2)}) collective-permute-start(f32[2,104,512]{2,1,0:T(8,128)} %get-tuple-element.37), channel_id=1, source_target_pairs={{0,3},{1,2},{2,1},{3,0},{4,7},{5,6},{6,5},{7,4},{8,11},{9,10},{10,... | collective-permute-start | bytes 1277960 | tf_op jit(solution)/shard_map/ppermute | solution.py:387
  10.2 2.6 %collective-permute-start.4 = (f32[2,104,512]{2,1,0:T(8,128)}, f32[2,104,512]{2,1,0:T(8,128)S(1)}, u32[]{:S(2)}, u32[]{:S(2)}) collective-permute-start(f32[2,104,512]{2,1,0:T(8,128)} %get-tuple-element.38), channel_id=1, source_target_pairs={{0,2},{1,3},{2,0},{3,1},{4,6},{5,7},{6,4},{7,5},{8,10},{9,11},{10,... | collective-permute-start | bytes 1277960 | tf_op jit(solution)/shard_map/ppermute | solution.py:387
  13.8 3.8 %collective-permute-done.main_b_ref = f32[2,104,512]{2,1,0:T(8,128)S(1)} collective-permute-done((f32[2,104,512]{2,1,0:T(8,128)}, f32[2,104,512]{2,1,0:T(8,128)S(1)}, u32[]{:S(2)}, u32[]{:S(2)}) %collective-permute-start) | collective-permute-done | bytes 426016 | tf_op jit(solution)/shard_map/ppermute | solution.py:387
  19.6 2.9 %collective-permute-start.2 = (f32[2,104,512]{2,1,0:T(8,128)S(1)}, f32[2,104,512]{2,1,0:T(8,128)S(1)}, u32[]{:S(2)}, u32[]{:S(2)}) collective-permute-start(f32[2,104,512]{2,1,0:T(8,128)S(1)} %pad_maximum_fusion.1), channel_id=1, source_target_pairs={{16,32},{48,64},{80,96},{112,128},{144,160},{176,192},{208,224},{2... | collective-permute-start | bytes 1277960 | tf_op jit(solution)/shard_map/ppermute | solution.py:350
  22.5 7.4 %collective-permute-done.3.main_a_ref = f32[2,104,512]{2,1,0:T(8,128)S(1)} collective-permute-done((f32[2,104,512]{2,1,0:T(8,128)}, f32[2,104,512]{2,1,0:T(8,128)S(1)}, u32[]{:S(2)}, u32[]{:S(2)}) %collective-permute-start.3) | collective-permute-done | bytes 426016 | tf_op jit(solution)/shard_map/ppermute | solution.py:387
  32.0 2.8 %collective-permute-start.6 = (f32[2,104,512]{2,1,0:T(8,128)S(1)}, f32[2,104,512]{2,1,0:T(8,128)S(1)}, u32[]{:S(2)}, u32[]{:S(2)}) collective-permute-start(f32[2,104,512]{2,1,0:T(8,128)S(1)} %pad_maximum_fusion.3), channel_id=1, source_target_pairs={{16,32},{48,64},{80,96},{112,128},{144,160},{176,192},{208,224},{2... | collective-permute-start | bytes 1277960 | tf_op jit(solution)/shard_map/ppermute | solution.py:350
  34.9 2.9 %energy.2.refs_0_.logit_a_ref = f32[4,64,640]{2,1,0:T(8,128)S(1)} custom-call(s32[3]{0:T(128)S(1)} %pad_add_fusion.place_ref, f32[2,104,512]{2,1,0:T(8,128)S(1)} %copy-done.1, f32[2,104,512]{2,1,0:T(8,128)S(1)} %collective-permute-done.main_b_ref, f32[2,104,512]{2,1,0:T(8,128)S(1)} %collective-permute-done.1.near_ref, ...), custom_call_target="tpu_custom_call" | custom-call | flops 2000000000 | bytes 6000000 | tf_op jit(solution)/shard_map/energy/pallas_call | solution.py:394
  37.8 3.6 %collective-permute-done.6.far_ref = f32[2,104,512]{2,1,0:T(8,128)S(1)} collective-permute-done((f32[2,104,512]{2,1,0:T(8,128)S(1)}, f32[2,104,512]{2,1,0:T(8,128)S(1)}, u32[]{:S(2)}, u32[]{:S(2)}) %collective-permute-start.6) | collective-permute-done | bytes 426016 | tf_op jit(solution)/shard_map/ppermute | solution.py:350
  41.4 3.2 %energy.3 = (f32[4,64,640]{2,1,0:T(8,128)S(1)}, f32[56,640]{1,0:T(8,128)S(1)}) custom-call(s32[3]{0:T(128)S(1)} %pad_add_fusion.place_ref, f32[2,104,512]{2,1,0:T(8,128)S(1)} %collective-permute-done.3.main_a_ref, f32[2,104,512]{2,1,0:T(8,128)S(1)} %collective-permute-done.4.main_b_ref, f32[2,104,512]{2,1,0:T(8,128)S(1)} %collective-permute-done.5.near_ref, ...), custom_call_target="tpu_custom_call" | custom-call | flops 2000000000 | bytes 6000000 | tf_op jit(solution)/shard_map/energy/pallas_call | solution.py:394
  44.7 9.1 %collective-permute-start.7 = (f32[56,640]{1,0:T(8,128)S(1)}, f32[56,640]{1,0:T(8,128)S(1)}, u32[]{:S(2)}, u32[]{:S(2)}) collective-permute-start(f32[56,640]{1,0:T(8,128)S(1)} %get-tuple-element.40), channel_id=1, source_target_pairs={{0,4},{4,0},{8,12},{12,8},{16,28},{20,24},{24,20},{28,16},{1,5},{5... | collective-permute-start | bytes 430088 | tf_op jit(solution)/shard_map/ppermute | solution.py:359
  53.8 3.5 %pyramid.2 = (f32[384,512]{1,0:T(8,128)S(1)}, f32[384,384]{1,0:T(8,128)S(1)}, f32[192,256]{1,0:T(8,128)S(1)}) custom-call(s32[3]{0:T(128)S(1)} %pad_add_fusion.place_ref, f32[2,104,512]{2,1,0:T(8,128)S(1)} %copy-done.1, f32[2,104,512]{2,1,0:T(8,128)S(1)} %collective-permute-done.main_b_ref, f32[2,104,512]{2,1,0:T(8,128)S(1)} %collective-permute-done.1.near_ref, ...), custom_call_target="tpu_custom_call" | custom-call | flops 2000000000 | bytes 6000000 | tf_op jit(solution)/shard_map/pyramid/pallas_call | solution.py:421
  57.4 4.1 %collective-permute-done.7 = f32[56,640]{1,0:T(8,128)S(1)} collective-permute-done((f32[56,640]{1,0:T(8,128)S(1)}, f32[56,640]{1,0:T(8,128)S(1)}, u32[]{:S(2)}, u32[]{:S(2)}) %collective-permute-start.7) | collective-permute-done | bytes 143392 | tf_op jit(solution)/shard_map/ppermute | solution.py:359
  61.5 8.6 %collective-permute-start.8 = (f32[56,640]{1,0:T(8,128)S(1)}, f32[56,640]{1,0:T(8,128)S(1)}, u32[]{:S(2)}, u32[]{:S(2)}) collective-permute-start(f32[56,640]{1,0:T(8,128)S(1)} %log_add_fusion.1), channel_id=1, source_target_pairs={{0,12},{4,8},{8,4},{12,0},{16,20},{20,16},{24,28},{28,24},{1,13},{... | collective-permute-start | bytes 430088 | tf_op jit(solution)/shard_map/ppermute | solution.py:359
  70.2 3.5 %pyramid.3 = (f32[384,512]{1,0:T(8,128)S(1)}, f32[384,384]{1,0:T(8,128)S(1)}, f32[192,256]{1,0:T(8,128)S(1)}) custom-call(s32[3]{0:T(128)S(1)} %pad_add_fusion.place_ref, f32[2,104,512]{2,1,0:T(8,128)S(1)} %collective-permute-done.3.main_a_ref, f32[2,104,512]{2,1,0:T(8,128)S(1)} %collective-permute-done.4.main_b_ref, ...), custom_call_target="tpu_custom_call" | custom-call | flops 2000000000 | bytes 6000000 | tf_op jit(solution)/shard_map/pyramid/pallas_call | solution.py:421
  74.3 2.7 %mix.1 = (f32[3,32,256]{2,1,0:T(8,128)S(1)}, f32[3,32,256]{2,1,0:T(8,128)S(1)}) custom-call(s32[3]{0:T(128)S(1)} %pad_add_fusion.place_ref, f32[4,64,640]{2,1,0:T(8,128)S(1)} %energy.2.refs_0_.logit_a_ref, f32[4,64,640]{2,1,0:T(8,128)S(1)} %get-tuple-element.39.logit_b_ref, f32[56,640]{1,0:T(8,128)S(1)} %log_add_fusion.lse_ref, ...), custom_call_target="tpu_custom_call" | custom-call | tf_op jit(solution)/shard_map/mix/pallas_call | solution.py:446
  77.0 10.0 %collective-permute-start.9 = (f32[3,32,256]{2,1,0:T(8,128)S(1)}, f32[3,32,256]{2,1,0:T(8,128)S(1)}, u32[]{:S(2)}, u32[]{:S(2)}) collective-permute-start(f32[3,32,256]{2,1,0:T(8,128)S(1)} %get-tuple-element.55), channel_id=1, source_target_pairs={{0,4},{4,0},{8,12},{12,8},{1,5},{5,1},{9,13},{13,9},{2,6},{6,2},{1... | collective-permute-start | bytes 294920 | tf_op jit(solution)/shard_map/ppermute | solution.py:354
  87.1 7.6 %collective-permute-start.11 = (f32[3,32,256]{2,1,0:T(8,128)S(1)}, f32[3,32,256]{2,1,0:T(8,128)S(1)}, u32[]{:S(2)}, u32[]{:S(2)}) collective-permute-start(f32[3,32,256]{2,1,0:T(8,128)S(1)} %get-tuple-element.56), channel_id=1, source_target_pairs={{0,12},{4,8},{8,4},{12,0},{1,13},{5,9},{9,5},{13,1},{2,14},{6,10},... | collective-permute-start | bytes 294920 | tf_op jit(solution)/shard_map/ppermute | solution.py:354
  95.5 4.2 %collective-permute-start.10 = (f32[3,32,256]{2,1,0:T(8,128)S(1)}, f32[3,32,256]{2,1,0:T(8,128)S(1)}, u32[]{:S(2)}, u32[]{:S(2)}) collective-permute-start(f32[3,32,256]{2,1,0:T(8,128)S(1)} %add.52), channel_id=1, source_target_pairs={{0,12},{4,8},{8,4},{12,0},{1,13},{5,9},{9,5},{13,1},{2,14},{6,10},... | collective-permute-start | bytes 294920 | tf_op jit(solution)/shard_map/ppermute | solution.py:354
  99.8 3.4 %collective-permute-done.11 = f32[3,32,256]{2,1,0:T(8,128)S(1)} collective-permute-done((f32[3,32,256]{2,1,0:T(8,128)S(1)}, f32[3,32,256]{2,1,0:T(8,128)S(1)}, u32[]{:S(2)}, u32[]{:S(2)}) %collective-permute-start.11) | collective-permute-done | bytes 98336 | tf_op jit(solution)/shard_map/ppermute | solution.py:354
  103.2 4.1 %collective-permute-start.12 = (f32[3,32,256]{2,1,0:T(8,128)S(1)}, f32[3,32,256]{2,1,0:T(8,128)S(1)}, u32[]{:S(2)}, u32[]{:S(2)}) collective-permute-start(f32[3,32,256]{2,1,0:T(8,128)S(1)} %add.54), channel_id=1, source_target_pairs={{0,4},{4,0},{8,12},{12,8},{1,5},{5,1},{9,13},{13,9},{2,6},{6,2},{1... | collective-permute-start | bytes 294920 | tf_op jit(solution)/shard_map/ppermute | solution.py:354
  107.4 9.1 %collective-permute-done.12 = f32[3,32,256]{2,1,0:T(8,128)S(1)} collective-permute-done((f32[3,32,256]{2,1,0:T(8,128)S(1)}, f32[3,32,256]{2,1,0:T(8,128)S(1)}, u32[]{:S(2)}, u32[]{:S(2)}) %collective-permute-start.12) | collective-permute-done | bytes 98336 | tf_op jit(solution)/shard_map/ppermute | solution.py:354
  116.6 12.7 %all_to_all.5 = f32[4,3,32,512]{3,2,1,0:T(8,128)S(1)} all-to-all(f32[4,3,32,512]{3,2,1,0:T(8,128)S(1)} %broadcast_in_dim.3), channel_id=1, replica_groups=mesh['zl'=4,'y'=4,'c'=2,'zh'=4,'x'=4] {'x'}, dimensions={0} | all-to-all | bytes 1572864 | tf_op jit(solution)/shard_map/all_to_all | solution.py:467
  (37 shorter events, 7.8 us)
Async XLA Ops:
  2.8 14.8 %collective-permute-start = (f32[2,104,512]{2,1,0:T(8,128)}, f32[2,104,512]{2,1,0:T(8,128)S(1)}, u32[]{:S(2)}, u32[]{:S(2)}) collective-permute-start(f32[2,104,512]{2,1,0:T(8,128)} %get-tuple-element.36), channel_id=1, source_target_pairs={{0,1},{1,0},{2,3},{3,2},{4,5},{5,4},{6,7},{7,6},{8,9},{9,8},{10,11... | collective-permute-start | bytes 1277960 | tf_op jit(solution)/shard_map/ppermute | solution.py:387
  6.2 23.7 %collective-permute-start.3 = (f32[2,104,512]{2,1,0:T(8,128)}, f32[2,104,512]{2,1,0:T(8,128)S(1)}, u32[]{:S(2)}, u32[]{:S(2)}) collective-permute-start(f32[2,104,512]{2,1,0:T(8,128)} %get-tuple-element.37), channel_id=1, source_target_pairs={{0,3},{1,2},{2,1},{3,0},{4,7},{5,6},{6,5},{7,4},{8,11},{9,10},{10,... | collective-permute-start | bytes 1277960 | tf_op jit(solution)/shard_map/ppermute | solution.py:387
  10.2 19.7 %collective-permute-start.4 = (f32[2,104,512]{2,1,0:T(8,128)}, f32[2,104,512]{2,1,0:T(8,128)S(1)}, u32[]{:S(2)}, u32[]{:S(2)}) collective-permute-start(f32[2,104,512]{2,1,0:T(8,128)} %get-tuple-element.38), channel_id=1, source_target_pairs={{0,2},{1,3},{2,0},{3,1},{4,6},{5,7},{6,4},{7,5},{8,10},{9,11},{10,... | collective-permute-start | bytes 1277960 | tf_op jit(solution)/shard_map/ppermute | solution.py:387
  17.7 17.2 %collective-permute-start.1 = (f32[2,104,512]{2,1,0:T(8,128)S(1)}, f32[2,104,512]{2,1,0:T(8,128)S(1)}, u32[]{:S(2)}, u32[]{:S(2)}) collective-permute-start(f32[2,104,512]{2,1,0:T(8,128)S(1)} %pad_maximum_fusion), channel_id=1, source_target_pairs={{0,16},{16,0},{1,17},{17,1},{2,18},{18,2},{3,19},{19,3},{4,20},{20... | collective-permute-start | bytes 1277960 | tf_op jit(solution)/shard_map/ppermute | solution.py:350
  19.6 15.2 %copy-start.1 = (f32[2,104,512]{2,1,0:T(8,128)S(1)}, f32[2,104,512]{2,1,0:T(8,128)}, u32[]{:S(2)}) copy-start(f32[2,104,512]{2,1,0:T(8,128)} %get-tuple-element.35.main_a_ref) | copy-start | bytes 1277956
  19.6 15.2 %collective-permute-start.2 = (f32[2,104,512]{2,1,0:T(8,128)S(1)}, f32[2,104,512]{2,1,0:T(8,128)S(1)}, u32[]{:S(2)}, u32[]{:S(2)}) collective-permute-start(f32[2,104,512]{2,1,0:T(8,128)S(1)} %pad_maximum_fusion.1), channel_id=1, source_target_pairs={{16,32},{48,64},{80,96},{112,128},{144,160},{176,192},{208,224},{2... | collective-permute-start | bytes 1277960 | tf_op jit(solution)/shard_map/ppermute | solution.py:350
  30.0 7.8 %collective-permute-start.5 = (f32[2,104,512]{2,1,0:T(8,128)S(1)}, f32[2,104,512]{2,1,0:T(8,128)S(1)}, u32[]{:S(2)}, u32[]{:S(2)}) collective-permute-start(f32[2,104,512]{2,1,0:T(8,128)S(1)} %pad_maximum_fusion.2), channel_id=1, source_target_pairs={{0,16},{16,0},{1,17},{17,1},{2,18},{18,2},{3,19},{19,3},{4,20},{20... | collective-permute-start | bytes 1277960 | tf_op jit(solution)/shard_map/ppermute | solution.py:350
  32.0 9.4 %collective-permute-start.6 = (f32[2,104,512]{2,1,0:T(8,128)S(1)}, f32[2,104,512]{2,1,0:T(8,128)S(1)}, u32[]{:S(2)}, u32[]{:S(2)}) collective-permute-start(f32[2,104,512]{2,1,0:T(8,128)S(1)} %pad_maximum_fusion.3), channel_id=1, source_target_pairs={{16,32},{48,64},{80,96},{112,128},{144,160},{176,192},{208,224},{2... | collective-permute-start | bytes 1277960 | tf_op jit(solution)/shard_map/ppermute | solution.py:350
  37.8 16.0 %copy-start = (bf16[640,384]{1,0:T(8,128)(2,1)S(1)}, bf16[640,384]{1,0:T(8,128)(2,1)}, u32[]{:S(2)}) copy-start(bf16[640,384]{1,0:T(8,128)(2,1)} %constant.55.clone.d1_ref) | copy-start | bytes 1474564
  37.8 16.0 %copy-start.2 = (bf16[384,512]{1,0:T(8,128)(2,1)S(1)}, bf16[384,512]{1,0:T(8,128)(2,1)}, u32[]{:S(2)}) copy-start(bf16[384,512]{1,0:T(8,128)(2,1)} %constant.58.clone.u1_ref) | copy-start | bytes 1179652
  37.8 16.0 %copy-start.3 = (bf16[256,384]{1,0:T(8,128)(2,1)S(1)}, bf16[256,384]{1,0:T(8,128)(2,1)}, u32[]{:S(2)}) copy-start(bf16[256,384]{1,0:T(8,128)(2,1)} %constant.57.clone.u2_ref) | copy-start | bytes 589828
  37.8 16.0 %copy-start.4 = (bf16[384,256]{1,0:T(8,128)(2,1)S(1)}, bf16[384,256]{1,0:T(8,128)(2,1)}, u32[]{:S(2)}) copy-start(bf16[384,256]{1,0:T(8,128)(2,1)} %constant.56.clone.d2_ref) | copy-start | bytes 589828
  44.7 16.8 %collective-permute-start.7 = (f32[56,640]{1,0:T(8,128)S(1)}, f32[56,640]{1,0:T(8,128)S(1)}, u32[]{:S(2)}, u32[]{:S(2)}) collective-permute-start(f32[56,640]{1,0:T(8,128)S(1)} %get-tuple-element.40), channel_id=1, source_target_pairs={{0,4},{4,0},{8,12},{12,8},{16,28},{20,24},{24,20},{28,16},{1,5},{5... | collective-permute-start | bytes 430088 | tf_op jit(solution)/shard_map/ppermute | solution.py:359
  61.5 12.7 %collective-permute-start.8 = (f32[56,640]{1,0:T(8,128)S(1)}, f32[56,640]{1,0:T(8,128)S(1)}, u32[]{:S(2)}, u32[]{:S(2)}) collective-permute-start(f32[56,640]{1,0:T(8,128)S(1)} %log_add_fusion.1), channel_id=1, source_target_pairs={{0,12},{4,8},{8,4},{12,0},{16,20},{20,16},{24,28},{28,24},{1,13},{... | collective-permute-start | bytes 430088 | tf_op jit(solution)/shard_map/ppermute | solution.py:359
  77.0 18.5 %collective-permute-start.9 = (f32[3,32,256]{2,1,0:T(8,128)S(1)}, f32[3,32,256]{2,1,0:T(8,128)S(1)}, u32[]{:S(2)}, u32[]{:S(2)}) collective-permute-start(f32[3,32,256]{2,1,0:T(8,128)S(1)} %get-tuple-element.55), channel_id=1, source_target_pairs={{0,4},{4,0},{8,12},{12,8},{1,5},{5,1},{9,13},{13,9},{2,6},{6,2},{1... | collective-permute-start | bytes 294920 | tf_op jit(solution)/shard_map/ppermute | solution.py:354
  87.1 16.1 %collective-permute-start.11 = (f32[3,32,256]{2,1,0:T(8,128)S(1)}, f32[3,32,256]{2,1,0:T(8,128)S(1)}, u32[]{:S(2)}, u32[]{:S(2)}) collective-permute-start(f32[3,32,256]{2,1,0:T(8,128)S(1)} %get-tuple-element.56), channel_id=1, source_target_pairs={{0,12},{4,8},{8,4},{12,0},{1,13},{5,9},{9,5},{13,1},{2,14},{6,10},... | collective-permute-start | bytes 294920 | tf_op jit(solution)/shard_map/ppermute | solution.py:354
  95.5 11.8 %collective-permute-start.10 = (f32[3,32,256]{2,1,0:T(8,128)S(1)}, f32[3,32,256]{2,1,0:T(8,128)S(1)}, u32[]{:S(2)}, u32[]{:S(2)}) collective-permute-start(f32[3,32,256]{2,1,0:T(8,128)S(1)} %add.52), channel_id=1, source_target_pairs={{0,12},{4,8},{8,4},{12,0},{1,13},{5,9},{9,5},{13,1},{2,14},{6,10},... | collective-permute-start | bytes 294920 | tf_op jit(solution)/shard_map/ppermute | solution.py:354
  103.2 13.3 %collective-permute-start.12 = (f32[3,32,256]{2,1,0:T(8,128)S(1)}, f32[3,32,256]{2,1,0:T(8,128)S(1)}, u32[]{:S(2)}, u32[]{:S(2)}) collective-permute-start(f32[3,32,256]{2,1,0:T(8,128)S(1)} %add.54), channel_id=1, source_target_pairs={{0,4},{4,0},{8,12},{12,8},{1,5},{5,1},{9,13},{13,9},{2,6},{6,2},{1... | collective-permute-start | bytes 294920 | tf_op jit(solution)/shard_map/ppermute | solution.py:354

commit v9 on v8

--- a/solution.py
+++ b/solution.py
@@ -277,7 +277,7 @@
     place_ref, logit_a_ref, logit_b_ref, lse_ref,
     fine_a_ref, mid_a_ref, low_a_ref, fine_b_ref, mid_b_ref, low_b_ref,
     d1_ref, d2_ref, u2_ref, u1_ref,
-    left_ref, right_ref, w0_ref, s1_ref, w1_ref, s2_ref, s3_ref, s4_ref,
+    out_ref, w0_ref, s1_ref, w1_ref, s2_ref, s3_ref, s4_ref,
 ):
     strip, k = place_ref[0], place_ref[1]
     v1 = down_rows(32, 64, 2, strip * 16 - 8, 512)
@@ -326,9 +326,7 @@
         total = rise[c * 32 : c * 32 + 32]
         for i in range(8):
             total = total + w0_ref[i, 16:48, 0:M0] * piece((fine_a_ref, fine_b_ref), i, c, 32)
-        total = total * (1.0 / 255.0)
-        left_ref[c] = total[:, :256]
-        right_ref[c] = total[:, 256:]
+        out_ref[c] = total * (1.0 / 255.0)
 
 
 def vmem(count):
@@ -350,13 +348,9 @@
     return lax.ppermute(half(1 - core), "c", [(0, 1), (1, 0)]), lax.ppermute(half(core), ROWS, swaps)
 
 
-def partner(value, flip):
-    return lax.ppermute(value, "zh", [(i, i ^ flip) for i in range(4)])
-
-
 def crossed(value, flips):
-    pairs = [(4 * c + i, 4 * c + (i ^ flip)) for c, flip in enumerate(flips) for i in range(4)]
-    return lax.ppermute(value, ("c", "zh"), pairs)
+    pairs = [(4 * low + i, 4 * low + (i ^ flips[low % 2])) for low in range(4) for i in range(4)]
+    return lax.ppermute(value, ("zl", "zh"), pairs)
 
 
 def join_lse(a, b):
@@ -443,11 +437,11 @@
         details += detail
         lse = join_lse(lse, other)
 
-    left, right = pl.pallas_call(
+    whole = pl.pallas_call(
         mix_kernel,
-        out_shape=(jax.ShapeDtypeStruct((3, 32, 256), F32),) * 2,
+        out_shape=jax.ShapeDtypeStruct((3, 32, M0), F32),
         in_specs=smem() + vmem(13),
-        out_specs=tuple(vmem(2)),
+        out_specs=vmem(1)[0],
         scratch_shapes=[
             pltpu.VMEM((8, 64, W0), F32),
             pltpu.VMEM((512, W0), BF),
@@ -460,10 +454,8 @@
         name="mix",
     )(place, *logits, lse, *details, *taps)
 
-    for a, b in ((1, 3), (3, 1)):
-        left_in, right_in = partner(left, a), partner(right, b)
-        left, right = left + left_in, right + right_in
-    whole = jnp.concatenate([left, right], axis=-1)
+    for flips in ((1, 3), (3, 1)):
+        whole = whole + crossed(whole, flips)
     joined = lax.all_to_all(jnp.broadcast_to(whole, (4, 3, 32, 512)), "x", 0, 0)
     return joined.transpose(1, 2, 0, 3).reshape(3, 32, 2048)
 

time: 131 us -> 142 us (1.084)
  the two profiles are of different devices: /device:TPU:24 before, /device:TPU:16 now
where the time goes in v9:
time: 142 us
  starting transfers between devices  52.2 us (37%)
  waiting for transfers between devices  52 us (37%)
  Pallas kernels  18.7 us (13%)
  blocking collectives  15.7 us (11%)
  local copies, waits for them, and re-layouts  2.23 us (2%)
    ppermute x4, waiting for transfers between devices, crossed(): return lax.ppermute(value, ('zl', 'zh'), pairs)  36.7 us
    ppermute x4, starting transfers between devices, crossed(): return lax.ppermute(value, ('zl', 'zh'), pairs)  33.4 us
    all_to_all x1, blocking collectives, on_device(): joined = lax.all_to_all(jnp.broadcast_to(whole, (4, 3, 32, 512)), 'x', 0, 0)  15.7 us
    ppermute x3, waiting for transfers between devices, on_device(): lax.ppermute(packed[m], 'x', [(i, i ^ FLIPS[m]) for i in range(4)])  11.4 us
    ppermute x3, starting transfers between devices, on_device(): lax.ppermute(packed[m], 'x', [(i, i ^ FLIPS[m]) for i in range(4)])  9.96 us
    pallas_call x2, Pallas kernels, on_device(): pl.pallas_call(pyramid_kernel, out_shape=(jax.ShapeDtypeStruct((384, M0),...  7.06 us
    pallas_call x2, Pallas kernels, energy(): pl.pallas_call(functools.partial(energy_kernel, step == 1), out_shape=(lo...  6.14 us
    ppermute x2, starting transfers between devices, neighbours(): lax.ppermute(half(core), ROWS, swaps)  5.05 us
  transfers between devices with their start and end apart: 11, of which 7 were waited for; matrix products, arithmetic and copies ran while one was open for 1% of the time, Pallas kernels for 7%

profile of v9, /device:TPU:16, one launch (start us, length us, event | category | flops | bytes accessed | tf_op | source)
XLA Modules:
  0.0 141.5 jit_solution(8275585502005983384)
XLA Ops:
  0.0 2.8 %pack.1 = (f32[2,104,512]{2,1,0:T(8,128)}, f32[2,104,512]{2,1,0:T(8,128)}, f32[2,104,512]{2,1,0:T(8,128)}, f32[2,104,512]{2,1,0:T(8,128)}) custom-call(s32[2,3,32,2048]{3,2,1,0:T(8,128)} %samples_ref, f32[2]{0:T(128)} %gain_hbm_ref.1), custom_call_target="tpu_custom_call" | custom-call | tf_op jit(solution)/shard_map/pack/pallas_call | solution.py:364
  2.8 3.4 %collective-permute-start = (f32[2,104,512]{2,1,0:T(8,128)}, f32[2,104,512]{2,1,0:T(8,128)S(1)}, u32[]{:S(2)}, u32[]{:S(2)}) collective-permute-start(f32[2,104,512]{2,1,0:T(8,128)} %get-tuple-element.34), channel_id=1, source_target_pairs={{0,1},{1,0},{2,3},{3,2},{4,5},{5,4},{6,7},{7,6},{8,9},{9,8},{10,11... | collective-permute-start | bytes 1277960 | tf_op jit(solution)/shard_map/ppermute | solution.py:381
  6.2 4.0 %collective-permute-start.3 = (f32[2,104,512]{2,1,0:T(8,128)}, f32[2,104,512]{2,1,0:T(8,128)S(1)}, u32[]{:S(2)}, u32[]{:S(2)}) collective-permute-start(f32[2,104,512]{2,1,0:T(8,128)} %get-tuple-element.35), channel_id=1, source_target_pairs={{0,3},{1,2},{2,1},{3,0},{4,7},{5,6},{6,5},{7,4},{8,11},{9,10},{10,... | collective-permute-start | bytes 1277960 | tf_op jit(solution)/shard_map/ppermute | solution.py:381
  10.2 2.6 %collective-permute-start.4 = (f32[2,104,512]{2,1,0:T(8,128)}, f32[2,104,512]{2,1,0:T(8,128)S(1)}, u32[]{:S(2)}, u32[]{:S(2)}) collective-permute-start(f32[2,104,512]{2,1,0:T(8,128)} %get-tuple-element.36), channel_id=1, source_target_pairs={{0,2},{1,3},{2,0},{3,1},{4,6},{5,7},{6,4},{7,5},{8,10},{9,11},{10,... | collective-permute-start | bytes 1277960 | tf_op jit(solution)/shard_map/ppermute | solution.py:381
  13.8 3.8 %collective-permute-done.main_b_ref = f32[2,104,512]{2,1,0:T(8,128)S(1)} collective-permute-done((f32[2,104,512]{2,1,0:T(8,128)}, f32[2,104,512]{2,1,0:T(8,128)S(1)}, u32[]{:S(2)}, u32[]{:S(2)}) %collective-permute-start) | collective-permute-done | bytes 426016 | tf_op jit(solution)/shard_map/ppermute | solution.py:381
  17.7 1.9 %collective-permute-start.1 = (f32[2,104,512]{2,1,0:T(8,128)S(1)}, f32[2,104,512]{2,1,0:T(8,128)S(1)}, u32[]{:S(2)}, u32[]{:S(2)}) collective-permute-start(f32[2,104,512]{2,1,0:T(8,128)S(1)} %pad_maximum_fusion), channel_id=1, source_target_pairs={{0,16},{16,0},{1,17},{17,1},{2,18},{18,2},{3,19},{19,3},{4,20},{20... | collective-permute-start | bytes 1277960 | tf_op jit(solution)/shard_map/ppermute | solution.py:348
  19.6 2.6 %collective-permute-start.2 = (f32[2,104,512]{2,1,0:T(8,128)S(1)}, f32[2,104,512]{2,1,0:T(8,128)S(1)}, u32[]{:S(2)}, u32[]{:S(2)}) collective-permute-start(f32[2,104,512]{2,1,0:T(8,128)S(1)} %pad_maximum_fusion.1), channel_id=1, source_target_pairs={{16,32},{48,64},{80,96},{112,128},{144,160},{176,192},{208,224},{2... | collective-permute-start | bytes 1277960 | tf_op jit(solution)/shard_map/ppermute | solution.py:348
  22.2 7.7 %collective-permute-done.3.main_a_ref = f32[2,104,512]{2,1,0:T(8,128)S(1)} collective-permute-done((f32[2,104,512]{2,1,0:T(8,128)}, f32[2,104,512]{2,1,0:T(8,128)S(1)}, u32[]{:S(2)}, u32[]{:S(2)}) %collective-permute-start.3) | collective-permute-done | bytes 426016 | tf_op jit(solution)/shard_map/ppermute | solution.py:381
  32.0 2.5 %collective-permute-start.6 = (f32[2,104,512]{2,1,0:T(8,128)S(1)}, f32[2,104,512]{2,1,0:T(8,128)S(1)}, u32[]{:S(2)}, u32[]{:S(2)}) collective-permute-start(f32[2,104,512]{2,1,0:T(8,128)S(1)} %pad_maximum_fusion.3), channel_id=1, source_target_pairs={{16,32},{48,64},{80,96},{112,128},{144,160},{176,192},{208,224},{2... | collective-permute-start | bytes 1277960 | tf_op jit(solution)/shard_map/ppermute | solution.py:348
  34.6 2.9 %energy.2.refs_0_.logit_a_ref = f32[4,64,640]{2,1,0:T(8,128)S(1)} custom-call(s32[3]{0:T(128)S(1)} %pad_add_fusion.place_ref, f32[2,104,512]{2,1,0:T(8,128)S(1)} %copy-done.1, f32[2,104,512]{2,1,0:T(8,128)S(1)} %collective-permute-done.main_b_ref, f32[2,104,512]{2,1,0:T(8,128)S(1)} %collective-permute-done.1.near_ref, ...), custom_call_target="tpu_custom_call" | custom-call | flops 2000000000 | bytes 6000000 | tf_op jit(solution)/shard_map/energy/pallas_call | solution.py:388
  37.5 3.9 %collective-permute-done.6.far_ref = f32[2,104,512]{2,1,0:T(8,128)S(1)} collective-permute-done((f32[2,104,512]{2,1,0:T(8,128)S(1)}, f32[2,104,512]{2,1,0:T(8,128)S(1)}, u32[]{:S(2)}, u32[]{:S(2)}) %collective-permute-start.6) | collective-permute-done | bytes 426016 | tf_op jit(solution)/shard_map/ppermute | solution.py:348
  41.4 3.2 %energy.3 = (f32[4,64,640]{2,1,0:T(8,128)S(1)}, f32[56,640]{1,0:T(8,128)S(1)}) custom-call(s32[3]{0:T(128)S(1)} %pad_add_fusion.place_ref, f32[2,104,512]{2,1,0:T(8,128)S(1)} %collective-permute-done.3.main_a_ref, f32[2,104,512]{2,1,0:T(8,128)S(1)} %collective-permute-done.4.main_b_ref, f32[2,104,512]{2,1,0:T(8,128)S(1)} %collective-permute-done.5.near_ref, ...), custom_call_target="tpu_custom_call" | custom-call | flops 2000000000 | bytes 6000000 | tf_op jit(solution)/shard_map/energy/pallas_call | solution.py:388
  44.7 9.1 %collective-permute-start.7 = (f32[56,640]{1,0:T(8,128)S(1)}, f32[56,640]{1,0:T(8,128)S(1)}, u32[]{:S(2)}, u32[]{:S(2)}) collective-permute-start(f32[56,640]{1,0:T(8,128)S(1)} %get-tuple-element.38), channel_id=1, source_target_pairs={{0,4},{4,0},{8,12},{12,8},{128,140},{132,136},{136,132},{140,128},... | collective-permute-start | bytes 430088 | tf_op jit(solution)/shard_map/ppermute | solution.py:353
  53.8 3.5 %pyramid.2 = (f32[384,512]{1,0:T(8,128)S(1)}, f32[384,384]{1,0:T(8,128)S(1)}, f32[192,256]{1,0:T(8,128)S(1)}) custom-call(s32[3]{0:T(128)S(1)} %pad_add_fusion.place_ref, f32[2,104,512]{2,1,0:T(8,128)S(1)} %copy-done.1, f32[2,104,512]{2,1,0:T(8,128)S(1)} %collective-permute-done.main_b_ref, f32[2,104,512]{2,1,0:T(8,128)S(1)} %collective-permute-done.1.near_ref, ...), custom_call_target="tpu_custom_call" | custom-call | flops 2000000000 | bytes 6000000 | tf_op jit(solution)/shard_map/pyramid/pallas_call | solution.py:415
  57.4 6.2 %collective-permute-done.7 = f32[56,640]{1,0:T(8,128)S(1)} collective-permute-done((f32[56,640]{1,0:T(8,128)S(1)}, f32[56,640]{1,0:T(8,128)S(1)}, u32[]{:S(2)}, u32[]{:S(2)}) %collective-permute-start.7) | collective-permute-done | bytes 143392 | tf_op jit(solution)/shard_map/ppermute | solution.py:353
  63.6 11.9 %collective-permute-start.8 = (f32[56,640]{1,0:T(8,128)S(1)}, f32[56,640]{1,0:T(8,128)S(1)}, u32[]{:S(2)}, u32[]{:S(2)}) collective-permute-start(f32[56,640]{1,0:T(8,128)S(1)} %log_add_fusion.1), channel_id=1, source_target_pairs={{0,12},{4,8},{8,4},{12,0},{128,132},{132,128},{136,140},{140,136},... | collective-permute-start | bytes 430088 | tf_op jit(solution)/shard_map/ppermute | solution.py:353
  75.6 3.5 %pyramid.3 = (f32[384,512]{1,0:T(8,128)S(1)}, f32[384,384]{1,0:T(8,128)S(1)}, f32[192,256]{1,0:T(8,128)S(1)}) custom-call(s32[3]{0:T(128)S(1)} %pad_add_fusion.place_ref, f32[2,104,512]{2,1,0:T(8,128)S(1)} %collective-permute-done.3.main_a_ref, f32[2,104,512]{2,1,0:T(8,128)S(1)} %collective-permute-done.4.main_b_ref, ...), custom_call_target="tpu_custom_call" | custom-call | flops 2000000000 | bytes 6000000 | tf_op jit(solution)/shard_map/pyramid/pallas_call | solution.py:415
  79.1 5.1 %collective-permute-done.8 = f32[56,640]{1,0:T(8,128)S(1)} collective-permute-done((f32[56,640]{1,0:T(8,128)S(1)}, f32[56,640]{1,0:T(8,128)S(1)}, u32[]{:S(2)}, u32[]{:S(2)}) %collective-permute-start.8) | collective-permute-done | bytes 143392 | tf_op jit(solution)/shard_map/ppermute | solution.py:353
  84.2 2.7 %mix.1 = f32[3,32,512]{2,1,0:T(8,128)S(1)} custom-call(s32[3]{0:T(128)S(1)} %pad_add_fusion.place_ref, f32[4,64,640]{2,1,0:T(8,128)S(1)} %energy.2.refs_0_.logit_a_ref, f32[4,64,640]{2,1,0:T(8,128)S(1)} %get-tuple-element.37.logit_b_ref, f32[56,640]{1,0:T(8,128)S(1)} %log_add_fusion.lse_ref, f32[384,512]{1,0:T(8,128)S(1)} %get-tuple-element.47.fine_a_ref, ...), custom_call_target="tpu_custom_call" | custom-call | tf_op jit(solution)/shard_map/mix/pallas_call | solution.py:440
  87.0 2.9 %collective-permute-start.9 = (f32[3,32,512]{2,1,0:T(8,128)S(1)}, f32[3,32,512]{2,1,0:T(8,128)S(1)}, u32[]{:S(2)}, u32[]{:S(2)}) collective-permute-start(f32[3,32,512]{2,1,0:T(8,128)S(1)} %mix.1), channel_id=1, source_target_pairs={{0,4},{4,0},{8,12},{12,8},{128,140},{132,136},{136,132},{140,128},... | collective-permute-start | bytes 589832 | tf_op jit(solution)/shard_map/ppermute | solution.py:353
  89.8 13.0 %collective-permute-done.9 = f32[3,32,512]{2,1,0:T(8,128)S(1)} collective-permute-done((f32[3,32,512]{2,1,0:T(8,128)S(1)}, f32[3,32,512]{2,1,0:T(8,128)S(1)}, u32[]{:S(2)}, u32[]{:S(2)}) %collective-permute-start.9) | collective-permute-done | bytes 196640 | tf_op jit(solution)/shard_map/ppermute | solution.py:353
  102.8 9.5 %collective-permute-start.10 = (f32[3,32,512]{2,1,0:T(8,128)S(1)}, f32[3,32,512]{2,1,0:T(8,128)S(1)}, u32[]{:S(2)}, u32[]{:S(2)}) collective-permute-start(f32[3,32,512]{2,1,0:T(8,128)S(1)} %add.46), channel_id=1, source_target_pairs={{0,12},{4,8},{8,4},{12,0},{128,132},{132,128},{136,140},{140,136},... | collective-permute-start | bytes 589832 | tf_op jit(solution)/shard_map/ppermute | solution.py:353
  112.3 12.5 %collective-permute-done.10 = f32[3,32,512]{2,1,0:T(8,128)S(1)} collective-permute-done((f32[3,32,512]{2,1,0:T(8,128)S(1)}, f32[3,32,512]{2,1,0:T(8,128)S(1)}, u32[]{:S(2)}, u32[]{:S(2)}) %collective-permute-start.10) | collective-permute-done | bytes 196640 | tf_op jit(solution)/shard_map/ppermute | solution.py:353
  124.9 15.7 %all_to_all.5 = f32[4,3,32,512]{3,2,1,0:T(8,128)S(1)} all-to-all(f32[4,3,32,512]{3,2,1,0:T(8,128)S(1)} %broadcast_in_dim.3), channel_id=1, replica_groups=mesh['zl'=4,'y'=4,'c'=2,'zh'=4,'x'=4] {'x'}, dimensions={0} | all-to-all | bytes 1572864 | tf_op jit(solution)/shard_map/all_to_all | solution.py:459
  (30 shorter events, 4.5 us)
Async XLA Ops:
  2.8 14.8 %collective-permute-start = (f32[2,104,512]{2,1,0:T(8,128)}, f32[2,104,512]{2,1,0:T(8,128)S(1)}, u32[]{:S(2)}, u32[]{:S(2)}) collective-permute-start(f32[2,104,512]{2,1,0:T(8,128)} %get-tuple-element.34), channel_id=1, source_target_pairs={{0,1},{1,0},{2,3},{3,2},{4,5},{5,4},{6,7},{7,6},{8,9},{9,8},{10,11... | collective-permute-start | bytes 1277960 | tf_op jit(solution)/shard_map/ppermute | solution.py:381
  6.2 23.7 %collective-permute-start.3 = (f32[2,104,512]{2,1,0:T(8,128)}, f32[2,104,512]{2,1,0:T(8,128)S(1)}, u32[]{:S(2)}, u32[]{:S(2)}) collective-permute-start(f32[2,104,512]{2,1,0:T(8,128)} %get-tuple-element.35), channel_id=1, source_target_pairs={{0,3},{1,2},{2,1},{3,0},{4,7},{5,6},{6,5},{7,4},{8,11},{9,10},{10,... | collective-permute-start | bytes 1277960 | tf_op jit(solution)/shard_map/ppermute | solution.py:381
  10.2 19.7 %collective-permute-start.4 = (f32[2,104,512]{2,1,0:T(8,128)}, f32[2,104,512]{2,1,0:T(8,128)S(1)}, u32[]{:S(2)}, u32[]{:S(2)}) collective-permute-start(f32[2,104,512]{2,1,0:T(8,128)} %get-tuple-element.36), channel_id=1, source_target_pairs={{0,2},{1,3},{2,0},{3,1},{4,6},{5,7},{6,4},{7,5},{8,10},{9,11},{10,... | collective-permute-start | bytes 1277960 | tf_op jit(solution)/shard_map/ppermute | solution.py:381
  17.7 16.9 %collective-permute-start.1 = (f32[2,104,512]{2,1,0:T(8,128)S(1)}, f32[2,104,512]{2,1,0:T(8,128)S(1)}, u32[]{:S(2)}, u32[]{:S(2)}) collective-permute-start(f32[2,104,512]{2,1,0:T(8,128)S(1)} %pad_maximum_fusion), channel_id=1, source_target_pairs={{0,16},{16,0},{1,17},{17,1},{2,18},{18,2},{3,19},{19,3},{4,20},{20... | collective-permute-start | bytes 1277960 | tf_op jit(solution)/shard_map/ppermute | solution.py:348
  19.6 14.9 %copy-start.1 = (f32[2,104,512]{2,1,0:T(8,128)S(1)}, f32[2,104,512]{2,1,0:T(8,128)}, u32[]{:S(2)}) copy-start(f32[2,104,512]{2,1,0:T(8,128)} %get-tuple-element.33.main_a_ref) | copy-start | bytes 1277956
  19.6 14.9 %collective-permute-start.2 = (f32[2,104,512]{2,1,0:T(8,128)S(1)}, f32[2,104,512]{2,1,0:T(8,128)S(1)}, u32[]{:S(2)}, u32[]{:S(2)}) collective-permute-start(f32[2,104,512]{2,1,0:T(8,128)S(1)} %pad_maximum_fusion.1), channel_id=1, source_target_pairs={{16,32},{48,64},{80,96},{112,128},{144,160},{176,192},{208,224},{2... | collective-permute-start | bytes 1277960 | tf_op jit(solution)/shard_map/ppermute | solution.py:348
  30.0 7.5 %collective-permute-start.5 = (f32[2,104,512]{2,1,0:T(8,128)S(1)}, f32[2,104,512]{2,1,0:T(8,128)S(1)}, u32[]{:S(2)}, u32[]{:S(2)}) collective-permute-start(f32[2,104,512]{2,1,0:T(8,128)S(1)} %pad_maximum_fusion.2), channel_id=1, source_target_pairs={{0,16},{16,0},{1,17},{17,1},{2,18},{18,2},{3,19},{19,3},{4,20},{20... | collective-permute-start | bytes 1277960 | tf_op jit(solution)/shard_map/ppermute | solution.py:348
  32.0 9.4 %collective-permute-start.6 = (f32[2,104,512]{2,1,0:T(8,128)S(1)}, f32[2,104,512]{2,1,0:T(8,128)S(1)}, u32[]{:S(2)}, u32[]{:S(2)}) collective-permute-start(f32[2,104,512]{2,1,0:T(8,128)S(1)} %pad_maximum_fusion.3), channel_id=1, source_target_pairs={{16,32},{48,64},{80,96},{112,128},{144,160},{176,192},{208,224},{2... | collective-permute-start | bytes 1277960 | tf_op jit(solution)/shard_map/ppermute | solution.py:348
  37.5 16.3 %copy-start = (bf16[640,384]{1,0:T(8,128)(2,1)S(1)}, bf16[640,384]{1,0:T(8,128)(2,1)}, u32[]{:S(2)}) copy-start(bf16[640,384]{1,0:T(8,128)(2,1)} %constant.55.clone.d1_ref) | copy-start | bytes 1474564
  37.5 16.3 %copy-start.2 = (bf16[384,512]{1,0:T(8,128)(2,1)S(1)}, bf16[384,512]{1,0:T(8,128)(2,1)}, u32[]{:S(2)}) copy-start(bf16[384,512]{1,0:T(8,128)(2,1)} %constant.58.clone.u1_ref) | copy-start | bytes 1179652
  37.5 16.3 %copy-start.3 = (bf16[256,384]{1,0:T(8,128)(2,1)S(1)}, bf16[256,384]{1,0:T(8,128)(2,1)}, u32[]{:S(2)}) copy-start(bf16[256,384]{1,0:T(8,128)(2,1)} %constant.57.clone.u2_ref) | copy-start | bytes 589828
  37.5 16.3 %copy-start.4 = (bf16[384,256]{1,0:T(8,128)(2,1)S(1)}, bf16[384,256]{1,0:T(8,128)(2,1)}, u32[]{:S(2)}) copy-start(bf16[384,256]{1,0:T(8,128)(2,1)} %constant.56.clone.d2_ref) | copy-start | bytes 589828
  44.7 18.9 %collective-permute-start.7 = (f32[56,640]{1,0:T(8,128)S(1)}, f32[56,640]{1,0:T(8,128)S(1)}, u32[]{:S(2)}, u32[]{:S(2)}) collective-permute-start(f32[56,640]{1,0:T(8,128)S(1)} %get-tuple-element.38), channel_id=1, source_target_pairs={{0,4},{4,0},{8,12},{12,8},{128,140},{132,136},{136,132},{140,128},... | collective-permute-start | bytes 430088 | tf_op jit(solution)/shard_map/ppermute | solution.py:353
  63.6 20.5 %collective-permute-start.8 = (f32[56,640]{1,0:T(8,128)S(1)}, f32[56,640]{1,0:T(8,128)S(1)}, u32[]{:S(2)}, u32[]{:S(2)}) collective-permute-start(f32[56,640]{1,0:T(8,128)S(1)} %log_add_fusion.1), channel_id=1, source_target_pairs={{0,12},{4,8},{8,4},{12,0},{128,132},{132,128},{136,140},{140,136},... | collective-permute-start | bytes 430088 | tf_op jit(solution)/shard_map/ppermute | solution.py:353
  87.0 15.8 %collective-permute-start.9 = (f32[3,32,512]{2,1,0:T(8,128)S(1)}, f32[3,32,512]{2,1,0:T(8,128)S(1)}, u32[]{:S(2)}, u32[]{:S(2)}) collective-permute-start(f32[3,32,512]{2,1,0:T(8,128)S(1)} %mix.1), channel_id=1, source_target_pairs={{0,4},{4,0},{8,12},{12,8},{128,140},{132,136},{136,132},{140,128},... | collective-permute-start | bytes 589832 | tf_op jit(solution)/shard_map/ppermute | solution.py:353
  102.8 22.0 %collective-permute-start.10 = (f32[3,32,512]{2,1,0:T(8,128)S(1)}, f32[3,32,512]{2,1,0:T(8,128)S(1)}, u32[]{:S(2)}, u32[]{:S(2)}) collective-permute-start(f32[3,32,512]{2,1,0:T(8,128)S(1)} %add.46), channel_id=1, source_target_pairs={{0,12},{4,8},{8,4},{12,0},{128,132},{132,128},{136,140},{140,136},... | collective-permute-start | bytes 589832 | tf_op jit(solution)/shard_map/ppermute | solution.py:353

commit v10 on v8

--- a/solution.py
+++ b/solution.py
@@ -339,15 +339,19 @@
     return [pl.BlockSpec(memory_space=pltpu.SMEM)]
 
 
-def neighbours(group, core):
+def half(group, index):
+    return jnp.stack([lax.dynamic_index_in_dim(main, index, axis=0, keepdims=False) for main in group])
+
+
+def near_rows(group, core):
+    return lax.ppermute(half(group, 1 - core), "c", [(0, 1), (1, 0)])
+
+
+def far_rows(group, core):
     count = lax.axis_size(ROWS)
     swaps = [(i, i + 1) for i in range(1, count - 1, 2)]
     swaps += [(b, a) for a, b in swaps]
-
-    def half(index):
-        return jnp.stack([lax.dynamic_index_in_dim(main, index, axis=0, keepdims=False) for main in group])
-
-    return lax.ppermute(half(1 - core), "c", [(0, 1), (1, 0)]), lax.ppermute(half(core), ROWS, swaps)
+    return lax.ppermute(half(group, core), ROWS, swaps)
 
 
 def partner(value, flip):
@@ -387,10 +391,10 @@
         lax.ppermute(packed[m], "x", [(i, i ^ FLIPS[m]) for i in range(4)]) for m in (1, 2, 3)
     ]
     place = jnp.stack([strip, column, core]).astype(jnp.int32)
-    groups = [(*pair, *neighbours(pair, core)) for pair in (mains[:2], mains[2:])]
+    far = [far_rows(pair, core) for pair in (mains[:2], mains[2:])]
     logit_shape = jax.ShapeDtypeStruct((4, 64, W0), F32)
 
-    def energy(step, *earlier):
+    def energy(step, group, *earlier):
         return pl.pallas_call(
             functools.partial(energy_kernel, step == 1),
             out_shape=(logit_shape,) + (jax.ShapeDtypeStruct((56, W0), F32),) * step,
@@ -400,10 +404,13 @@
             compiler_params=PARAMS,
             cost_estimate=pl.CostEstimate(flops=2_000_000_000, bytes_accessed=6_000_000, transcendentals=0),
             name="energy",
-        )(place, *groups[step], *earlier)
-
-    logits = energy(0)
-    *more, lse = energy(1, *logits)
+        )(place, *group, *earlier)
+
+    groups = [(*mains[:2], near_rows(mains[:2], core), far[0])]
+    logits = energy(0, groups[0])
+    late, _ = lax.optimization_barrier((mains[2:], logits))
+    groups.append((*mains[2:], near_rows(late, core), far[1]))
+    *more, lse = energy(1, groups[1], *logits)
     logits = [*logits, *more]
 
     taps = [

time: 131 us -> 130 us (level)
  the two profiles are of different devices: /device:TPU:24 before, /device:TPU:8 now
where the time goes in v10:
time: 130 us; the launch traced here: 129 us
  starting transfers between devices  66.1 us (51%)
  waiting for transfers between devices  28.9 us (22%)
  Pallas kernels  18.7 us (14%)
  blocking collectives  12.7 us (10%)
  local copies, waits for them, and re-layouts  2.24 us (2%)
    ppermute x4, starting transfers between devices, partner(): return lax.ppermute(value, 'zh', [(i, i ^ flip) for i in range(4)])  21.6 us
    ppermute x2, starting transfers between devices, crossed(): return lax.ppermute(value, ('c', 'zh'), pairs)  20.4 us
    all_to_all x1, blocking collectives, on_device(): joined = lax.all_to_all(jnp.broadcast_to(whole, (4, 3, 32, 512)), 'x', 0, 0)  12.7 us
    ppermute x4, waiting for transfers between devices, partner(): return lax.ppermute(value, 'zh', [(i, i ^ flip) for i in range(4)])  12.5 us
    ppermute x3, starting transfers between devices, on_device(): lax.ppermute(packed[m], 'x', [(i, i ^ FLIPS[m]) for i in range(4)])  9.96 us
    ppermute x2, starting transfers between devices, far_rows(): return lax.ppermute(half(group, core), ROWS, swaps)  9.42 us
    ppermute x2, waiting for transfers between devices, crossed(): return lax.ppermute(value, ('c', 'zh'), pairs)  7.6 us
    pallas_call x2, Pallas kernels, on_device(): pl.pallas_call(pyramid_kernel, out_shape=(jax.ShapeDtypeStruct((384, M0),...  7.06 us
  transfers between devices with their start and end apart: 13, of which 10 were waited for; matrix products, arithmetic and copies ran while one was open for 1% of the time, Pallas kernels for 8%

profile of v10, /device:TPU:8, one launch (start us, length us, event | category | flops | bytes accessed | tf_op | source)
XLA Modules:
  0.0 129.4 jit_solution(9556822801861696622)
XLA Ops:
  0.0 2.8 %pack.1 = (f32[2,104,512]{2,1,0:T(8,128)}, f32[2,104,512]{2,1,0:T(8,128)}, f32[2,104,512]{2,1,0:T(8,128)}, f32[2,104,512]{2,1,0:T(8,128)}) custom-call(s32[2,3,32,2048]{3,2,1,0:T(8,128)} %samples_ref, f32[2]{0:T(128)} %gain_hbm_ref.1), custom_call_target="tpu_custom_call" | custom-call | tf_op jit(solution)/shard_map/pack/pallas_call | solution.py:374
  2.8 3.4 %collective-permute-start = (f32[2,104,512]{2,1,0:T(8,128)}, f32[2,104,512]{2,1,0:T(8,128)S(1)}, u32[]{:S(2)}, u32[]{:S(2)}) collective-permute-start(f32[2,104,512]{2,1,0:T(8,128)} %get-tuple-element.38), channel_id=1, source_target_pairs={{0,1},{1,0},{2,3},{3,2},{4,5},{5,4},{6,7},{7,6},{8,9},{9,8},{10,11... | collective-permute-start | bytes 1277960 | tf_op jit(solution)/shard_map/ppermute | solution.py:391
  6.2 4.0 %collective-permute-start.3 = (f32[2,104,512]{2,1,0:T(8,128)}, f32[2,104,512]{2,1,0:T(8,128)S(1)}, u32[]{:S(2)}, u32[]{:S(2)}) collective-permute-start(f32[2,104,512]{2,1,0:T(8,128)} %get-tuple-element.39), channel_id=1, source_target_pairs={{0,3},{1,2},{2,1},{3,0},{4,7},{5,6},{6,5},{7,4},{8,11},{9,10},{10,... | collective-permute-start | bytes 1277960 | tf_op jit(solution)/shard_map/ppermute | solution.py:391
  10.2 2.6 %collective-permute-start.4 = (f32[2,104,512]{2,1,0:T(8,128)}, f32[2,104,512]{2,1,0:T(8,128)S(1)}, u32[]{:S(2)}, u32[]{:S(2)}) collective-permute-start(f32[2,104,512]{2,1,0:T(8,128)} %get-tuple-element.40), channel_id=1, source_target_pairs={{0,2},{1,3},{2,0},{3,1},{4,6},{5,7},{6,4},{7,5},{8,10},{9,11},{10,... | collective-permute-start | bytes 1277960 | tf_op jit(solution)/shard_map/ppermute | solution.py:391
  13.8 3.8 %collective-permute-done.main_b_ref = f32[2,104,512]{2,1,0:T(8,128)S(1)} collective-permute-done((f32[2,104,512]{2,1,0:T(8,128)}, f32[2,104,512]{2,1,0:T(8,128)S(1)}, u32[]{:S(2)}, u32[]{:S(2)}) %collective-permute-start) | collective-permute-done | bytes 426016 | tf_op jit(solution)/shard_map/ppermute | solution.py:391
  19.8 7.5 %collective-permute-start.2 = (f32[2,104,512]{2,1,0:T(8,128)S(1)}, f32[2,104,512]{2,1,0:T(8,128)S(1)}, u32[]{:S(2)}, u32[]{:S(2)}) collective-permute-start(f32[2,104,512]{2,1,0:T(8,128)S(1)} %pad_maximum_fusion.1), channel_id=1, source_target_pairs={{16,32},{48,64},{80,96},{112,128},{144,160},{176,192},{208,224},{2... | collective-permute-start | bytes 1277960 | tf_op jit(solution)/shard_map/ppermute | solution.py:354
  27.3 2.6 %collective-permute-done.3.main_a_ref = f32[2,104,512]{2,1,0:T(8,128)S(1)} collective-permute-done((f32[2,104,512]{2,1,0:T(8,128)}, f32[2,104,512]{2,1,0:T(8,128)S(1)}, u32[]{:S(2)}, u32[]{:S(2)}) %collective-permute-start.3) | collective-permute-done | bytes 426016 | tf_op jit(solution)/shard_map/ppermute | solution.py:391
  33.1 2.9 %energy.2.refs_0_.logit_a_ref = f32[4,64,640]{2,1,0:T(8,128)S(1)} custom-call(s32[3]{0:T(128)S(1)} %pad_add_fusion.place_ref, f32[2,104,512]{2,1,0:T(8,128)S(1)} %copy-done.1, f32[2,104,512]{2,1,0:T(8,128)S(1)} %collective-permute-done.main_b_ref, f32[2,104,512]{2,1,0:T(8,128)S(1)} %collective-permute-done.1.near_ref, ...), custom_call_target="tpu_custom_call" | custom-call | flops 2000000000 | bytes 6000000 | tf_op jit(solution)/shard_map/energy/pallas_call | solution.py:398
  36.1 2.6 %collective-permute-start.5 = (f32[2,104,512]{2,1,0:T(8,128)S(1)}, f32[2,104,512]{2,1,0:T(8,128)S(1)}, u32[]{:S(2)}, u32[]{:S(2)}) collective-permute-start(f32[2,104,512]{2,1,0:T(8,128)S(1)} %pad_maximum_fusion.2), channel_id=1, source_target_pairs={{0,16},{16,0},{1,17},{17,1},{2,18},{18,2},{3,19},{19,3},{4,20},{20... | collective-permute-start | bytes 1277960 | tf_op jit(solution)/shard_map/ppermute | solution.py:347
  40.1 3.2 %energy.3 = (f32[4,64,640]{2,1,0:T(8,128)S(1)}, f32[56,640]{1,0:T(8,128)S(1)}) custom-call(s32[3]{0:T(128)S(1)} %pad_add_fusion.place_ref, f32[2,104,512]{2,1,0:T(8,128)S(1)} %collective-permute-done.3.main_a_ref, f32[2,104,512]{2,1,0:T(8,128)S(1)} %collective-permute-done.4.main_b_ref, f32[2,104,512]{2,1,0:T(8,128)S(1)} %collective-permute-done.5.near_ref, ...), custom_call_target="tpu_custom_call" | custom-call | flops 2000000000 | bytes 6000000 | tf_op jit(solution)/shard_map/energy/pallas_call | solution.py:398
  43.3 9.1 %collective-permute-start.7 = (f32[56,640]{1,0:T(8,128)S(1)}, f32[56,640]{1,0:T(8,128)S(1)}, u32[]{:S(2)}, u32[]{:S(2)}) collective-permute-start(f32[56,640]{1,0:T(8,128)S(1)} %get-tuple-element.44), channel_id=1, source_target_pairs={{0,4},{4,0},{8,12},{12,8},{16,28},{20,24},{24,20},{28,16},{1,5},{5... | collective-permute-start | bytes 430088 | tf_op jit(solution)/shard_map/ppermute | solution.py:363
  52.5 3.5 %pyramid.2 = (f32[384,512]{1,0:T(8,128)S(1)}, f32[384,384]{1,0:T(8,128)S(1)}, f32[192,256]{1,0:T(8,128)S(1)}) custom-call(s32[3]{0:T(128)S(1)} %pad_add_fusion.place_ref, f32[2,104,512]{2,1,0:T(8,128)S(1)} %copy-done.1, f32[2,104,512]{2,1,0:T(8,128)S(1)} %collective-permute-done.main_b_ref, f32[2,104,512]{2,1,0:T(8,128)S(1)} %collective-permute-done.1.near_ref, ...), custom_call_target="tpu_custom_call" | custom-call | flops 2000000000 | bytes 6000000 | tf_op jit(solution)/shard_map/pyramid/pallas_call | solution.py:428
  56.0 4.2 %collective-permute-done.7 = f32[56,640]{1,0:T(8,128)S(1)} collective-permute-done((f32[56,640]{1,0:T(8,128)S(1)}, f32[56,640]{1,0:T(8,128)S(1)}, u32[]{:S(2)}, u32[]{:S(2)}) %collective-permute-start.7) | collective-permute-done | bytes 143392 | tf_op jit(solution)/shard_map/ppermute | solution.py:363
  60.3 11.3 %collective-permute-start.8 = (f32[56,640]{1,0:T(8,128)S(1)}, f32[56,640]{1,0:T(8,128)S(1)}, u32[]{:S(2)}, u32[]{:S(2)}) collective-permute-start(f32[56,640]{1,0:T(8,128)S(1)} %log_add_fusion.1), channel_id=1, source_target_pairs={{0,12},{4,8},{8,4},{12,0},{16,20},{20,16},{24,28},{28,24},{1,13},{... | collective-permute-start | bytes 430088 | tf_op jit(solution)/shard_map/ppermute | solution.py:363
  71.7 3.5 %pyramid.3 = (f32[384,512]{1,0:T(8,128)S(1)}, f32[384,384]{1,0:T(8,128)S(1)}, f32[192,256]{1,0:T(8,128)S(1)}) custom-call(s32[3]{0:T(128)S(1)} %pad_add_fusion.place_ref, f32[2,104,512]{2,1,0:T(8,128)S(1)} %collective-permute-done.3.main_a_ref, f32[2,104,512]{2,1,0:T(8,128)S(1)} %collective-permute-done.4.main_b_ref, ...), custom_call_target="tpu_custom_call" | custom-call | flops 2000000000 | bytes 6000000 | tf_op jit(solution)/shard_map/pyramid/pallas_call | solution.py:428
  75.2 3.4 %collective-permute-done.8 = f32[56,640]{1,0:T(8,128)S(1)} collective-permute-done((f32[56,640]{1,0:T(8,128)S(1)}, f32[56,640]{1,0:T(8,128)S(1)}, u32[]{:S(2)}, u32[]{:S(2)}) %collective-permute-start.8) | collective-permute-done | bytes 143392 | tf_op jit(solution)/shard_map/ppermute | solution.py:363
  78.6 2.7 %mix.1 = (f32[3,32,256]{2,1,0:T(8,128)S(1)}, f32[3,32,256]{2,1,0:T(8,128)S(1)}) custom-call(s32[3]{0:T(128)S(1)} %pad_add_fusion.place_ref, f32[4,64,640]{2,1,0:T(8,128)S(1)} %energy.2.refs_0_.logit_a_ref, f32[4,64,640]{2,1,0:T(8,128)S(1)} %get-tuple-element.43.logit_b_ref, f32[56,640]{1,0:T(8,128)S(1)} %log_add_fusion.lse_ref, ...), custom_call_target="tpu_custom_call" | custom-call | tf_op jit(solution)/shard_map/mix/pallas_call | solution.py:453
  81.4 4.2 %collective-permute-start.9 = (f32[3,32,256]{2,1,0:T(8,128)S(1)}, f32[3,32,256]{2,1,0:T(8,128)S(1)}, u32[]{:S(2)}, u32[]{:S(2)}) collective-permute-start(f32[3,32,256]{2,1,0:T(8,128)S(1)} %get-tuple-element.59), channel_id=1, source_target_pairs={{0,4},{4,0},{8,12},{12,8},{1,5},{5,1},{9,13},{13,9},{2,6},{6,2},{1... | collective-permute-start | bytes 294920 | tf_op jit(solution)/shard_map/ppermute | solution.py:358
  85.6 5.9 %collective-permute-start.11 = (f32[3,32,256]{2,1,0:T(8,128)S(1)}, f32[3,32,256]{2,1,0:T(8,128)S(1)}, u32[]{:S(2)}, u32[]{:S(2)}) collective-permute-start(f32[3,32,256]{2,1,0:T(8,128)S(1)} %get-tuple-element.60), channel_id=1, source_target_pairs={{0,12},{4,8},{8,4},{12,0},{1,13},{5,9},{9,5},{13,1},{2,14},{6,10},... | collective-permute-start | bytes 294920 | tf_op jit(solution)/shard_map/ppermute | solution.py:358
  93.8 5.7 %collective-permute-start.10 = (f32[3,32,256]{2,1,0:T(8,128)S(1)}, f32[3,32,256]{2,1,0:T(8,128)S(1)}, u32[]{:S(2)}, u32[]{:S(2)}) collective-permute-start(f32[3,32,256]{2,1,0:T(8,128)S(1)} %add.52), channel_id=1, source_target_pairs={{0,12},{4,8},{8,4},{12,0},{1,13},{5,9},{9,5},{13,1},{2,14},{6,10},... | collective-permute-start | bytes 294920 | tf_op jit(solution)/shard_map/ppermute | solution.py:358
  99.5 5.7 %collective-permute-done.11 = f32[3,32,256]{2,1,0:T(8,128)S(1)} collective-permute-done((f32[3,32,256]{2,1,0:T(8,128)S(1)}, f32[3,32,256]{2,1,0:T(8,128)S(1)}, u32[]{:S(2)}, u32[]{:S(2)}) %collective-permute-start.11) | collective-permute-done | bytes 98336 | tf_op jit(solution)/shard_map/ppermute | solution.py:358
  105.2 5.8 %collective-permute-start.12 = (f32[3,32,256]{2,1,0:T(8,128)S(1)}, f32[3,32,256]{2,1,0:T(8,128)S(1)}, u32[]{:S(2)}, u32[]{:S(2)}) collective-permute-start(f32[3,32,256]{2,1,0:T(8,128)S(1)} %add.54), channel_id=1, source_target_pairs={{0,4},{4,0},{8,12},{12,8},{1,5},{5,1},{9,13},{13,9},{2,6},{6,2},{1... | collective-permute-start | bytes 294920 | tf_op jit(solution)/shard_map/ppermute | solution.py:358
  111.1 4.6 %collective-permute-done.12 = f32[3,32,256]{2,1,0:T(8,128)S(1)} collective-permute-done((f32[3,32,256]{2,1,0:T(8,128)S(1)}, f32[3,32,256]{2,1,0:T(8,128)S(1)}, u32[]{:S(2)}, u32[]{:S(2)}) %collective-permute-start.12) | collective-permute-done | bytes 98336 | tf_op jit(solution)/shard_map/ppermute | solution.py:358
  115.8 12.7 %all_to_all.5 = f32[4,3,32,512]{3,2,1,0:T(8,128)S(1)} all-to-all(f32[4,3,32,512]{3,2,1,0:T(8,128)S(1)} %broadcast_in_dim.3), channel_id=1, replica_groups=mesh['zl'=4,'y'=4,'c'=2,'zh'=4,'x'=4] {'x'}, dimensions={0} | all-to-all | bytes 1572864 | tf_op jit(solution)/shard_map/all_to_all | solution.py:474
  (38 shorter events, 11.3 us)
Async XLA Ops:
  2.8 14.8 %collective-permute-start = (f32[2,104,512]{2,1,0:T(8,128)}, f32[2,104,512]{2,1,0:T(8,128)S(1)}, u32[]{:S(2)}, u32[]{:S(2)}) collective-permute-start(f32[2,104,512]{2,1,0:T(8,128)} %get-tuple-element.38), channel_id=1, source_target_pairs={{0,1},{1,0},{2,3},{3,2},{4,5},{5,4},{6,7},{7,6},{8,9},{9,8},{10,11... | collective-permute-start | bytes 1277960 | tf_op jit(solution)/shard_map/ppermute | solution.py:391
  6.2 23.7 %collective-permute-start.3 = (f32[2,104,512]{2,1,0:T(8,128)}, f32[2,104,512]{2,1,0:T(8,128)S(1)}, u32[]{:S(2)}, u32[]{:S(2)}) collective-permute-start(f32[2,104,512]{2,1,0:T(8,128)} %get-tuple-element.39), channel_id=1, source_target_pairs={{0,3},{1,2},{2,1},{3,0},{4,7},{5,6},{6,5},{7,4},{8,11},{9,10},{10,... | collective-permute-start | bytes 1277960 | tf_op jit(solution)/shard_map/ppermute | solution.py:391
  10.2 19.7 %collective-permute-start.4 = (f32[2,104,512]{2,1,0:T(8,128)}, f32[2,104,512]{2,1,0:T(8,128)S(1)}, u32[]{:S(2)}, u32[]{:S(2)}) collective-permute-start(f32[2,104,512]{2,1,0:T(8,128)} %get-tuple-element.40), channel_id=1, source_target_pairs={{0,2},{1,3},{2,0},{3,1},{4,6},{5,7},{6,4},{7,5},{8,10},{9,11},{10,... | collective-permute-start | bytes 1277960 | tf_op jit(solution)/shard_map/ppermute | solution.py:391
  17.6 15.5 %copy-start.1 = (f32[2,104,512]{2,1,0:T(8,128)S(1)}, f32[2,104,512]{2,1,0:T(8,128)}, u32[]{:S(2)}) copy-start(f32[2,104,512]{2,1,0:T(8,128)} %get-tuple-element.37.main_a_ref) | copy-start | bytes 1277956
  17.7 14.3 %collective-permute-start.1 = (f32[2,104,512]{2,1,0:T(8,128)S(1)}, f32[2,104,512]{2,1,0:T(8,128)S(1)}, u32[]{:S(2)}, u32[]{:S(2)}) collective-permute-start(f32[2,104,512]{2,1,0:T(8,128)S(1)} %pad_maximum_fusion), channel_id=1, source_target_pairs={{0,16},{16,0},{1,17},{17,1},{2,18},{18,2},{3,19},{19,3},{4,20},{20... | collective-permute-start | bytes 1277960 | tf_op jit(solution)/shard_map/ppermute | solution.py:347
  19.8 13.3 %collective-permute-start.2 = (f32[2,104,512]{2,1,0:T(8,128)S(1)}, f32[2,104,512]{2,1,0:T(8,128)S(1)}, u32[]{:S(2)}, u32[]{:S(2)}) collective-permute-start(f32[2,104,512]{2,1,0:T(8,128)S(1)} %pad_maximum_fusion.1), channel_id=1, source_target_pairs={{16,32},{48,64},{80,96},{112,128},{144,160},{176,192},{208,224},{2... | collective-permute-start | bytes 1277960 | tf_op jit(solution)/shard_map/ppermute | solution.py:354
  30.0 9.4 %collective-permute-start.6 = (f32[2,104,512]{2,1,0:T(8,128)S(1)}, f32[2,104,512]{2,1,0:T(8,128)S(1)}, u32[]{:S(2)}, u32[]{:S(2)}) collective-permute-start(f32[2,104,512]{2,1,0:T(8,128)S(1)} %pad_maximum_fusion.3), channel_id=1, source_target_pairs={{16,32},{48,64},{80,96},{112,128},{144,160},{176,192},{208,224},{2... | collective-permute-start | bytes 1277960 | tf_op jit(solution)/shard_map/ppermute | solution.py:354
  36.1 16.4 %copy-start = (bf16[640,384]{1,0:T(8,128)(2,1)S(1)}, bf16[640,384]{1,0:T(8,128)(2,1)}, u32[]{:S(2)}) copy-start(bf16[640,384]{1,0:T(8,128)(2,1)} %constant.55.clone.d1_ref) | copy-start | bytes 1474564
  36.1 16.4 %copy-start.2 = (bf16[384,512]{1,0:T(8,128)(2,1)S(1)}, bf16[384,512]{1,0:T(8,128)(2,1)}, u32[]{:S(2)}) copy-start(bf16[384,512]{1,0:T(8,128)(2,1)} %constant.58.clone.u1_ref) | copy-start | bytes 1179652
  36.1 16.4 %copy-start.3 = (bf16[256,384]{1,0:T(8,128)(2,1)S(1)}, bf16[256,384]{1,0:T(8,128)(2,1)}, u32[]{:S(2)}) copy-start(bf16[256,384]{1,0:T(8,128)(2,1)} %constant.57.clone.u2_ref) | copy-start | bytes 589828
  36.1 16.4 %copy-start.4 = (bf16[384,256]{1,0:T(8,128)(2,1)S(1)}, bf16[384,256]{1,0:T(8,128)(2,1)}, u32[]{:S(2)}) copy-start(bf16[384,256]{1,0:T(8,128)(2,1)} %constant.56.clone.d2_ref) | copy-start | bytes 589828
  36.1 4.0 %collective-permute-start.5 = (f32[2,104,512]{2,1,0:T(8,128)S(1)}, f32[2,104,512]{2,1,0:T(8,128)S(1)}, u32[]{:S(2)}, u32[]{:S(2)}) collective-permute-start(f32[2,104,512]{2,1,0:T(8,128)S(1)} %pad_maximum_fusion.2), channel_id=1, source_target_pairs={{0,16},{16,0},{1,17},{17,1},{2,18},{18,2},{3,19},{19,3},{4,20},{20... | collective-permute-start | bytes 1277960 | tf_op jit(solution)/shard_map/ppermute | solution.py:347
  43.3 16.9 %collective-permute-start.7 = (f32[56,640]{1,0:T(8,128)S(1)}, f32[56,640]{1,0:T(8,128)S(1)}, u32[]{:S(2)}, u32[]{:S(2)}) collective-permute-start(f32[56,640]{1,0:T(8,128)S(1)} %get-tuple-element.44), channel_id=1, source_target_pairs={{0,4},{4,0},{8,12},{12,8},{16,28},{20,24},{24,20},{28,16},{1,5},{5... | collective-permute-start | bytes 430088 | tf_op jit(solution)/shard_map/ppermute | solution.py:363
  60.3 18.2 %collective-permute-start.8 = (f32[56,640]{1,0:T(8,128)S(1)}, f32[56,640]{1,0:T(8,128)S(1)}, u32[]{:S(2)}, u32[]{:S(2)}) collective-permute-start(f32[56,640]{1,0:T(8,128)S(1)} %log_add_fusion.1), channel_id=1, source_target_pairs={{0,12},{4,8},{8,4},{12,0},{16,20},{20,16},{24,28},{28,24},{1,13},{... | collective-permute-start | bytes 430088 | tf_op jit(solution)/shard_map/ppermute | solution.py:363
  81.4 12.4 %collective-permute-start.9 = (f32[3,32,256]{2,1,0:T(8,128)S(1)}, f32[3,32,256]{2,1,0:T(8,128)S(1)}, u32[]{:S(2)}, u32[]{:S(2)}) collective-permute-start(f32[3,32,256]{2,1,0:T(8,128)S(1)} %get-tuple-element.59), channel_id=1, source_target_pairs={{0,4},{4,0},{8,12},{12,8},{1,5},{5,1},{9,13},{13,9},{2,6},{6,2},{1... | collective-permute-start | bytes 294920 | tf_op jit(solution)/shard_map/ppermute | solution.py:358
  85.6 19.6 %collective-permute-start.11 = (f32[3,32,256]{2,1,0:T(8,128)S(1)}, f32[3,32,256]{2,1,0:T(8,128)S(1)}, u32[]{:S(2)}, u32[]{:S(2)}) collective-permute-start(f32[3,32,256]{2,1,0:T(8,128)S(1)} %get-tuple-element.60), channel_id=1, source_target_pairs={{0,12},{4,8},{8,4},{12,0},{1,13},{5,9},{9,5},{13,1},{2,14},{6,10},... | collective-permute-start | bytes 294920 | tf_op jit(solution)/shard_map/ppermute | solution.py:358
  93.8 17.2 %collective-permute-start.10 = (f32[3,32,256]{2,1,0:T(8,128)S(1)}, f32[3,32,256]{2,1,0:T(8,128)S(1)}, u32[]{:S(2)}, u32[]{:S(2)}) collective-permute-start(f32[3,32,256]{2,1,0:T(8,128)S(1)} %add.52), channel_id=1, source_target_pairs={{0,12},{4,8},{8,4},{12,0},{1,13},{5,9},{9,5},{13,1},{2,14},{6,10},... | collective-permute-start | bytes 294920 | tf_op jit(solution)/shard_map/ppermute | solution.py:358
  105.2 10.4 %collective-permute-start.12 = (f32[3,32,256]{2,1,0:T(8,128)S(1)}, f32[3,32,256]{2,1,0:T(8,128)S(1)}, u32[]{:S(2)}, u32[]{:S(2)}) collective-permute-start(f32[3,32,256]{2,1,0:T(8,128)S(1)} %add.54), channel_id=1, source_target_pairs={{0,4},{4,0},{8,12},{12,8},{1,5},{5,1},{9,13},{13,9},{2,6},{6,2},{1... | collective-permute-start | bytes 294920 | tf_op jit(solution)/shard_map/ppermute | solution.py:358

commit v11 on v10

--- a/solution.py
+++ b/solution.py
@@ -16,7 +16,7 @@
 GREY = (0.299 / 255.0, 0.587 / 255.0, 0.114 / 255.0)
 W0, W1, W2 = 640, 384, 256
 M0, M1, M2 = 512, 256, 128
-FLIPS = (0, 1, 3, 2)
+FLIPS = (0, 2, 1, 3)
 PARAMS = pltpu.CompilerParams(vmem_limit_bytes=20 * 1024 * 1024)
 
 

time: 130 us -> 131 us (level)
  the two profiles are of different devices: /device:TPU:8 before, /device:TPU:56 now
where the time goes in v11:
time: 131 us; the launch traced here: 130 us
  starting transfers between devices  63.9 us (49%)
  waiting for transfers between devices  28.2 us (22%)
  Pallas kernels  18.7 us (14%)
  blocking collectives  16.6 us (13%)
  local copies, waits for them, and re-layouts  2.24 us (2%)
    ppermute x4, starting transfers between devices, partner(): return lax.ppermute(value, 'zh', [(i, i ^ flip) for i in range(4)])  23.8 us
    ppermute x2, starting transfers between devices, crossed(): return lax.ppermute(value, ('c', 'zh'), pairs)  18.7 us
    all_to_all x1, blocking collectives, on_device(): joined = lax.all_to_all(jnp.broadcast_to(whole, (4, 3, 32, 512)), 'x', 0, 0)  16.6 us
    ppermute x4, waiting for transfers between devices, partner(): return lax.ppermute(value, 'zh', [(i, i ^ flip) for i in range(4)])  11.7 us
    ppermute x3, starting transfers between devices, on_device(): lax.ppermute(packed[m], 'x', [(i, i ^ FLIPS[m]) for i in range(4)])  9.9 us
    ppermute x3, waiting for transfers between devices, on_device(): lax.ppermute(packed[m], 'x', [(i, i ^ FLIPS[m]) for i in range(4)])  8.4 us
    pallas_call x2, Pallas kernels, on_device(): pl.pallas_call(pyramid_kernel, out_shape=(jax.ShapeDtypeStruct((384, M0),...  7.07 us
    ppermute x2, starting transfers between devices, near_rows(): return lax.ppermute(half(group, 1 - core), 'c', [(0, 1), (1, 0)])  6.7 us
  transfers between devices with their start and end apart: 13, of which 9 were waited for; matrix products, arithmetic and copies ran while one was open for 1% of the time, Pallas kernels for 8%

profile of v11, /device:TPU:56, one launch (start us, length us, event | category | flops | bytes accessed | tf_op | source)
XLA Modules:
  0.0 130.4 jit_solution(15070616873822131982)
XLA Ops:
  0.0 2.8 %pack.1 = (f32[2,104,512]{2,1,0:T(8,128)}, f32[2,104,512]{2,1,0:T(8,128)}, f32[2,104,512]{2,1,0:T(8,128)}, f32[2,104,512]{2,1,0:T(8,128)}) custom-call(s32[2,3,32,2048]{3,2,1,0:T(8,128)} %samples_ref, f32[2]{0:T(128)} %gain_hbm_ref.1), custom_call_target="tpu_custom_call" | custom-call | tf_op jit(solution)/shard_map/pack/pallas_call | solution.py:374
  2.8 4.9 %collective-permute-start = (f32[2,104,512]{2,1,0:T(8,128)}, f32[2,104,512]{2,1,0:T(8,128)S(1)}, u32[]{:S(2)}, u32[]{:S(2)}) collective-permute-start(f32[2,104,512]{2,1,0:T(8,128)} %get-tuple-element.38), channel_id=1, source_target_pairs={{0,2},{1,3},{2,0},{3,1},{4,6},{5,7},{6,4},{7,5},{8,10},{9,11},{10,... | collective-permute-start | bytes 1277960 | tf_op jit(solution)/shard_map/ppermute | solution.py:391
  7.7 2.5 %collective-permute-start.3 = (f32[2,104,512]{2,1,0:T(8,128)}, f32[2,104,512]{2,1,0:T(8,128)S(1)}, u32[]{:S(2)}, u32[]{:S(2)}) collective-permute-start(f32[2,104,512]{2,1,0:T(8,128)} %get-tuple-element.39), channel_id=1, source_target_pairs={{0,1},{1,0},{2,3},{3,2},{4,5},{5,4},{6,7},{7,6},{8,9},{9,8},{10,11... | collective-permute-start | bytes 1277960 | tf_op jit(solution)/shard_map/ppermute | solution.py:391
  10.2 2.5 %collective-permute-start.4 = (f32[2,104,512]{2,1,0:T(8,128)}, f32[2,104,512]{2,1,0:T(8,128)S(1)}, u32[]{:S(2)}, u32[]{:S(2)}) collective-permute-start(f32[2,104,512]{2,1,0:T(8,128)} %get-tuple-element.40), channel_id=1, source_target_pairs={{0,3},{1,2},{2,1},{3,0},{4,7},{5,6},{6,5},{7,4},{8,11},{9,10},{10,... | collective-permute-start | bytes 1277960 | tf_op jit(solution)/shard_map/ppermute | solution.py:391
  13.8 5.3 %collective-permute-done.main_b_ref = f32[2,104,512]{2,1,0:T(8,128)S(1)} collective-permute-done((f32[2,104,512]{2,1,0:T(8,128)}, f32[2,104,512]{2,1,0:T(8,128)S(1)}, u32[]{:S(2)}, u32[]{:S(2)}) %collective-permute-start) | collective-permute-done | bytes 426016 | tf_op jit(solution)/shard_map/ppermute | solution.py:391
  21.3 2.8 %collective-permute-start.2 = (f32[2,104,512]{2,1,0:T(8,128)S(1)}, f32[2,104,512]{2,1,0:T(8,128)S(1)}, u32[]{:S(2)}, u32[]{:S(2)}) collective-permute-start(f32[2,104,512]{2,1,0:T(8,128)S(1)} %pad_maximum_fusion.1), channel_id=1, source_target_pairs={{16,32},{48,64},{80,96},{112,128},{144,160},{176,192},{208,224},{2... | collective-permute-start | bytes 1277960 | tf_op jit(solution)/shard_map/ppermute | solution.py:354
  24.1 3.1 %collective-permute-done.3.main_a_ref = f32[2,104,512]{2,1,0:T(8,128)S(1)} collective-permute-done((f32[2,104,512]{2,1,0:T(8,128)}, f32[2,104,512]{2,1,0:T(8,128)S(1)}, u32[]{:S(2)}, u32[]{:S(2)}) %collective-permute-start.3) | collective-permute-done | bytes 426016 | tf_op jit(solution)/shard_map/ppermute | solution.py:391
  30.7 2.9 %energy.2.refs_0_.logit_a_ref = f32[4,64,640]{2,1,0:T(8,128)S(1)} custom-call(s32[3]{0:T(128)S(1)} %pad_add_fusion.place_ref, f32[2,104,512]{2,1,0:T(8,128)S(1)} %copy-done.1, f32[2,104,512]{2,1,0:T(8,128)S(1)} %collective-permute-done.main_b_ref, f32[2,104,512]{2,1,0:T(8,128)S(1)} %collective-permute-done.1.near_ref, ...), custom_call_target="tpu_custom_call" | custom-call | flops 2000000000 | bytes 6000000 | tf_op jit(solution)/shard_map/energy/pallas_call | solution.py:398
  33.8 4.6 %collective-permute-start.5 = (f32[2,104,512]{2,1,0:T(8,128)S(1)}, f32[2,104,512]{2,1,0:T(8,128)S(1)}, u32[]{:S(2)}, u32[]{:S(2)}) collective-permute-start(f32[2,104,512]{2,1,0:T(8,128)S(1)} %pad_maximum_fusion.2), channel_id=1, source_target_pairs={{0,16},{16,0},{1,17},{17,1},{2,18},{18,2},{3,19},{19,3},{4,20},{20... | collective-permute-start | bytes 1277960 | tf_op jit(solution)/shard_map/ppermute | solution.py:347
  39.8 3.2 %energy.3 = (f32[4,64,640]{2,1,0:T(8,128)S(1)}, f32[56,640]{1,0:T(8,128)S(1)}) custom-call(s32[3]{0:T(128)S(1)} %pad_add_fusion.place_ref, f32[2,104,512]{2,1,0:T(8,128)S(1)} %collective-permute-done.3.main_a_ref, f32[2,104,512]{2,1,0:T(8,128)S(1)} %collective-permute-done.4.main_b_ref, f32[2,104,512]{2,1,0:T(8,128)S(1)} %collective-permute-done.5.near_ref, ...), custom_call_target="tpu_custom_call" | custom-call | flops 2000000000 | bytes 6000000 | tf_op jit(solution)/shard_map/energy/pallas_call | solution.py:398
  43.0 9.1 %collective-permute-start.7 = (f32[56,640]{1,0:T(8,128)S(1)}, f32[56,640]{1,0:T(8,128)S(1)}, u32[]{:S(2)}, u32[]{:S(2)}) collective-permute-start(f32[56,640]{1,0:T(8,128)S(1)} %get-tuple-element.44), channel_id=1, source_target_pairs={{0,4},{4,0},{8,12},{12,8},{16,28},{20,24},{24,20},{28,16},{1,5},{5... | collective-permute-start | bytes 430088 | tf_op jit(solution)/shard_map/ppermute | solution.py:363
  52.2 3.5 %pyramid.2 = (f32[384,512]{1,0:T(8,128)S(1)}, f32[384,384]{1,0:T(8,128)S(1)}, f32[192,256]{1,0:T(8,128)S(1)}) custom-call(s32[3]{0:T(128)S(1)} %pad_add_fusion.place_ref, f32[2,104,512]{2,1,0:T(8,128)S(1)} %copy-done.1, f32[2,104,512]{2,1,0:T(8,128)S(1)} %collective-permute-done.main_b_ref, f32[2,104,512]{2,1,0:T(8,128)S(1)} %collective-permute-done.1.near_ref, ...), custom_call_target="tpu_custom_call" | custom-call | flops 2000000000 | bytes 6000000 | tf_op jit(solution)/shard_map/pyramid/pallas_call | solution.py:428
  55.7 2.9 %collective-permute-done.7 = f32[56,640]{1,0:T(8,128)S(1)} collective-permute-done((f32[56,640]{1,0:T(8,128)S(1)}, f32[56,640]{1,0:T(8,128)S(1)}, u32[]{:S(2)}, u32[]{:S(2)}) %collective-permute-start.7) | collective-permute-done | bytes 143392 | tf_op jit(solution)/shard_map/ppermute | solution.py:363
  58.6 9.6 %collective-permute-start.8 = (f32[56,640]{1,0:T(8,128)S(1)}, f32[56,640]{1,0:T(8,128)S(1)}, u32[]{:S(2)}, u32[]{:S(2)}) collective-permute-start(f32[56,640]{1,0:T(8,128)S(1)} %log_add_fusion.1), channel_id=1, source_target_pairs={{0,12},{4,8},{8,4},{12,0},{16,20},{20,16},{24,28},{28,24},{1,13},{... | collective-permute-start | bytes 430088 | tf_op jit(solution)/shard_map/ppermute | solution.py:363
  68.2 3.5 %pyramid.3 = (f32[384,512]{1,0:T(8,128)S(1)}, f32[384,384]{1,0:T(8,128)S(1)}, f32[192,256]{1,0:T(8,128)S(1)}) custom-call(s32[3]{0:T(128)S(1)} %pad_add_fusion.place_ref, f32[2,104,512]{2,1,0:T(8,128)S(1)} %collective-permute-done.3.main_a_ref, f32[2,104,512]{2,1,0:T(8,128)S(1)} %collective-permute-done.4.main_b_ref, ...), custom_call_target="tpu_custom_call" | custom-call | flops 2000000000 | bytes 6000000 | tf_op jit(solution)/shard_map/pyramid/pallas_call | solution.py:428
  71.8 2.5 %collective-permute-done.8 = f32[56,640]{1,0:T(8,128)S(1)} collective-permute-done((f32[56,640]{1,0:T(8,128)S(1)}, f32[56,640]{1,0:T(8,128)S(1)}, u32[]{:S(2)}, u32[]{:S(2)}) %collective-permute-start.8) | collective-permute-done | bytes 143392 | tf_op jit(solution)/shard_map/ppermute | solution.py:363
  74.3 2.7 %mix.1 = (f32[3,32,256]{2,1,0:T(8,128)S(1)}, f32[3,32,256]{2,1,0:T(8,128)S(1)}) custom-call(s32[3]{0:T(128)S(1)} %pad_add_fusion.place_ref, f32[4,64,640]{2,1,0:T(8,128)S(1)} %energy.2.refs_0_.logit_a_ref, f32[4,64,640]{2,1,0:T(8,128)S(1)} %get-tuple-element.43.logit_b_ref, f32[56,640]{1,0:T(8,128)S(1)} %log_add_fusion.lse_ref, ...), custom_call_target="tpu_custom_call" | custom-call | tf_op jit(solution)/shard_map/mix/pallas_call | solution.py:453
  77.0 2.5 %collective-permute-start.9 = (f32[3,32,256]{2,1,0:T(8,128)S(1)}, f32[3,32,256]{2,1,0:T(8,128)S(1)}, u32[]{:S(2)}, u32[]{:S(2)}) collective-permute-start(f32[3,32,256]{2,1,0:T(8,128)S(1)} %get-tuple-element.59), channel_id=1, source_target_pairs={{0,4},{4,0},{8,12},{12,8},{1,5},{5,1},{9,13},{13,9},{2,6},{6,2},{1... | collective-permute-start | bytes 294920 | tf_op jit(solution)/shard_map/ppermute | solution.py:358
  79.5 8.1 %collective-permute-start.11 = (f32[3,32,256]{2,1,0:T(8,128)S(1)}, f32[3,32,256]{2,1,0:T(8,128)S(1)}, u32[]{:S(2)}, u32[]{:S(2)}) collective-permute-start(f32[3,32,256]{2,1,0:T(8,128)S(1)} %get-tuple-element.60), channel_id=1, source_target_pairs={{0,12},{4,8},{8,4},{12,0},{1,13},{5,9},{9,5},{13,1},{2,14},{6,10},... | collective-permute-start | bytes 294920 | tf_op jit(solution)/shard_map/ppermute | solution.py:358
  88.0 9.7 %collective-permute-start.10 = (f32[3,32,256]{2,1,0:T(8,128)S(1)}, f32[3,32,256]{2,1,0:T(8,128)S(1)}, u32[]{:S(2)}, u32[]{:S(2)}) collective-permute-start(f32[3,32,256]{2,1,0:T(8,128)S(1)} %add.52), channel_id=1, source_target_pairs={{0,12},{4,8},{8,4},{12,0},{1,13},{5,9},{9,5},{13,1},{2,14},{6,10},... | collective-permute-start | bytes 294920 | tf_op jit(solution)/shard_map/ppermute | solution.py:358
  97.7 3.6 %collective-permute-start.12 = (f32[3,32,256]{2,1,0:T(8,128)S(1)}, f32[3,32,256]{2,1,0:T(8,128)S(1)}, u32[]{:S(2)}, u32[]{:S(2)}) collective-permute-start(f32[3,32,256]{2,1,0:T(8,128)S(1)} %add.54), channel_id=1, source_target_pairs={{0,4},{4,0},{8,12},{12,8},{1,5},{5,1},{9,13},{13,9},{2,6},{6,2},{1... | collective-permute-start | bytes 294920 | tf_op jit(solution)/shard_map/ppermute | solution.py:358
  101.3 2.7 %collective-permute-done.10 = f32[3,32,256]{2,1,0:T(8,128)S(1)} collective-permute-done((f32[3,32,256]{2,1,0:T(8,128)S(1)}, f32[3,32,256]{2,1,0:T(8,128)S(1)}, u32[]{:S(2)}, u32[]{:S(2)}) %collective-permute-start.10) | collective-permute-done | bytes 98336 | tf_op jit(solution)/shard_map/ppermute | solution.py:358
  104.1 8.7 %collective-permute-done.12 = f32[3,32,256]{2,1,0:T(8,128)S(1)} collective-permute-done((f32[3,32,256]{2,1,0:T(8,128)S(1)}, f32[3,32,256]{2,1,0:T(8,128)S(1)}, u32[]{:S(2)}, u32[]{:S(2)}) %collective-permute-start.12) | collective-permute-done | bytes 98336 | tf_op jit(solution)/shard_map/ppermute | solution.py:358
  112.8 16.6 %all_to_all.5 = f32[4,3,32,512]{3,2,1,0:T(8,128)S(1)} all-to-all(f32[4,3,32,512]{3,2,1,0:T(8,128)S(1)} %broadcast_in_dim.3), channel_id=1, replica_groups=mesh['zl'=4,'y'=4,'c'=2,'zh'=4,'x'=4] {'x'}, dimensions={0} | all-to-all | bytes 1572864 | tf_op jit(solution)/shard_map/all_to_all | solution.py:474
  (38 shorter events, 9.8 us)
Async XLA Ops:
  2.8 16.3 %collective-permute-start = (f32[2,104,512]{2,1,0:T(8,128)}, f32[2,104,512]{2,1,0:T(8,128)S(1)}, u32[]{:S(2)}, u32[]{:S(2)}) collective-permute-start(f32[2,104,512]{2,1,0:T(8,128)} %get-tuple-element.38), channel_id=1, source_target_pairs={{0,2},{1,3},{2,0},{3,1},{4,6},{5,7},{6,4},{7,5},{8,10},{9,11},{10,... | collective-permute-start | bytes 1277960 | tf_op jit(solution)/shard_map/ppermute | solution.py:391
  7.7 19.5 %collective-permute-start.3 = (f32[2,104,512]{2,1,0:T(8,128)}, f32[2,104,512]{2,1,0:T(8,128)S(1)}, u32[]{:S(2)}, u32[]{:S(2)}) collective-permute-start(f32[2,104,512]{2,1,0:T(8,128)} %get-tuple-element.39), channel_id=1, source_target_pairs={{0,1},{1,0},{2,3},{3,2},{4,5},{5,4},{6,7},{7,6},{8,9},{9,8},{10,11... | collective-permute-start | bytes 1277960 | tf_op jit(solution)/shard_map/ppermute | solution.py:391
  10.2 17.0 %collective-permute-start.4 = (f32[2,104,512]{2,1,0:T(8,128)}, f32[2,104,512]{2,1,0:T(8,128)S(1)}, u32[]{:S(2)}, u32[]{:S(2)}) collective-permute-start(f32[2,104,512]{2,1,0:T(8,128)} %get-tuple-element.40), channel_id=1, source_target_pairs={{0,3},{1,2},{2,1},{3,0},{4,7},{5,6},{6,5},{7,4},{8,11},{9,10},{10,... | collective-permute-start | bytes 1277960 | tf_op jit(solution)/shard_map/ppermute | solution.py:391
  19.1 11.6 %copy-start.1 = (f32[2,104,512]{2,1,0:T(8,128)S(1)}, f32[2,104,512]{2,1,0:T(8,128)}, u32[]{:S(2)}) copy-start(f32[2,104,512]{2,1,0:T(8,128)} %get-tuple-element.37.main_a_ref) | copy-start | bytes 1277956
  19.2 10.2 %collective-permute-start.1 = (f32[2,104,512]{2,1,0:T(8,128)S(1)}, f32[2,104,512]{2,1,0:T(8,128)S(1)}, u32[]{:S(2)}, u32[]{:S(2)}) collective-permute-start(f32[2,104,512]{2,1,0:T(8,128)S(1)} %pad_maximum_fusion), channel_id=1, source_target_pairs={{0,16},{16,0},{1,17},{17,1},{2,18},{18,2},{3,19},{19,3},{4,20},{20... | collective-permute-start | bytes 1277960 | tf_op jit(solution)/shard_map/ppermute | solution.py:347
  21.3 9.4 %collective-permute-start.2 = (f32[2,104,512]{2,1,0:T(8,128)S(1)}, f32[2,104,512]{2,1,0:T(8,128)S(1)}, u32[]{:S(2)}, u32[]{:S(2)}) collective-permute-start(f32[2,104,512]{2,1,0:T(8,128)S(1)} %pad_maximum_fusion.1), channel_id=1, source_target_pairs={{16,32},{48,64},{80,96},{112,128},{144,160},{176,192},{208,224},{2... | collective-permute-start | bytes 1277960 | tf_op jit(solution)/shard_map/ppermute | solution.py:354
  27.3 11.1 %collective-permute-start.6 = (f32[2,104,512]{2,1,0:T(8,128)S(1)}, f32[2,104,512]{2,1,0:T(8,128)S(1)}, u32[]{:S(2)}, u32[]{:S(2)}) collective-permute-start(f32[2,104,512]{2,1,0:T(8,128)S(1)} %pad_maximum_fusion.3), channel_id=1, source_target_pairs={{16,32},{48,64},{80,96},{112,128},{144,160},{176,192},{208,224},{2... | collective-permute-start | bytes 1277960 | tf_op jit(solution)/shard_map/ppermute | solution.py:354
  33.7 18.4 %copy-start = (bf16[640,384]{1,0:T(8,128)(2,1)S(1)}, bf16[640,384]{1,0:T(8,128)(2,1)}, u32[]{:S(2)}) copy-start(bf16[640,384]{1,0:T(8,128)(2,1)} %constant.55.clone.d1_ref) | copy-start | bytes 1474564
  33.7 18.4 %copy-start.2 = (bf16[384,512]{1,0:T(8,128)(2,1)S(1)}, bf16[384,512]{1,0:T(8,128)(2,1)}, u32[]{:S(2)}) copy-start(bf16[384,512]{1,0:T(8,128)(2,1)} %constant.58.clone.u1_ref) | copy-start | bytes 1179652
  33.7 18.4 %copy-start.3 = (bf16[256,384]{1,0:T(8,128)(2,1)S(1)}, bf16[256,384]{1,0:T(8,128)(2,1)}, u32[]{:S(2)}) copy-start(bf16[256,384]{1,0:T(8,128)(2,1)} %constant.57.clone.u2_ref) | copy-start | bytes 589828
  33.8 18.4 %copy-start.4 = (bf16[384,256]{1,0:T(8,128)(2,1)S(1)}, bf16[384,256]{1,0:T(8,128)(2,1)}, u32[]{:S(2)}) copy-start(bf16[384,256]{1,0:T(8,128)(2,1)} %constant.56.clone.d2_ref) | copy-start | bytes 589828
  33.8 6.0 %collective-permute-start.5 = (f32[2,104,512]{2,1,0:T(8,128)S(1)}, f32[2,104,512]{2,1,0:T(8,128)S(1)}, u32[]{:S(2)}, u32[]{:S(2)}) collective-permute-start(f32[2,104,512]{2,1,0:T(8,128)S(1)} %pad_maximum_fusion.2), channel_id=1, source_target_pairs={{0,16},{16,0},{1,17},{17,1},{2,18},{18,2},{3,19},{19,3},{4,20},{20... | collective-permute-start | bytes 1277960 | tf_op jit(solution)/shard_map/ppermute | solution.py:347
  43.0 15.5 %collective-permute-start.7 = (f32[56,640]{1,0:T(8,128)S(1)}, f32[56,640]{1,0:T(8,128)S(1)}, u32[]{:S(2)}, u32[]{:S(2)}) collective-permute-start(f32[56,640]{1,0:T(8,128)S(1)} %get-tuple-element.44), channel_id=1, source_target_pairs={{0,4},{4,0},{8,12},{12,8},{16,28},{20,24},{24,20},{28,16},{1,5},{5... | collective-permute-start | bytes 430088 | tf_op jit(solution)/shard_map/ppermute | solution.py:363
  58.6 15.6 %collective-permute-start.8 = (f32[56,640]{1,0:T(8,128)S(1)}, f32[56,640]{1,0:T(8,128)S(1)}, u32[]{:S(2)}, u32[]{:S(2)}) collective-permute-start(f32[56,640]{1,0:T(8,128)S(1)} %log_add_fusion.1), channel_id=1, source_target_pairs={{0,12},{4,8},{8,4},{12,0},{16,20},{20,16},{24,28},{28,24},{1,13},{... | collective-permute-start | bytes 430088 | tf_op jit(solution)/shard_map/ppermute | solution.py:363
  77.0 11.0 %collective-permute-start.9 = (f32[3,32,256]{2,1,0:T(8,128)S(1)}, f32[3,32,256]{2,1,0:T(8,128)S(1)}, u32[]{:S(2)}, u32[]{:S(2)}) collective-permute-start(f32[3,32,256]{2,1,0:T(8,128)S(1)} %get-tuple-element.59), channel_id=1, source_target_pairs={{0,4},{4,0},{8,12},{12,8},{1,5},{5,1},{9,13},{13,9},{2,6},{6,2},{1... | collective-permute-start | bytes 294920 | tf_op jit(solution)/shard_map/ppermute | solution.py:358
  79.5 18.2 %collective-permute-start.11 = (f32[3,32,256]{2,1,0:T(8,128)S(1)}, f32[3,32,256]{2,1,0:T(8,128)S(1)}, u32[]{:S(2)}, u32[]{:S(2)}) collective-permute-start(f32[3,32,256]{2,1,0:T(8,128)S(1)} %get-tuple-element.60), channel_id=1, source_target_pairs={{0,12},{4,8},{8,4},{12,0},{1,13},{5,9},{9,5},{13,1},{2,14},{6,10},... | collective-permute-start | bytes 294920 | tf_op jit(solution)/shard_map/ppermute | solution.py:358
  88.0 16.0 %collective-permute-start.10 = (f32[3,32,256]{2,1,0:T(8,128)S(1)}, f32[3,32,256]{2,1,0:T(8,128)S(1)}, u32[]{:S(2)}, u32[]{:S(2)}) collective-permute-start(f32[3,32,256]{2,1,0:T(8,128)S(1)} %add.52), channel_id=1, source_target_pairs={{0,12},{4,8},{8,4},{12,0},{1,13},{5,9},{9,5},{13,1},{2,14},{6,10},... | collective-permute-start | bytes 294920 | tf_op jit(solution)/shard_map/ppermute | solution.py:358
  97.7 15.0 %collective-permute-start.12 = (f32[3,32,256]{2,1,0:T(8,128)S(1)}, f32[3,32,256]{2,1,0:T(8,128)S(1)}, u32[]{:S(2)}, u32[]{:S(2)}) collective-permute-start(f32[3,32,256]{2,1,0:T(8,128)S(1)} %add.54), channel_id=1, source_target_pairs={{0,4},{4,0},{8,12},{12,8},{1,5},{5,1},{9,13},{13,9},{2,6},{6,2},{1... | collective-permute-start | bytes 294920 | tf_op jit(solution)/shard_map/ppermute | solution.py:358

commit v12 on v11

--- a/solution.py
+++ b/solution.py
@@ -354,10 +354,6 @@
     return lax.ppermute(half(group, core), ROWS, swaps)
 
 
-def partner(value, flip):
-    return lax.ppermute(value, "zh", [(i, i ^ flip) for i in range(4)])
-
-
 def crossed(value, flips):
     pairs = [(4 * c + i, 4 * c + (i ^ flip)) for c, flip in enumerate(flips) for i in range(4)]
     return lax.ppermute(value, ("c", "zh"), pairs)
@@ -468,7 +464,7 @@
     )(place, *logits, lse, *details, *taps)
 
     for a, b in ((1, 3), (3, 1)):
-        left_in, right_in = partner(left, a), partner(right, b)
+        left_in, right_in = crossed(left, (a, b)), crossed(right, (b, a))
         left, right = left + left_in, right + right_in
     whole = jnp.concatenate([left, right], axis=-1)
     joined = lax.all_to_all(jnp.broadcast_to(whole, (4, 3, 32, 512)), "x", 0, 0)

time: 131 us -> 128 us (0.977)
  the two profiles are of different devices: /device:TPU:56 before, /device:TPU:24 now
where the time goes in v12:
time: 128 us; the launch traced here: 126 us
  starting transfers between devices  70.5 us (55%)
  waiting for transfers between devices  19.9 us (16%)
  Pallas kernels  18.7 us (15%)
  blocking collectives  13.6 us (11%)
  local copies, waits for them, and re-layouts  2.24 us (2%)
    ppermute x6, starting transfers between devices, crossed(): return lax.ppermute(value, ('c', 'zh'), pairs)  49.1 us
    all_to_all x1, blocking collectives, on_device(): joined = lax.all_to_all(jnp.broadcast_to(whole, (4, 3, 32, 512)), 'x', 0, 0)  13.6 us
    ppermute x3, starting transfers between devices, on_device(): lax.ppermute(packed[m], 'x', [(i, i ^ FLIPS[m]) for i in range(4)])  9.9 us
    ppermute x6, waiting for transfers between devices, crossed(): return lax.ppermute(value, ('c', 'zh'), pairs)  8.76 us
    ppermute x3, waiting for transfers between devices, on_device(): lax.ppermute(packed[m], 'x', [(i, i ^ FLIPS[m]) for i in range(4)])  8.4 us
    pallas_call x2, Pallas kernels, on_device(): pl.pallas_call(pyramid_kernel, out_shape=(jax.ShapeDtypeStruct((384, M0),...  7.06 us
    ppermute x2, starting transfers between devices, near_rows(): return lax.ppermute(half(group, 1 - core), 'c', [(0, 1), (1, 0)])  6.7 us
    pallas_call x2, Pallas kernels, energy(): pl.pallas_call(functools.partial(energy_kernel, step == 1), out_shape=(lo...  6.13 us
  transfers between devices with their start and end apart: 13, of which 7 were waited for; matrix products, arithmetic and copies ran while one was open for 1% of the time, Pallas kernels for 8%

profile of v12, /device:TPU:24, one launch (start us, length us, event | category | flops | bytes accessed | tf_op | source)
XLA Modules:
  0.0 125.6 jit_solution(14850975714138235527)
XLA Ops:
  0.0 2.8 %pack.1 = (f32[2,104,512]{2,1,0:T(8,128)}, f32[2,104,512]{2,1,0:T(8,128)}, f32[2,104,512]{2,1,0:T(8,128)}, f32[2,104,512]{2,1,0:T(8,128)}) custom-call(s32[2,3,32,2048]{3,2,1,0:T(8,128)} %samples_ref, f32[2]{0:T(128)} %gain_hbm_ref.1), custom_call_target="tpu_custom_call" | custom-call | tf_op jit(solution)/shard_map/pack/pallas_call | solution.py:370
  2.8 4.9 %collective-permute-start = (f32[2,104,512]{2,1,0:T(8,128)}, f32[2,104,512]{2,1,0:T(8,128)S(1)}, u32[]{:S(2)}, u32[]{:S(2)}) collective-permute-start(f32[2,104,512]{2,1,0:T(8,128)} %get-tuple-element.38), channel_id=1, source_target_pairs={{0,2},{1,3},{2,0},{3,1},{4,6},{5,7},{6,4},{7,5},{8,10},{9,11},{10,... | collective-permute-start | bytes 1277960 | tf_op jit(solution)/shard_map/ppermute | solution.py:387
  7.7 2.5 %collective-permute-start.3 = (f32[2,104,512]{2,1,0:T(8,128)}, f32[2,104,512]{2,1,0:T(8,128)S(1)}, u32[]{:S(2)}, u32[]{:S(2)}) collective-permute-start(f32[2,104,512]{2,1,0:T(8,128)} %get-tuple-element.39), channel_id=1, source_target_pairs={{0,1},{1,0},{2,3},{3,2},{4,5},{5,4},{6,7},{7,6},{8,9},{9,8},{10,11... | collective-permute-start | bytes 1277960 | tf_op jit(solution)/shard_map/ppermute | solution.py:387
  10.2 2.5 %collective-permute-start.4 = (f32[2,104,512]{2,1,0:T(8,128)}, f32[2,104,512]{2,1,0:T(8,128)S(1)}, u32[]{:S(2)}, u32[]{:S(2)}) collective-permute-start(f32[2,104,512]{2,1,0:T(8,128)} %get-tuple-element.40), channel_id=1, source_target_pairs={{0,3},{1,2},{2,1},{3,0},{4,7},{5,6},{6,5},{7,4},{8,11},{9,10},{10,... | collective-permute-start | bytes 1277960 | tf_op jit(solution)/shard_map/ppermute | solution.py:387
  13.8 5.3 %collective-permute-done.main_b_ref = f32[2,104,512]{2,1,0:T(8,128)S(1)} collective-permute-done((f32[2,104,512]{2,1,0:T(8,128)}, f32[2,104,512]{2,1,0:T(8,128)S(1)}, u32[]{:S(2)}, u32[]{:S(2)}) %collective-permute-start) | collective-permute-done | bytes 426016 | tf_op jit(solution)/shard_map/ppermute | solution.py:387
  19.2 2.1 %collective-permute-start.1 = (f32[2,104,512]{2,1,0:T(8,128)S(1)}, f32[2,104,512]{2,1,0:T(8,128)S(1)}, u32[]{:S(2)}, u32[]{:S(2)}) collective-permute-start(f32[2,104,512]{2,1,0:T(8,128)S(1)} %pad_maximum_fusion), channel_id=1, source_target_pairs={{0,16},{16,0},{1,17},{17,1},{2,18},{18,2},{3,19},{19,3},{4,20},{20... | collective-permute-start | bytes 1277960 | tf_op jit(solution)/shard_map/ppermute | solution.py:347
  21.3 2.8 %collective-permute-start.2 = (f32[2,104,512]{2,1,0:T(8,128)S(1)}, f32[2,104,512]{2,1,0:T(8,128)S(1)}, u32[]{:S(2)}, u32[]{:S(2)}) collective-permute-start(f32[2,104,512]{2,1,0:T(8,128)S(1)} %pad_maximum_fusion.1), channel_id=1, source_target_pairs={{16,32},{48,64},{80,96},{112,128},{144,160},{176,192},{208,224},{2... | collective-permute-start | bytes 1277960 | tf_op jit(solution)/shard_map/ppermute | solution.py:354
  24.1 3.1 %collective-permute-done.3.main_a_ref = f32[2,104,512]{2,1,0:T(8,128)S(1)} collective-permute-done((f32[2,104,512]{2,1,0:T(8,128)}, f32[2,104,512]{2,1,0:T(8,128)S(1)}, u32[]{:S(2)}, u32[]{:S(2)}) %collective-permute-start.3) | collective-permute-done | bytes 426016 | tf_op jit(solution)/shard_map/ppermute | solution.py:387
  27.3 2.0 %collective-permute-start.6 = (f32[2,104,512]{2,1,0:T(8,128)S(1)}, f32[2,104,512]{2,1,0:T(8,128)S(1)}, u32[]{:S(2)}, u32[]{:S(2)}) collective-permute-start(f32[2,104,512]{2,1,0:T(8,128)S(1)} %pad_maximum_fusion.3), channel_id=1, source_target_pairs={{16,32},{48,64},{80,96},{112,128},{144,160},{176,192},{208,224},{2... | collective-permute-start | bytes 1277960 | tf_op jit(solution)/shard_map/ppermute | solution.py:354
  30.7 2.9 %energy.2.refs_0_.logit_a_ref = f32[4,64,640]{2,1,0:T(8,128)S(1)} custom-call(s32[3]{0:T(128)S(1)} %pad_add_fusion.place_ref, f32[2,104,512]{2,1,0:T(8,128)S(1)} %copy-done.1, f32[2,104,512]{2,1,0:T(8,128)S(1)} %collective-permute-done.main_b_ref, f32[2,104,512]{2,1,0:T(8,128)S(1)} %collective-permute-done.1.near_ref, ...), custom_call_target="tpu_custom_call" | custom-call | flops 2000000000 | bytes 6000000 | tf_op jit(solution)/shard_map/energy/pallas_call | solution.py:394
  33.8 4.6 %collective-permute-start.5 = (f32[2,104,512]{2,1,0:T(8,128)S(1)}, f32[2,104,512]{2,1,0:T(8,128)S(1)}, u32[]{:S(2)}, u32[]{:S(2)}) collective-permute-start(f32[2,104,512]{2,1,0:T(8,128)S(1)} %pad_maximum_fusion.2), channel_id=1, source_target_pairs={{0,16},{16,0},{1,17},{17,1},{2,18},{18,2},{3,19},{19,3},{4,20},{20... | collective-permute-start | bytes 1277960 | tf_op jit(solution)/shard_map/ppermute | solution.py:347
  39.8 3.2 %energy.3 = (f32[4,64,640]{2,1,0:T(8,128)S(1)}, f32[56,640]{1,0:T(8,128)S(1)}) custom-call(s32[3]{0:T(128)S(1)} %pad_add_fusion.place_ref, f32[2,104,512]{2,1,0:T(8,128)S(1)} %collective-permute-done.3.main_a_ref, f32[2,104,512]{2,1,0:T(8,128)S(1)} %collective-permute-done.4.main_b_ref, f32[2,104,512]{2,1,0:T(8,128)S(1)} %collective-permute-done.5.near_ref, ...), custom_call_target="tpu_custom_call" | custom-call | flops 2000000000 | bytes 6000000 | tf_op jit(solution)/shard_map/energy/pallas_call | solution.py:394
  43.0 9.1 %collective-permute-start.7 = (f32[56,640]{1,0:T(8,128)S(1)}, f32[56,640]{1,0:T(8,128)S(1)}, u32[]{:S(2)}, u32[]{:S(2)}) collective-permute-start(f32[56,640]{1,0:T(8,128)S(1)} %get-tuple-element.44), channel_id=1, source_target_pairs={{0,4},{4,0},{8,12},{12,8},{16,28},{20,24},{24,20},{28,16},{1,5},{5... | collective-permute-start | bytes 430088 | tf_op jit(solution)/shard_map/ppermute | solution.py:359
  52.2 3.5 %pyramid.2 = (f32[384,512]{1,0:T(8,128)S(1)}, f32[384,384]{1,0:T(8,128)S(1)}, f32[192,256]{1,0:T(8,128)S(1)}) custom-call(s32[3]{0:T(128)S(1)} %pad_add_fusion.place_ref, f32[2,104,512]{2,1,0:T(8,128)S(1)} %copy-done.1, f32[2,104,512]{2,1,0:T(8,128)S(1)} %collective-permute-done.main_b_ref, f32[2,104,512]{2,1,0:T(8,128)S(1)} %collective-permute-done.1.near_ref, ...), custom_call_target="tpu_custom_call" | custom-call | flops 2000000000 | bytes 6000000 | tf_op jit(solution)/shard_map/pyramid/pallas_call | solution.py:424
  55.7 4.4 %collective-permute-done.7 = f32[56,640]{1,0:T(8,128)S(1)} collective-permute-done((f32[56,640]{1,0:T(8,128)S(1)}, f32[56,640]{1,0:T(8,128)S(1)}, u32[]{:S(2)}, u32[]{:S(2)}) %collective-permute-start.7) | collective-permute-done | bytes 143392 | tf_op jit(solution)/shard_map/ppermute | solution.py:359
  60.2 7.5 %collective-permute-start.8 = (f32[56,640]{1,0:T(8,128)S(1)}, f32[56,640]{1,0:T(8,128)S(1)}, u32[]{:S(2)}, u32[]{:S(2)}) collective-permute-start(f32[56,640]{1,0:T(8,128)S(1)} %log_add_fusion.1), channel_id=1, source_target_pairs={{0,12},{4,8},{8,4},{12,0},{16,20},{20,16},{24,28},{28,24},{1,13},{... | collective-permute-start | bytes 430088 | tf_op jit(solution)/shard_map/ppermute | solution.py:359
  67.7 3.5 %pyramid.3 = (f32[384,512]{1,0:T(8,128)S(1)}, f32[384,384]{1,0:T(8,128)S(1)}, f32[192,256]{1,0:T(8,128)S(1)}) custom-call(s32[3]{0:T(128)S(1)} %pad_add_fusion.place_ref, f32[2,104,512]{2,1,0:T(8,128)S(1)} %collective-permute-done.3.main_a_ref, f32[2,104,512]{2,1,0:T(8,128)S(1)} %collective-permute-done.4.main_b_ref, ...), custom_call_target="tpu_custom_call" | custom-call | flops 2000000000 | bytes 6000000 | tf_op jit(solution)/shard_map/pyramid/pallas_call | solution.py:424
  72.9 2.7 %mix.1 = (f32[3,32,256]{2,1,0:T(8,128)S(1)}, f32[3,32,256]{2,1,0:T(8,128)S(1)}) custom-call(s32[3]{0:T(128)S(1)} %pad_add_fusion.place_ref, f32[4,64,640]{2,1,0:T(8,128)S(1)} %energy.2.refs_0_.logit_a_ref, f32[4,64,640]{2,1,0:T(8,128)S(1)} %get-tuple-element.43.logit_b_ref, f32[56,640]{1,0:T(8,128)S(1)} %log_add_fusion.lse_ref, ...), custom_call_target="tpu_custom_call" | custom-call | tf_op jit(solution)/shard_map/mix/pallas_call | solution.py:449
  75.6 8.2 %collective-permute-start.9 = (f32[3,32,256]{2,1,0:T(8,128)S(1)}, f32[3,32,256]{2,1,0:T(8,128)S(1)}, u32[]{:S(2)}, u32[]{:S(2)}) collective-permute-start(f32[3,32,256]{2,1,0:T(8,128)S(1)} %get-tuple-element.59), channel_id=1, source_target_pairs={{0,4},{4,0},{8,12},{12,8},{16,28},{20,24},{24,20},{28,16},{1,5},{5... | collective-permute-start | bytes 294920 | tf_op jit(solution)/shard_map/ppermute | solution.py:359
  83.8 5.8 %collective-permute-start.11 = (f32[3,32,256]{2,1,0:T(8,128)S(1)}, f32[3,32,256]{2,1,0:T(8,128)S(1)}, u32[]{:S(2)}, u32[]{:S(2)}) collective-permute-start(f32[3,32,256]{2,1,0:T(8,128)S(1)} %get-tuple-element.60), channel_id=1, source_target_pairs={{0,12},{4,8},{8,4},{12,0},{16,20},{20,16},{24,28},{28,24},{1,13},{... | collective-permute-start | bytes 294920 | tf_op jit(solution)/shard_map/ppermute | solution.py:359
  89.7 9.9 %collective-permute-start.10 = (f32[3,32,256]{2,1,0:T(8,128)S(1)}, f32[3,32,256]{2,1,0:T(8,128)S(1)}, u32[]{:S(2)}, u32[]{:S(2)}) collective-permute-start(f32[3,32,256]{2,1,0:T(8,128)S(1)} %add.52), channel_id=1, source_target_pairs={{0,12},{4,8},{8,4},{12,0},{16,20},{20,16},{24,28},{28,24},{1,13},{... | collective-permute-start | bytes 294920 | tf_op jit(solution)/shard_map/ppermute | solution.py:359
  99.6 8.5 %collective-permute-start.12 = (f32[3,32,256]{2,1,0:T(8,128)S(1)}, f32[3,32,256]{2,1,0:T(8,128)S(1)}, u32[]{:S(2)}, u32[]{:S(2)}) collective-permute-start(f32[3,32,256]{2,1,0:T(8,128)S(1)} %add.54), channel_id=1, source_target_pairs={{0,4},{4,0},{8,12},{12,8},{16,28},{20,24},{24,20},{28,16},{1,5},{5... | collective-permute-start | bytes 294920 | tf_op jit(solution)/shard_map/ppermute | solution.py:359
  108.2 2.8 %collective-permute-done.12 = f32[3,32,256]{2,1,0:T(8,128)S(1)} collective-permute-done((f32[3,32,256]{2,1,0:T(8,128)S(1)}, f32[3,32,256]{2,1,0:T(8,128)S(1)}, u32[]{:S(2)}, u32[]{:S(2)}) %collective-permute-start.12) | collective-permute-done | bytes 98336 | tf_op jit(solution)/shard_map/ppermute | solution.py:359
  111.1 13.6 %all_to_all.5 = f32[4,3,32,512]{3,2,1,0:T(8,128)S(1)} all-to-all(f32[4,3,32,512]{3,2,1,0:T(8,128)S(1)} %broadcast_in_dim.3), channel_id=1, replica_groups=mesh['zl'=4,'y'=4,'c'=2,'zh'=4,'x'=4] {'x'}, dimensions={0} | all-to-all | bytes 1572864 | tf_op jit(solution)/shard_map/all_to_all | solution.py:470
  (38 shorter events, 7.0 us)
Async XLA Ops:
  2.8 16.3 %collective-permute-start = (f32[2,104,512]{2,1,0:T(8,128)}, f32[2,104,512]{2,1,0:T(8,128)S(1)}, u32[]{:S(2)}, u32[]{:S(2)}) collective-permute-start(f32[2,104,512]{2,1,0:T(8,128)} %get-tuple-element.38), channel_id=1, source_target_pairs={{0,2},{1,3},{2,0},{3,1},{4,6},{5,7},{6,4},{7,5},{8,10},{9,11},{10,... | collective-permute-start | bytes 1277960 | tf_op jit(solution)/shard_map/ppermute | solution.py:387
  7.7 19.5 %collective-permute-start.3 = (f32[2,104,512]{2,1,0:T(8,128)}, f32[2,104,512]{2,1,0:T(8,128)S(1)}, u32[]{:S(2)}, u32[]{:S(2)}) collective-permute-start(f32[2,104,512]{2,1,0:T(8,128)} %get-tuple-element.39), channel_id=1, source_target_pairs={{0,1},{1,0},{2,3},{3,2},{4,5},{5,4},{6,7},{7,6},{8,9},{9,8},{10,11... | collective-permute-start | bytes 1277960 | tf_op jit(solution)/shard_map/ppermute | solution.py:387
  10.2 17.0 %collective-permute-start.4 = (f32[2,104,512]{2,1,0:T(8,128)}, f32[2,104,512]{2,1,0:T(8,128)S(1)}, u32[]{:S(2)}, u32[]{:S(2)}) collective-permute-start(f32[2,104,512]{2,1,0:T(8,128)} %get-tuple-element.40), channel_id=1, source_target_pairs={{0,3},{1,2},{2,1},{3,0},{4,7},{5,6},{6,5},{7,4},{8,11},{9,10},{10,... | collective-permute-start | bytes 1277960 | tf_op jit(solution)/shard_map/ppermute | solution.py:387
  19.1 11.6 %copy-start.1 = (f32[2,104,512]{2,1,0:T(8,128)S(1)}, f32[2,104,512]{2,1,0:T(8,128)}, u32[]{:S(2)}) copy-start(f32[2,104,512]{2,1,0:T(8,128)} %get-tuple-element.37.main_a_ref) | copy-start | bytes 1277956
  19.2 10.2 %collective-permute-start.1 = (f32[2,104,512]{2,1,0:T(8,128)S(1)}, f32[2,104,512]{2,1,0:T(8,128)S(1)}, u32[]{:S(2)}, u32[]{:S(2)}) collective-permute-start(f32[2,104,512]{2,1,0:T(8,128)S(1)} %pad_maximum_fusion), channel_id=1, source_target_pairs={{0,16},{16,0},{1,17},{17,1},{2,18},{18,2},{3,19},{19,3},{4,20},{20... | collective-permute-start | bytes 1277960 | tf_op jit(solution)/shard_map/ppermute | solution.py:347
  21.3 9.4 %collective-permute-start.2 = (f32[2,104,512]{2,1,0:T(8,128)S(1)}, f32[2,104,512]{2,1,0:T(8,128)S(1)}, u32[]{:S(2)}, u32[]{:S(2)}) collective-permute-start(f32[2,104,512]{2,1,0:T(8,128)S(1)} %pad_maximum_fusion.1), channel_id=1, source_target_pairs={{16,32},{48,64},{80,96},{112,128},{144,160},{176,192},{208,224},{2... | collective-permute-start | bytes 1277960 | tf_op jit(solution)/shard_map/ppermute | solution.py:354
  27.3 11.1 %collective-permute-start.6 = (f32[2,104,512]{2,1,0:T(8,128)S(1)}, f32[2,104,512]{2,1,0:T(8,128)S(1)}, u32[]{:S(2)}, u32[]{:S(2)}) collective-permute-start(f32[2,104,512]{2,1,0:T(8,128)S(1)} %pad_maximum_fusion.3), channel_id=1, source_target_pairs={{16,32},{48,64},{80,96},{112,128},{144,160},{176,192},{208,224},{2... | collective-permute-start | bytes 1277960 | tf_op jit(solution)/shard_map/ppermute | solution.py:354
  33.7 18.4 %copy-start = (bf16[640,384]{1,0:T(8,128)(2,1)S(1)}, bf16[640,384]{1,0:T(8,128)(2,1)}, u32[]{:S(2)}) copy-start(bf16[640,384]{1,0:T(8,128)(2,1)} %constant.55.clone.d1_ref) | copy-start | bytes 1474564
  33.7 18.4 %copy-start.2 = (bf16[384,512]{1,0:T(8,128)(2,1)S(1)}, bf16[384,512]{1,0:T(8,128)(2,1)}, u32[]{:S(2)}) copy-start(bf16[384,512]{1,0:T(8,128)(2,1)} %constant.58.clone.u1_ref) | copy-start | bytes 1179652
  33.7 18.4 %copy-start.3 = (bf16[256,384]{1,0:T(8,128)(2,1)S(1)}, bf16[256,384]{1,0:T(8,128)(2,1)}, u32[]{:S(2)}) copy-start(bf16[256,384]{1,0:T(8,128)(2,1)} %constant.57.clone.u2_ref) | copy-start | bytes 589828
  33.8 18.4 %copy-start.4 = (bf16[384,256]{1,0:T(8,128)(2,1)S(1)}, bf16[384,256]{1,0:T(8,128)(2,1)}, u32[]{:S(2)}) copy-start(bf16[384,256]{1,0:T(8,128)(2,1)} %constant.56.clone.d2_ref) | copy-start | bytes 589828
  33.8 6.0 %collective-permute-start.5 = (f32[2,104,512]{2,1,0:T(8,128)S(1)}, f32[2,104,512]{2,1,0:T(8,128)S(1)}, u32[]{:S(2)}, u32[]{:S(2)}) collective-permute-start(f32[2,104,512]{2,1,0:T(8,128)S(1)} %pad_maximum_fusion.2), channel_id=1, source_target_pairs={{0,16},{16,0},{1,17},{17,1},{2,18},{18,2},{3,19},{19,3},{4,20},{20... | collective-permute-start | bytes 1277960 | tf_op jit(solution)/shard_map/ppermute | solution.py:347
  43.0 17.1 %collective-permute-start.7 = (f32[56,640]{1,0:T(8,128)S(1)}, f32[56,640]{1,0:T(8,128)S(1)}, u32[]{:S(2)}, u32[]{:S(2)}) collective-permute-start(f32[56,640]{1,0:T(8,128)S(1)} %get-tuple-element.44), channel_id=1, source_target_pairs={{0,4},{4,0},{8,12},{12,8},{16,28},{20,24},{24,20},{28,16},{1,5},{5... | collective-permute-start | bytes 430088 | tf_op jit(solution)/shard_map/ppermute | solution.py:359
  60.2 12.6 %collective-permute-start.8 = (f32[56,640]{1,0:T(8,128)S(1)}, f32[56,640]{1,0:T(8,128)S(1)}, u32[]{:S(2)}, u32[]{:S(2)}) collective-permute-start(f32[56,640]{1,0:T(8,128)S(1)} %log_add_fusion.1), channel_id=1, source_target_pairs={{0,12},{4,8},{8,4},{12,0},{16,20},{20,16},{24,28},{28,24},{1,13},{... | collective-permute-start | bytes 430088 | tf_op jit(solution)/shard_map/ppermute | solution.py:359
  75.6 14.0 %collective-permute-start.9 = (f32[3,32,256]{2,1,0:T(8,128)S(1)}, f32[3,32,256]{2,1,0:T(8,128)S(1)}, u32[]{:S(2)}, u32[]{:S(2)}) collective-permute-start(f32[3,32,256]{2,1,0:T(8,128)S(1)} %get-tuple-element.59), channel_id=1, source_target_pairs={{0,4},{4,0},{8,12},{12,8},{16,28},{20,24},{24,20},{28,16},{1,5},{5... | collective-permute-start | bytes 294920 | tf_op jit(solution)/shard_map/ppermute | solution.py:359
  83.8 15.8 %collective-permute-start.11 = (f32[3,32,256]{2,1,0:T(8,128)S(1)}, f32[3,32,256]{2,1,0:T(8,128)S(1)}, u32[]{:S(2)}, u32[]{:S(2)}) collective-permute-start(f32[3,32,256]{2,1,0:T(8,128)S(1)} %get-tuple-element.60), channel_id=1, source_target_pairs={{0,12},{4,8},{8,4},{12,0},{16,20},{20,16},{24,28},{28,24},{1,13},{... | collective-permute-start | bytes 294920 | tf_op jit(solution)/shard_map/ppermute | solution.py:359
  89.7 18.5 %collective-permute-start.10 = (f32[3,32,256]{2,1,0:T(8,128)S(1)}, f32[3,32,256]{2,1,0:T(8,128)S(1)}, u32[]{:S(2)}, u32[]{:S(2)}) collective-permute-start(f32[3,32,256]{2,1,0:T(8,128)S(1)} %add.52), channel_id=1, source_target_pairs={{0,12},{4,8},{8,4},{12,0},{16,20},{20,16},{24,28},{28,24},{1,13},{... | collective-permute-start | bytes 294920 | tf_op jit(solution)/shard_map/ppermute | solution.py:359
  99.6 11.3 %collective-permute-start.12 = (f32[3,32,256]{2,1,0:T(8,128)S(1)}, f32[3,32,256]{2,1,0:T(8,128)S(1)}, u32[]{:S(2)}, u32[]{:S(2)}) collective-permute-start(f32[3,32,256]{2,1,0:T(8,128)S(1)} %add.54), channel_id=1, source_target_pairs={{0,4},{4,0},{8,12},{12,8},{16,28},{20,24},{24,20},{28,16},{1,5},{5... | collective-permute-start | bytes 294920 | tf_op jit(solution)/shard_map/ppermute | solution.py:359

commit v13 on v12

--- a/solution.py
+++ b/solution.py
@@ -168,7 +168,18 @@
         total = 0.0
         for ref in logits:
             total = total + jnp.exp(ref[...] - peak)
-        lse_ref[...] = pltpu.roll(peak + jnp.log(total), 58, 0)[0:56]
+        lse = pltpu.roll(peak + jnp.log(total), 58, 0)[0:56]
+        lane = lax.broadcasted_iota(jnp.int32, (8, 128), 1)
+        shared = [jnp.zeros((8, 128), F32)] * 2
+        for i in range(7):
+            rows = slice(8 * i, 8 * i + 8)
+            for j in range(4):
+                lse_ref[4 * i + j] = lse[rows, 128 * j : 128 * j + 128]
+            at = 32 * (i % 4)
+            piece = pltpu.roll(lse[rows, M0:W0], (16 + at) % 128, 1)
+            shared[i // 4] = jnp.where((lane >= at) & (lane < at + 32), piece, shared[i // 4])
+        lse_ref[28] = shared[0]
+        lse_ref[29] = shared[1]
 
 
 def split2(value):
@@ -277,7 +288,7 @@
     place_ref, logit_a_ref, logit_b_ref, lse_ref,
     fine_a_ref, mid_a_ref, low_a_ref, fine_b_ref, mid_b_ref, low_b_ref,
     d1_ref, d2_ref, u2_ref, u1_ref,
-    left_ref, right_ref, w0_ref, s1_ref, w1_ref, s2_ref, s3_ref, s4_ref,
+    left_ref, right_ref, tiles_ref, w0_ref, s1_ref, w1_ref, s2_ref, s3_ref, s4_ref,
 ):
     strip, k = place_ref[0], place_ref[1]
     v1 = down_rows(32, 64, 2, strip * 16 - 8, 512)
@@ -285,7 +296,13 @@
     col = column_of((16, W0), M0, W0)
     inside_col = (col >= -10) & (col <= 522) & (col + k * M0 >= 0) & (col + k * M0 < 2048)
     row = lax.broadcasted_iota(jnp.int32, (16, W0), 0)
-    lse = pltpu.roll(jnp.concatenate([lse_ref[...], jnp.zeros((8, W0), F32)], axis=0), 6, 0)
+    for i in range(7):
+        rows = slice(8 * i, 8 * i + 8)
+        for j in range(4):
+            tiles_ref[rows, 128 * j : 128 * j + 128] = lse_ref[4 * i + j]
+        tiles_ref[rows, M0:W0] = pltpu.roll(lse_ref[28 + i // 4], (112 - 32 * (i % 4)) % 128, 1)
+    tiles_ref[56:64] = jnp.zeros((8, W0), F32)
+    lse = pltpu.roll(tiles_ref[...], 6, 0)
     keeps = []
     for b in range(4):
         r = row + (16 * b - 16)
@@ -393,7 +410,7 @@
     def energy(step, group, *earlier):
         return pl.pallas_call(
             functools.partial(energy_kernel, step == 1),
-            out_shape=(logit_shape,) + (jax.ShapeDtypeStruct((56, W0), F32),) * step,
+            out_shape=(logit_shape,) + (jax.ShapeDtypeStruct((30, 8, 128), F32),) * step,
             in_specs=smem() + vmem(4 + step),
             out_specs=tuple(vmem(1 + step)),
             scratch_shapes=[pltpu.VMEM((64, W0), F32)],
@@ -452,6 +469,7 @@
         in_specs=smem() + vmem(13),
         out_specs=tuple(vmem(2)),
         scratch_shapes=[
+            pltpu.VMEM((64, W0), F32),
             pltpu.VMEM((8, 64, W0), F32),
             pltpu.VMEM((512, W0), BF),
             pltpu.VMEM((256, W1), F32),

time: 128 us -> 127 us (level)
  waiting for transfers between devices: 19.9 us -> 14.7 us
  starting transfers between devices: 70.5 us -> 75.1 us
    ppermute x6, waiting for transfers between devices: 8.76 us -> 3.58 us  [crossed(): return lax.ppermute(value, ('c', 'zh'), pairs)]
    ppermute x6, starting transfers between devices: 49.1 us -> 53.7 us  [crossed(): return lax.ppermute(value, ('c', 'zh'), pairs)]
  transfers between devices with their start and end apart: 13 -> 13, of which waited for: 7 -> 5; matrix products, arithmetic and copies ran while one was open for 1% -> 1% of each run, Pallas kernels for 8% -> 8%
where the time goes in v13:
time: 127 us; the launch traced here: 125 us
  starting transfers between devices  75.1 us (59%)
  Pallas kernels  18.7 us (15%)
  waiting for transfers between devices  14.7 us (12%)
  blocking collectives  13.6 us (11%)
  local copies, waits for them, and re-layouts  2.24 us (2%)
    ppermute x6, starting transfers between devices, crossed(): return lax.ppermute(value, ('c', 'zh'), pairs)  53.7 us
    all_to_all x1, blocking collectives, on_device(): joined = lax.all_to_all(jnp.broadcast_to(whole, (4, 3, 32, 512)), 'x', 0, 0)  13.6 us
    ppermute x3, starting transfers between devices, on_device(): lax.ppermute(packed[m], 'x', [(i, i ^ FLIPS[m]) for i in range(4)])  9.9 us
    ppermute x3, waiting for transfers between devices, on_device(): lax.ppermute(packed[m], 'x', [(i, i ^ FLIPS[m]) for i in range(4)])  8.41 us
    pallas_call x2, Pallas kernels, on_device(): pl.pallas_call(pyramid_kernel, out_shape=(jax.ShapeDtypeStruct((384, M0),...  7.06 us
    ppermute x2, starting transfers between devices, near_rows(): return lax.ppermute(half(group, 1 - core), 'c', [(0, 1), (1, 0)])  6.7 us
    pallas_call x2, Pallas kernels, energy(): pl.pallas_call(functools.partial(energy_kernel, step == 1), out_shape=(lo...  6.04 us
    ppermute x2, starting transfers between devices, far_rows(): return lax.ppermute(half(group, core), ROWS, swaps)  4.8 us
  transfers between devices with their start and end apart: 13, of which 5 were waited for; matrix products, arithmetic and copies ran while one was open for 1% of the time, Pallas kernels for 8%

profile of v13, /device:TPU:24, one launch (start us, length us, event | category | flops | bytes accessed | tf_op | source)
XLA Modules:
  0.0 125.1 jit_solution(2021879213865283716)
XLA Ops:
  0.0 2.8 %pack.1 = (f32[2,104,512]{2,1,0:T(8,128)}, f32[2,104,512]{2,1,0:T(8,128)}, f32[2,104,512]{2,1,0:T(8,128)}, f32[2,104,512]{2,1,0:T(8,128)}) custom-call(s32[2,3,32,2048]{3,2,1,0:T(8,128)} %samples_ref, f32[2]{0:T(128)} %gain_hbm_ref.1), custom_call_target="tpu_custom_call" | custom-call | tf_op jit(solution)/shard_map/pack/pallas_call | solution.py:387
  2.8 4.9 %collective-permute-start = (f32[2,104,512]{2,1,0:T(8,128)}, f32[2,104,512]{2,1,0:T(8,128)S(1)}, u32[]{:S(2)}, u32[]{:S(2)}) collective-permute-start(f32[2,104,512]{2,1,0:T(8,128)} %get-tuple-element.38), channel_id=1, source_target_pairs={{0,2},{1,3},{2,0},{3,1},{4,6},{5,7},{6,4},{7,5},{8,10},{9,11},{10,... | collective-permute-start | bytes 1277960 | tf_op jit(solution)/shard_map/ppermute | solution.py:404
  7.7 2.5 %collective-permute-start.3 = (f32[2,104,512]{2,1,0:T(8,128)}, f32[2,104,512]{2,1,0:T(8,128)S(1)}, u32[]{:S(2)}, u32[]{:S(2)}) collective-permute-start(f32[2,104,512]{2,1,0:T(8,128)} %get-tuple-element.39), channel_id=1, source_target_pairs={{0,1},{1,0},{2,3},{3,2},{4,5},{5,4},{6,7},{7,6},{8,9},{9,8},{10,11... | collective-permute-start | bytes 1277960 | tf_op jit(solution)/shard_map/ppermute | solution.py:404
  10.2 2.5 %collective-permute-start.4 = (f32[2,104,512]{2,1,0:T(8,128)}, f32[2,104,512]{2,1,0:T(8,128)S(1)}, u32[]{:S(2)}, u32[]{:S(2)}) collective-permute-start(f32[2,104,512]{2,1,0:T(8,128)} %get-tuple-element.40), channel_id=1, source_target_pairs={{0,3},{1,2},{2,1},{3,0},{4,7},{5,6},{6,5},{7,4},{8,11},{9,10},{10,... | collective-permute-start | bytes 1277960 | tf_op jit(solution)/shard_map/ppermute | solution.py:404
  13.8 5.3 %collective-permute-done.main_b_ref = f32[2,104,512]{2,1,0:T(8,128)S(1)} collective-permute-done((f32[2,104,512]{2,1,0:T(8,128)}, f32[2,104,512]{2,1,0:T(8,128)S(1)}, u32[]{:S(2)}, u32[]{:S(2)}) %collective-permute-start) | collective-permute-done | bytes 426016 | tf_op jit(solution)/shard_map/ppermute | solution.py:404
  19.2 2.1 %collective-permute-start.1 = (f32[2,104,512]{2,1,0:T(8,128)S(1)}, f32[2,104,512]{2,1,0:T(8,128)S(1)}, u32[]{:S(2)}, u32[]{:S(2)}) collective-permute-start(f32[2,104,512]{2,1,0:T(8,128)S(1)} %pad_maximum_fusion), channel_id=1, source_target_pairs={{0,16},{16,0},{1,17},{17,1},{2,18},{18,2},{3,19},{19,3},{4,20},{20... | collective-permute-start | bytes 1277960 | tf_op jit(solution)/shard_map/ppermute | solution.py:364
  21.3 2.8 %collective-permute-start.2 = (f32[2,104,512]{2,1,0:T(8,128)S(1)}, f32[2,104,512]{2,1,0:T(8,128)S(1)}, u32[]{:S(2)}, u32[]{:S(2)}) collective-permute-start(f32[2,104,512]{2,1,0:T(8,128)S(1)} %pad_maximum_fusion.1), channel_id=1, source_target_pairs={{16,32},{48,64},{80,96},{112,128},{144,160},{176,192},{208,224},{2... | collective-permute-start | bytes 1277960 | tf_op jit(solution)/shard_map/ppermute | solution.py:371
  24.1 3.1 %collective-permute-done.3.main_a_ref = f32[2,104,512]{2,1,0:T(8,128)S(1)} collective-permute-done((f32[2,104,512]{2,1,0:T(8,128)}, f32[2,104,512]{2,1,0:T(8,128)S(1)}, u32[]{:S(2)}, u32[]{:S(2)}) %collective-permute-start.3) | collective-permute-done | bytes 426016 | tf_op jit(solution)/shard_map/ppermute | solution.py:404
  27.3 2.0 %collective-permute-start.6 = (f32[2,104,512]{2,1,0:T(8,128)S(1)}, f32[2,104,512]{2,1,0:T(8,128)S(1)}, u32[]{:S(2)}, u32[]{:S(2)}) collective-permute-start(f32[2,104,512]{2,1,0:T(8,128)S(1)} %pad_maximum_fusion.3), channel_id=1, source_target_pairs={{16,32},{48,64},{80,96},{112,128},{144,160},{176,192},{208,224},{2... | collective-permute-start | bytes 1277960 | tf_op jit(solution)/shard_map/ppermute | solution.py:371
  30.7 2.9 %energy.2.refs_0_.logit_a_ref = f32[4,64,640]{2,1,0:T(8,128)S(1)} custom-call(s32[3]{0:T(128)S(1)} %pad_add_fusion.place_ref, f32[2,104,512]{2,1,0:T(8,128)S(1)} %copy-done.1, f32[2,104,512]{2,1,0:T(8,128)S(1)} %collective-permute-done.main_b_ref, f32[2,104,512]{2,1,0:T(8,128)S(1)} %collective-permute-done.1.near_ref, ...), custom_call_target="tpu_custom_call" | custom-call | flops 2000000000 | bytes 6000000 | tf_op jit(solution)/shard_map/energy/pallas_call | solution.py:411
  33.8 4.6 %collective-permute-start.5 = (f32[2,104,512]{2,1,0:T(8,128)S(1)}, f32[2,104,512]{2,1,0:T(8,128)S(1)}, u32[]{:S(2)}, u32[]{:S(2)}) collective-permute-start(f32[2,104,512]{2,1,0:T(8,128)S(1)} %pad_maximum_fusion.2), channel_id=1, source_target_pairs={{0,16},{16,0},{1,17},{17,1},{2,18},{18,2},{3,19},{19,3},{4,20},{20... | collective-permute-start | bytes 1277960 | tf_op jit(solution)/shard_map/ppermute | solution.py:364
  38.4 1.4 %collective-permute-done.5.near_ref = f32[2,104,512]{2,1,0:T(8,128)S(1)} collective-permute-done((f32[2,104,512]{2,1,0:T(8,128)S(1)}, f32[2,104,512]{2,1,0:T(8,128)S(1)}, u32[]{:S(2)}, u32[]{:S(2)}) %collective-permute-start.5) | collective-permute-done | bytes 426016 | tf_op jit(solution)/shard_map/ppermute | solution.py:364
  39.8 3.1 %energy.3 = (f32[4,64,640]{2,1,0:T(8,128)S(1)}, f32[30,8,128]{2,1,0:T(8,128)S(1)}) custom-call(s32[3]{0:T(128)S(1)} %pad_add_fusion.place_ref, f32[2,104,512]{2,1,0:T(8,128)S(1)} %collective-permute-done.3.main_a_ref, f32[2,104,512]{2,1,0:T(8,128)S(1)} %collective-permute-done.4.main_b_ref, f32[2,104,512]{2,1,0:T(8,128)S(1)} %collective-permute-done.5.near_ref, ...), custom_call_target="tpu_custom_call" | custom-call | flops 2000000000 | bytes 6000000 | tf_op jit(solution)/shard_map/energy/pallas_call | solution.py:411
  42.9 9.1 %collective-permute-start.7 = (f32[30,8,128]{2,1,0:T(8,128)S(1)}, f32[30,8,128]{2,1,0:T(8,128)S(1)}, u32[]{:S(2)}, u32[]{:S(2)}) collective-permute-start(f32[30,8,128]{2,1,0:T(8,128)S(1)} %get-tuple-element.44), channel_id=1, source_target_pairs={{0,4},{4,0},{8,12},{12,8},{16,28},{20,24},{24,20},{28,16},{1,5},{5... | collective-permute-start | bytes 368648 | tf_op jit(solution)/shard_map/ppermute | solution.py:376
  52.1 3.5 %pyramid.2 = (f32[384,512]{1,0:T(8,128)S(1)}, f32[384,384]{1,0:T(8,128)S(1)}, f32[192,256]{1,0:T(8,128)S(1)}) custom-call(s32[3]{0:T(128)S(1)} %pad_add_fusion.place_ref, f32[2,104,512]{2,1,0:T(8,128)S(1)} %copy-done.1, f32[2,104,512]{2,1,0:T(8,128)S(1)} %collective-permute-done.main_b_ref, f32[2,104,512]{2,1,0:T(8,128)S(1)} %collective-permute-done.1.near_ref, ...), custom_call_target="tpu_custom_call" | custom-call | flops 2000000000 | bytes 6000000 | tf_op jit(solution)/shard_map/pyramid/pallas_call | solution.py:441
  55.7 11.0 %collective-permute-start.8 = (f32[30,8,128]{2,1,0:T(8,128)S(1)}, f32[30,8,128]{2,1,0:T(8,128)S(1)}, u32[]{:S(2)}, u32[]{:S(2)}) collective-permute-start(f32[30,8,128]{2,1,0:T(8,128)S(1)} %log_add_fusion.1), channel_id=1, source_target_pairs={{0,12},{4,8},{8,4},{12,0},{16,20},{20,16},{24,28},{28,24},{1,13},{... | collective-permute-start | bytes 368648 | tf_op jit(solution)/shard_map/ppermute | solution.py:376
  66.7 3.5 %pyramid.3 = (f32[384,512]{1,0:T(8,128)S(1)}, f32[384,384]{1,0:T(8,128)S(1)}, f32[192,256]{1,0:T(8,128)S(1)}) custom-call(s32[3]{0:T(128)S(1)} %pad_add_fusion.place_ref, f32[2,104,512]{2,1,0:T(8,128)S(1)} %collective-permute-done.3.main_a_ref, f32[2,104,512]{2,1,0:T(8,128)S(1)} %collective-permute-done.4.main_b_ref, ...), custom_call_target="tpu_custom_call" | custom-call | flops 2000000000 | bytes 6000000 | tf_op jit(solution)/shard_map/pyramid/pallas_call | solution.py:441
  70.3 2.8 %mix.1 = (f32[3,32,256]{2,1,0:T(8,128)S(1)}, f32[3,32,256]{2,1,0:T(8,128)S(1)}) custom-call(s32[3]{0:T(128)S(1)} %pad_add_fusion.place_ref, f32[4,64,640]{2,1,0:T(8,128)S(1)} %energy.2.refs_0_.logit_a_ref, f32[4,64,640]{2,1,0:T(8,128)S(1)} %get-tuple-element.43.logit_b_ref, f32[30,8,128]{2,1,0:T(8,128)S(1)} %log_add_fusion.lse_ref, ...), custom_call_target="tpu_custom_call" | custom-call | tf_op jit(solution)/shard_map/mix/pallas_call | solution.py:466
  73.1 9.7 %collective-permute-start.9 = (f32[3,32,256]{2,1,0:T(8,128)S(1)}, f32[3,32,256]{2,1,0:T(8,128)S(1)}, u32[]{:S(2)}, u32[]{:S(2)}) collective-permute-start(f32[3,32,256]{2,1,0:T(8,128)S(1)} %get-tuple-element.59), channel_id=1, source_target_pairs={{0,4},{4,0},{8,12},{12,8},{16,28},{20,24},{24,20},{28,16},{1,5},{5... | collective-permute-start | bytes 294920 | tf_op jit(solution)/shard_map/ppermute | solution.py:376
  82.8 5.7 %collective-permute-start.11 = (f32[3,32,256]{2,1,0:T(8,128)S(1)}, f32[3,32,256]{2,1,0:T(8,128)S(1)}, u32[]{:S(2)}, u32[]{:S(2)}) collective-permute-start(f32[3,32,256]{2,1,0:T(8,128)S(1)} %get-tuple-element.60), channel_id=1, source_target_pairs={{0,12},{4,8},{8,4},{12,0},{16,20},{20,16},{24,28},{28,24},{1,13},{... | collective-permute-start | bytes 294920 | tf_op jit(solution)/shard_map/ppermute | solution.py:376
  88.5 9.6 %collective-permute-start.10 = (f32[3,32,256]{2,1,0:T(8,128)S(1)}, f32[3,32,256]{2,1,0:T(8,128)S(1)}, u32[]{:S(2)}, u32[]{:S(2)}) collective-permute-start(f32[3,32,256]{2,1,0:T(8,128)S(1)} %add.52), channel_id=1, source_target_pairs={{0,12},{4,8},{8,4},{12,0},{16,20},{20,16},{24,28},{28,24},{1,13},{... | collective-permute-start | bytes 294920 | tf_op jit(solution)/shard_map/ppermute | solution.py:376
  98.2 8.6 %collective-permute-start.12 = (f32[3,32,256]{2,1,0:T(8,128)S(1)}, f32[3,32,256]{2,1,0:T(8,128)S(1)}, u32[]{:S(2)}, u32[]{:S(2)}) collective-permute-start(f32[3,32,256]{2,1,0:T(8,128)S(1)} %add.54), channel_id=1, source_target_pairs={{0,4},{4,0},{8,12},{12,8},{16,28},{20,24},{24,20},{28,16},{1,5},{5... | collective-permute-start | bytes 294920 | tf_op jit(solution)/shard_map/ppermute | solution.py:376
  106.8 3.6 %collective-permute-done.12 = f32[3,32,256]{2,1,0:T(8,128)S(1)} collective-permute-done((f32[3,32,256]{2,1,0:T(8,128)S(1)}, f32[3,32,256]{2,1,0:T(8,128)S(1)}, u32[]{:S(2)}, u32[]{:S(2)}) %collective-permute-start.12) | collective-permute-done | bytes 98336 | tf_op jit(solution)/shard_map/ppermute | solution.py:376
  110.5 13.6 %all_to_all.5 = f32[4,3,32,512]{3,2,1,0:T(8,128)S(1)} all-to-all(f32[4,3,32,512]{3,2,1,0:T(8,128)S(1)} %broadcast_in_dim.3), channel_id=1, replica_groups=mesh['zl'=4,'y'=4,'c'=2,'zh'=4,'x'=4] {'x'}, dimensions={0} | all-to-all | bytes 1572864 | tf_op jit(solution)/shard_map/all_to_all | solution.py:488
  (38 shorter events, 4.0 us)
Async XLA Ops:
  2.8 16.3 %collective-permute-start = (f32[2,104,512]{2,1,0:T(8,128)}, f32[2,104,512]{2,1,0:T(8,128)S(1)}, u32[]{:S(2)}, u32[]{:S(2)}) collective-permute-start(f32[2,104,512]{2,1,0:T(8,128)} %get-tuple-element.38), channel_id=1, source_target_pairs={{0,2},{1,3},{2,0},{3,1},{4,6},{5,7},{6,4},{7,5},{8,10},{9,11},{10,... | collective-permute-start | bytes 1277960 | tf_op jit(solution)/shard_map/ppermute | solution.py:404
  7.7 19.5 %collective-permute-start.3 = (f32[2,104,512]{2,1,0:T(8,128)}, f32[2,104,512]{2,1,0:T(8,128)S(1)}, u32[]{:S(2)}, u32[]{:S(2)}) collective-permute-start(f32[2,104,512]{2,1,0:T(8,128)} %get-tuple-element.39), channel_id=1, source_target_pairs={{0,1},{1,0},{2,3},{3,2},{4,5},{5,4},{6,7},{7,6},{8,9},{9,8},{10,11... | collective-permute-start | bytes 1277960 | tf_op jit(solution)/shard_map/ppermute | solution.py:404
  10.2 17.0 %collective-permute-start.4 = (f32[2,104,512]{2,1,0:T(8,128)}, f32[2,104,512]{2,1,0:T(8,128)S(1)}, u32[]{:S(2)}, u32[]{:S(2)}) collective-permute-start(f32[2,104,512]{2,1,0:T(8,128)} %get-tuple-element.40), channel_id=1, source_target_pairs={{0,3},{1,2},{2,1},{3,0},{4,7},{5,6},{6,5},{7,4},{8,11},{9,10},{10,... | collective-permute-start | bytes 1277960 | tf_op jit(solution)/shard_map/ppermute | solution.py:404
  19.1 11.6 %copy-start.1 = (f32[2,104,512]{2,1,0:T(8,128)S(1)}, f32[2,104,512]{2,1,0:T(8,128)}, u32[]{:S(2)}) copy-start(f32[2,104,512]{2,1,0:T(8,128)} %get-tuple-element.37.main_a_ref) | copy-start | bytes 1277956
  19.2 10.2 %collective-permute-start.1 = (f32[2,104,512]{2,1,0:T(8,128)S(1)}, f32[2,104,512]{2,1,0:T(8,128)S(1)}, u32[]{:S(2)}, u32[]{:S(2)}) collective-permute-start(f32[2,104,512]{2,1,0:T(8,128)S(1)} %pad_maximum_fusion), channel_id=1, source_target_pairs={{0,16},{16,0},{1,17},{17,1},{2,18},{18,2},{3,19},{19,3},{4,20},{20... | collective-permute-start | bytes 1277960 | tf_op jit(solution)/shard_map/ppermute | solution.py:364
  21.3 9.4 %collective-permute-start.2 = (f32[2,104,512]{2,1,0:T(8,128)S(1)}, f32[2,104,512]{2,1,0:T(8,128)S(1)}, u32[]{:S(2)}, u32[]{:S(2)}) collective-permute-start(f32[2,104,512]{2,1,0:T(8,128)S(1)} %pad_maximum_fusion.1), channel_id=1, source_target_pairs={{16,32},{48,64},{80,96},{112,128},{144,160},{176,192},{208,224},{2... | collective-permute-start | bytes 1277960 | tf_op jit(solution)/shard_map/ppermute | solution.py:371
  27.3 11.1 %collective-permute-start.6 = (f32[2,104,512]{2,1,0:T(8,128)S(1)}, f32[2,104,512]{2,1,0:T(8,128)S(1)}, u32[]{:S(2)}, u32[]{:S(2)}) collective-permute-start(f32[2,104,512]{2,1,0:T(8,128)S(1)} %pad_maximum_fusion.3), channel_id=1, source_target_pairs={{16,32},{48,64},{80,96},{112,128},{144,160},{176,192},{208,224},{2... | collective-permute-start | bytes 1277960 | tf_op jit(solution)/shard_map/ppermute | solution.py:371
  33.7 18.3 %copy-start = (bf16[640,384]{1,0:T(8,128)(2,1)S(1)}, bf16[640,384]{1,0:T(8,128)(2,1)}, u32[]{:S(2)}) copy-start(bf16[640,384]{1,0:T(8,128)(2,1)} %constant.55.clone.d1_ref) | copy-start | bytes 1474564
  33.7 18.3 %copy-start.2 = (bf16[384,512]{1,0:T(8,128)(2,1)S(1)}, bf16[384,512]{1,0:T(8,128)(2,1)}, u32[]{:S(2)}) copy-start(bf16[384,512]{1,0:T(8,128)(2,1)} %constant.58.clone.u1_ref) | copy-start | bytes 1179652
  33.7 18.3 %copy-start.3 = (bf16[256,384]{1,0:T(8,128)(2,1)S(1)}, bf16[256,384]{1,0:T(8,128)(2,1)}, u32[]{:S(2)}) copy-start(bf16[256,384]{1,0:T(8,128)(2,1)} %constant.57.clone.u2_ref) | copy-start | bytes 589828
  33.8 18.3 %copy-start.4 = (bf16[384,256]{1,0:T(8,128)(2,1)S(1)}, bf16[384,256]{1,0:T(8,128)(2,1)}, u32[]{:S(2)}) copy-start(bf16[384,256]{1,0:T(8,128)(2,1)} %constant.56.clone.d2_ref) | copy-start | bytes 589828
  33.8 6.0 %collective-permute-start.5 = (f32[2,104,512]{2,1,0:T(8,128)S(1)}, f32[2,104,512]{2,1,0:T(8,128)S(1)}, u32[]{:S(2)}, u32[]{:S(2)}) collective-permute-start(f32[2,104,512]{2,1,0:T(8,128)S(1)} %pad_maximum_fusion.2), channel_id=1, source_target_pairs={{0,16},{16,0},{1,17},{17,1},{2,18},{18,2},{3,19},{19,3},{4,20},{20... | collective-permute-start | bytes 1277960 | tf_op jit(solution)/shard_map/ppermute | solution.py:364
  42.9 12.7 %collective-permute-start.7 = (f32[30,8,128]{2,1,0:T(8,128)S(1)}, f32[30,8,128]{2,1,0:T(8,128)S(1)}, u32[]{:S(2)}, u32[]{:S(2)}) collective-permute-start(f32[30,8,128]{2,1,0:T(8,128)S(1)} %get-tuple-element.44), channel_id=1, source_target_pairs={{0,4},{4,0},{8,12},{12,8},{16,28},{20,24},{24,20},{28,16},{1,5},{5... | collective-permute-start | bytes 368648 | tf_op jit(solution)/shard_map/ppermute | solution.py:376
  55.7 14.5 %collective-permute-start.8 = (f32[30,8,128]{2,1,0:T(8,128)S(1)}, f32[30,8,128]{2,1,0:T(8,128)S(1)}, u32[]{:S(2)}, u32[]{:S(2)}) collective-permute-start(f32[30,8,128]{2,1,0:T(8,128)S(1)} %log_add_fusion.1), channel_id=1, source_target_pairs={{0,12},{4,8},{8,4},{12,0},{16,20},{20,16},{24,28},{28,24},{1,13},{... | collective-permute-start | bytes 368648 | tf_op jit(solution)/shard_map/ppermute | solution.py:376
  73.1 15.4 %collective-permute-start.9 = (f32[3,32,256]{2,1,0:T(8,128)S(1)}, f32[3,32,256]{2,1,0:T(8,128)S(1)}, u32[]{:S(2)}, u32[]{:S(2)}) collective-permute-start(f32[3,32,256]{2,1,0:T(8,128)S(1)} %get-tuple-element.59), channel_id=1, source_target_pairs={{0,4},{4,0},{8,12},{12,8},{16,28},{20,24},{24,20},{28,16},{1,5},{5... | collective-permute-start | bytes 294920 | tf_op jit(solution)/shard_map/ppermute | solution.py:376
  82.8 15.4 %collective-permute-start.11 = (f32[3,32,256]{2,1,0:T(8,128)S(1)}, f32[3,32,256]{2,1,0:T(8,128)S(1)}, u32[]{:S(2)}, u32[]{:S(2)}) collective-permute-start(f32[3,32,256]{2,1,0:T(8,128)S(1)} %get-tuple-element.60), channel_id=1, source_target_pairs={{0,12},{4,8},{8,4},{12,0},{16,20},{20,16},{24,28},{28,24},{1,13},{... | collective-permute-start | bytes 294920 | tf_op jit(solution)/shard_map/ppermute | solution.py:376
  88.5 18.3 %collective-permute-start.10 = (f32[3,32,256]{2,1,0:T(8,128)S(1)}, f32[3,32,256]{2,1,0:T(8,128)S(1)}, u32[]{:S(2)}, u32[]{:S(2)}) collective-permute-start(f32[3,32,256]{2,1,0:T(8,128)S(1)} %add.52), channel_id=1, source_target_pairs={{0,12},{4,8},{8,4},{12,0},{16,20},{20,16},{24,28},{28,24},{1,13},{... | collective-permute-start | bytes 294920 | tf_op jit(solution)/shard_map/ppermute | solution.py:376
  98.2 12.2 %collective-permute-start.12 = (f32[3,32,256]{2,1,0:T(8,128)S(1)}, f32[3,32,256]{2,1,0:T(8,128)S(1)}, u32[]{:S(2)}, u32[]{:S(2)}) collective-permute-start(f32[3,32,256]{2,1,0:T(8,128)S(1)} %add.54), channel_id=1, source_target_pairs={{0,4},{4,0},{8,12},{12,8},{16,28},{20,24},{24,20},{28,16},{1,5},{5... | collective-permute-start | bytes 294920 | tf_op jit(solution)/shard_map/ppermute | solution.py:376

commit v14 on v13

--- a/solution.py
+++ b/solution.py
@@ -421,7 +421,7 @@
 
     groups = [(*mains[:2], near_rows(mains[:2], core), far[0])]
     logits = energy(0, groups[0])
-    late, _ = lax.optimization_barrier((mains[2:], logits))
+    late, _ = lax.optimization_barrier((mains[2:], groups[0][3]))
     groups.append((*mains[2:], near_rows(late, core), far[1]))
     *more, lse = energy(1, groups[1], *logits)
     logits = [*logits, *more]

time: 127 us -> 124 us (0.976)
  starting transfers between devices: 75.1 us -> 72.3 us
    ppermute x6, starting transfers between devices: 53.7 us -> 51.2 us  [crossed(): return lax.ppermute(value, ('c', 'zh'), pairs)]
    ppermute x6, waiting for transfers between devices: 3.58 us -> 5.09 us  [crossed(): return lax.ppermute(value, ('c', 'zh'), pairs)]
    ppermute x2, waiting for transfers between devices: 1.37 us -> 0.01 us  [near_rows(): return lax.ppermute(half(group, 1 - core), 'c', [(0, 1), (1, 0)])]
  transfers between devices with their start and end apart: 13 -> 13, of which waited for: 5 -> 6; matrix products, arithmetic and copies ran while one was open for 1% -> 1% of each run, Pallas kernels for 8% -> 8%
where the time goes in v14:
time: 124 us; the launch traced here: 122 us
  starting transfers between devices  72.3 us (58%)
  Pallas kernels  18.7 us (15%)
  blocking collectives  14.7 us (12%)
  waiting for transfers between devices  13.7 us (11%)
  local copies, waits for them, and re-layouts  2.24 us (2%)
    ppermute x6, starting transfers between devices, crossed(): return lax.ppermute(value, ('c', 'zh'), pairs)  51.2 us
    all_to_all x1, blocking collectives, on_device(): joined = lax.all_to_all(jnp.broadcast_to(whole, (4, 3, 32, 512)), 'x', 0, 0)  14.7 us
    ppermute x3, starting transfers between devices, on_device(): lax.ppermute(packed[m], 'x', [(i, i ^ FLIPS[m]) for i in range(4)])  9.9 us
    ppermute x3, waiting for transfers between devices, on_device(): lax.ppermute(packed[m], 'x', [(i, i ^ FLIPS[m]) for i in range(4)])  7.79 us
    ppermute x2, starting transfers between devices, near_rows(): return lax.ppermute(half(group, 1 - core), 'c', [(0, 1), (1, 0)])  7.18 us
    pallas_call x2, Pallas kernels, on_device(): pl.pallas_call(pyramid_kernel, out_shape=(jax.ShapeDtypeStruct((384, M0),...  7.07 us
    pallas_call x2, Pallas kernels, energy(): pl.pallas_call(functools.partial(energy_kernel, step == 1), out_shape=(lo...  6.05 us
    ppermute x6, waiting for transfers between devices, crossed(): return lax.ppermute(value, ('c', 'zh'), pairs)  5.09 us
  transfers between devices with their start and end apart: 13, of which 6 were waited for; matrix products, arithmetic and copies ran while one was open for 1% of the time, Pallas kernels for 8%

profile of v14, /device:TPU:24, one launch (start us, length us, event | category | flops | bytes accessed | tf_op | source)
XLA Modules:
  0.0 122.2 jit_solution(9820059045096576284)
XLA Ops:
  0.0 2.8 %pack.1 = (f32[2,104,512]{2,1,0:T(8,128)}, f32[2,104,512]{2,1,0:T(8,128)}, f32[2,104,512]{2,1,0:T(8,128)}, f32[2,104,512]{2,1,0:T(8,128)}) custom-call(s32[2,3,32,2048]{3,2,1,0:T(8,128)} %samples_ref, f32[2]{0:T(128)} %gain_hbm_ref.1), custom_call_target="tpu_custom_call" | custom-call | tf_op jit(solution)/shard_map/pack/pallas_call | solution.py:387
  2.8 4.9 %collective-permute-start = (f32[2,104,512]{2,1,0:T(8,128)}, f32[2,104,512]{2,1,0:T(8,128)S(1)}, u32[]{:S(2)}, u32[]{:S(2)}) collective-permute-start(f32[2,104,512]{2,1,0:T(8,128)} %get-tuple-element.38), channel_id=1, source_target_pairs={{0,2},{1,3},{2,0},{3,1},{4,6},{5,7},{6,4},{7,5},{8,10},{9,11},{10,... | collective-permute-start | bytes 1277960 | tf_op jit(solution)/shard_map/ppermute | solution.py:404
  7.7 2.5 %collective-permute-start.3 = (f32[2,104,512]{2,1,0:T(8,128)}, f32[2,104,512]{2,1,0:T(8,128)S(1)}, u32[]{:S(2)}, u32[]{:S(2)}) collective-permute-start(f32[2,104,512]{2,1,0:T(8,128)} %get-tuple-element.39), channel_id=1, source_target_pairs={{0,1},{1,0},{2,3},{3,2},{4,5},{5,4},{6,7},{7,6},{8,9},{9,8},{10,11... | collective-permute-start | bytes 1277960 | tf_op jit(solution)/shard_map/ppermute | solution.py:404
  10.2 2.5 %collective-permute-start.4 = (f32[2,104,512]{2,1,0:T(8,128)}, f32[2,104,512]{2,1,0:T(8,128)S(1)}, u32[]{:S(2)}, u32[]{:S(2)}) collective-permute-start(f32[2,104,512]{2,1,0:T(8,128)} %get-tuple-element.40), channel_id=1, source_target_pairs={{0,3},{1,2},{2,1},{3,0},{4,7},{5,6},{6,5},{7,4},{8,11},{9,10},{10,... | collective-permute-start | bytes 1277960 | tf_op jit(solution)/shard_map/ppermute | solution.py:404
  12.7 1.1 constant_dynamic-slice_fusion.5
  13.8 5.3 %collective-permute-done.main_b_ref = f32[2,104,512]{2,1,0:T(8,128)S(1)} collective-permute-done((f32[2,104,512]{2,1,0:T(8,128)}, f32[2,104,512]{2,1,0:T(8,128)S(1)}, u32[]{:S(2)}, u32[]{:S(2)}) %collective-permute-start) | collective-permute-done | bytes 426016 | tf_op jit(solution)/shard_map/ppermute | solution.py:404
  19.2 1.9 %collective-permute-start.2 = (f32[2,104,512]{2,1,0:T(8,128)S(1)}, f32[2,104,512]{2,1,0:T(8,128)S(1)}, u32[]{:S(2)}, u32[]{:S(2)}) collective-permute-start(f32[2,104,512]{2,1,0:T(8,128)S(1)} %pad_maximum_fusion.1), channel_id=1, source_target_pairs={{16,32},{48,64},{80,96},{112,128},{144,160},{176,192},{208,224},{2... | collective-permute-start | bytes 1277960 | tf_op jit(solution)/shard_map/ppermute | solution.py:371
  21.1 3.6 %collective-permute-start.1 = (f32[2,104,512]{2,1,0:T(8,128)S(1)}, f32[2,104,512]{2,1,0:T(8,128)S(1)}, u32[]{:S(2)}, u32[]{:S(2)}) collective-permute-start(f32[2,104,512]{2,1,0:T(8,128)S(1)} %pad_maximum_fusion), channel_id=1, source_target_pairs={{0,16},{16,0},{1,17},{17,1},{2,18},{18,2},{3,19},{19,3},{4,20},{20... | collective-permute-start | bytes 1277960 | tf_op jit(solution)/shard_map/ppermute | solution.py:364
  24.7 2.5 %collective-permute-done.3.main_a_ref = f32[2,104,512]{2,1,0:T(8,128)S(1)} collective-permute-done((f32[2,104,512]{2,1,0:T(8,128)}, f32[2,104,512]{2,1,0:T(8,128)S(1)}, u32[]{:S(2)}, u32[]{:S(2)}) %collective-permute-start.3) | collective-permute-done | bytes 426016 | tf_op jit(solution)/shard_map/ppermute | solution.py:404
  27.3 2.1 %collective-permute-start.6 = (f32[2,104,512]{2,1,0:T(8,128)S(1)}, f32[2,104,512]{2,1,0:T(8,128)S(1)}, u32[]{:S(2)}, u32[]{:S(2)}) collective-permute-start(f32[2,104,512]{2,1,0:T(8,128)S(1)} %pad_maximum_fusion.3), channel_id=1, source_target_pairs={{16,32},{48,64},{80,96},{112,128},{144,160},{176,192},{208,224},{2... | collective-permute-start | bytes 1277960 | tf_op jit(solution)/shard_map/ppermute | solution.py:371
  29.5 3.6 %collective-permute-start.5 = (f32[2,104,512]{2,1,0:T(8,128)S(1)}, f32[2,104,512]{2,1,0:T(8,128)S(1)}, u32[]{:S(2)}, u32[]{:S(2)}) collective-permute-start(f32[2,104,512]{2,1,0:T(8,128)S(1)} %pad_maximum_fusion.2), channel_id=1, source_target_pairs={{0,16},{16,0},{1,17},{17,1},{2,18},{18,2},{3,19},{19,3},{4,20},{20... | collective-permute-start | bytes 1277960 | tf_op jit(solution)/shard_map/ppermute | solution.py:364
  33.1 2.9 %energy.2.refs_0_.logit_a_ref = f32[4,64,640]{2,1,0:T(8,128)S(1)} custom-call(s32[3]{0:T(128)S(1)} %pad_add_fusion.place_ref, f32[2,104,512]{2,1,0:T(8,128)S(1)} %copy-done.1, f32[2,104,512]{2,1,0:T(8,128)S(1)} %collective-permute-done.main_b_ref, f32[2,104,512]{2,1,0:T(8,128)S(1)} %collective-permute-done.1.near_ref, ...), custom_call_target="tpu_custom_call" | custom-call | flops 2000000000 | bytes 6000000 | tf_op jit(solution)/shard_map/energy/pallas_call | solution.py:411
  36.9 3.1 %energy.3 = (f32[4,64,640]{2,1,0:T(8,128)S(1)}, f32[30,8,128]{2,1,0:T(8,128)S(1)}) custom-call(s32[3]{0:T(128)S(1)} %pad_add_fusion.place_ref, f32[2,104,512]{2,1,0:T(8,128)S(1)} %collective-permute-done.3.main_a_ref, f32[2,104,512]{2,1,0:T(8,128)S(1)} %collective-permute-done.4.main_b_ref, f32[2,104,512]{2,1,0:T(8,128)S(1)} %collective-permute-done.5.near_ref, ...), custom_call_target="tpu_custom_call" | custom-call | flops 2000000000 | bytes 6000000 | tf_op jit(solution)/shard_map/energy/pallas_call | solution.py:411
  40.0 9.1 %collective-permute-start.7 = (f32[30,8,128]{2,1,0:T(8,128)S(1)}, f32[30,8,128]{2,1,0:T(8,128)S(1)}, u32[]{:S(2)}, u32[]{:S(2)}) collective-permute-start(f32[30,8,128]{2,1,0:T(8,128)S(1)} %get-tuple-element.44), channel_id=1, source_target_pairs={{0,4},{4,0},{8,12},{12,8},{16,28},{20,24},{24,20},{28,16},{1,5},{5... | collective-permute-start | bytes 368648 | tf_op jit(solution)/shard_map/ppermute | solution.py:376
  49.2 3.5 %pyramid.2 = (f32[384,512]{1,0:T(8,128)S(1)}, f32[384,384]{1,0:T(8,128)S(1)}, f32[192,256]{1,0:T(8,128)S(1)}) custom-call(s32[3]{0:T(128)S(1)} %pad_add_fusion.place_ref, f32[2,104,512]{2,1,0:T(8,128)S(1)} %copy-done.1, f32[2,104,512]{2,1,0:T(8,128)S(1)} %collective-permute-done.main_b_ref, f32[2,104,512]{2,1,0:T(8,128)S(1)} %collective-permute-done.1.near_ref, ...), custom_call_target="tpu_custom_call" | custom-call | flops 2000000000 | bytes 6000000 | tf_op jit(solution)/shard_map/pyramid/pallas_call | solution.py:441
  52.8 11.9 %collective-permute-start.8 = (f32[30,8,128]{2,1,0:T(8,128)S(1)}, f32[30,8,128]{2,1,0:T(8,128)S(1)}, u32[]{:S(2)}, u32[]{:S(2)}) collective-permute-start(f32[30,8,128]{2,1,0:T(8,128)S(1)} %log_add_fusion.1), channel_id=1, source_target_pairs={{0,12},{4,8},{8,4},{12,0},{16,20},{20,16},{24,28},{28,24},{1,13},{... | collective-permute-start | bytes 368648 | tf_op jit(solution)/shard_map/ppermute | solution.py:376
  64.6 3.5 %pyramid.3 = (f32[384,512]{1,0:T(8,128)S(1)}, f32[384,384]{1,0:T(8,128)S(1)}, f32[192,256]{1,0:T(8,128)S(1)}) custom-call(s32[3]{0:T(128)S(1)} %pad_add_fusion.place_ref, f32[2,104,512]{2,1,0:T(8,128)S(1)} %collective-permute-done.3.main_a_ref, f32[2,104,512]{2,1,0:T(8,128)S(1)} %collective-permute-done.4.main_b_ref, ...), custom_call_target="tpu_custom_call" | custom-call | flops 2000000000 | bytes 6000000 | tf_op jit(solution)/shard_map/pyramid/pallas_call | solution.py:441
  69.1 2.8 %mix.1 = (f32[3,32,256]{2,1,0:T(8,128)S(1)}, f32[3,32,256]{2,1,0:T(8,128)S(1)}) custom-call(s32[3]{0:T(128)S(1)} %pad_add_fusion.place_ref, f32[4,64,640]{2,1,0:T(8,128)S(1)} %energy.2.refs_0_.logit_a_ref, f32[4,64,640]{2,1,0:T(8,128)S(1)} %get-tuple-element.43.logit_b_ref, f32[30,8,128]{2,1,0:T(8,128)S(1)} %log_add_fusion.lse_ref, ...), custom_call_target="tpu_custom_call" | custom-call | tf_op jit(solution)/shard_map/mix/pallas_call | solution.py:466
  71.9 10.0 %collective-permute-start.9 = (f32[3,32,256]{2,1,0:T(8,128)S(1)}, f32[3,32,256]{2,1,0:T(8,128)S(1)}, u32[]{:S(2)}, u32[]{:S(2)}) collective-permute-start(f32[3,32,256]{2,1,0:T(8,128)S(1)} %get-tuple-element.59), channel_id=1, source_target_pairs={{0,4},{4,0},{8,12},{12,8},{16,28},{20,24},{24,20},{28,16},{1,5},{5... | collective-permute-start | bytes 294920 | tf_op jit(solution)/shard_map/ppermute | solution.py:376
  81.9 5.8 %collective-permute-start.11 = (f32[3,32,256]{2,1,0:T(8,128)S(1)}, f32[3,32,256]{2,1,0:T(8,128)S(1)}, u32[]{:S(2)}, u32[]{:S(2)}) collective-permute-start(f32[3,32,256]{2,1,0:T(8,128)S(1)} %get-tuple-element.60), channel_id=1, source_target_pairs={{0,12},{4,8},{8,4},{12,0},{16,20},{20,16},{24,28},{28,24},{1,13},{... | collective-permute-start | bytes 294920 | tf_op jit(solution)/shard_map/ppermute | solution.py:376
  88.7 6.0 %collective-permute-start.10 = (f32[3,32,256]{2,1,0:T(8,128)S(1)}, f32[3,32,256]{2,1,0:T(8,128)S(1)}, u32[]{:S(2)}, u32[]{:S(2)}) collective-permute-start(f32[3,32,256]{2,1,0:T(8,128)S(1)} %add.52), channel_id=1, source_target_pairs={{0,12},{4,8},{8,4},{12,0},{16,20},{20,16},{24,28},{28,24},{1,13},{... | collective-permute-start | bytes 294920 | tf_op jit(solution)/shard_map/ppermute | solution.py:376
  94.7 8.4 %collective-permute-start.12 = (f32[3,32,256]{2,1,0:T(8,128)S(1)}, f32[3,32,256]{2,1,0:T(8,128)S(1)}, u32[]{:S(2)}, u32[]{:S(2)}) collective-permute-start(f32[3,32,256]{2,1,0:T(8,128)S(1)} %add.54), channel_id=1, source_target_pairs={{0,4},{4,0},{8,12},{12,8},{16,28},{20,24},{24,20},{28,16},{1,5},{5... | collective-permute-start | bytes 294920 | tf_op jit(solution)/shard_map/ppermute | solution.py:376
  103.2 3.3 %collective-permute-done.12 = f32[3,32,256]{2,1,0:T(8,128)S(1)} collective-permute-done((f32[3,32,256]{2,1,0:T(8,128)S(1)}, f32[3,32,256]{2,1,0:T(8,128)S(1)}, u32[]{:S(2)}, u32[]{:S(2)}) %collective-permute-start.12) | collective-permute-done | bytes 98336 | tf_op jit(solution)/shard_map/ppermute | solution.py:376
  106.6 14.7 %all_to_all.5 = f32[4,3,32,512]{3,2,1,0:T(8,128)S(1)} all-to-all(f32[4,3,32,512]{3,2,1,0:T(8,128)S(1)} %broadcast_in_dim.3), channel_id=1, replica_groups=mesh['zl'=4,'y'=4,'c'=2,'zh'=4,'x'=4] {'x'}, dimensions={0} | all-to-all | bytes 1572864 | tf_op jit(solution)/shard_map/all_to_all | solution.py:488
  (38 shorter events, 4.1 us)
Async XLA Ops:
  2.8 16.3 %collective-permute-start = (f32[2,104,512]{2,1,0:T(8,128)}, f32[2,104,512]{2,1,0:T(8,128)S(1)}, u32[]{:S(2)}, u32[]{:S(2)}) collective-permute-start(f32[2,104,512]{2,1,0:T(8,128)} %get-tuple-element.38), channel_id=1, source_target_pairs={{0,2},{1,3},{2,0},{3,1},{4,6},{5,7},{6,4},{7,5},{8,10},{9,11},{10,... | collective-permute-start | bytes 1277960 | tf_op jit(solution)/shard_map/ppermute | solution.py:404
  7.7 19.5 %collective-permute-start.3 = (f32[2,104,512]{2,1,0:T(8,128)}, f32[2,104,512]{2,1,0:T(8,128)S(1)}, u32[]{:S(2)}, u32[]{:S(2)}) collective-permute-start(f32[2,104,512]{2,1,0:T(8,128)} %get-tuple-element.39), channel_id=1, source_target_pairs={{0,1},{1,0},{2,3},{3,2},{4,5},{5,4},{6,7},{7,6},{8,9},{9,8},{10,11... | collective-permute-start | bytes 1277960 | tf_op jit(solution)/shard_map/ppermute | solution.py:404
  10.2 17.0 %collective-permute-start.4 = (f32[2,104,512]{2,1,0:T(8,128)}, f32[2,104,512]{2,1,0:T(8,128)S(1)}, u32[]{:S(2)}, u32[]{:S(2)}) collective-permute-start(f32[2,104,512]{2,1,0:T(8,128)} %get-tuple-element.40), channel_id=1, source_target_pairs={{0,3},{1,2},{2,1},{3,0},{4,7},{5,6},{6,5},{7,4},{8,11},{9,10},{10,... | collective-permute-start | bytes 1277960 | tf_op jit(solution)/shard_map/ppermute | solution.py:404
  19.2 10.2 %collective-permute-start.2 = (f32[2,104,512]{2,1,0:T(8,128)S(1)}, f32[2,104,512]{2,1,0:T(8,128)S(1)}, u32[]{:S(2)}, u32[]{:S(2)}) collective-permute-start(f32[2,104,512]{2,1,0:T(8,128)S(1)} %pad_maximum_fusion.1), channel_id=1, source_target_pairs={{16,32},{48,64},{80,96},{112,128},{144,160},{176,192},{208,224},{2... | collective-permute-start | bytes 1277960 | tf_op jit(solution)/shard_map/ppermute | solution.py:371
  21.1 12.0 %collective-permute-start.1 = (f32[2,104,512]{2,1,0:T(8,128)S(1)}, f32[2,104,512]{2,1,0:T(8,128)S(1)}, u32[]{:S(2)}, u32[]{:S(2)}) collective-permute-start(f32[2,104,512]{2,1,0:T(8,128)S(1)} %pad_maximum_fusion), channel_id=1, source_target_pairs={{0,16},{16,0},{1,17},{17,1},{2,18},{18,2},{3,19},{19,3},{4,20},{20... | collective-permute-start | bytes 1277960 | tf_op jit(solution)/shard_map/ppermute | solution.py:364
  27.2 5.9 %copy-start.1 = (f32[2,104,512]{2,1,0:T(8,128)S(1)}, f32[2,104,512]{2,1,0:T(8,128)}, u32[]{:S(2)}) copy-start(f32[2,104,512]{2,1,0:T(8,128)} %get-tuple-element.37.main_a_ref) | copy-start | bytes 1277956
  27.3 9.6 %collective-permute-start.6 = (f32[2,104,512]{2,1,0:T(8,128)S(1)}, f32[2,104,512]{2,1,0:T(8,128)S(1)}, u32[]{:S(2)}, u32[]{:S(2)}) collective-permute-start(f32[2,104,512]{2,1,0:T(8,128)S(1)} %pad_maximum_fusion.3), channel_id=1, source_target_pairs={{16,32},{48,64},{80,96},{112,128},{144,160},{176,192},{208,224},{2... | collective-permute-start | bytes 1277960 | tf_op jit(solution)/shard_map/ppermute | solution.py:371
  29.5 7.4 %collective-permute-start.5 = (f32[2,104,512]{2,1,0:T(8,128)S(1)}, f32[2,104,512]{2,1,0:T(8,128)S(1)}, u32[]{:S(2)}, u32[]{:S(2)}) collective-permute-start(f32[2,104,512]{2,1,0:T(8,128)S(1)} %pad_maximum_fusion.2), channel_id=1, source_target_pairs={{0,16},{16,0},{1,17},{17,1},{2,18},{18,2},{3,19},{19,3},{4,20},{20... | collective-permute-start | bytes 1277960 | tf_op jit(solution)/shard_map/ppermute | solution.py:364
  36.1 13.1 %copy-start = (bf16[640,384]{1,0:T(8,128)(2,1)S(1)}, bf16[640,384]{1,0:T(8,128)(2,1)}, u32[]{:S(2)}) copy-start(bf16[640,384]{1,0:T(8,128)(2,1)} %constant.55.clone.d1_ref) | copy-start | bytes 1474564
  36.1 13.1 %copy-start.2 = (bf16[384,512]{1,0:T(8,128)(2,1)S(1)}, bf16[384,512]{1,0:T(8,128)(2,1)}, u32[]{:S(2)}) copy-start(bf16[384,512]{1,0:T(8,128)(2,1)} %constant.58.clone.u1_ref) | copy-start | bytes 1179652
  36.1 13.0 %copy-start.3 = (bf16[256,384]{1,0:T(8,128)(2,1)S(1)}, bf16[256,384]{1,0:T(8,128)(2,1)}, u32[]{:S(2)}) copy-start(bf16[256,384]{1,0:T(8,128)(2,1)} %constant.57.clone.u2_ref) | copy-start | bytes 589828
  36.1 13.0 %copy-start.4 = (bf16[384,256]{1,0:T(8,128)(2,1)S(1)}, bf16[384,256]{1,0:T(8,128)(2,1)}, u32[]{:S(2)}) copy-start(bf16[384,256]{1,0:T(8,128)(2,1)} %constant.56.clone.d2_ref) | copy-start | bytes 589828
  40.0 12.7 %collective-permute-start.7 = (f32[30,8,128]{2,1,0:T(8,128)S(1)}, f32[30,8,128]{2,1,0:T(8,128)S(1)}, u32[]{:S(2)}, u32[]{:S(2)}) collective-permute-start(f32[30,8,128]{2,1,0:T(8,128)S(1)} %get-tuple-element.44), channel_id=1, source_target_pairs={{0,4},{4,0},{8,12},{12,8},{16,28},{20,24},{24,20},{28,16},{1,5},{5... | collective-permute-start | bytes 368648 | tf_op jit(solution)/shard_map/ppermute | solution.py:376
  52.8 16.2 %collective-permute-start.8 = (f32[30,8,128]{2,1,0:T(8,128)S(1)}, f32[30,8,128]{2,1,0:T(8,128)S(1)}, u32[]{:S(2)}, u32[]{:S(2)}) collective-permute-start(f32[30,8,128]{2,1,0:T(8,128)S(1)} %log_add_fusion.1), channel_id=1, source_target_pairs={{0,12},{4,8},{8,4},{12,0},{16,20},{20,16},{24,28},{28,24},{1,13},{... | collective-permute-start | bytes 368648 | tf_op jit(solution)/shard_map/ppermute | solution.py:376
  71.9 16.8 %collective-permute-start.9 = (f32[3,32,256]{2,1,0:T(8,128)S(1)}, f32[3,32,256]{2,1,0:T(8,128)S(1)}, u32[]{:S(2)}, u32[]{:S(2)}) collective-permute-start(f32[3,32,256]{2,1,0:T(8,128)S(1)} %get-tuple-element.59), channel_id=1, source_target_pairs={{0,4},{4,0},{8,12},{12,8},{16,28},{20,24},{24,20},{28,16},{1,5},{5... | collective-permute-start | bytes 294920 | tf_op jit(solution)/shard_map/ppermute | solution.py:376
  81.9 12.8 %collective-permute-start.11 = (f32[3,32,256]{2,1,0:T(8,128)S(1)}, f32[3,32,256]{2,1,0:T(8,128)S(1)}, u32[]{:S(2)}, u32[]{:S(2)}) collective-permute-start(f32[3,32,256]{2,1,0:T(8,128)S(1)} %get-tuple-element.60), channel_id=1, source_target_pairs={{0,12},{4,8},{8,4},{12,0},{16,20},{20,16},{24,28},{28,24},{1,13},{... | collective-permute-start | bytes 294920 | tf_op jit(solution)/shard_map/ppermute | solution.py:376
  88.7 14.5 %collective-permute-start.10 = (f32[3,32,256]{2,1,0:T(8,128)S(1)}, f32[3,32,256]{2,1,0:T(8,128)S(1)}, u32[]{:S(2)}, u32[]{:S(2)}) collective-permute-start(f32[3,32,256]{2,1,0:T(8,128)S(1)} %add.52), channel_id=1, source_target_pairs={{0,12},{4,8},{8,4},{12,0},{16,20},{20,16},{24,28},{28,24},{1,13},{... | collective-permute-start | bytes 294920 | tf_op jit(solution)/shard_map/ppermute | solution.py:376
  94.7 11.8 %collective-permute-start.12 = (f32[3,32,256]{2,1,0:T(8,128)S(1)}, f32[3,32,256]{2,1,0:T(8,128)S(1)}, u32[]{:S(2)}, u32[]{:S(2)}) collective-permute-start(f32[3,32,256]{2,1,0:T(8,128)S(1)} %add.54), channel_id=1, source_target_pairs={{0,4},{4,0},{8,12},{12,8},{16,28},{20,24},{24,20},{28,16},{1,5},{5... | collective-permute-start | bytes 294920 | tf_op jit(solution)/shard_map/ppermute | solution.py:376

commit v15 on v14

--- a/solution.py
+++ b/solution.py
@@ -125,7 +125,10 @@
 
 
 def energy_kernel(second, place_ref, main_a_ref, main_b_ref, near_ref, far_ref, *refs):
-    earlier_ref, logit_ref, lse_ref, grey_ref = refs if second else (None, refs[0], None, refs[1])
+    if second:
+        earlier_ref, logit_ref, lse_ref, grey_ref = refs
+    else:
+        logit_ref, part_ref, grey_ref = refs
     row = lax.broadcasted_iota(jnp.int32, (64, W0), 0) + (place_ref[0] * 32 - 16)
     col = column_of((64, W0), M0, W0) + place_ref[1] * M0
     keep = (row >= 0) & (row < 1024) & (col >= 0) & (col < 2048)
@@ -160,14 +163,19 @@
             gain = mains[s][0, 96:97, 192 + 32 * p : 193 + 32 * p]
             logit_ref[2 * s + p] = gain * field
 
+    peak = logit_ref[0]
+    for i in range(1, 4):
+        peak = jnp.maximum(peak, logit_ref[i])
     if second:
-        logits = [ref.at[i] for ref in (earlier_ref, logit_ref) for i in range(4)]
-        peak = logits[0][...]
-        for ref in logits[1:]:
-            peak = jnp.maximum(peak, ref[...])
-        total = 0.0
-        for ref in logits:
-            total = total + jnp.exp(ref[...] - peak)
+        peak = jnp.maximum(peak, earlier_ref[0])
+    total = 0.0
+    for i in range(4):
+        total = total + jnp.exp(logit_ref[i] - peak)
+    if not second:
+        part_ref[0] = peak
+        part_ref[1] = total
+    else:
+        total = total + earlier_ref[1] * jnp.exp(earlier_ref[0] - peak)
         lse = pltpu.roll(peak + jnp.log(total), 58, 0)[0:56]
         lane = lax.broadcasted_iota(jnp.int32, (8, 128), 1)
         shared = [jnp.zeros((8, 128), F32)] * 2
@@ -410,9 +418,9 @@
     def energy(step, group, *earlier):
         return pl.pallas_call(
             functools.partial(energy_kernel, step == 1),
-            out_shape=(logit_shape,) + (jax.ShapeDtypeStruct((30, 8, 128), F32),) * step,
+            out_shape=(logit_shape, jax.ShapeDtypeStruct((30, 8, 128) if step else (2, 64, W0), F32)),
             in_specs=smem() + vmem(4 + step),
-            out_specs=tuple(vmem(1 + step)),
+            out_specs=tuple(vmem(2)),
             scratch_shapes=[pltpu.VMEM((64, W0), F32)],
             compiler_params=PARAMS,
             cost_estimate=pl.CostEstimate(flops=2_000_000_000, bytes_accessed=6_000_000, transcendentals=0),
@@ -420,11 +428,11 @@
         )(place, *group, *earlier)
 
     groups = [(*mains[:2], near_rows(mains[:2], core), far[0])]
-    logits = energy(0, groups[0])
+    logits, part = energy(0, groups[0])
     late, _ = lax.optimization_barrier((mains[2:], groups[0][3]))
     groups.append((*mains[2:], near_rows(late, core), far[1]))
-    *more, lse = energy(1, groups[1], *logits)
-    logits = [*logits, *more]
+    more, lse = energy(1, groups[1], part)
+    logits = [logits, more]
 
     taps = [
         jnp.asarray(t, BF)

time: 124 us -> 124 us (level)
  the two profiles are of different devices: /device:TPU:24 before, /device:TPU:40 now
where the time goes in v15:
time: 124 us
  starting transfers between devices  64 us (52%)
  waiting for transfers between devices  25 us (20%)
  Pallas kernels  18.8 us (15%)
  blocking collectives  13.3 us (11%)
  local copies, waits for them, and re-layouts  2.23 us (2%)
    ppermute x6, starting transfers between devices, crossed(): return lax.ppermute(value, ('c', 'zh'), pairs)  43 us
    ppermute x6, waiting for transfers between devices, crossed(): return lax.ppermute(value, ('c', 'zh'), pairs)  16.5 us
    all_to_all x1, blocking collectives, on_device(): joined = lax.all_to_all(jnp.broadcast_to(whole, (4, 3, 32, 512)), 'x', 0, 0)  13.3 us
    ppermute x3, starting transfers between devices, on_device(): lax.ppermute(packed[m], 'x', [(i, i ^ FLIPS[m]) for i in range(4)])  9.9 us
    ppermute x3, waiting for transfers between devices, on_device(): lax.ppermute(packed[m], 'x', [(i, i ^ FLIPS[m]) for i in range(4)])  7.79 us
    ppermute x2, starting transfers between devices, near_rows(): return lax.ppermute(half(group, 1 - core), 'c', [(0, 1), (1, 0)])  7.18 us
    pallas_call x2, Pallas kernels, on_device(): pl.pallas_call(pyramid_kernel, out_shape=(jax.ShapeDtypeStruct((384, M0),...  7.06 us
    pallas_call x2, Pallas kernels, energy(): pl.pallas_call(functools.partial(energy_kernel, step == 1), out_shape=(lo...  6.14 us
  transfers between devices with their start and end apart: 13, of which 8 were waited for; matrix products, arithmetic and copies ran while one was open for 1% of the time, Pallas kernels for 8%

profile of v15, /device:TPU:40, one launch (start us, length us, event | category | flops | bytes accessed | tf_op | source)
XLA Modules:
  0.0 124.0 jit_solution(15588047325684783337)
XLA Ops:
  0.0 2.8 %pack.1 = (f32[2,104,512]{2,1,0:T(8,128)}, f32[2,104,512]{2,1,0:T(8,128)}, f32[2,104,512]{2,1,0:T(8,128)}, f32[2,104,512]{2,1,0:T(8,128)}) custom-call(s32[2,3,32,2048]{3,2,1,0:T(8,128)} %samples_ref, f32[2]{0:T(128)} %gain_hbm_ref.1), custom_call_target="tpu_custom_call" | custom-call | tf_op jit(solution)/shard_map/pack/pallas_call | solution.py:395
  2.8 4.9 %collective-permute-start = (f32[2,104,512]{2,1,0:T(8,128)}, f32[2,104,512]{2,1,0:T(8,128)S(1)}, u32[]{:S(2)}, u32[]{:S(2)}) collective-permute-start(f32[2,104,512]{2,1,0:T(8,128)} %get-tuple-element.40), channel_id=1, source_target_pairs={{0,2},{1,3},{2,0},{3,1},{4,6},{5,7},{6,4},{7,5},{8,10},{9,11},{10,... | collective-permute-start | bytes 1277960 | tf_op jit(solution)/shard_map/ppermute | solution.py:412
  7.7 2.5 %collective-permute-start.3 = (f32[2,104,512]{2,1,0:T(8,128)}, f32[2,104,512]{2,1,0:T(8,128)S(1)}, u32[]{:S(2)}, u32[]{:S(2)}) collective-permute-start(f32[2,104,512]{2,1,0:T(8,128)} %get-tuple-element.42), channel_id=1, source_target_pairs={{0,1},{1,0},{2,3},{3,2},{4,5},{5,4},{6,7},{7,6},{8,9},{9,8},{10,11... | collective-permute-start | bytes 1277960 | tf_op jit(solution)/shard_map/ppermute | solution.py:412
  10.2 2.5 %collective-permute-start.4 = (f32[2,104,512]{2,1,0:T(8,128)}, f32[2,104,512]{2,1,0:T(8,128)S(1)}, u32[]{:S(2)}, u32[]{:S(2)}) collective-permute-start(f32[2,104,512]{2,1,0:T(8,128)} %get-tuple-element.43), channel_id=1, source_target_pairs={{0,3},{1,2},{2,1},{3,0},{4,7},{5,6},{6,5},{7,4},{8,11},{9,10},{10,... | collective-permute-start | bytes 1277960 | tf_op jit(solution)/shard_map/ppermute | solution.py:412
  13.8 5.3 %collective-permute-done.main_b_ref = f32[2,104,512]{2,1,0:T(8,128)S(1)} collective-permute-done((f32[2,104,512]{2,1,0:T(8,128)}, f32[2,104,512]{2,1,0:T(8,128)S(1)}, u32[]{:S(2)}, u32[]{:S(2)}) %collective-permute-start) | collective-permute-done | bytes 426016 | tf_op jit(solution)/shard_map/ppermute | solution.py:412
  21.1 3.6 %collective-permute-start.1 = (f32[2,104,512]{2,1,0:T(8,128)S(1)}, f32[2,104,512]{2,1,0:T(8,128)S(1)}, u32[]{:S(2)}, u32[]{:S(2)}) collective-permute-start(f32[2,104,512]{2,1,0:T(8,128)S(1)} %pad_maximum_fusion), channel_id=1, source_target_pairs={{0,16},{16,0},{1,17},{17,1},{2,18},{18,2},{3,19},{19,3},{4,20},{20... | collective-permute-start | bytes 1277960 | tf_op jit(solution)/shard_map/ppermute | solution.py:372
  24.7 2.5 %collective-permute-done.3.main_a_ref = f32[2,104,512]{2,1,0:T(8,128)S(1)} collective-permute-done((f32[2,104,512]{2,1,0:T(8,128)}, f32[2,104,512]{2,1,0:T(8,128)S(1)}, u32[]{:S(2)}, u32[]{:S(2)}) %collective-permute-start.3) | collective-permute-done | bytes 426016 | tf_op jit(solution)/shard_map/ppermute | solution.py:412
  27.3 2.1 %collective-permute-start.6 = (f32[2,104,512]{2,1,0:T(8,128)S(1)}, f32[2,104,512]{2,1,0:T(8,128)S(1)}, u32[]{:S(2)}, u32[]{:S(2)}) collective-permute-start(f32[2,104,512]{2,1,0:T(8,128)S(1)} %pad_maximum_fusion.3), channel_id=1, source_target_pairs={{16,32},{48,64},{80,96},{112,128},{144,160},{176,192},{208,224},{2... | collective-permute-start | bytes 1277960 | tf_op jit(solution)/shard_map/ppermute | solution.py:379
  29.5 3.6 %collective-permute-start.5 = (f32[2,104,512]{2,1,0:T(8,128)S(1)}, f32[2,104,512]{2,1,0:T(8,128)S(1)}, u32[]{:S(2)}, u32[]{:S(2)}) collective-permute-start(f32[2,104,512]{2,1,0:T(8,128)S(1)} %pad_maximum_fusion.2), channel_id=1, source_target_pairs={{0,16},{16,0},{1,17},{17,1},{2,18},{18,2},{3,19},{19,3},{4,20},{20... | collective-permute-start | bytes 1277960 | tf_op jit(solution)/shard_map/ppermute | solution.py:372
  33.1 3.1 %energy.2 = (f32[4,64,640]{2,1,0:T(8,128)S(1)}, f32[2,64,640]{2,1,0:T(8,128)S(1)}) custom-call(s32[3]{0:T(128)S(1)} %pad_add_fusion.place_ref, f32[2,104,512]{2,1,0:T(8,128)S(1)} %copy-done.1, f32[2,104,512]{2,1,0:T(8,128)S(1)} %collective-permute-done.main_b_ref, f32[2,104,512]{2,1,0:T(8,128)S(1)} %collective-permute-done.1.near_ref, ...), custom_call_target="tpu_custom_call" | custom-call | flops 2000000000 | bytes 6000000 | tf_op jit(solution)/shard_map/energy/pallas_call | solution.py:419
  36.9 3.1 %energy.3 = (f32[4,64,640]{2,1,0:T(8,128)S(1)}, f32[30,8,128]{2,1,0:T(8,128)S(1)}) custom-call(s32[3]{0:T(128)S(1)} %pad_add_fusion.place_ref, f32[2,104,512]{2,1,0:T(8,128)S(1)} %collective-permute-done.3.main_a_ref, f32[2,104,512]{2,1,0:T(8,128)S(1)} %collective-permute-done.4.main_b_ref, f32[2,104,512]{2,1,0:T(8,128)S(1)} %collective-permute-done.5.near_ref, ...), custom_call_target="tpu_custom_call" | custom-call | flops 2000000000 | bytes 6000000 | tf_op jit(solution)/shard_map/energy/pallas_call | solution.py:419
  40.0 9.1 %collective-permute-start.7 = (f32[30,8,128]{2,1,0:T(8,128)S(1)}, f32[30,8,128]{2,1,0:T(8,128)S(1)}, u32[]{:S(2)}, u32[]{:S(2)}) collective-permute-start(f32[30,8,128]{2,1,0:T(8,128)S(1)} %get-tuple-element.48), channel_id=1, source_target_pairs={{0,4},{4,0},{8,12},{12,8},{16,28},{20,24},{24,20},{28,16},{1,5},{5... | collective-permute-start | bytes 368648 | tf_op jit(solution)/shard_map/ppermute | solution.py:384
  49.1 3.5 %pyramid.2 = (f32[384,512]{1,0:T(8,128)S(1)}, f32[384,384]{1,0:T(8,128)S(1)}, f32[192,256]{1,0:T(8,128)S(1)}) custom-call(s32[3]{0:T(128)S(1)} %pad_add_fusion.place_ref, f32[2,104,512]{2,1,0:T(8,128)S(1)} %copy-done.1, f32[2,104,512]{2,1,0:T(8,128)S(1)} %collective-permute-done.main_b_ref, f32[2,104,512]{2,1,0:T(8,128)S(1)} %collective-permute-done.1.near_ref, ...), custom_call_target="tpu_custom_call" | custom-call | flops 2000000000 | bytes 6000000 | tf_op jit(solution)/shard_map/pyramid/pallas_call | solution.py:449
  53.5 12.4 %collective-permute-start.8 = (f32[30,8,128]{2,1,0:T(8,128)S(1)}, f32[30,8,128]{2,1,0:T(8,128)S(1)}, u32[]{:S(2)}, u32[]{:S(2)}) collective-permute-start(f32[30,8,128]{2,1,0:T(8,128)S(1)} %log_add_fusion.1), channel_id=1, source_target_pairs={{0,12},{4,8},{8,4},{12,0},{16,20},{20,16},{24,28},{28,24},{1,13},{... | collective-permute-start | bytes 368648 | tf_op jit(solution)/shard_map/ppermute | solution.py:384
  66.0 3.5 %pyramid.3 = (f32[384,512]{1,0:T(8,128)S(1)}, f32[384,384]{1,0:T(8,128)S(1)}, f32[192,256]{1,0:T(8,128)S(1)}) custom-call(s32[3]{0:T(128)S(1)} %pad_add_fusion.place_ref, f32[2,104,512]{2,1,0:T(8,128)S(1)} %collective-permute-done.3.main_a_ref, f32[2,104,512]{2,1,0:T(8,128)S(1)} %collective-permute-done.4.main_b_ref, ...), custom_call_target="tpu_custom_call" | custom-call | flops 2000000000 | bytes 6000000 | tf_op jit(solution)/shard_map/pyramid/pallas_call | solution.py:449
  69.5 2.7 %collective-permute-done.8 = f32[30,8,128]{2,1,0:T(8,128)S(1)} collective-permute-done((f32[30,8,128]{2,1,0:T(8,128)S(1)}, f32[30,8,128]{2,1,0:T(8,128)S(1)}, u32[]{:S(2)}, u32[]{:S(2)}) %collective-permute-start.8) | collective-permute-done | bytes 122912 | tf_op jit(solution)/shard_map/ppermute | solution.py:384
  72.3 2.8 %mix.1 = (f32[3,32,256]{2,1,0:T(8,128)S(1)}, f32[3,32,256]{2,1,0:T(8,128)S(1)}) custom-call(s32[3]{0:T(128)S(1)} %pad_add_fusion.place_ref, f32[4,64,640]{2,1,0:T(8,128)S(1)} %get-tuple-element.41.logit_a_ref, f32[4,64,640]{2,1,0:T(8,128)S(1)} %get-tuple-element.47.logit_b_ref, f32[30,8,128]{2,1,0:T(8,128)S(1)} %log_add_fusion.lse_ref, ...), custom_call_target="tpu_custom_call" | custom-call | tf_op jit(solution)/shard_map/mix/pallas_call | solution.py:474
  75.1 3.7 %collective-permute-start.9 = (f32[3,32,256]{2,1,0:T(8,128)S(1)}, f32[3,32,256]{2,1,0:T(8,128)S(1)}, u32[]{:S(2)}, u32[]{:S(2)}) collective-permute-start(f32[3,32,256]{2,1,0:T(8,128)S(1)} %get-tuple-element.63), channel_id=1, source_target_pairs={{0,4},{4,0},{8,12},{12,8},{16,28},{20,24},{24,20},{28,16},{1,5},{5... | collective-permute-start | bytes 294920 | tf_op jit(solution)/shard_map/ppermute | solution.py:384
  78.7 7.9 %collective-permute-start.11 = (f32[3,32,256]{2,1,0:T(8,128)S(1)}, f32[3,32,256]{2,1,0:T(8,128)S(1)}, u32[]{:S(2)}, u32[]{:S(2)}) collective-permute-start(f32[3,32,256]{2,1,0:T(8,128)S(1)} %get-tuple-element.64), channel_id=1, source_target_pairs={{0,12},{4,8},{8,4},{12,0},{16,20},{20,16},{24,28},{28,24},{1,13},{... | collective-permute-start | bytes 294920 | tf_op jit(solution)/shard_map/ppermute | solution.py:384
  86.6 4.5 %collective-permute-done.9 = f32[3,32,256]{2,1,0:T(8,128)S(1)} collective-permute-done((f32[3,32,256]{2,1,0:T(8,128)S(1)}, f32[3,32,256]{2,1,0:T(8,128)S(1)}, u32[]{:S(2)}, u32[]{:S(2)}) %collective-permute-start.9) | collective-permute-done | bytes 98336 | tf_op jit(solution)/shard_map/ppermute | solution.py:384
  91.1 4.3 %collective-permute-start.10 = (f32[3,32,256]{2,1,0:T(8,128)S(1)}, f32[3,32,256]{2,1,0:T(8,128)S(1)}, u32[]{:S(2)}, u32[]{:S(2)}) collective-permute-start(f32[3,32,256]{2,1,0:T(8,128)S(1)} %add.52), channel_id=1, source_target_pairs={{0,12},{4,8},{8,4},{12,0},{16,20},{20,16},{24,28},{28,24},{1,13},{... | collective-permute-start | bytes 294920 | tf_op jit(solution)/shard_map/ppermute | solution.py:384
  95.5 5.5 %collective-permute-start.12 = (f32[3,32,256]{2,1,0:T(8,128)S(1)}, f32[3,32,256]{2,1,0:T(8,128)S(1)}, u32[]{:S(2)}, u32[]{:S(2)}) collective-permute-start(f32[3,32,256]{2,1,0:T(8,128)S(1)} %add.54), channel_id=1, source_target_pairs={{0,4},{4,0},{8,12},{12,8},{16,28},{20,24},{24,20},{28,16},{1,5},{5... | collective-permute-start | bytes 294920 | tf_op jit(solution)/shard_map/ppermute | solution.py:384
  102.0 7.6 %collective-permute-done.12 = f32[3,32,256]{2,1,0:T(8,128)S(1)} collective-permute-done((f32[3,32,256]{2,1,0:T(8,128)S(1)}, f32[3,32,256]{2,1,0:T(8,128)S(1)}, u32[]{:S(2)}, u32[]{:S(2)}) %collective-permute-start.12) | collective-permute-done | bytes 98336 | tf_op jit(solution)/shard_map/ppermute | solution.py:384
  109.7 13.3 %all_to_all.5 = f32[4,3,32,512]{3,2,1,0:T(8,128)S(1)} all-to-all(f32[4,3,32,512]{3,2,1,0:T(8,128)S(1)} %broadcast_in_dim.3), channel_id=1, replica_groups=mesh['zl'=4,'y'=4,'c'=2,'zh'=4,'x'=4] {'x'}, dimensions={0} | all-to-all | bytes 1572864 | tf_op jit(solution)/shard_map/all_to_all | solution.py:496
  (38 shorter events, 6.9 us)
Async XLA Ops:
  2.8 16.3 %collective-permute-start = (f32[2,104,512]{2,1,0:T(8,128)}, f32[2,104,512]{2,1,0:T(8,128)S(1)}, u32[]{:S(2)}, u32[]{:S(2)}) collective-permute-start(f32[2,104,512]{2,1,0:T(8,128)} %get-tuple-element.40), channel_id=1, source_target_pairs={{0,2},{1,3},{2,0},{3,1},{4,6},{5,7},{6,4},{7,5},{8,10},{9,11},{10,... | collective-permute-start | bytes 1277960 | tf_op jit(solution)/shard_map/ppermute | solution.py:412
  7.7 19.5 %collective-permute-start.3 = (f32[2,104,512]{2,1,0:T(8,128)}, f32[2,104,512]{2,1,0:T(8,128)S(1)}, u32[]{:S(2)}, u32[]{:S(2)}) collective-permute-start(f32[2,104,512]{2,1,0:T(8,128)} %get-tuple-element.42), channel_id=1, source_target_pairs={{0,1},{1,0},{2,3},{3,2},{4,5},{5,4},{6,7},{7,6},{8,9},{9,8},{10,11... | collective-permute-start | bytes 1277960 | tf_op jit(solution)/shard_map/ppermute | solution.py:412
  10.2 17.0 %collective-permute-start.4 = (f32[2,104,512]{2,1,0:T(8,128)}, f32[2,104,512]{2,1,0:T(8,128)S(1)}, u32[]{:S(2)}, u32[]{:S(2)}) collective-permute-start(f32[2,104,512]{2,1,0:T(8,128)} %get-tuple-element.43), channel_id=1, source_target_pairs={{0,3},{1,2},{2,1},{3,0},{4,7},{5,6},{6,5},{7,4},{8,11},{9,10},{10,... | collective-permute-start | bytes 1277960 | tf_op jit(solution)/shard_map/ppermute | solution.py:412
  19.2 10.2 %collective-permute-start.2 = (f32[2,104,512]{2,1,0:T(8,128)S(1)}, f32[2,104,512]{2,1,0:T(8,128)S(1)}, u32[]{:S(2)}, u32[]{:S(2)}) collective-permute-start(f32[2,104,512]{2,1,0:T(8,128)S(1)} %pad_maximum_fusion.1), channel_id=1, source_target_pairs={{16,32},{48,64},{80,96},{112,128},{144,160},{176,192},{208,224},{2... | collective-permute-start | bytes 1277960 | tf_op jit(solution)/shard_map/ppermute | solution.py:379
  21.1 12.0 %collective-permute-start.1 = (f32[2,104,512]{2,1,0:T(8,128)S(1)}, f32[2,104,512]{2,1,0:T(8,128)S(1)}, u32[]{:S(2)}, u32[]{:S(2)}) collective-permute-start(f32[2,104,512]{2,1,0:T(8,128)S(1)} %pad_maximum_fusion), channel_id=1, source_target_pairs={{0,16},{16,0},{1,17},{17,1},{2,18},{18,2},{3,19},{19,3},{4,20},{20... | collective-permute-start | bytes 1277960 | tf_op jit(solution)/shard_map/ppermute | solution.py:372
  27.2 5.9 %copy-start.1 = (f32[2,104,512]{2,1,0:T(8,128)S(1)}, f32[2,104,512]{2,1,0:T(8,128)}, u32[]{:S(2)}) copy-start(f32[2,104,512]{2,1,0:T(8,128)} %get-tuple-element.39.main_a_ref) | copy-start | bytes 1277956
  27.3 9.6 %collective-permute-start.6 = (f32[2,104,512]{2,1,0:T(8,128)S(1)}, f32[2,104,512]{2,1,0:T(8,128)S(1)}, u32[]{:S(2)}, u32[]{:S(2)}) collective-permute-start(f32[2,104,512]{2,1,0:T(8,128)S(1)} %pad_maximum_fusion.3), channel_id=1, source_target_pairs={{16,32},{48,64},{80,96},{112,128},{144,160},{176,192},{208,224},{2... | collective-permute-start | bytes 1277960 | tf_op jit(solution)/shard_map/ppermute | solution.py:379
  29.5 7.4 %collective-permute-start.5 = (f32[2,104,512]{2,1,0:T(8,128)S(1)}, f32[2,104,512]{2,1,0:T(8,128)S(1)}, u32[]{:S(2)}, u32[]{:S(2)}) collective-permute-start(f32[2,104,512]{2,1,0:T(8,128)S(1)} %pad_maximum_fusion.2), channel_id=1, source_target_pairs={{0,16},{16,0},{1,17},{17,1},{2,18},{18,2},{3,19},{19,3},{4,20},{20... | collective-permute-start | bytes 1277960 | tf_op jit(solution)/shard_map/ppermute | solution.py:372
  36.9 12.2 %copy-start = (bf16[640,384]{1,0:T(8,128)(2,1)S(1)}, bf16[640,384]{1,0:T(8,128)(2,1)}, u32[]{:S(2)}) copy-start(bf16[640,384]{1,0:T(8,128)(2,1)} %constant.55.clone.d1_ref) | copy-start | bytes 1474564
  36.9 12.2 %copy-start.2 = (bf16[384,512]{1,0:T(8,128)(2,1)S(1)}, bf16[384,512]{1,0:T(8,128)(2,1)}, u32[]{:S(2)}) copy-start(bf16[384,512]{1,0:T(8,128)(2,1)} %constant.58.clone.u1_ref) | copy-start | bytes 1179652
  36.9 12.2 %copy-start.3 = (bf16[256,384]{1,0:T(8,128)(2,1)S(1)}, bf16[256,384]{1,0:T(8,128)(2,1)}, u32[]{:S(2)}) copy-start(bf16[256,384]{1,0:T(8,128)(2,1)} %constant.57.clone.u2_ref) | copy-start | bytes 589828
  36.9 12.2 %copy-start.4 = (bf16[384,256]{1,0:T(8,128)(2,1)S(1)}, bf16[384,256]{1,0:T(8,128)(2,1)}, u32[]{:S(2)}) copy-start(bf16[384,256]{1,0:T(8,128)(2,1)} %constant.56.clone.d2_ref) | copy-start | bytes 589828
  40.0 13.5 %collective-permute-start.7 = (f32[30,8,128]{2,1,0:T(8,128)S(1)}, f32[30,8,128]{2,1,0:T(8,128)S(1)}, u32[]{:S(2)}, u32[]{:S(2)}) collective-permute-start(f32[30,8,128]{2,1,0:T(8,128)S(1)} %get-tuple-element.48), channel_id=1, source_target_pairs={{0,4},{4,0},{8,12},{12,8},{16,28},{20,24},{24,20},{28,16},{1,5},{5... | collective-permute-start | bytes 368648 | tf_op jit(solution)/shard_map/ppermute | solution.py:384
  53.5 18.7 %collective-permute-start.8 = (f32[30,8,128]{2,1,0:T(8,128)S(1)}, f32[30,8,128]{2,1,0:T(8,128)S(1)}, u32[]{:S(2)}, u32[]{:S(2)}) collective-permute-start(f32[30,8,128]{2,1,0:T(8,128)S(1)} %log_add_fusion.1), channel_id=1, source_target_pairs={{0,12},{4,8},{8,4},{12,0},{16,20},{20,16},{24,28},{28,24},{1,13},{... | collective-permute-start | bytes 368648 | tf_op jit(solution)/shard_map/ppermute | solution.py:384
  75.1 16.0 %collective-permute-start.9 = (f32[3,32,256]{2,1,0:T(8,128)S(1)}, f32[3,32,256]{2,1,0:T(8,128)S(1)}, u32[]{:S(2)}, u32[]{:S(2)}) collective-permute-start(f32[3,32,256]{2,1,0:T(8,128)S(1)} %get-tuple-element.63), channel_id=1, source_target_pairs={{0,4},{4,0},{8,12},{12,8},{16,28},{20,24},{24,20},{28,16},{1,5},{5... | collective-permute-start | bytes 294920 | tf_op jit(solution)/shard_map/ppermute | solution.py:384
  78.7 16.7 %collective-permute-start.11 = (f32[3,32,256]{2,1,0:T(8,128)S(1)}, f32[3,32,256]{2,1,0:T(8,128)S(1)}, u32[]{:S(2)}, u32[]{:S(2)}) collective-permute-start(f32[3,32,256]{2,1,0:T(8,128)S(1)} %get-tuple-element.64), channel_id=1, source_target_pairs={{0,12},{4,8},{8,4},{12,0},{16,20},{20,16},{24,28},{28,24},{1,13},{... | collective-permute-start | bytes 294920 | tf_op jit(solution)/shard_map/ppermute | solution.py:384
  91.1 10.8 %collective-permute-start.10 = (f32[3,32,256]{2,1,0:T(8,128)S(1)}, f32[3,32,256]{2,1,0:T(8,128)S(1)}, u32[]{:S(2)}, u32[]{:S(2)}) collective-permute-start(f32[3,32,256]{2,1,0:T(8,128)S(1)} %add.52), channel_id=1, source_target_pairs={{0,12},{4,8},{8,4},{12,0},{16,20},{20,16},{24,28},{28,24},{1,13},{... | collective-permute-start | bytes 294920 | tf_op jit(solution)/shard_map/ppermute | solution.py:384
  95.5 14.1 %collective-permute-start.12 = (f32[3,32,256]{2,1,0:T(8,128)S(1)}, f32[3,32,256]{2,1,0:T(8,128)S(1)}, u32[]{:S(2)}, u32[]{:S(2)}) collective-permute-start(f32[3,32,256]{2,1,0:T(8,128)S(1)} %add.54), channel_id=1, source_target_pairs={{0,4},{4,0},{8,12},{12,8},{16,28},{20,24},{24,20},{28,16},{1,5},{5... | collective-permute-start | bytes 294920 | tf_op jit(solution)/shard_map/ppermute | solution.py:384

commit v16 on v14

--- a/solution.py
+++ b/solution.py
@@ -376,6 +376,14 @@
     return lax.ppermute(value, ("c", "zh"), pairs)
 
 
+def woven(value, flips):
+    pairs = [
+        (8 * low + 4 * c + i, 8 * low + 4 * c + (i ^ flips[(low + c) % 2]))
+        for low in range(4) for c in range(2) for i in range(4)
+    ]
+    return lax.ppermute(value, ("zl", "c", "zh"), pairs)
+
+
 def join_lse(a, b):
     return jnp.maximum(a, b) + jnp.log(1.0 + jnp.exp(-jnp.abs(a - b)))
 
@@ -482,7 +490,7 @@
     )(place, *logits, lse, *details, *taps)
 
     for a, b in ((1, 3), (3, 1)):
-        left_in, right_in = crossed(left, (a, b)), crossed(right, (b, a))
+        left_in, right_in = woven(left, (a, b)), woven(right, (b, a))
         left, right = left + left_in, right + right_in
     whole = jnp.concatenate([left, right], axis=-1)
     joined = lax.all_to_all(jnp.broadcast_to(whole, (4, 3, 32, 512)), "x", 0, 0)

time: 124 us -> 123 us (level); the launches traced: 122 us -> 123 us
    ppermute x0 -> x4, starting transfers between devices: none -> 30.5 us  [woven(): return lax.ppermute(value, ('zl', 'c', 'zh'), pairs)]
    ppermute x6 -> x2, starting transfers between devices: 51.2 us -> 21 us  [crossed(): return lax.ppermute(value, ('c', 'zh'), pairs)]
    ppermute x6 -> x2, waiting for transfers between devices: 5.09 us -> 0.82 us  [crossed(): return lax.ppermute(value, ('c', 'zh'), pairs)]
    ppermute x0 -> x4, waiting for transfers between devices: none -> 3.73 us  [woven(): return lax.ppermute(value, ('zl', 'c', 'zh'), pairs)]
where the time goes in v16:
time: 123 us
  starting transfers between devices  72.5 us (59%)
  Pallas kernels  18.7 us (15%)
  blocking collectives  15.3 us (12%)
  waiting for transfers between devices  13.1 us (11%)
  local copies, waits for them, and re-layouts  2.24 us (2%)
    ppermute x4, starting transfers between devices, woven(): return lax.ppermute(value, ('zl', 'c', 'zh'), pairs)  30.5 us
    ppermute x2, starting transfers between devices, crossed(): return lax.ppermute(value, ('c', 'zh'), pairs)  21 us
    all_to_all x1, blocking collectives, on_device(): joined = lax.all_to_all(jnp.broadcast_to(whole, (4, 3, 32, 512)), 'x', 0, 0)  15.3 us
    ppermute x3, starting transfers between devices, on_device(): lax.ppermute(packed[m], 'x', [(i, i ^ FLIPS[m]) for i in range(4)])  9.9 us
    ppermute x3, waiting for transfers between devices, on_device(): lax.ppermute(packed[m], 'x', [(i, i ^ FLIPS[m]) for i in range(4)])  7.79 us
    ppermute x2, starting transfers between devices, near_rows(): return lax.ppermute(half(group, 1 - core), 'c', [(0, 1), (1, 0)])  7.18 us
    pallas_call x2, Pallas kernels, on_device(): pl.pallas_call(pyramid_kernel, out_shape=(jax.ShapeDtypeStruct((384, M0),...  7.07 us
    pallas_call x2, Pallas kernels, energy(): pl.pallas_call(functools.partial(energy_kernel, step == 1), out_shape=(lo...  6.05 us
  transfers between devices with their start and end apart: 13, of which 6 were waited for; matrix products, arithmetic and copies ran while one was open for 1% of the time, Pallas kernels for 8%

profile of v16, /device:TPU:24, one launch (start us, length us, event | category | flops | bytes accessed | tf_op | source)
XLA Modules:
  0.0 122.6 jit_solution(9518067145041842184)
XLA Ops:
  0.0 2.8 %pack.1 = (f32[2,104,512]{2,1,0:T(8,128)}, f32[2,104,512]{2,1,0:T(8,128)}, f32[2,104,512]{2,1,0:T(8,128)}, f32[2,104,512]{2,1,0:T(8,128)}) custom-call(s32[2,3,32,2048]{3,2,1,0:T(8,128)} %samples_ref, f32[2]{0:T(128)} %gain_hbm_ref.1), custom_call_target="tpu_custom_call" | custom-call | tf_op jit(solution)/shard_map/pack/pallas_call | solution.py:395
  2.8 4.9 %collective-permute-start = (f32[2,104,512]{2,1,0:T(8,128)}, f32[2,104,512]{2,1,0:T(8,128)S(1)}, u32[]{:S(2)}, u32[]{:S(2)}) collective-permute-start(f32[2,104,512]{2,1,0:T(8,128)} %get-tuple-element.38), channel_id=1, source_target_pairs={{0,2},{1,3},{2,0},{3,1},{4,6},{5,7},{6,4},{7,5},{8,10},{9,11},{10,... | collective-permute-start | bytes 1277960 | tf_op jit(solution)/shard_map/ppermute | solution.py:412
  7.7 2.5 %collective-permute-start.3 = (f32[2,104,512]{2,1,0:T(8,128)}, f32[2,104,512]{2,1,0:T(8,128)S(1)}, u32[]{:S(2)}, u32[]{:S(2)}) collective-permute-start(f32[2,104,512]{2,1,0:T(8,128)} %get-tuple-element.39), channel_id=1, source_target_pairs={{0,1},{1,0},{2,3},{3,2},{4,5},{5,4},{6,7},{7,6},{8,9},{9,8},{10,11... | collective-permute-start | bytes 1277960 | tf_op jit(solution)/shard_map/ppermute | solution.py:412
  10.2 2.5 %collective-permute-start.4 = (f32[2,104,512]{2,1,0:T(8,128)}, f32[2,104,512]{2,1,0:T(8,128)S(1)}, u32[]{:S(2)}, u32[]{:S(2)}) collective-permute-start(f32[2,104,512]{2,1,0:T(8,128)} %get-tuple-element.40), channel_id=1, source_target_pairs={{0,3},{1,2},{2,1},{3,0},{4,7},{5,6},{6,5},{7,4},{8,11},{9,10},{10,... | collective-permute-start | bytes 1277960 | tf_op jit(solution)/shard_map/ppermute | solution.py:412
  12.7 1.1 constant_dynamic-slice_fusion.5
  13.8 5.3 %collective-permute-done.main_b_ref = f32[2,104,512]{2,1,0:T(8,128)S(1)} collective-permute-done((f32[2,104,512]{2,1,0:T(8,128)}, f32[2,104,512]{2,1,0:T(8,128)S(1)}, u32[]{:S(2)}, u32[]{:S(2)}) %collective-permute-start) | collective-permute-done | bytes 426016 | tf_op jit(solution)/shard_map/ppermute | solution.py:412
  19.2 1.9 %collective-permute-start.2 = (f32[2,104,512]{2,1,0:T(8,128)S(1)}, f32[2,104,512]{2,1,0:T(8,128)S(1)}, u32[]{:S(2)}, u32[]{:S(2)}) collective-permute-start(f32[2,104,512]{2,1,0:T(8,128)S(1)} %pad_maximum_fusion.1), channel_id=1, source_target_pairs={{16,32},{48,64},{80,96},{112,128},{144,160},{176,192},{208,224},{2... | collective-permute-start | bytes 1277960 | tf_op jit(solution)/shard_map/ppermute | solution.py:371
  21.1 3.6 %collective-permute-start.1 = (f32[2,104,512]{2,1,0:T(8,128)S(1)}, f32[2,104,512]{2,1,0:T(8,128)S(1)}, u32[]{:S(2)}, u32[]{:S(2)}) collective-permute-start(f32[2,104,512]{2,1,0:T(8,128)S(1)} %pad_maximum_fusion), channel_id=1, source_target_pairs={{0,16},{16,0},{1,17},{17,1},{2,18},{18,2},{3,19},{19,3},{4,20},{20... | collective-permute-start | bytes 1277960 | tf_op jit(solution)/shard_map/ppermute | solution.py:364
  24.7 2.5 %collective-permute-done.3.main_a_ref = f32[2,104,512]{2,1,0:T(8,128)S(1)} collective-permute-done((f32[2,104,512]{2,1,0:T(8,128)}, f32[2,104,512]{2,1,0:T(8,128)S(1)}, u32[]{:S(2)}, u32[]{:S(2)}) %collective-permute-start.3) | collective-permute-done | bytes 426016 | tf_op jit(solution)/shard_map/ppermute | solution.py:412
  27.3 2.1 %collective-permute-start.6 = (f32[2,104,512]{2,1,0:T(8,128)S(1)}, f32[2,104,512]{2,1,0:T(8,128)S(1)}, u32[]{:S(2)}, u32[]{:S(2)}) collective-permute-start(f32[2,104,512]{2,1,0:T(8,128)S(1)} %pad_maximum_fusion.3), channel_id=1, source_target_pairs={{16,32},{48,64},{80,96},{112,128},{144,160},{176,192},{208,224},{2... | collective-permute-start | bytes 1277960 | tf_op jit(solution)/shard_map/ppermute | solution.py:371
  29.5 3.6 %collective-permute-start.5 = (f32[2,104,512]{2,1,0:T(8,128)S(1)}, f32[2,104,512]{2,1,0:T(8,128)S(1)}, u32[]{:S(2)}, u32[]{:S(2)}) collective-permute-start(f32[2,104,512]{2,1,0:T(8,128)S(1)} %pad_maximum_fusion.2), channel_id=1, source_target_pairs={{0,16},{16,0},{1,17},{17,1},{2,18},{18,2},{3,19},{19,3},{4,20},{20... | collective-permute-start | bytes 1277960 | tf_op jit(solution)/shard_map/ppermute | solution.py:364
  33.1 2.9 %energy.2.refs_0_.logit_a_ref = f32[4,64,640]{2,1,0:T(8,128)S(1)} custom-call(s32[3]{0:T(128)S(1)} %pad_add_fusion.place_ref, f32[2,104,512]{2,1,0:T(8,128)S(1)} %copy-done.1, f32[2,104,512]{2,1,0:T(8,128)S(1)} %collective-permute-done.main_b_ref, f32[2,104,512]{2,1,0:T(8,128)S(1)} %collective-permute-done.1.near_ref, ...), custom_call_target="tpu_custom_call" | custom-call | flops 2000000000 | bytes 6000000 | tf_op jit(solution)/shard_map/energy/pallas_call | solution.py:419
  36.9 3.1 %energy.3 = (f32[4,64,640]{2,1,0:T(8,128)S(1)}, f32[30,8,128]{2,1,0:T(8,128)S(1)}) custom-call(s32[3]{0:T(128)S(1)} %pad_add_fusion.place_ref, f32[2,104,512]{2,1,0:T(8,128)S(1)} %collective-permute-done.3.main_a_ref, f32[2,104,512]{2,1,0:T(8,128)S(1)} %collective-permute-done.4.main_b_ref, f32[2,104,512]{2,1,0:T(8,128)S(1)} %collective-permute-done.5.near_ref, ...), custom_call_target="tpu_custom_call" | custom-call | flops 2000000000 | bytes 6000000 | tf_op jit(solution)/shard_map/energy/pallas_call | solution.py:419
  40.0 9.1 %collective-permute-start.7 = (f32[30,8,128]{2,1,0:T(8,128)S(1)}, f32[30,8,128]{2,1,0:T(8,128)S(1)}, u32[]{:S(2)}, u32[]{:S(2)}) collective-permute-start(f32[30,8,128]{2,1,0:T(8,128)S(1)} %get-tuple-element.44), channel_id=1, source_target_pairs={{0,4},{4,0},{8,12},{12,8},{16,28},{20,24},{24,20},{28,16},{1,5},{5... | collective-permute-start | bytes 368648 | tf_op jit(solution)/shard_map/ppermute | solution.py:376
  49.2 3.5 %pyramid.2 = (f32[384,512]{1,0:T(8,128)S(1)}, f32[384,384]{1,0:T(8,128)S(1)}, f32[192,256]{1,0:T(8,128)S(1)}) custom-call(s32[3]{0:T(128)S(1)} %pad_add_fusion.place_ref, f32[2,104,512]{2,1,0:T(8,128)S(1)} %copy-done.1, f32[2,104,512]{2,1,0:T(8,128)S(1)} %collective-permute-done.main_b_ref, f32[2,104,512]{2,1,0:T(8,128)S(1)} %collective-permute-done.1.near_ref, ...), custom_call_target="tpu_custom_call" | custom-call | flops 2000000000 | bytes 6000000 | tf_op jit(solution)/shard_map/pyramid/pallas_call | solution.py:449
  52.8 11.9 %collective-permute-start.8 = (f32[30,8,128]{2,1,0:T(8,128)S(1)}, f32[30,8,128]{2,1,0:T(8,128)S(1)}, u32[]{:S(2)}, u32[]{:S(2)}) collective-permute-start(f32[30,8,128]{2,1,0:T(8,128)S(1)} %log_add_fusion.1), channel_id=1, source_target_pairs={{0,12},{4,8},{8,4},{12,0},{16,20},{20,16},{24,28},{28,24},{1,13},{... | collective-permute-start | bytes 368648 | tf_op jit(solution)/shard_map/ppermute | solution.py:376
  64.6 3.5 %pyramid.3 = (f32[384,512]{1,0:T(8,128)S(1)}, f32[384,384]{1,0:T(8,128)S(1)}, f32[192,256]{1,0:T(8,128)S(1)}) custom-call(s32[3]{0:T(128)S(1)} %pad_add_fusion.place_ref, f32[2,104,512]{2,1,0:T(8,128)S(1)} %collective-permute-done.3.main_a_ref, f32[2,104,512]{2,1,0:T(8,128)S(1)} %collective-permute-done.4.main_b_ref, ...), custom_call_target="tpu_custom_call" | custom-call | flops 2000000000 | bytes 6000000 | tf_op jit(solution)/shard_map/pyramid/pallas_call | solution.py:449
  69.1 2.8 %mix.1 = (f32[3,32,256]{2,1,0:T(8,128)S(1)}, f32[3,32,256]{2,1,0:T(8,128)S(1)}) custom-call(s32[3]{0:T(128)S(1)} %pad_add_fusion.place_ref, f32[4,64,640]{2,1,0:T(8,128)S(1)} %energy.2.refs_0_.logit_a_ref, f32[4,64,640]{2,1,0:T(8,128)S(1)} %get-tuple-element.43.logit_b_ref, f32[30,8,128]{2,1,0:T(8,128)S(1)} %log_add_fusion.lse_ref, ...), custom_call_target="tpu_custom_call" | custom-call | tf_op jit(solution)/shard_map/mix/pallas_call | solution.py:474
  71.9 10.0 %collective-permute-start.9 = (f32[3,32,256]{2,1,0:T(8,128)S(1)}, f32[3,32,256]{2,1,0:T(8,128)S(1)}, u32[]{:S(2)}, u32[]{:S(2)}) collective-permute-start(f32[3,32,256]{2,1,0:T(8,128)S(1)} %get-tuple-element.59), channel_id=1, source_target_pairs={{0,4},{4,0},{8,12},{12,8},{16,28},{20,24},{24,20},{28,16},{128,140... | collective-permute-start | bytes 294920 | tf_op jit(solution)/shard_map/ppermute | solution.py:384
  81.9 5.8 %collective-permute-start.11 = (f32[3,32,256]{2,1,0:T(8,128)S(1)}, f32[3,32,256]{2,1,0:T(8,128)S(1)}, u32[]{:S(2)}, u32[]{:S(2)}) collective-permute-start(f32[3,32,256]{2,1,0:T(8,128)S(1)} %get-tuple-element.60), channel_id=1, source_target_pairs={{0,12},{4,8},{8,4},{12,0},{16,20},{20,16},{24,28},{28,24},{128,132... | collective-permute-start | bytes 294920 | tf_op jit(solution)/shard_map/ppermute | solution.py:384
  88.2 5.8 %collective-permute-start.10 = (f32[3,32,256]{2,1,0:T(8,128)S(1)}, f32[3,32,256]{2,1,0:T(8,128)S(1)}, u32[]{:S(2)}, u32[]{:S(2)}) collective-permute-start(f32[3,32,256]{2,1,0:T(8,128)S(1)} %add.52), channel_id=1, source_target_pairs={{0,12},{4,8},{8,4},{12,0},{16,20},{20,16},{24,28},{28,24},{128,132... | collective-permute-start | bytes 294920 | tf_op jit(solution)/shard_map/ppermute | solution.py:384
  94.1 8.9 %collective-permute-start.12 = (f32[3,32,256]{2,1,0:T(8,128)S(1)}, f32[3,32,256]{2,1,0:T(8,128)S(1)}, u32[]{:S(2)}, u32[]{:S(2)}) collective-permute-start(f32[3,32,256]{2,1,0:T(8,128)S(1)} %add.54), channel_id=1, source_target_pairs={{0,4},{4,0},{8,12},{12,8},{16,28},{20,24},{24,20},{28,16},{128,140... | collective-permute-start | bytes 294920 | tf_op jit(solution)/shard_map/ppermute | solution.py:384
  103.0 3.2 %collective-permute-done.12 = f32[3,32,256]{2,1,0:T(8,128)S(1)} collective-permute-done((f32[3,32,256]{2,1,0:T(8,128)S(1)}, f32[3,32,256]{2,1,0:T(8,128)S(1)}, u32[]{:S(2)}, u32[]{:S(2)}) %collective-permute-start.12) | collective-permute-done | bytes 98336 | tf_op jit(solution)/shard_map/ppermute | solution.py:384
  106.3 15.3 %all_to_all.5 = f32[4,3,32,512]{3,2,1,0:T(8,128)S(1)} all-to-all(f32[4,3,32,512]{3,2,1,0:T(8,128)S(1)} %broadcast_in_dim.3), channel_id=1, replica_groups=mesh['zl'=4,'y'=4,'c'=2,'zh'=4,'x'=4] {'x'}, dimensions={0} | all-to-all | bytes 1572864 | tf_op jit(solution)/shard_map/all_to_all | solution.py:496
  (38 shorter events, 3.7 us)
Async XLA Ops:
  2.8 16.3 %collective-permute-start = (f32[2,104,512]{2,1,0:T(8,128)}, f32[2,104,512]{2,1,0:T(8,128)S(1)}, u32[]{:S(2)}, u32[]{:S(2)}) collective-permute-start(f32[2,104,512]{2,1,0:T(8,128)} %get-tuple-element.38), channel_id=1, source_target_pairs={{0,2},{1,3},{2,0},{3,1},{4,6},{5,7},{6,4},{7,5},{8,10},{9,11},{10,... | collective-permute-start | bytes 1277960 | tf_op jit(solution)/shard_map/ppermute | solution.py:412
  7.7 19.5 %collective-permute-start.3 = (f32[2,104,512]{2,1,0:T(8,128)}, f32[2,104,512]{2,1,0:T(8,128)S(1)}, u32[]{:S(2)}, u32[]{:S(2)}) collective-permute-start(f32[2,104,512]{2,1,0:T(8,128)} %get-tuple-element.39), channel_id=1, source_target_pairs={{0,1},{1,0},{2,3},{3,2},{4,5},{5,4},{6,7},{7,6},{8,9},{9,8},{10,11... | collective-permute-start | bytes 1277960 | tf_op jit(solution)/shard_map/ppermute | solution.py:412
  10.2 17.0 %collective-permute-start.4 = (f32[2,104,512]{2,1,0:T(8,128)}, f32[2,104,512]{2,1,0:T(8,128)S(1)}, u32[]{:S(2)}, u32[]{:S(2)}) collective-permute-start(f32[2,104,512]{2,1,0:T(8,128)} %get-tuple-element.40), channel_id=1, source_target_pairs={{0,3},{1,2},{2,1},{3,0},{4,7},{5,6},{6,5},{7,4},{8,11},{9,10},{10,... | collective-permute-start | bytes 1277960 | tf_op jit(solution)/shard_map/ppermute | solution.py:412
  19.2 10.2 %collective-permute-start.2 = (f32[2,104,512]{2,1,0:T(8,128)S(1)}, f32[2,104,512]{2,1,0:T(8,128)S(1)}, u32[]{:S(2)}, u32[]{:S(2)}) collective-permute-start(f32[2,104,512]{2,1,0:T(8,128)S(1)} %pad_maximum_fusion.1), channel_id=1, source_target_pairs={{16,32},{48,64},{80,96},{112,128},{144,160},{176,192},{208,224},{2... | collective-permute-start | bytes 1277960 | tf_op jit(solution)/shard_map/ppermute | solution.py:371
  21.1 12.0 %collective-permute-start.1 = (f32[2,104,512]{2,1,0:T(8,128)S(1)}, f32[2,104,512]{2,1,0:T(8,128)S(1)}, u32[]{:S(2)}, u32[]{:S(2)}) collective-permute-start(f32[2,104,512]{2,1,0:T(8,128)S(1)} %pad_maximum_fusion), channel_id=1, source_target_pairs={{0,16},{16,0},{1,17},{17,1},{2,18},{18,2},{3,19},{19,3},{4,20},{20... | collective-permute-start | bytes 1277960 | tf_op jit(solution)/shard_map/ppermute | solution.py:364
  27.2 5.9 %copy-start.1 = (f32[2,104,512]{2,1,0:T(8,128)S(1)}, f32[2,104,512]{2,1,0:T(8,128)}, u32[]{:S(2)}) copy-start(f32[2,104,512]{2,1,0:T(8,128)} %get-tuple-element.37.main_a_ref) | copy-start | bytes 1277956
  27.3 9.6 %collective-permute-start.6 = (f32[2,104,512]{2,1,0:T(8,128)S(1)}, f32[2,104,512]{2,1,0:T(8,128)S(1)}, u32[]{:S(2)}, u32[]{:S(2)}) collective-permute-start(f32[2,104,512]{2,1,0:T(8,128)S(1)} %pad_maximum_fusion.3), channel_id=1, source_target_pairs={{16,32},{48,64},{80,96},{112,128},{144,160},{176,192},{208,224},{2... | collective-permute-start | bytes 1277960 | tf_op jit(solution)/shard_map/ppermute | solution.py:371
  29.5 7.4 %collective-permute-start.5 = (f32[2,104,512]{2,1,0:T(8,128)S(1)}, f32[2,104,512]{2,1,0:T(8,128)S(1)}, u32[]{:S(2)}, u32[]{:S(2)}) collective-permute-start(f32[2,104,512]{2,1,0:T(8,128)S(1)} %pad_maximum_fusion.2), channel_id=1, source_target_pairs={{0,16},{16,0},{1,17},{17,1},{2,18},{18,2},{3,19},{19,3},{4,20},{20... | collective-permute-start | bytes 1277960 | tf_op jit(solution)/shard_map/ppermute | solution.py:364
  36.1 13.1 %copy-start = (bf16[640,384]{1,0:T(8,128)(2,1)S(1)}, bf16[640,384]{1,0:T(8,128)(2,1)}, u32[]{:S(2)}) copy-start(bf16[640,384]{1,0:T(8,128)(2,1)} %constant.55.clone.d1_ref) | copy-start | bytes 1474564
  36.1 13.1 %copy-start.2 = (bf16[384,512]{1,0:T(8,128)(2,1)S(1)}, bf16[384,512]{1,0:T(8,128)(2,1)}, u32[]{:S(2)}) copy-start(bf16[384,512]{1,0:T(8,128)(2,1)} %constant.58.clone.u1_ref) | copy-start | bytes 1179652
  36.1 13.0 %copy-start.3 = (bf16[256,384]{1,0:T(8,128)(2,1)S(1)}, bf16[256,384]{1,0:T(8,128)(2,1)}, u32[]{:S(2)}) copy-start(bf16[256,384]{1,0:T(8,128)(2,1)} %constant.57.clone.u2_ref) | copy-start | bytes 589828
  36.1 13.0 %copy-start.4 = (bf16[384,256]{1,0:T(8,128)(2,1)S(1)}, bf16[384,256]{1,0:T(8,128)(2,1)}, u32[]{:S(2)}) copy-start(bf16[384,256]{1,0:T(8,128)(2,1)} %constant.56.clone.d2_ref) | copy-start | bytes 589828
  40.0 12.7 %collective-permute-start.7 = (f32[30,8,128]{2,1,0:T(8,128)S(1)}, f32[30,8,128]{2,1,0:T(8,128)S(1)}, u32[]{:S(2)}, u32[]{:S(2)}) collective-permute-start(f32[30,8,128]{2,1,0:T(8,128)S(1)} %get-tuple-element.44), channel_id=1, source_target_pairs={{0,4},{4,0},{8,12},{12,8},{16,28},{20,24},{24,20},{28,16},{1,5},{5... | collective-permute-start | bytes 368648 | tf_op jit(solution)/shard_map/ppermute | solution.py:376
  52.8 16.2 %collective-permute-start.8 = (f32[30,8,128]{2,1,0:T(8,128)S(1)}, f32[30,8,128]{2,1,0:T(8,128)S(1)}, u32[]{:S(2)}, u32[]{:S(2)}) collective-permute-start(f32[30,8,128]{2,1,0:T(8,128)S(1)} %log_add_fusion.1), channel_id=1, source_target_pairs={{0,12},{4,8},{8,4},{12,0},{16,20},{20,16},{24,28},{28,24},{1,13},{... | collective-permute-start | bytes 368648 | tf_op jit(solution)/shard_map/ppermute | solution.py:376
  71.9 16.4 %collective-permute-start.9 = (f32[3,32,256]{2,1,0:T(8,128)S(1)}, f32[3,32,256]{2,1,0:T(8,128)S(1)}, u32[]{:S(2)}, u32[]{:S(2)}) collective-permute-start(f32[3,32,256]{2,1,0:T(8,128)S(1)} %get-tuple-element.59), channel_id=1, source_target_pairs={{0,4},{4,0},{8,12},{12,8},{16,28},{20,24},{24,20},{28,16},{128,140... | collective-permute-start | bytes 294920 | tf_op jit(solution)/shard_map/ppermute | solution.py:384
  81.9 12.2 %collective-permute-start.11 = (f32[3,32,256]{2,1,0:T(8,128)S(1)}, f32[3,32,256]{2,1,0:T(8,128)S(1)}, u32[]{:S(2)}, u32[]{:S(2)}) collective-permute-start(f32[3,32,256]{2,1,0:T(8,128)S(1)} %get-tuple-element.60), channel_id=1, source_target_pairs={{0,12},{4,8},{8,4},{12,0},{16,20},{20,16},{24,28},{28,24},{128,132... | collective-permute-start | bytes 294920 | tf_op jit(solution)/shard_map/ppermute | solution.py:384
  88.2 14.8 %collective-permute-start.10 = (f32[3,32,256]{2,1,0:T(8,128)S(1)}, f32[3,32,256]{2,1,0:T(8,128)S(1)}, u32[]{:S(2)}, u32[]{:S(2)}) collective-permute-start(f32[3,32,256]{2,1,0:T(8,128)S(1)} %add.52), channel_id=1, source_target_pairs={{0,12},{4,8},{8,4},{12,0},{16,20},{20,16},{24,28},{28,24},{128,132... | collective-permute-start | bytes 294920 | tf_op jit(solution)/shard_map/ppermute | solution.py:384
  94.1 12.1 %collective-permute-start.12 = (f32[3,32,256]{2,1,0:T(8,128)S(1)}, f32[3,32,256]{2,1,0:T(8,128)S(1)}, u32[]{:S(2)}, u32[]{:S(2)}) collective-permute-start(f32[3,32,256]{2,1,0:T(8,128)S(1)} %add.54), channel_id=1, source_target_pairs={{0,4},{4,0},{8,12},{12,8},{16,28},{20,24},{24,20},{28,16},{128,140... | collective-permute-start | bytes 294920 | tf_op jit(solution)/shard_map/ppermute | solution.py:384
